TPU v7x, 32 devices: a whole 2x2x4 slice. The times are simulated.
32 devices in a mesh: dp: 4 (over y, x), hid: 4 (over z), wid: 2 (over core).
Axes of the slice: x: 2, y: 2, z: 4, core: 2. Of those that a mesh axis runs over, the one named last changes fastest.
Arguments:
- layer_in: bfloat16 [8, 1024, 1536], P('dp', ('hid', 'wid')), may hold values from -6 to 6
- segment_ids: int32 [8, 1024], P('dp', ('hid', 'wid')), may hold values from 0 to 2, never falling along the last dimension, each value on 1 to 768 neighbouring positions
- out_grad: bfloat16 [8, 1024, 1536], P('dp', ('hid', 'wid')), may hold values from -6 to 6
- gain_attn: bfloat16 [1536], P(('dp', 'hid', 'wid')), may hold values from 0.5 to 1.5
- w_query: bfloat16 [1536, 1536], P(('dp', 'hid', 'wid')), may hold values from -0.15625 to 0.15625
- w_key: bfloat16 [1536, 1536], P(('dp', 'hid', 'wid')), may hold values from -0.15625 to 0.15625
- w_value: bfloat16 [1536, 1536], P(('dp', 'hid', 'wid')), may hold values from -0.15625 to 0.15625
- w_dir: bfloat16 [1536, 1536], P(('dp', 'hid', 'wid')), may hold values from -0.15625 to 0.15625
- w_beta: bfloat16 [1536, 12], P(('dp', 'hid', 'wid')), may hold values from -0.3125 to 0.3125
- b_beta: bfloat16 [12], replicated, may hold values from -2 to 2
- w_out: bfloat16 [1536, 1536], P(('dp', 'hid', 'wid')), may hold values from -0.875 to 0.875
- gain_mlp: bfloat16 [1536], P(('dp', 'hid', 'wid')), may hold values from 0.5 to 1.5
- w_gate: bfloat16 [1536, 4096], P(('dp', 'wid'), 'hid'), may hold values from -0.15625 to 0.15625
- w_up: bfloat16 [1536, 4096], P(('dp', 'wid'), 'hid'), may hold values from -0.15625 to 0.15625
- w_down: bfloat16 [4096, 1536], P('hid', ('dp', 'wid')), may hold values from -0.09375 to 0.09375
Outputs:
- layer_out: bfloat16 [8, 1024, 1536], P('dp', ('hid', 'wid'))
- grad_in: bfloat16 [8, 1024, 1536], P('dp', ('hid', 'wid'))
- grad_gain_attn: float32 [1536], P(('dp', 'hid', 'wid'))
- grad_query: float32 [1536, 1536], P(('dp', 'hid', 'wid'))
- grad_key: float32 [1536, 1536], P(('dp', 'hid', 'wid'))
- grad_value: float32 [1536, 1536], P(('dp', 'hid', 'wid'))
- grad_dir: float32 [1536, 1536], P(('dp', 'hid', 'wid'))
- grad_beta: float32 [1536, 12], P(('dp', 'hid', 'wid'))
- grad_bias: float32 [12], replicated
- grad_out_proj: float32 [1536, 1536], P(('dp', 'hid', 'wid'))
- grad_gain_mlp: float32 [1536], P(('dp', 'hid', 'wid'))
- grad_gate: float32 [1536, 4096], P(('dp', 'wid'), 'hid')
- grad_up: float32 [1536, 4096], P(('dp', 'wid'), 'hid')
- grad_down: float32 [4096, 1536], P('hid', ('dp', 'wid'))
Inputs may be any that keep to these rules, and one draw needn't show every extreme that they name: `segment_ids`: within a row the document numbers never fall; each document has 1 to 768 tokens and one has exactly 768.
All inputs are finite; a program needn't handle non-finite values.
Results may differ from a plain program's by a relative error of at most 0.017.
Values may be sent and summed in bfloat16 or wider, within the bound.
No kernel may reach another device: no remote copies, remote signals or barrier semaphores. Data moves between devices by JAX's collectives and lax.ppermute only.
A program may use at most 512 MiB of HBM per device.

v0:
```python
import math

import jax
import jax.numpy as jnp
from jax import lax
from jax.sharding import PartitionSpec as P

EPS = 1e-06
NEG = -1e30
HIGH = lax.Precision.HIGHEST


def shifted_2(value, axis, steps):
    count = lax.axis_size(axis)
    leading, last = (max(0, -steps), min(count, count - steps))
    return lax.ppermute(value, axis, [(source, source + steps) for source in range(leading, last)])


def norm_in(tensor, gain_vec):
    return tensor * lax.rsqrt(jnp.mean(tensor * tensor, axis=-1, keepdims=True) + EPS) * gain_vec


def span_local(queries, keys_in, directions, logits):
    unit_dirs = directions * lax.rsqrt(
        jnp.sum(directions * directions, axis=-1, keepdims=True) + EPS
    )
    beta_rate = 2.0 * jax.nn.sigmoid(logits)
    block_size = queries.shape[-2]
    row_index = lax.broadcasted_iota(jnp.int32, (block_size, block_size), 0)
    col_index = lax.broadcasted_iota(jnp.int32, (block_size, block_size), 1)
    strict_mask = row_index > col_index
    lower_mask = row_index >= col_index
    dir_gram = jnp.einsum("...me,...ne->...mn", unit_dirs, unit_dirs, precision=HIGH)
    system = jnp.where(strict_mask, dir_gram, 0.0) + jnp.where(
        row_index == col_index, 1.0 / beta_rate[..., :, None], 0.0
    )
    query_dirs = jnp.where(
        lower_mask, jnp.einsum("...ie,...me->...im", queries, unit_dirs, precision=HIGH), 0.0
    )
    dirs_keys = jnp.where(
        strict_mask, jnp.einsum("...me,...je->...mj", unit_dirs, keys_in, precision=HIGH), 0.0
    )
    solved_keys = lax.linalg.triangular_solve(system, dirs_keys, left_side=True, lower=True)
    solved_query = lax.linalg.triangular_solve(system, query_dirs, left_side=False, lower=True)
    solved_dirs = lax.linalg.triangular_solve(system, unit_dirs, left_side=True, lower=True)
    intra_score = jnp.einsum("...ie,...je->...ij", queries, keys_in, precision=HIGH) - jnp.einsum(
        "...im,...mj->...ij", query_dirs, solved_keys, precision=HIGH
    )
    q_in = queries - jnp.einsum("...im,...me->...ie", solved_query, unit_dirs, precision=HIGH)
    k_out = keys_in - jnp.einsum("...mj,...me->...je", solved_keys, unit_dirs, precision=HIGH)
    identity = jnp.eye(queries.shape[-1], dtype=queries.dtype)
    transform = identity - jnp.einsum("...me,...mf->...ef", unit_dirs, solved_dirs, precision=HIGH)
    return (q_in, k_out, transform, intra_score)


def split_heads(tensor, head_count):
    row_count, tok_count, width = tensor.shape
    return tensor.reshape(row_count, tok_count, head_count, width // head_count).transpose(
        0, 2, 1, 3
    )


def merge_heads(tensor):
    row_count, head_count, tok_count, head_size = tensor.shape
    return tensor.transpose(0, 2, 1, 3).reshape(row_count, tok_count, head_count * head_size)


def per_device(
    layer_in,
    segment_ids,
    out_grad,
    gain_attn,
    w_query,
    w_key,
    w_value,
    w_dir,
    w_beta,
    b_beta,
    w_out,
    gain_mlp,
    w_gate,
    w_up,
    w_down,
):
    f32 = jnp.float32
    bf16 = jnp.bfloat16
    row_count, tok_count, width = layer_in.shape
    head_count = b_beta.shape[0]
    head_size = width // head_count
    score_scale = 1.0 / math.sqrt(head_size)
    gathered = (
        lax.all_gather(gain_attn, ("dp", "hid", "wid"), axis=0, tiled=True),
        lax.all_gather(w_query, ("dp", "hid", "wid"), axis=0, tiled=True),
        lax.all_gather(w_key, ("dp", "hid", "wid"), axis=0, tiled=True),
        lax.all_gather(w_value, ("dp", "hid", "wid"), axis=0, tiled=True),
        lax.all_gather(w_dir, ("dp", "hid", "wid"), axis=0, tiled=True),
        lax.all_gather(w_beta, ("dp", "hid", "wid"), axis=0, tiled=True),
        lax.all_gather(w_out, ("dp", "hid", "wid"), axis=0, tiled=True),
        lax.all_gather(gain_mlp, ("dp", "hid", "wid"), axis=0, tiled=True),
    )
    gain_one, wq_full, wk_full, wv_full, wdir_full, wbeta_full, wout_full, gain_two = gathered
    layer_f = layer_in.astype(f32)
    gain_onef = gain_one.astype(f32)
    act_one = norm_in(layer_f, gain_onef).astype(bf16)
    query_b = jnp.dot(act_one, wq_full, preferred_element_type=f32).astype(bf16)
    key_b = jnp.dot(act_one, wk_full, preferred_element_type=f32).astype(bf16)
    value_b = jnp.dot(act_one, wv_full, preferred_element_type=f32).astype(bf16)
    dir_raw = jnp.dot(act_one, wdir_full, preferred_element_type=f32)
    logit_raw = jnp.dot(act_one, wbeta_full, preferred_element_type=f32) + b_beta.astype(f32)
    values_h = split_heads(value_b, head_count)
    local_args = (
        split_heads(query_b, head_count).astype(f32),
        split_heads(key_b, head_count).astype(f32),
        split_heads(dir_raw, head_count),
        logit_raw.transpose(0, 2, 1),
    )
    q_in, k_out, transform, intra_score = span_local(
        local_args[0], local_args[1], local_args[2], local_args[3]
    )
    qin_b = q_in.astype(bf16)
    row_index = lax.broadcasted_iota(jnp.int32, (tok_count, tok_count), 0)
    col_index = lax.broadcasted_iota(jnp.int32, (tok_count, tok_count), 1)
    allow_intra = (
        (row_index >= col_index)[None] & (segment_ids[:, :, None] == segment_ids[:, None, :])
    )[:, None]
    intra_masked = jnp.where(allow_intra, score_scale * intra_score, NEG)
    run_max = jnp.max(intra_masked, axis=-1, keepdims=True)
    run_sum = jnp.sum(jnp.exp(intra_masked - run_max), axis=-1, keepdims=True)
    group_size = lax.axis_size(("hid", "wid"))
    my_place = lax.axis_index(("hid", "wid"))
    hop_total = group_size - 1

    def cross_score(keys_b, seg_rows, usable):
        raw_score = score_scale * jnp.einsum(
            "rhie,rhje->rhij", qin_b, keys_b, preferred_element_type=f32
        )
        permit = usable & (segment_ids[:, None, :, None] == seg_rows[:, None, None, :])
        return jnp.where(permit, raw_score, NEG)

    def forward_hop(hop_index, carried):
        send_keys, send_values, send_segs, old_max, old_sum, kept_keys, kept_values, kept_segs = (
            carried
        )
        got_keys, got_values, got_segs = shifted_2(
            (send_keys, send_values, send_segs), ("hid", "wid"), 1
        )
        scores = cross_score(got_keys, got_segs, my_place >= hop_index + 1)
        new_max = jnp.maximum(old_max, jnp.max(scores, axis=-1, keepdims=True))
        new_sum = old_sum * jnp.exp(old_max - new_max) + jnp.sum(
            jnp.exp(scores - new_max), axis=-1, keepdims=True
        )
        kept_keys = lax.dynamic_update_index_in_dim(kept_keys, got_keys, hop_index, 0)
        kept_values = lax.dynamic_update_index_in_dim(kept_values, got_values, hop_index, 0)
        kept_segs = lax.dynamic_update_index_in_dim(kept_segs, got_segs, hop_index, 0)
        shifted = jnp.einsum(
            "rhjf,rhef->rhje", got_keys.astype(f32), transform, precision=HIGH
        ).astype(bf16)
        return (shifted, got_values, got_segs, new_max, new_sum, kept_keys, kept_values, kept_segs)

    kept_start = jnp.zeros((hop_total,) + values_h.shape, bf16)
    start_state = (
        k_out.astype(bf16),
        values_h,
        segment_ids,
        run_max,
        run_sum,
        kept_start,
        kept_start,
        jnp.zeros((hop_total,) + segment_ids.shape, jnp.int32),
    )
    final_state = lax.fori_loop(0, hop_total, forward_hop, start_state)
    run_max, run_sum, kept_keys, kept_values, kept_segs = (
        final_state[3],
        final_state[4],
        final_state[5],
        final_state[6],
        final_state[7],
    )

    def stored(slot_index):
        keys_b = lax.dynamic_index_in_dim(kept_keys, slot_index, 0, keepdims=False)
        vals_b = lax.dynamic_index_in_dim(kept_values, slot_index, 0, keepdims=False)
        seg_rows = lax.dynamic_index_in_dim(kept_segs, slot_index, 0, keepdims=False)
        return (keys_b, vals_b, seg_rows)

    prob_intra = jnp.exp(intra_masked - run_max) / run_sum
    attn_start = jnp.einsum(
        "rhij,rhje->rhie", prob_intra.astype(bf16), values_h, preferred_element_type=f32
    )

    def output_hop(hop_index, attn_acc):
        keys_b, vals_b, seg_rows = stored(hop_index)
        prob_vals = (
            jnp.exp(cross_score(keys_b, seg_rows, my_place >= hop_index + 1) - run_max) / run_sum
        )
        return attn_acc + jnp.einsum(
            "rhij,rhje->rhie", prob_vals.astype(bf16), vals_b, preferred_element_type=f32
        )

    attn_acc = lax.fori_loop(0, hop_total, output_hop, attn_start)
    attn_b = merge_heads(attn_acc).astype(bf16)
    middle = layer_f + jnp.dot(attn_b, wout_full, preferred_element_type=f32)
    gain_twof = gain_two.astype(f32)
    act_two = norm_in(middle, gain_twof).astype(bf16)
    gate_part, up_part, down_part = (
        lax.all_gather(w_gate, ("dp", "wid"), axis=0, tiled=True),
        lax.all_gather(w_up, ("dp", "wid"), axis=0, tiled=True),
        lax.all_gather(w_down, ("dp", "wid"), axis=1, tiled=True),
    )
    gate_all, up_all, down_all = (
        lax.all_gather(gate_part, "hid", axis=1, tiled=True),
        lax.all_gather(up_part, "hid", axis=1, tiled=True),
        lax.all_gather(down_part, "hid", axis=0, tiled=True),
    )
    gate_val = jnp.dot(act_two, gate_all, preferred_element_type=f32)
    up_val = jnp.dot(act_two, up_all, preferred_element_type=f32)
    gate_sig = jax.nn.sigmoid(gate_val)
    silu_val = gate_val * gate_sig
    hidden_b = (silu_val * up_val).astype(bf16)
    mlp_term = jnp.dot(hidden_b, down_all, preferred_element_type=f32)
    layer_out = (middle + mlp_term).astype(bf16)
    d_hidden = jnp.dot(out_grad, down_all.T, preferred_element_type=f32)
    d_down_w = jnp.einsum("rtf,rtd->fd", hidden_b, out_grad, preferred_element_type=f32)
    d_gate_b = (d_hidden * up_val * gate_sig * (1.0 + gate_val * (1.0 - gate_sig))).astype(bf16)
    d_up_b = (d_hidden * silu_val).astype(bf16)
    d_gate_w = jnp.einsum("rtd,rtf->df", act_two, d_gate_b, preferred_element_type=f32)
    d_up_w = jnp.einsum("rtd,rtf->df", act_two, d_up_b, preferred_element_type=f32)
    d_act_term = jnp.dot(d_gate_b, gate_all.T, preferred_element_type=f32) + jnp.dot(
        d_up_b, up_all.T, preferred_element_type=f32
    )
    grads_part = (
        lax.psum_scatter(
            d_gate_w.astype(jnp.bfloat16), "hid", scatter_dimension=1, tiled=True
        ).astype(jnp.float32),
        lax.psum_scatter(
            d_up_w.astype(jnp.bfloat16), "hid", scatter_dimension=1, tiled=True
        ).astype(jnp.float32),
        lax.psum_scatter(
            d_down_w.astype(jnp.bfloat16), "hid", scatter_dimension=0, tiled=True
        ).astype(jnp.float32),
    )
    grad_gate, grad_up, grad_down = (
        lax.psum_scatter(
            grads_part[0].astype(jnp.bfloat16), ("dp", "wid"), scatter_dimension=0, tiled=True
        ).astype(jnp.float32),
        lax.psum_scatter(
            grads_part[1].astype(jnp.bfloat16), ("dp", "wid"), scatter_dimension=0, tiled=True
        ).astype(jnp.float32),
        lax.psum_scatter(
            grads_part[2].astype(jnp.bfloat16), ("dp", "wid"), scatter_dimension=1, tiled=True
        ).astype(jnp.float32),
    )
    unused, norm_pull_two = jax.vjp(norm_in, middle, gain_twof)
    d_middle_norm, d_gain_two = norm_pull_two(d_act_term)
    d_middle = out_grad.astype(f32) + d_middle_norm
    d_branch_b = d_middle.astype(bf16)
    grad_out_w = jnp.einsum("rtd,rte->de", attn_b, d_branch_b, preferred_element_type=f32)
    d_attn_h = split_heads(
        jnp.dot(d_branch_b, wout_full.T, preferred_element_type=f32).astype(bf16), head_count
    )
    d_prob_intra = jnp.einsum("rhie,rhje->rhij", d_attn_h, values_h, preferred_element_type=f32)
    delta_start = jnp.sum(prob_intra * d_prob_intra, axis=-1, keepdims=True)

    def delta_hop(hop_index, delta_sum):
        keys_b, vals_b, seg_rows = stored(hop_index)
        prob_vals = (
            jnp.exp(cross_score(keys_b, seg_rows, my_place >= hop_index + 1) - run_max) / run_sum
        )
        d_prob = jnp.einsum("rhie,rhje->rhij", d_attn_h, vals_b, preferred_element_type=f32)
        return delta_sum + jnp.sum(prob_vals * d_prob, axis=-1, keepdims=True)

    delta_sum = lax.fori_loop(0, hop_total, delta_hop, delta_start)
    d_score_intra = (prob_intra * (d_prob_intra - delta_sum)).astype(bf16)
    d_val_intra = jnp.einsum(
        "rhij,rhie->rhje", prob_intra.astype(bf16), d_attn_h, preferred_element_type=f32
    )

    def backward_hop(hop_index, carried):
        send_grad, send_vgrad, d_trans, d_query = carried
        got_grad, got_vgrad = (
            shifted_2(send_grad.astype(jnp.bfloat16), ("hid", "wid"), -1).astype(send_grad.dtype),
            shifted_2(send_vgrad.astype(jnp.bfloat16), ("hid", "wid"), -1).astype(send_vgrad.dtype),
        )
        depth_now = hop_total - hop_index
        slot_index = jnp.maximum(depth_now - 1, 0)
        usable = (my_place >= depth_now) & (depth_now >= 1)
        keys_b, vals_b, seg_rows = stored(slot_index)
        prob_vals = jnp.exp(cross_score(keys_b, seg_rows, usable) - run_max) / run_sum
        d_prob = jnp.einsum("rhie,rhje->rhij", d_attn_h, vals_b, preferred_element_type=f32)
        d_score = (prob_vals * (d_prob - delta_sum)).astype(bf16)
        d_query = d_query + score_scale * jnp.einsum(
            "rhij,rhje->rhie", d_score, keys_b, preferred_element_type=f32
        )
        d_frame = score_scale * jnp.einsum(
            "rhij,rhie->rhje", d_score, qin_b, preferred_element_type=f32
        )
        d_vals = jnp.einsum(
            "rhij,rhie->rhje", prob_vals.astype(bf16), d_attn_h, preferred_element_type=f32
        )
        trans_term = jnp.einsum("rhje,rhjf->rhef", got_grad, keys_b.astype(f32), precision=HIGH)
        d_trans = d_trans + jnp.where(usable, trans_term, 0.0)
        back_grad = jnp.einsum("rhje,rhef->rhjf", got_grad, transform, precision=HIGH) + d_frame
        new_grad = jnp.where(depth_now == 0, got_grad, jnp.where(usable, back_grad, 0.0))
        new_vgrad = jnp.where(depth_now == 0, got_vgrad, jnp.where(usable, got_vgrad + d_vals, 0.0))
        return (new_grad, new_vgrad, d_trans, d_query)

    zero_keys = jnp.zeros(values_h.shape, f32)
    back_start = (zero_keys, zero_keys, jnp.zeros(transform.shape, f32), zero_keys)
    d_kout, d_val_cross, d_trans, d_query = lax.fori_loop(0, group_size, backward_hop, back_start)
    unused, local_pull = jax.vjp(
        span_local, local_args[0], local_args[1], local_args[2], local_args[3]
    )
    d_qh, d_kh, d_dirs, d_logit = local_pull(
        (d_query, d_kout, d_trans, score_scale * d_score_intra.astype(f32))
    )
    dq_b = merge_heads(d_qh).astype(bf16)
    dk_b = merge_heads(d_kh).astype(bf16)
    dv_b = merge_heads(d_val_intra + d_val_cross).astype(bf16)
    ddir_b = merge_heads(d_dirs).astype(bf16)
    dlogit_b = d_logit.transpose(0, 2, 1).astype(bf16)

    def weight_grad(grad_b):
        return jnp.einsum("rtd,rte->de", act_one, grad_b, preferred_element_type=f32)

    d_act_one = jnp.dot(dq_b, wq_full.T, preferred_element_type=f32) + jnp.dot(
        dk_b, wk_full.T, preferred_element_type=f32
    )
    d_act_one = (
        d_act_one
        + jnp.dot(dv_b, wv_full.T, preferred_element_type=f32)
        + jnp.dot(ddir_b, wdir_full.T, preferred_element_type=f32)
    )
    d_act_one = d_act_one + jnp.dot(dlogit_b, wbeta_full.T, preferred_element_type=f32)
    bias_part = jnp.sum(dlogit_b.astype(f32), axis=(0, 1))
    unused, norm_pull_one = jax.vjp(norm_in, layer_f, gain_onef)
    d_layer_norm, d_gain_one = norm_pull_one(d_act_one)
    grad_in = (d_middle + d_layer_norm).astype(bf16)
    reduced = (
        lax.psum_scatter(d_gain_one, ("dp", "hid", "wid"), scatter_dimension=0, tiled=True),
        lax.psum_scatter(weight_grad(dq_b), ("dp", "hid", "wid"), scatter_dimension=0, tiled=True),
        lax.psum_scatter(weight_grad(dk_b), ("dp", "hid", "wid"), scatter_dimension=0, tiled=True),
        lax.psum_scatter(weight_grad(dv_b), ("dp", "hid", "wid"), scatter_dimension=0, tiled=True),
        lax.psum_scatter(
            weight_grad(ddir_b), ("dp", "hid", "wid"), scatter_dimension=0, tiled=True
        ),
        lax.psum_scatter(
            weight_grad(dlogit_b), ("dp", "hid", "wid"), scatter_dimension=0, tiled=True
        ),
        lax.psum_scatter(grad_out_w, ("dp", "hid", "wid"), scatter_dimension=0, tiled=True),
        lax.psum_scatter(d_gain_two, ("dp", "hid", "wid"), scatter_dimension=0, tiled=True),
    )
    grad_bias = lax.psum(bias_part, ("dp", "hid", "wid"))
    return (
        layer_out,
        grad_in,
        reduced[0],
        reduced[1],
        reduced[2],
        reduced[3],
        reduced[4],
        reduced[5],
        grad_bias,
        reduced[6],
        reduced[7],
        grad_gate,
        grad_up,
        grad_down,
    )


def solution(mesh):
    in_specs = (
        P("dp", ("hid", "wid"), None),
        P("dp", ("hid", "wid")),
        P("dp", ("hid", "wid"), None),
        P(("dp", "hid", "wid")),
        P(("dp", "hid", "wid"), None),
        P(("dp", "hid", "wid"), None),
        P(("dp", "hid", "wid"), None),
        P(("dp", "hid", "wid"), None),
        P(("dp", "hid", "wid"), None),
        P(),
        P(("dp", "hid", "wid"), None),
        P(("dp", "hid", "wid")),
        P(("dp", "wid"), "hid"),
        P(("dp", "wid"), "hid"),
        P("hid", ("dp", "wid")),
    )
    out_specs = (
        P("dp", ("hid", "wid"), None),
        P("dp", ("hid", "wid"), None),
        P(("dp", "hid", "wid")),
        P(("dp", "hid", "wid"), None),
        P(("dp", "hid", "wid"), None),
        P(("dp", "hid", "wid"), None),
        P(("dp", "hid", "wid"), None),
        P(("dp", "hid", "wid"), None),
        P(),
        P(("dp", "hid", "wid"), None),
        P(("dp", "hid", "wid")),
        P(("dp", "wid"), "hid"),
        P(("dp", "wid"), "hid"),
        P("hid", ("dp", "wid")),
    )
    return jax.shard_map(
        per_device, mesh=mesh, in_specs=in_specs, out_specs=out_specs, check_vma=False
    )
```

profile of v0, /device:TPU:8, one launch (start us, length us, event | category | flops | bytes accessed | tf_op | source)
XLA Modules:
  0.0 2999.0 jit_solution(14622056150132619798)
XLA Ops:
  12.7 30.7 %all-gather.31.cloned.1.call-done = bf16[1024,1536]{0,1:T(8,128)(2,1)} async-done(((bf16[1024,192]{0,1:T(8,128)(2,1)}), bf16[1024,1536]{0,1:T(8,128)(2,1)}) %all-gather.31.cloned.1.call-update) | async-done | bytes 3145744 | tf_op jit(solution)/shard_map/all_gather | solution.py:208
  48.1 29.5 all-gather.27.cloned.1.call-done
  78.7 39.5 %all-reduce.5 = (bf16[1536]{0:T(1024)(128)(2,1)S(1)}, bf16[1536]{0:T(1024)(128)(2,1)S(1)}) all-reduce(bf16[1536]{0:T(1024)(128)(2,1)S(1)} %dynamic-update-slice, bf16[1536]{0:T(1024)(128)(2,1)S(1)} %dynamic-update-slice.1), channel_id=1, replica_groups=mesh['dp'=4,'hid'=4,'wid'=2] {'dp','hid','wid'}, use_global_device_ids=true, to_apply=%add | all-reduce | flops 3072 | bytes 12288
  118.2 38.4 %all-gather = bf16[32,48,12]{1,2,0:T(8,128)(2,1)S(1)} all-gather(bf16[1,48,12]{1,2,0:T(8,128)(2,1)S(1)} %bitcast.559), channel_id=1, replica_groups=mesh['dp'=4,'hid'=4,'wid'=2] {'dp','hid','wid'}, dimensions={0}, use_global_device_ids=true | all-gather | bytes 38016 | tf_op jit(solution)/shard_map/all_gather | solution.py:97
  158.6 20.6 all-gather.17.cloned.1.call-done
  188.2 236.7 %custom-call.21 = f32[2,12,1,128,128]{3,4,2,1,0:T(8,128)S(1)} custom-call(f32[2,12,1,128,128]{4,3,2,1,0:T(8,128)} %select_bitcast_fusion), custom_call_target="InvertDiagBlocksLowerTriangular" | custom-call | tf_op jit(solution)/shard_map/triangular_solve/custom-call.1 | solution.py:43
  487.8 516.1 %while.77 = (s32[]{:T(128)}, bf16[2,12,128,128]{3,2,1,0:T(8,128)(2,1)}, bf16[2,12,128,128]{3,2,1,0:T(8,128)(2,1)}, s32[2,128]{1,0:T(2,128)S(1)}, f32[2,12,128,1]...) while((s32[]{:T(128)}, ...), condition=%wide.region_7.10_spmd, body=%wide.region_4.9_spmd.sunk | while | flops 707860480 | bytes 19142940 | solution.py:171
  494.9 23.3 collective-permute-done.2
  521.5 21.9 collective-permute-done.1
  547.9 32.3 %collective-permute-start = (bf16[2,12,128,128]{3,2,1,0:T(8,128)(2,1)}, bf16[2,12,128,128]{3,2,1,0:T(8,128)(2,1)S(1)}, u32[]{:S(2)}, u32[]{:S(2)}) collective-permute-start(bf16[2,12,128,128]{3,2,1,0:T(8,128)(2,1)} %get-tuple-element.1734), channel_id=1, source_target_pairs={{0,1},{1,2},{2,3},{3,4},{4,5},{5,6},{6,7},{8,9},{9,10},{10,11},{11... | collective-permute-start | bytes 2359304 | tf_op jit(solution)/shard_map/while/body/eval_jaxpr/ppermute | solution.py:16
  584.5 11.1 collective-permute-start.1
  598.9 15.9 collective-permute-done.1
  619.3 53.6 %collective-permute-start = (bf16[2,12,128,128]{3,2,1,0:T(8,128)(2,1)}, bf16[2,12,128,128]{3,2,1,0:T(8,128)(2,1)S(1)}, u32[]{:S(2)}, u32[]{:S(2)}) collective-permute-start(bf16[2,12,128,128]{3,2,1,0:T(8,128)(2,1)} %get-tuple-element.1734), channel_id=1, source_target_pairs={{0,1},{1,2},{2,3},{3,4},{4,5},{5,6},{6,7},{8,9},{9,10},{10,11},{11... | collective-permute-start | bytes 2359304 | tf_op jit(solution)/shard_map/while/body/eval_jaxpr/ppermute | solution.py:16
  677.3 11.8 collective-permute-start.1
  692.4 15.2 collective-permute-done.1
  721.2 10.0 collective-permute-done.2
  734.6 21.9 collective-permute-done.1
  761.0 30.2 %collective-permute-start = (bf16[2,12,128,128]{3,2,1,0:T(8,128)(2,1)}, bf16[2,12,128,128]{3,2,1,0:T(8,128)(2,1)S(1)}, u32[]{:S(2)}, u32[]{:S(2)}) collective-permute-start(bf16[2,12,128,128]{3,2,1,0:T(8,128)(2,1)} %get-tuple-element.1734), channel_id=1, source_target_pairs={{0,1},{1,2},{2,3},{3,4},{4,5},{5,6},{6,7},{8,9},{9,10},{10,11},{11... | collective-permute-start | bytes 2359304 | tf_op jit(solution)/shard_map/while/body/eval_jaxpr/ppermute | solution.py:16
  807.8 18.1 collective-permute-done.1
  830.3 52.7 %collective-permute-start = (bf16[2,12,128,128]{3,2,1,0:T(8,128)(2,1)}, bf16[2,12,128,128]{3,2,1,0:T(8,128)(2,1)S(1)}, u32[]{:S(2)}, u32[]{:S(2)}) collective-permute-start(bf16[2,12,128,128]{3,2,1,0:T(8,128)(2,1)} %get-tuple-element.1734), channel_id=1, source_target_pairs={{0,1},{1,2},{2,3},{3,4},{4,5},{5,6},{6,7},{8,9},{9,10},{10,11},{11... | collective-permute-start | bytes 2359304 | tf_op jit(solution)/shard_map/while/body/eval_jaxpr/ppermute | solution.py:16
  887.3 9.9 collective-permute-start.1
  900.5 17.1 collective-permute-done.1
  922.1 54.4 %collective-permute-start = (bf16[2,12,128,128]{3,2,1,0:T(8,128)(2,1)}, bf16[2,12,128,128]{3,2,1,0:T(8,128)(2,1)S(1)}, u32[]{:S(2)}, u32[]{:S(2)}) collective-permute-start(bf16[2,12,128,128]{3,2,1,0:T(8,128)(2,1)} %get-tuple-element.1734), channel_id=1, source_target_pairs={{0,1},{1,2},{2,3},{3,4},{4,5},{5,6},{6,7},{8,9},{9,10},{10,11},{11... | collective-permute-start | bytes 2359304 | tf_op jit(solution)/shard_map/while/body/eval_jaxpr/ppermute | solution.py:16
  986.3 13.0 collective-permute-done.1
  1008.0 28.6 while.78
  1043.6 10.9 fusion.49
  1064.1 135.3 %all-gather.25.cloned.1.call-done = bf16[1536,4096]{1,0:T(8,128)(2,1)} async-done(((bf16[1536,1024]{1,0:T(8,128)(2,1)}), bf16[1536,4096]{1,0:T(8,128)(2,1)}) %all-gather.25.cloned.1.call-update) | async-done | bytes 12582928 | tf_op jit(solution)/shard_map/all_gather | solution.py:211
  1199.4 13.2 multiply_convert_fusion.1
  1228.6 10.9 fusion.53
  1239.5 10.7 multiply_reduce_fusion
  1260.5 27.3 while.79
  1295.9 710.8 %while.80 = (s32[]{:T(128)}, f32[2,12,128,128]{3,2,1,0:T(8,128)}, f32[2,12,128,128]{3,2,1,0:T(8,128)}, f32[2,12,128,128]{2,3,1,0:T(8,128)}, f32[2,12,128,128]{3,...) while((s32[]{:T(128)}, f32[2,12,128,128]{3,2,1,0:T(8,128)}, ...), condition=%wide.region_17.20_spmd.clone, body=%wide.region_16.19_spmd.clone.sunk | while | flops 1217855488 | bytes 85041728 | solution.py:309
  1312.1 70.8 %collective-permute-done.4 = bf16[2,12,128,128]{3,2,1,0:T(8,128)(2,1)} collective-permute-done((bf16[2,12,128,128]{3,2,1,0:T(8,128)(2,1)}, bf16[2,12,128,128]{3,2,1,0:T(8,128)(2,1)}, u32[]{:S(2)}, u32[]{:S(2)}) %collective-permute-start.4) | collective-permute-done | bytes 786464 | tf_op jit(solution)/shard_map/while/body/eval_jaxpr/ppermute | solution.py:16
  1414.6 46.3 %collective-permute-done.4 = bf16[2,12,128,128]{3,2,1,0:T(8,128)(2,1)} collective-permute-done((bf16[2,12,128,128]{3,2,1,0:T(8,128)(2,1)}, bf16[2,12,128,128]{3,2,1,0:T(8,128)(2,1)}, u32[]{:S(2)}, u32[]{:S(2)}) %collective-permute-start.4) | collective-permute-done | bytes 786464 | tf_op jit(solution)/shard_map/while/body/eval_jaxpr/ppermute | solution.py:16
  1492.0 37.8 %collective-permute-done.4 = bf16[2,12,128,128]{3,2,1,0:T(8,128)(2,1)} collective-permute-done((bf16[2,12,128,128]{3,2,1,0:T(8,128)(2,1)}, bf16[2,12,128,128]{3,2,1,0:T(8,128)(2,1)}, u32[]{:S(2)}, u32[]{:S(2)}) %collective-permute-start.4) | collective-permute-done | bytes 786464 | tf_op jit(solution)/shard_map/while/body/eval_jaxpr/ppermute | solution.py:16
  1561.1 70.5 %collective-permute-done.4 = bf16[2,12,128,128]{3,2,1,0:T(8,128)(2,1)} collective-permute-done((bf16[2,12,128,128]{3,2,1,0:T(8,128)(2,1)}, bf16[2,12,128,128]{3,2,1,0:T(8,128)(2,1)}, u32[]{:S(2)}, u32[]{:S(2)}) %collective-permute-start.4) | collective-permute-done | bytes 786464 | tf_op jit(solution)/shard_map/while/body/eval_jaxpr/ppermute | solution.py:16
  1663.2 63.7 %collective-permute-done.4 = bf16[2,12,128,128]{3,2,1,0:T(8,128)(2,1)} collective-permute-done((bf16[2,12,128,128]{3,2,1,0:T(8,128)(2,1)}, bf16[2,12,128,128]{3,2,1,0:T(8,128)(2,1)}, u32[]{:S(2)}, u32[]{:S(2)}) %collective-permute-start.4) | collective-permute-done | bytes 786464 | tf_op jit(solution)/shard_map/while/body/eval_jaxpr/ppermute | solution.py:16
  1757.9 57.2 %collective-permute-done.4 = bf16[2,12,128,128]{3,2,1,0:T(8,128)(2,1)} collective-permute-done((bf16[2,12,128,128]{3,2,1,0:T(8,128)(2,1)}, bf16[2,12,128,128]{3,2,1,0:T(8,128)(2,1)}, u32[]{:S(2)}, u32[]{:S(2)}) %collective-permute-start.4) | collective-permute-done | bytes 786464 | tf_op jit(solution)/shard_map/while/body/eval_jaxpr/ppermute | solution.py:16
  1846.5 70.8 %collective-permute-done.4 = bf16[2,12,128,128]{3,2,1,0:T(8,128)(2,1)} collective-permute-done((bf16[2,12,128,128]{3,2,1,0:T(8,128)(2,1)}, bf16[2,12,128,128]{3,2,1,0:T(8,128)(2,1)}, u32[]{:S(2)}, u32[]{:S(2)}) %collective-permute-start.4) | collective-permute-done | bytes 786464 | tf_op jit(solution)/shard_map/while/body/eval_jaxpr/ppermute | solution.py:16
  1948.7 48.3 %collective-permute-done.4 = bf16[2,12,128,128]{3,2,1,0:T(8,128)(2,1)} collective-permute-done((bf16[2,12,128,128]{3,2,1,0:T(8,128)(2,1)}, bf16[2,12,128,128]{3,2,1,0:T(8,128)(2,1)}, u32[]{:S(2)}, u32[]{:S(2)}) %collective-permute-start.4) | collective-permute-done | bytes 786464 | tf_op jit(solution)/shard_map/while/body/eval_jaxpr/ppermute | solution.py:16
  2139.5 40.1 %all-reduce.4 = (f32[1536]{0:T(1024)S(1)}, f32[12]{0:T(128)}, f32[1536]{0:T(1024)S(1)}) all-reduce(f32[1536]{0:T(1024)S(1)} %get-tuple-element.1283, f32[12]{0:T(128)S(1)} %get-tuple-element.1390, f32[1536]{0:T(1024)S(1)} %copy-done.101), channel_id=2, replica_groups=mesh['dp'=4,'hid'=4,'wid'=2] {'dp','hid','wid'}, use_global_device_ids=true, to_apply=%region_22.27.clone | all-reduce | flops 3084 | bytes 24672
  2194.9 38.8 %reduce-scatter.29.cloned.1.call-done = bf16[192,1024]{1,0:T(8,128)(2,1)} async-done(((bf16[1536,1024]{1,0:T(8,128)(2,1)}), bf16[192,1024]{1,0:T(8,128)(2,1)}) %reduce-scatter.29.cloned.1.call-update) | async-done | bytes 393232 | tf_op jit(solution)/shard_map/reduce_scatter | solution.py:243
  2235.7 47.6 %reduce-scatter.33.cloned.1.call-done = bf16[192,1024]{1,0:T(8,128)(2,1)} async-done(((bf16[1536,1024]{1,0:T(8,128)(2,1)}), bf16[192,1024]{1,0:T(8,128)(2,1)}) %reduce-scatter.33.cloned.1.call-update) | async-done | bytes 393232 | tf_op jit(solution)/shard_map/reduce_scatter | solution.py:246
  2285.2 140.8 %reduce-scatter.23.cloned.1.call-done = f32[48,1536]{1,0:T(8,128)} async-done(((f32[1536,1536]{1,0:T(8,128)}), f32[48,1536]{1,0:T(8,128)}) %reduce-scatter.23.cloned.1.call-update) | async-done | bytes 294928 | tf_op jit(solution)/shard_map/reduce_scatter | solution.py:343
  2425.9 141.0 %reduce-scatter.25.cloned.1.call-done = f32[48,1536]{1,0:T(8,128)} async-done(((f32[1536,1536]{1,0:T(8,128)}), f32[48,1536]{1,0:T(8,128)}) %reduce-scatter.25.cloned.1.call-update) | async-done | bytes 294928 | tf_op jit(solution)/shard_map/reduce_scatter | solution.py:349
  2566.9 142.0 %reduce-scatter.21.cloned.1.call-done = f32[48,1536]{1,0:T(8,128)} async-done(((f32[1536,1536]{1,0:T(8,128)}), f32[48,1536]{1,0:T(8,128)}) %reduce-scatter.21.cloned.1.call-update) | async-done | bytes 294928 | tf_op jit(solution)/shard_map/reduce_scatter | solution.py:342
  2708.9 141.1 %reduce-scatter.17.cloned.1.call-done = f32[48,1536]{1,0:T(8,128)} async-done(((f32[1536,1536]{1,0:T(8,128)}), f32[48,1536]{1,0:T(8,128)}) %reduce-scatter.17.cloned.1.call-update) | async-done | bytes 294928 | tf_op jit(solution)/shard_map/reduce_scatter | solution.py:340
  2850.1 142.1 %reduce-scatter.19.cloned.1.call-done = f32[48,1536]{1,0:T(8,128)} async-done(((f32[1536,1536]{1,0:T(8,128)}), f32[48,1536]{1,0:T(8,128)}) %reduce-scatter.19.cloned.1.call-update) | async-done | bytes 294928 | tf_op jit(solution)/shard_map/reduce_scatter | solution.py:341
  (798 shorter events, 692.7 us)
Async XLA Ops:
  7.2 36.2 %all-gather.31.cloned.1.call-start = ((), (), s32[]{:S(2)}) async-start(), calls=%async_computation.21 | async-start | bytes 3538944 | tf_op jit(solution)/shard_map/all_gather | solution.py:208
  7.9 69.7 %all-gather.27.cloned.1.call-start = ((), (), s32[]{:S(2)}) async-start(), calls=%async_computation.19 | async-start | bytes 3538944 | tf_op jit(solution)/shard_map/all_gather | solution.py:207
  8.7 149.8 %all-gather.23.cloned.1.call-start = ((), (), s32[]{:S(2)}) async-start(), calls=%async_computation.17 | async-start | bytes 3538944 | tf_op jit(solution)/shard_map/all_gather | solution.py:206
  9.4 169.8 %all-gather.17.cloned.1.call-start = ((), (), s32[]{:S(2)}) async-start(), calls=%async_computation.14 | async-start | bytes 4866048 | tf_op jit(solution)/shard_map/all_gather | solution.py:96
  10.0 415.0 %all-gather.13.cloned.1.call-start = ((), (), s32[]{:S(2)}) async-start(), calls=%async_computation.12 | async-start | bytes 4866048 | tf_op jit(solution)/shard_map/all_gather | solution.py:93
  10.6 427.7 %all-gather.15.cloned.1.call-start = ((), (), s32[]{:S(2)}) async-start(), calls=%async_computation.13 | async-start | bytes 4866048 | tf_op jit(solution)/shard_map/all_gather | solution.py:94
  11.1 460.9 %all-gather.19.cloned.1.call-start = ((), (), s32[]{:S(2)}) async-start(), calls=%async_computation.15 | async-start | bytes 4866048 | tf_op jit(solution)/shard_map/all_gather | solution.py:95
  11.9 1027.3 %all-gather.21.cloned.1.call-start = ((), (), s32[]{:S(2)}) async-start(), calls=%async_computation.16 | async-start | bytes 4866048 | tf_op jit(solution)/shard_map/all_gather | solution.py:98
  12.6 1031.0 %all-gather.33.cloned.1.call-start = ((), (), s32[]{:S(2)}) async-start(), calls=%async_computation.22 | async-start | bytes 15728640 | tf_op jit(solution)/shard_map/all_gather | solution.py:213
  48.1 1006.4 %all-gather.29.cloned.1.call-start = ((), (), s32[]{:S(2)}) async-start(), calls=%async_computation.20 | async-start | bytes 15728640 | tf_op jit(solution)/shard_map/all_gather | solution.py:212
  77.7 1121.7 %all-gather.25.cloned.1.call-start = ((), (), s32[]{:S(2)}) async-start(), calls=%async_computation.18 | async-start | bytes 15728640 | tf_op jit(solution)/shard_map/all_gather | solution.py:211
  158.6 1880.4 %reduce-scatter.35.cloned.1.call-start = ((), (), s32[]{:S(2)}) async-start(), calls=%async_computation.32 | async-start | bytes 15728640 | tf_op jit(solution)/shard_map/reduce_scatter | solution.py:238
  487.8 30.5 %collective-permute-start = (bf16[2,12,128,128]{3,2,1,0:T(8,128)(2,1)}, bf16[2,12,128,128]{3,2,1,0:T(8,128)(2,1)S(1)}, u32[]{:S(2)}, u32[]{:S(2)}) collective-permute-start(bf16[2,12,128,128]{3,2,1,0:T(8,128)(2,1)} %get-tuple-element.1734), channel_id=1, source_target_pairs={{0,1},{1,2},{2,3},{3,4},{4,5},{5,6},{6,7},{8,9},{9,10},{10,11},{11... | collective-permute-start | bytes 2359304 | tf_op jit(solution)/shard_map/while/body/eval_jaxpr/ppermute | solution.py:16
  492.6 50.8 %collective-permute-start.1 = (bf16[2,12,128,128]{3,2,1,0:T(8,128)(2,1)}, bf16[2,12,128,128]{3,2,1,0:T(8,128)(2,1)S(1)}, u32[]{:S(2)}, u32[]{:S(2)}) collective-permute-start(bf16[2,12,128,128]{3,2,1,0:T(8,128)(2,1)} %get-tuple-element.1735), channel_id=1, source_target_pairs={{0,1},{1,2},{2,3},{3,4},{4,5},{5,6},{6,7},{8,9},{9,10},{10,11},{11... | collective-permute-start | bytes 2359304 | tf_op jit(solution)/shard_map/while/body/eval_jaxpr/ppermute | solution.py:16
  547.9 47.9 %collective-permute-start = (bf16[2,12,128,128]{3,2,1,0:T(8,128)(2,1)}, bf16[2,12,128,128]{3,2,1,0:T(8,128)(2,1)S(1)}, u32[]{:S(2)}, u32[]{:S(2)}) collective-permute-start(bf16[2,12,128,128]{3,2,1,0:T(8,128)(2,1)} %get-tuple-element.1734), channel_id=1, source_target_pairs={{0,1},{1,2},{2,3},{3,4},{4,5},{5,6},{6,7},{8,9},{9,10},{10,11},{11... | collective-permute-start | bytes 2359304 | tf_op jit(solution)/shard_map/while/body/eval_jaxpr/ppermute | solution.py:16
  619.3 70.0 %collective-permute-start = (bf16[2,12,128,128]{3,2,1,0:T(8,128)(2,1)}, bf16[2,12,128,128]{3,2,1,0:T(8,128)(2,1)S(1)}, u32[]{:S(2)}, u32[]{:S(2)}) collective-permute-start(bf16[2,12,128,128]{3,2,1,0:T(8,128)(2,1)} %get-tuple-element.1734), channel_id=1, source_target_pairs={{0,1},{1,2},{2,3},{3,4},{4,5},{5,6},{6,7},{8,9},{9,10},{10,11},{11... | collective-permute-start | bytes 2359304 | tf_op jit(solution)/shard_map/while/body/eval_jaxpr/ppermute | solution.py:16
  677.3 30.3 %collective-permute-start.1 = (bf16[2,12,128,128]{3,2,1,0:T(8,128)(2,1)}, bf16[2,12,128,128]{3,2,1,0:T(8,128)(2,1)S(1)}, u32[]{:S(2)}, u32[]{:S(2)}) collective-permute-start(bf16[2,12,128,128]{3,2,1,0:T(8,128)(2,1)} %get-tuple-element.1735), channel_id=1, source_target_pairs={{0,1},{1,2},{2,3},{3,4},{4,5},{5,6},{6,7},{8,9},{9,10},{10,11},{11... | collective-permute-start | bytes 2359304 | tf_op jit(solution)/shard_map/while/body/eval_jaxpr/ppermute | solution.py:16
  719.3 37.2 %collective-permute-start.1 = (bf16[2,12,128,128]{3,2,1,0:T(8,128)(2,1)}, bf16[2,12,128,128]{3,2,1,0:T(8,128)(2,1)S(1)}, u32[]{:S(2)}, u32[]{:S(2)}) collective-permute-start(bf16[2,12,128,128]{3,2,1,0:T(8,128)(2,1)} %get-tuple-element.1735), channel_id=1, source_target_pairs={{0,1},{1,2},{2,3},{3,4},{4,5},{5,6},{6,7},{8,9},{9,10},{10,11},{11... | collective-permute-start | bytes 2359304 | tf_op jit(solution)/shard_map/while/body/eval_jaxpr/ppermute | solution.py:16
  761.0 43.6 %collective-permute-start = (bf16[2,12,128,128]{3,2,1,0:T(8,128)(2,1)}, bf16[2,12,128,128]{3,2,1,0:T(8,128)(2,1)S(1)}, u32[]{:S(2)}, u32[]{:S(2)}) collective-permute-start(bf16[2,12,128,128]{3,2,1,0:T(8,128)(2,1)} %get-tuple-element.1734), channel_id=1, source_target_pairs={{0,1},{1,2},{2,3},{3,4},{4,5},{5,6},{6,7},{8,9},{9,10},{10,11},{11... | collective-permute-start | bytes 2359304 | tf_op jit(solution)/shard_map/while/body/eval_jaxpr/ppermute | solution.py:16
  830.3 67.0 %collective-permute-start = (bf16[2,12,128,128]{3,2,1,0:T(8,128)(2,1)}, bf16[2,12,128,128]{3,2,1,0:T(8,128)(2,1)S(1)}, u32[]{:S(2)}, u32[]{:S(2)}) collective-permute-start(bf16[2,12,128,128]{3,2,1,0:T(8,128)(2,1)} %get-tuple-element.1734), channel_id=1, source_target_pairs={{0,1},{1,2},{2,3},{3,4},{4,5},{5,6},{6,7},{8,9},{9,10},{10,11},{11... | collective-permute-start | bytes 2359304 | tf_op jit(solution)/shard_map/while/body/eval_jaxpr/ppermute | solution.py:16
  922.1 61.1 %collective-permute-start = (bf16[2,12,128,128]{3,2,1,0:T(8,128)(2,1)}, bf16[2,12,128,128]{3,2,1,0:T(8,128)(2,1)S(1)}, u32[]{:S(2)}, u32[]{:S(2)}) collective-permute-start(bf16[2,12,128,128]{3,2,1,0:T(8,128)(2,1)} %get-tuple-element.1734), channel_id=1, source_target_pairs={{0,1},{1,2},{2,3},{3,4},{4,5},{5,6},{6,7},{8,9},{9,10},{10,11},{11... | collective-permute-start | bytes 2359304 | tf_op jit(solution)/shard_map/while/body/eval_jaxpr/ppermute | solution.py:16
  1220.4 823.4 %reduce-scatter.27.cloned.1.call-start = ((), (), s32[]{:S(2)}) async-start(), calls=%async_computation.28 | async-start | bytes 15728640 | tf_op jit(solution)/shard_map/reduce_scatter | solution.py:232
  1228.5 815.8 %reduce-scatter.31.cloned.1.call-start = ((), (), s32[]{:S(2)}) async-start(), calls=%async_computation.30 | async-start | bytes 15728640 | tf_op jit(solution)/shard_map/reduce_scatter | solution.py:235
  1295.9 895.3 %reduce-scatter.37.cloned.1.call-start = ((), (), s32[]{:S(2)}) async-start(), calls=%async_computation.33 | async-start | bytes 811008
  1297.1 88.5 %collective-permute-start.3 = (bf16[2,12,128,128]{3,2,1,0:T(8,128)(2,1)}, bf16[2,12,128,128]{3,2,1,0:T(8,128)(2,1)}, u32[]{:S(2)}, u32[]{:S(2)}) collective-permute-start(bf16[2,12,128,128]{3,2,1,0:T(8,128)(2,1)} %select_convert_fusion.4), channel_id=1, source_target_pairs={{1,0},{2,1},{3,2},{4,3},{5,4},{6,5},{7,6},{9,8},{10,9},{11,10},{12... | collective-permute-start | bytes 2359304 | tf_op jit(solution)/shard_map/while/body/eval_jaxpr/ppermute | solution.py:16
  1300.1 82.8 %collective-permute-start.4 = (bf16[2,12,128,128]{3,2,1,0:T(8,128)(2,1)}, bf16[2,12,128,128]{3,2,1,0:T(8,128)(2,1)}, u32[]{:S(2)}, u32[]{:S(2)}) collective-permute-start(bf16[2,12,128,128]{3,2,1,0:T(8,128)(2,1)} %select_convert_fusion.5), channel_id=1, source_target_pairs={{1,0},{2,1},{3,2},{4,3},{5,4},{6,5},{7,6},{9,8},{10,9},{11,10},{12... | collective-permute-start | bytes 2359304 | tf_op jit(solution)/shard_map/while/body/eval_jaxpr/ppermute | solution.py:16
  1395.1 68.4 %collective-permute-start.3 = (bf16[2,12,128,128]{3,2,1,0:T(8,128)(2,1)}, bf16[2,12,128,128]{3,2,1,0:T(8,128)(2,1)}, u32[]{:S(2)}, u32[]{:S(2)}) collective-permute-start(bf16[2,12,128,128]{3,2,1,0:T(8,128)(2,1)} %select_convert_fusion.4), channel_id=1, source_target_pairs={{1,0},{2,1},{3,2},{4,3},{5,4},{6,5},{7,6},{9,8},{10,9},{11,10},{12... | collective-permute-start | bytes 2359304 | tf_op jit(solution)/shard_map/while/body/eval_jaxpr/ppermute | solution.py:16
  1402.2 58.7 %collective-permute-start.4 = (bf16[2,12,128,128]{3,2,1,0:T(8,128)(2,1)}, bf16[2,12,128,128]{3,2,1,0:T(8,128)(2,1)}, u32[]{:S(2)}, u32[]{:S(2)}) collective-permute-start(bf16[2,12,128,128]{3,2,1,0:T(8,128)(2,1)} %select_convert_fusion.5), channel_id=1, source_target_pairs={{1,0},{2,1},{3,2},{4,3},{5,4},{6,5},{7,6},{9,8},{10,9},{11,10},{12... | collective-permute-start | bytes 2359304 | tf_op jit(solution)/shard_map/while/body/eval_jaxpr/ppermute | solution.py:16
  1473.1 59.4 %collective-permute-start.3 = (bf16[2,12,128,128]{3,2,1,0:T(8,128)(2,1)}, bf16[2,12,128,128]{3,2,1,0:T(8,128)(2,1)}, u32[]{:S(2)}, u32[]{:S(2)}) collective-permute-start(bf16[2,12,128,128]{3,2,1,0:T(8,128)(2,1)} %select_convert_fusion.4), channel_id=1, source_target_pairs={{1,0},{2,1},{3,2},{4,3},{5,4},{6,5},{7,6},{9,8},{10,9},{11,10},{12... | collective-permute-start | bytes 2359304 | tf_op jit(solution)/shard_map/while/body/eval_jaxpr/ppermute | solution.py:16
  1479.4 50.4 %collective-permute-start.4 = (bf16[2,12,128,128]{3,2,1,0:T(8,128)(2,1)}, bf16[2,12,128,128]{3,2,1,0:T(8,128)(2,1)}, u32[]{:S(2)}, u32[]{:S(2)}) collective-permute-start(bf16[2,12,128,128]{3,2,1,0:T(8,128)(2,1)} %select_convert_fusion.5), channel_id=1, source_target_pairs={{1,0},{2,1},{3,2},{4,3},{5,4},{6,5},{7,6},{9,8},{10,9},{11,10},{12... | collective-permute-start | bytes 2359304 | tf_op jit(solution)/shard_map/while/body/eval_jaxpr/ppermute | solution.py:16
  1542.0 92.3 %collective-permute-start.3 = (bf16[2,12,128,128]{3,2,1,0:T(8,128)(2,1)}, bf16[2,12,128,128]{3,2,1,0:T(8,128)(2,1)}, u32[]{:S(2)}, u32[]{:S(2)}) collective-permute-start(bf16[2,12,128,128]{3,2,1,0:T(8,128)(2,1)} %select_convert_fusion.4), channel_id=1, source_target_pairs={{1,0},{2,1},{3,2},{4,3},{5,4},{6,5},{7,6},{9,8},{10,9},{11,10},{12... | collective-permute-start | bytes 2359304 | tf_op jit(solution)/shard_map/while/body/eval_jaxpr/ppermute | solution.py:16
  1548.6 83.0 %collective-permute-start.4 = (bf16[2,12,128,128]{3,2,1,0:T(8,128)(2,1)}, bf16[2,12,128,128]{3,2,1,0:T(8,128)(2,1)}, u32[]{:S(2)}, u32[]{:S(2)}) collective-permute-start(bf16[2,12,128,128]{3,2,1,0:T(8,128)(2,1)} %select_convert_fusion.5), channel_id=1, source_target_pairs={{1,0},{2,1},{3,2},{4,3},{5,4},{6,5},{7,6},{9,8},{10,9},{11,10},{12... | collective-permute-start | bytes 2359304 | tf_op jit(solution)/shard_map/while/body/eval_jaxpr/ppermute | solution.py:16
  1643.8 85.7 %collective-permute-start.3 = (bf16[2,12,128,128]{3,2,1,0:T(8,128)(2,1)}, bf16[2,12,128,128]{3,2,1,0:T(8,128)(2,1)}, u32[]{:S(2)}, u32[]{:S(2)}) collective-permute-start(bf16[2,12,128,128]{3,2,1,0:T(8,128)(2,1)} %select_convert_fusion.4), channel_id=1, source_target_pairs={{1,0},{2,1},{3,2},{4,3},{5,4},{6,5},{7,6},{9,8},{10,9},{11,10},{12... | collective-permute-start | bytes 2359304 | tf_op jit(solution)/shard_map/while/body/eval_jaxpr/ppermute | solution.py:16
  1650.8 76.0 %collective-permute-start.4 = (bf16[2,12,128,128]{3,2,1,0:T(8,128)(2,1)}, bf16[2,12,128,128]{3,2,1,0:T(8,128)(2,1)}, u32[]{:S(2)}, u32[]{:S(2)}) collective-permute-start(bf16[2,12,128,128]{3,2,1,0:T(8,128)(2,1)} %select_convert_fusion.5), channel_id=1, source_target_pairs={{1,0},{2,1},{3,2},{4,3},{5,4},{6,5},{7,6},{9,8},{10,9},{11,10},{12... | collective-permute-start | bytes 2359304 | tf_op jit(solution)/shard_map/while/body/eval_jaxpr/ppermute | solution.py:16
  1739.1 78.8 %collective-permute-start.3 = (bf16[2,12,128,128]{3,2,1,0:T(8,128)(2,1)}, bf16[2,12,128,128]{3,2,1,0:T(8,128)(2,1)}, u32[]{:S(2)}, u32[]{:S(2)}) collective-permute-start(bf16[2,12,128,128]{3,2,1,0:T(8,128)(2,1)} %select_convert_fusion.4), channel_id=1, source_target_pairs={{1,0},{2,1},{3,2},{4,3},{5,4},{6,5},{7,6},{9,8},{10,9},{11,10},{12... | collective-permute-start | bytes 2359304 | tf_op jit(solution)/shard_map/while/body/eval_jaxpr/ppermute | solution.py:16
  1745.4 69.8 %collective-permute-start.4 = (bf16[2,12,128,128]{3,2,1,0:T(8,128)(2,1)}, bf16[2,12,128,128]{3,2,1,0:T(8,128)(2,1)}, u32[]{:S(2)}, u32[]{:S(2)}) collective-permute-start(bf16[2,12,128,128]{3,2,1,0:T(8,128)(2,1)} %select_convert_fusion.5), channel_id=1, source_target_pairs={{1,0},{2,1},{3,2},{4,3},{5,4},{6,5},{7,6},{9,8},{10,9},{11,10},{12... | collective-permute-start | bytes 2359304 | tf_op jit(solution)/shard_map/while/body/eval_jaxpr/ppermute | solution.py:16
  1827.4 92.6 %collective-permute-start.3 = (bf16[2,12,128,128]{3,2,1,0:T(8,128)(2,1)}, bf16[2,12,128,128]{3,2,1,0:T(8,128)(2,1)}, u32[]{:S(2)}, u32[]{:S(2)}) collective-permute-start(bf16[2,12,128,128]{3,2,1,0:T(8,128)(2,1)} %select_convert_fusion.4), channel_id=1, source_target_pairs={{1,0},{2,1},{3,2},{4,3},{5,4},{6,5},{7,6},{9,8},{10,9},{11,10},{12... | collective-permute-start | bytes 2359304 | tf_op jit(solution)/shard_map/while/body/eval_jaxpr/ppermute | solution.py:16
  1834.1 83.2 %collective-permute-start.4 = (bf16[2,12,128,128]{3,2,1,0:T(8,128)(2,1)}, bf16[2,12,128,128]{3,2,1,0:T(8,128)(2,1)}, u32[]{:S(2)}, u32[]{:S(2)}) collective-permute-start(bf16[2,12,128,128]{3,2,1,0:T(8,128)(2,1)} %select_convert_fusion.5), channel_id=1, source_target_pairs={{1,0},{2,1},{3,2},{4,3},{5,4},{6,5},{7,6},{9,8},{10,9},{11,10},{12... | collective-permute-start | bytes 2359304 | tf_op jit(solution)/shard_map/while/body/eval_jaxpr/ppermute | solution.py:16
  1929.5 70.2 %collective-permute-start.3 = (bf16[2,12,128,128]{3,2,1,0:T(8,128)(2,1)}, bf16[2,12,128,128]{3,2,1,0:T(8,128)(2,1)}, u32[]{:S(2)}, u32[]{:S(2)}) collective-permute-start(bf16[2,12,128,128]{3,2,1,0:T(8,128)(2,1)} %select_convert_fusion.4), channel_id=1, source_target_pairs={{1,0},{2,1},{3,2},{4,3},{5,4},{6,5},{7,6},{9,8},{10,9},{11,10},{12... | collective-permute-start | bytes 2359304 | tf_op jit(solution)/shard_map/while/body/eval_jaxpr/ppermute | solution.py:16
  1936.3 60.7 %collective-permute-start.4 = (bf16[2,12,128,128]{3,2,1,0:T(8,128)(2,1)}, bf16[2,12,128,128]{3,2,1,0:T(8,128)(2,1)}, u32[]{:S(2)}, u32[]{:S(2)}) collective-permute-start(bf16[2,12,128,128]{3,2,1,0:T(8,128)(2,1)} %select_convert_fusion.5), channel_id=1, source_target_pairs={{1,0},{2,1},{3,2},{4,3},{5,4},{6,5},{7,6},{9,8},{10,9},{11,10},{12... | collective-permute-start | bytes 2359304 | tf_op jit(solution)/shard_map/while/body/eval_jaxpr/ppermute | solution.py:16
  2038.9 153.7 %reduce-scatter.39.cloned.1.call-start = ((), (), s32[]{:S(2)}) async-start(), calls=%async_computation.34 | async-start | bytes 3538944
  2043.7 190.0 %reduce-scatter.29.cloned.1.call-start = ((), (), s32[]{:S(2)}) async-start(), calls=%async_computation.29 | async-start | bytes 3538944 | tf_op jit(solution)/shard_map/reduce_scatter | solution.py:243
  2044.3 239.0 %reduce-scatter.33.cloned.1.call-start = ((), (), s32[]{:S(2)}) async-start(), calls=%async_computation.31 | async-start | bytes 3538944 | tf_op jit(solution)/shard_map/reduce_scatter | solution.py:246
  2044.8 381.1 %reduce-scatter.23.cloned.1.call-start = ((), (), s32[]{:S(2)}) async-start(), calls=%async_computation.26 | async-start | bytes 9732096 | tf_op jit(solution)/shard_map/reduce_scatter | solution.py:343
  2081.8 485.2 %reduce-scatter.25.cloned.1.call-start = ((), (), s32[]{:S(2)}) async-start(), calls=%async_computation.27 | async-start | bytes 9732096 | tf_op jit(solution)/shard_map/reduce_scatter | solution.py:349
  2088.5 620.5 %reduce-scatter.21.cloned.1.call-start = ((), (), s32[]{:S(2)}) async-start(), calls=%async_computation.25 | async-start | bytes 9732096 | tf_op jit(solution)/shard_map/reduce_scatter | solution.py:342
  2100.4 749.6 %reduce-scatter.17.cloned.1.call-start = ((), (), s32[]{:S(2)}) async-start(), calls=%async_computation.23 | async-start | bytes 9732096 | tf_op jit(solution)/shard_map/reduce_scatter | solution.py:340
  2113.3 878.9 %reduce-scatter.19.cloned.1.call-start = ((), (), s32[]{:S(2)}) async-start(), calls=%async_computation.24 | async-start | bytes 9732096 | tf_op jit(solution)/shard_map/reduce_scatter | solution.py:341
  (180 other events, 5848.5 us)
Sparse Core Ops, SparseCore 0:
  9.9 33.4 all-gather.30
  45.3 32.3 all-gather.26
  79.5 32.5 all-gather.22
  115.0 64.1 all-gather.16
  182.1 63.1 all-gather.12
  248.1 63.3 all-gather.14
  314.6 63.8 all-gather.18
  381.5 62.7 all-gather.20
  445.9 263.9 all-gather.32
  711.3 267.6 all-gather.28
  980.5 218.8 all-gather.24
  1220.5 232.5 reduce-scatter.34
  1455.4 272.5 reduce-scatter.26
  1730.2 263.3 reduce-scatter.30
  2039.0 95.8 reduce-scatter.36
  2138.1 45.5 reduce-scatter.38
  2187.4 46.2 reduce-scatter.28
  2236.9 46.2 reduce-scatter.32
  2290.7 135.1 reduce-scatter.22
  2432.3 134.6 reduce-scatter.24
  2574.4 134.4 reduce-scatter.20
  2715.4 134.6 reduce-scatter.16
  2857.5 134.5 reduce-scatter.18
where the time goes:
time: 3010 us; the launch traced here: 3000 us
  waiting for transfers between devices  1640 us (54%)
  matrix products  505 us (17%)
  starting transfers between devices  352 us (12%)
  other arithmetic  293 us (10%)
  blocking collectives  118 us (4%)
  local copies, waits for them, and re-layouts  74.2 us (2%)
    ppermute x37, waiting for transfers between devices, shifted_2(): lax.ppermute(value, axis, [(source, source + steps) for source in range(l...  622 us
    ppermute x37, starting transfers between devices, shifted_2(): lax.ppermute(value, axis, [(source, source + steps) for source in range(l...  351 us
    another operation x1, other arithmetic, span_local(): lax.linalg.triangular_solve(system, dirs_keys, left_side=True, lower=True)  237 us
    reduce_scatter x1, waiting for transfers between devices, per_device(): lax.psum_scatter(weight_grad(dk_b), ('dp', 'hid', 'wid'), scatter_dimensi...  142 us
    reduce_scatter x1, waiting for transfers between devices, per_device(): lax.psum_scatter(weight_grad(dv_b), ('dp', 'hid', 'wid'), scatter_dimensi...  142 us
    reduce_scatter x1, waiting for transfers between devices, per_device(): lax.psum_scatter(weight_grad(dq_b), ('dp', 'hid', 'wid'), scatter_dimensi...  141 us
    reduce_scatter x1, waiting for transfers between devices, per_device(): lax.psum_scatter(grad_out_w, ('dp', 'hid', 'wid'), scatter_dimension=0, t...  141 us
    reduce_scatter x1, waiting for transfers between devices, per_device(): lax.psum_scatter(weight_grad(ddir_b), ('dp', 'hid', 'wid'), scatter_dimen...  141 us
  transfers between devices with their start and end apart: 60, of which 28 were waited for; matrix products, arithmetic and copies ran while one was open for 28% of the time, Pallas kernels for 0%

commit v1 on v0

v1 whole, which is shorter than its diff:
```python
import functools
import math

import jax
import jax.numpy as jnp
from jax import lax
from jax.experimental import pallas as pl
from jax.experimental.pallas import tpu as pltpu
from jax.sharding import PartitionSpec as P

EPS = 1e-06
NEG = -1e30
F32 = jnp.float32
BF16 = jnp.bfloat16
NN = ((1,), (0,))
NT = ((1,), (1,))
TN = ((0,), (0,))
VMEM_BYTES = 56 * 1024 * 1024


def halves(x):
    if x.dtype == BF16:
        return (x,)
    top = x.astype(BF16)
    return (top, (x - top.astype(F32)).astype(BF16))


def dot(left, right, dims):
    total = None
    for a, x in enumerate(left):
        for b, y in enumerate(right):
            if a + b > 1:
                continue
            term = lax.dot_general(x, y, (dims, ((), ())), preferred_element_type=F32)
            total = term if total is None else total + term
    return total


def iotas(size):
    rows = lax.broadcasted_iota(jnp.int32, (size, size), 0)
    cols = lax.broadcasted_iota(jnp.int32, (size, size), 1)
    return rows, cols


def unit_dirs(raw):
    inv = lax.rsqrt(jnp.sum(raw * raw, axis=-1, keepdims=True) + EPS)
    return raw * inv, inv


def local_forward(heads, q_ref, k_ref, raw_ref, logit_ref, qin_ref, kout_ref, ptop_ref, plow_ref,
                  intra_ref, t_ref, e_ref, cm_ref, s_ref):
    size = q_ref.shape[0]
    width = q_ref.shape[1] // heads
    rows, cols = iotas(size)
    strict, lower, diag = rows > cols, rows >= cols, rows == cols
    for h in range(heads):
        at = slice(h * width, (h + 1) * width)
        q, k = q_ref[:, at], k_ref[:, at]
        w, _ = unit_dirs(raw_ref[:, at])
        beta_row = 2.0 * jax.nn.sigmoid(logit_ref[0, h : h + 1, :])
        beta = jnp.where(diag, beta_row, 0.0)
        beta_col = jnp.sum(beta, axis=1, keepdims=True)
        ws = halves(w)
        gram = dot(ws, ws, NT)
        apart = rows ^ cols
        t = beta - jnp.where(strict & (apart == 1), beta_col * gram * beta_row, 0.0)
        shift = 1
        while (1 << shift) < size:
            part = jnp.where(strict & ((apart >> shift) == 1), gram, 0.0)
            ts = halves(t)
            t = t - dot(halves(dot(ts, halves(part), NN)), ts, NN)
            shift += 1
        ts = halves(t)
        b = jnp.where(lower, dot((q,), ws, NT), 0.0)
        m = jnp.where(strict, dot(ws, (k,), NT), 0.0)
        bs = halves(b)
        e = dot(ts, halves(m), NN)
        s = dot(ts, ws, NN)
        cm = dot(bs, ts, NN)
        es = halves(e)
        intra_ref[:, at] = dot((q,), (k,), NT) - dot(bs, es, NN)
        qin_ref[:, at] = (q.astype(F32) - dot(halves(cm), ws, NN)).astype(BF16)
        kout_ref[:, at] = (k.astype(F32) - dot(es, ws, TN)).astype(BF16)
        step = jnp.where(diag, 1.0, 0.0) - dot(ws, halves(s), TN)
        top, low = halves(step)
        ptop_ref[:, at] = top
        plow_ref[:, at] = low
        t_ref[:, at] = t
        e_ref[:, at] = e
        cm_ref[:, at] = cm
        s_ref[:, at] = s


def cross_forward(heads, group, scale, qin_ref, kout_ref, ptop_ref, plow_ref, intra_ref, v_ref,
                  segc_ref, segr_ref, out_ref, prob_ref, keep_ref, frame, score):
    size = qin_ref.shape[0]
    width = qin_ref.shape[1] // heads
    total = v_ref.shape[0]
    wide = group * size
    c = pl.program_id(0)

    @pl.when(c == 0)
    def _():
        frame[...] = jnp.zeros_like(frame)
        score[...] = jnp.full_like(score, NEG)

    rows, cols = iotas(size)
    own = pl.multiple_of(c * size, size)
    seg = segc_ref[...]
    for h in range(heads):
        at = slice(h * width, (h + 1) * width)
        q = qin_ref[:, at]
        for g in range(total // wide):
            part = slice(g * wide, (g + 1) * wide)

            @pl.when(g * group < c)
            def _():
                raw = scale * lax.dot_general(
                    q, frame[h, part, :], (NT, ((), ())), preferred_element_type=F32)
                place = lax.broadcasted_iota(jnp.int32, (size, wide), 1) + g * wide
                permit = (place < own) & (seg == segr_ref[:, part])
                score[h, :, part] = jnp.where(permit, raw, NEG)

        permit = (rows >= cols) & (seg == segr_ref[:, pl.ds(own, size)])
        score[h, :, pl.ds(own, size)] = jnp.where(permit, scale * intra_ref[:, at], NEG)
        s = score[h]
        e = jnp.exp(s - jnp.max(s, axis=-1, keepdims=True))
        p = (e / jnp.sum(e, axis=-1, keepdims=True)).astype(BF16)
        prob_ref[0, h] = p
        out_ref[:, at] = lax.dot_general(
            p, v_ref[:, at], (NN, ((), ())), preferred_element_type=F32).astype(BF16)
        keep_ref[0, h] = frame[h]
        step = (ptop_ref[:, at], plow_ref[:, at])
        for g in range(total // wide):
            part = slice(g * wide, (g + 1) * wide)

            @pl.when(g * group < c)
            def _():
                frame[h, part, :] = dot((frame[h, part, :],), step, NT).astype(BF16)

        frame[h, pl.ds(own, size), :] = kout_ref[:, at]


def cross_backward(heads, group, scale, grad_ref, v_ref, prob_ref, keep_ref, qin_ref, ptop_ref,
                   plow_ref, dqin_ref, dintra_ref, dkout_ref, dstep_ref, dv_ref, carry, dvals, ds_ref):
    size = grad_ref.shape[0]
    width = grad_ref.shape[1] // heads
    total = v_ref.shape[0]
    wide = group * size
    c = pl.num_programs(0) - 1 - pl.program_id(0)

    @pl.when(pl.program_id(0) == 0)
    def _():
        carry[...] = jnp.zeros_like(carry)
        dvals[...] = jnp.zeros_like(dvals)

    own = pl.multiple_of(c * size, size)
    for h in range(heads):
        at = slice(h * width, (h + 1) * width)
        grad, q = grad_ref[:, at], qin_ref[:, at]
        p = prob_ref[0, h]
        dp = lax.dot_general(grad, v_ref[:, at], (NT, ((), ())), preferred_element_type=F32)
        pf = p.astype(F32)
        delta = jnp.sum(pf * dp, axis=-1, keepdims=True)
        ds = (pf * (dp - delta)).astype(BF16)
        ds_ref[h] = ds
        dintra_ref[:, at] = ds_ref[h, :, pl.ds(own, size)]
        dqin_ref[:, at] = scale * lax.dot_general(
            ds, keep_ref[0, h], (NN, ((), ())), preferred_element_type=F32)
        dkout_ref[:, at] = carry[h, pl.ds(own, size), :]
        dstep_ref[:, at] = lax.dot_general(
            carry[h].astype(BF16), keep_ref[0, h], (TN, ((), ())), preferred_element_type=F32)
        step = (ptop_ref[:, at], plow_ref[:, at])
        for g in range(total // wide):
            part = slice(g * wide, (g + 1) * wide)

            @pl.when(g * group <= c)
            def _():
                dvals[h, part, :] += lax.dot_general(
                    prob_ref[0, h, :, part], grad, (TN, ((), ())), preferred_element_type=F32)

            @pl.when(g * group < c)
            def _():
                fresh = scale * lax.dot_general(
                    ds_ref[h, :, part], q, (TN, ((), ())), preferred_element_type=F32)
                carry[h, part, :] = fresh + dot((carry[h, part, :].astype(BF16),), step, NN)

        @pl.when(c == 0)
        def _():
            dv_ref[:, at] = dvals[h].astype(BF16)


def local_backward(heads, scale, q_ref, k_ref, raw_ref, logit_ref, t_ref, e_ref, cm_ref, s_ref,
                   dqin_ref, dintra_ref, dkout_ref, dstep_ref, dq_ref, dk_ref, draw_ref, dlogit_ref):
    size = q_ref.shape[0]
    width = q_ref.shape[1] // heads
    rows, cols = iotas(size)
    strict, lower, diag = rows > cols, rows >= cols, rows == cols
    for h in range(heads):
        at = slice(h * width, (h + 1) * width)
        q, k = (q_ref[:, at],), (k_ref[:, at],)
        raw = raw_ref[:, at]
        w, inv = unit_dirs(raw)
        beta_row = 2.0 * jax.nn.sigmoid(logit_ref[0, h : h + 1, :])
        ws = halves(w)
        ts, es, cms, ss = (halves(ref[:, at]) for ref in (t_ref, e_ref, cm_ref, s_ref))
        dqin, dkout = dqin_ref[:, at], dkout_ref[:, at]
        dintra = (dintra_ref[:, at],)
        dqs, dks, dps = halves(dqin), halves(dkout), halves(dstep_ref[:, at])
        b = jnp.where(lower, dot(q, ws, NT), 0.0)
        d_s = -dot(ws, dps, NN)
        d_e = -(dot(ws, dks, NT) + scale * dot(halves(b), dintra, TN))
        d_cm = -dot(dqs, ws, NT)
        y_s = dot(ts, halves(d_s), TN)
        y_e = dot(ts, halves(d_e), TN)
        y_c = dot(halves(d_cm), ts, NT)
        d_x = -(dot(halves(y_s), ss, NT) + dot(halves(y_e), es, NT) + dot(cms, halves(y_c), TN))
        d_b = halves(jnp.where(lower, y_c - scale * dot(dintra, es, NT), 0.0))
        d_m = halves(jnp.where(strict, y_e, 0.0))
        d_a = halves(jnp.where(strict, d_x, 0.0))
        dq_ref[:, at] = (dqin + scale * dot(dintra, k, NN) + dot(d_b, ws, NN)).astype(BF16)
        dk_ref[:, at] = (dkout + scale * dot(dintra, q, TN) + dot(d_m, ws, TN)).astype(BF16)
        d_w = (y_s - dot(ss, dps, NT) - dot(es, dks, NN) - dot(cms, dqs, TN)
               + dot(d_b, q, TN) + dot(d_m, k, NN) + dot(d_a, ws, NN) + dot(d_a, ws, TN))
        draw = inv * d_w - raw * (inv * inv * inv) * jnp.sum(raw * d_w, axis=-1, keepdims=True)
        draw_ref[:, at] = draw.astype(BF16)
        at_diag = jnp.sum(jnp.where(diag, d_x, 0.0), axis=0, keepdims=True)
        dlogit_ref[0, h : h + 1, :] = -at_diag * (1.0 - 0.5 * beta_row) / beta_row


def run(body, grid, inputs, in_specs, outputs, out_specs, scratch, flops):
    return pl.pallas_call(
        body, grid=(grid,), in_specs=in_specs, out_specs=out_specs, out_shape=outputs,
        scratch_shapes=scratch,
        compiler_params=pltpu.CompilerParams(
            dimension_semantics=("arbitrary",), vmem_limit_bytes=VMEM_BYTES),
        cost_estimate=pl.CostEstimate(
            flops=flops, transcendentals=0,
            bytes_accessed=sum(x.size * x.dtype.itemsize for x in (*inputs, *outputs))),
    )(*inputs)


def shape(dims, dtype):
    return jax.ShapeDtypeStruct(dims, dtype)


def group_of(blocks):
    return 4 if blocks % 4 == 0 else 1


def attention_forward(q, k, v, raw, logits, segments, size):
    tokens, width = q.shape
    blocks, heads, _ = logits.shape
    head = width // heads
    block = pl.BlockSpec((size, width), lambda c: (c, 0))
    square = pl.BlockSpec((head, width), lambda c: (c, 0))
    logit_block = pl.BlockSpec((1, heads, size), lambda c: (c, 0, 0))
    f, b = shape((tokens, width), F32), shape((tokens, width), BF16)
    stepped = shape((blocks * head, width), BF16)
    saved_s = shape((tokens, width), F32)
    qin, kout, ptop, plow, intra, t, e, cm, s = run(
        functools.partial(local_forward, heads), blocks, (q, k, raw, logits),
        [block, block, block, logit_block], (b, b, stepped, stepped, f, f, f, f, saved_s),
        [block, block, square, square, block, block, block, block, block], [],
        blocks * heads * 62 * 2 * size * size * head)
    group = group_of(blocks)
    whole = pl.BlockSpec((tokens, width), lambda c: (0, 0))
    wide_prob = pl.BlockSpec((1, heads, size, tokens), lambda c: (c, 0, 0, 0))
    wide_keep = pl.BlockSpec((1, heads, tokens, head), lambda c: (c, 0, 0, 0))
    out, prob, keep = run(
        functools.partial(cross_forward, heads, group, 1.0 / math.sqrt(head)), blocks,
        (qin, kout, ptop, plow, intra, v, segments.reshape(tokens, 1), segments.reshape(1, tokens)),
        [block, block, square, square, block, whole,
         pl.BlockSpec((size, 1), lambda c: (c, 0)), pl.BlockSpec((1, tokens), lambda c: (0, 0))],
        (b, shape((blocks, heads, size, tokens), BF16), shape((blocks, heads, tokens, head), BF16)),
        [block, wide_prob, wide_keep],
        [pltpu.VMEM((heads, tokens, head), BF16), pltpu.VMEM((heads, size, tokens), F32)],
        blocks * heads * 4 * 2 * size * tokens * head)
    return out, (q, k, v, raw, logits, qin, ptop, plow, t, e, cm, s, prob, keep)


def attention_backward(saved, grad, size):
    q, k, v, raw, logits, qin, ptop, plow, t, e, cm, s, prob, keep = saved
    tokens, width = q.shape
    blocks, heads, _ = logits.shape
    head = width // heads
    scale = 1.0 / math.sqrt(head)
    back = lambda c: (blocks - 1 - c, 0)
    block = pl.BlockSpec((size, width), back)
    square = pl.BlockSpec((head, width), back)
    whole = pl.BlockSpec((tokens, width), lambda c: (0, 0))
    wide_prob = pl.BlockSpec((1, heads, size, tokens), lambda c: (blocks - 1 - c, 0, 0, 0))
    wide_keep = pl.BlockSpec((1, heads, tokens, head), lambda c: (blocks - 1 - c, 0, 0, 0))
    f, b = shape((tokens, width), F32), shape((tokens, width), BF16)
    dqin, dintra, dkout, dstep, dv = run(
        functools.partial(cross_backward, heads, group_of(blocks), scale), blocks,
        (grad, v, prob, keep, qin, ptop, plow),
        [block, whole, wide_prob, wide_keep, block, square, square],
        (f, b, f, shape((blocks * head, width), F32), b),
        [block, block, block, square, whole],
        [pltpu.VMEM((heads, tokens, head), F32), pltpu.VMEM((heads, tokens, head), F32),
         pltpu.VMEM((heads, size, tokens), BF16)],
        blocks * heads * 7 * 2 * size * tokens * head)
    block = pl.BlockSpec((size, width), lambda c: (c, 0))
    square = pl.BlockSpec((head, width), lambda c: (c, 0))
    logit_block = pl.BlockSpec((1, heads, size), lambda c: (c, 0, 0))
    dq, dk, draw, dlogit = run(
        functools.partial(local_backward, heads, scale), blocks,
        (q, k, raw, logits, t, e, cm, s, dqin, dintra, dkout, dstep),
        [block, block, block, logit_block, block, block, block, block, block, block, block, square],
        (b, b, b, shape((blocks, heads, size), F32)), [block, block, block, logit_block], [],
        blocks * heads * 60 * 2 * size * size * head)
    return dq, dk, dv, draw, dlogit


def norm_in(tensor, gain_vec):
    return tensor * lax.rsqrt(jnp.mean(tensor * tensor, axis=-1, keepdims=True) + EPS) * gain_vec


def mm(left, right, dims=NN):
    return lax.dot_general(left, right, (dims, ((), ())), preferred_element_type=F32)


def to_row(x):
    cores, rows = lax.axis_size("wid"), x.shape[0]
    me = lax.axis_index("wid")
    if cores == rows == 2:
        got = lax.ppermute(lax.dynamic_index_in_dim(x, 1 - me, 0, False), "wid", [(0, 1), (1, 0)])
        mine = lax.dynamic_index_in_dim(x, me, 0, False)
        return jnp.concatenate([jnp.where(me == 0, mine, got), jnp.where(me == 0, got, mine)], axis=0)
    every = lax.all_gather(x, "wid", axis=0, tiled=False)
    every = lax.dynamic_index_in_dim(every, me // (cores // rows), 1, False)
    return every.reshape((-1,) + x.shape[2:])


def from_row(x, rows):
    cores = lax.axis_size("wid")
    me = lax.axis_index("wid")
    parts = x.reshape((cores, x.shape[0] // cores) + x.shape[1:])
    if cores == rows == 2:
        got = lax.ppermute(lax.dynamic_index_in_dim(parts, 1 - me, 0, False), "wid", [(0, 1), (1, 0)])
        mine = lax.dynamic_index_in_dim(parts, me, 0, False)
        return jnp.stack([jnp.where(me == 0, mine, got), jnp.where(me == 0, got, mine)], axis=0)
    return lax.all_to_all(parts, "wid", 0, 0, tiled=True)[:: cores // rows]


def per_device(layer_in, segment_ids, out_grad, gain_attn, w_query, w_key, w_value, w_dir, w_beta,
               b_beta, w_out, gain_mlp, w_gate, w_up, w_down):
    every = ("dp", "hid", "wid")
    n_dp, n_hid, n_wid = (lax.axis_size(axis) for axis in every)
    row_count, tok, width = layer_in.shape
    heads = b_beta.shape[0]
    own_heads = heads // n_hid
    span = width // n_hid
    shard = w_query.shape[0]
    held = n_wid * tok
    copies = n_wid // row_count
    my_hid = lax.axis_index("hid")

    row_in = lax.all_gather(to_row(layer_in), "hid", axis=0, tiled=True)
    segs = lax.all_gather(segment_ids, ("hid", "wid"), axis=0, tiled=False)
    segs = lax.dynamic_index_in_dim(segs, lax.axis_index("wid") // copies, 1, False).reshape(-1)

    small = jnp.concatenate([w_beta, gain_attn[:, None], gain_mlp[:, None]], axis=1)
    small = lax.all_gather(small.reshape(-1), every, axis=0, tiled=True).reshape(width, heads + 2)
    beta_own = lax.dynamic_slice_in_dim(small[:, :heads], my_hid * own_heads, own_heads, 1)
    bias_own = lax.dynamic_slice_in_dim(b_beta, my_hid * own_heads, own_heads, 0).astype(F32)
    gain_one, gain_two = small[:, heads].astype(F32), small[:, heads + 1].astype(F32)

    cat = jnp.stack([w_query, w_key, w_value, w_dir], axis=1).reshape(shard, 4, n_hid, span)
    cat = cat.transpose(2, 0, 1, 3).reshape(n_hid, shard, 4 * span)
    cat = lax.all_to_all(cat, "hid", 0, 0, tiled=True)
    cat = lax.all_gather(cat, ("dp", "wid"), axis=0, tiled=False)
    cat = cat.reshape(n_dp, n_wid, n_hid, shard, 4 * span).transpose(0, 2, 1, 3, 4)
    cat = cat.reshape(width, 4 * span)
    wout_full = lax.all_gather(w_out, every, axis=0, tiled=True)

    ff = jnp.stack([w_gate, w_up, w_down.T], axis=0)
    ff_rows, ff_cols = ff.shape[1], ff.shape[2]
    part = ff_cols // n_dp
    ff = ff.reshape(3, ff_rows, n_dp, part).transpose(2, 0, 1, 3)
    ff = lax.all_to_all(ff, "dp", 0, 0, tiled=True)
    ff = lax.all_gather(ff, ("hid", "wid"), axis=0, tiled=False)
    ff = ff.reshape(n_hid, n_wid, n_dp, 3, ff_rows, part).transpose(3, 2, 1, 4, 0, 5)
    ff = ff.reshape(3, width, ff_cols)
    gate_w, up_w, down_wt = ff[0], ff[1], ff[2]

    act_one = norm_in(row_in.astype(F32), gain_one).astype(BF16)
    query = mm(act_one, cat[:, :span]).astype(BF16)
    key = mm(act_one, cat[:, span : 2 * span]).astype(BF16)
    value = mm(act_one, cat[:, 2 * span : 3 * span]).astype(BF16)
    raw = mm(act_one, cat[:, 3 * span :])
    logits = mm(act_one, beta_own) + bias_own
    logits = logits.reshape(-1, tok, own_heads).transpose(0, 2, 1)
    att, saved = attention_forward(query, key, value, raw, logits, segs, tok)

    att = lax.all_to_all(att.reshape(n_hid, held, span), "hid", 0, 0, tiled=True)
    att = from_row(att.transpose(1, 0, 2).reshape(held, width), row_count)
    att = att.reshape(row_count * tok, width)

    layer_f = layer_in.astype(F32).reshape(row_count * tok, width)
    grad_b = out_grad.reshape(row_count * tok, width)
    middle = layer_f + mm(att, wout_full)
    act_two = norm_in(middle, gain_two).astype(BF16)
    act_all = lax.all_gather(act_two, "dp", axis=0, tiled=True)
    grad_all = lax.all_gather(grad_b, "dp", axis=0, tiled=True)
    gate, up = mm(act_all, gate_w), mm(act_all, up_w)
    sig = jax.nn.sigmoid(gate)
    silu = gate * sig
    hidden = (silu * up).astype(BF16)
    mlp = lax.psum_scatter(mm(hidden, down_wt, NT).astype(BF16), "dp", scatter_dimension=0, tiled=True)
    layer_out = (middle + mlp.astype(F32)).astype(BF16)
    d_hidden = mm(grad_all, down_wt)
    d_gate = (d_hidden * up * sig * (1.0 + gate * (1.0 - sig))).astype(BF16)
    d_up = (d_hidden * silu).astype(BF16)
    d_act = mm(d_gate, gate_w, NT) + mm(d_up, up_w, NT)
    d_act = lax.psum_scatter(d_act.astype(BF16), "dp", scatter_dimension=0, tiled=True).astype(F32)
    ff_grads = jnp.stack([mm(act_all, d_gate, TN).astype(BF16), mm(act_all, d_up, TN).astype(BF16),
                          mm(grad_all, hidden, TN).astype(BF16)], axis=0)
    ff_grads = ff_grads.reshape(3, n_dp, n_wid, ff_rows, n_hid, part).transpose(4, 2, 1, 0, 3, 5)
    ff_grads = ff_grads.reshape(n_hid * n_wid, n_dp, 3, ff_rows, part)
    ff_grads = lax.psum_scatter(ff_grads, ("hid", "wid"), scatter_dimension=0, tiled=True)[0]
    ff_grads = lax.all_to_all(ff_grads, "dp", 0, 0, tiled=True)
    ff_grads = ff_grads.transpose(1, 2, 0, 3).reshape(3, ff_rows, ff_cols).astype(F32)

    _, pull_two = jax.vjp(norm_in, middle, gain_two)
    d_mid_norm, d_gain_two = pull_two(d_act)
    d_middle = grad_b.astype(F32) + d_mid_norm
    d_branch = d_middle.astype(BF16)
    d_att = mm(d_branch, wout_full, NT).astype(BF16).reshape(row_count, tok, width)
    d_att = to_row(d_att).reshape(held, n_hid, span).transpose(1, 0, 2)
    d_att = lax.all_to_all(d_att, "hid", 0, 0, tiled=True).reshape(n_hid * held, span)
    grad_wout = mm(att, d_branch, TN).astype(BF16)
    grad_wout = lax.psum_scatter(grad_wout, every, scatter_dimension=0, tiled=True).astype(F32)

    dq, dk, dv, draw, dlogit = attention_backward(saved, d_att, tok)
    d_cat = jnp.concatenate([dq, dk, dv, draw], axis=1)
    d_logit = dlogit.transpose(0, 2, 1).reshape(-1, own_heads).astype(BF16)
    d_act_one = mm(d_cat, cat, NT) + mm(d_logit, beta_own, NT)
    d_act_one = lax.psum_scatter(d_act_one.astype(BF16), "hid", scatter_dimension=0, tiled=True)
    d_act_one = from_row(d_act_one, row_count).reshape(row_count * tok, width).astype(F32)
    if copies > 1:
        first = lax.axis_index("wid") % copies == 0
        d_cat, d_logit = jnp.where(first, d_cat, 0), jnp.where(first, d_logit, 0)
    cat_grad = mm(act_one, d_cat, TN).astype(BF16)
    cat_grad = cat_grad.reshape(n_dp, n_hid, n_wid, shard, 4 * span).transpose(0, 2, 1, 3, 4)
    cat_grad = cat_grad.reshape(n_dp * n_wid, n_hid, shard, 4 * span)
    cat_grad = lax.psum_scatter(cat_grad, ("dp", "wid"), scatter_dimension=0, tiled=True)[0]
    cat_grad = lax.all_to_all(cat_grad, "hid", 0, 0, tiled=True)
    cat_grad = cat_grad.reshape(n_hid, shard, 4, span).transpose(2, 1, 0, 3)
    cat_grad = cat_grad.reshape(4, shard, width).astype(F32)

    _, pull_one = jax.vjp(norm_in, layer_f, gain_one)
    d_in_norm, d_gain_one = pull_one(d_act_one)
    grad_in = (d_middle + d_in_norm).astype(BF16)

    beta_grad = lax.dynamic_update_slice_in_dim(
        jnp.zeros((width, heads), F32), mm(act_one, d_logit, TN), my_hid * own_heads, 1)
    bias_grad = lax.dynamic_update_slice_in_dim(
        jnp.zeros((heads,), F32), jnp.sum(d_logit.astype(F32), axis=0), my_hid * own_heads, 0)
    small_grad = jnp.concatenate([beta_grad, d_gain_one[:, None], d_gain_two[:, None]], axis=1)
    small_grad = lax.psum_scatter(
        small_grad.reshape(n_dp * n_hid * n_wid, -1), every, scatter_dimension=0, tiled=True)
    small_grad = small_grad.reshape(shard, heads + 2)
    bias_grad = lax.psum(bias_grad, every)

    return (
        layer_out.reshape(layer_in.shape), grad_in.reshape(layer_in.shape), small_grad[:, heads],
        cat_grad[0], cat_grad[1], cat_grad[2], cat_grad[3], small_grad[:, :heads], bias_grad,
        grad_wout, small_grad[:, heads + 1], ff_grads[0], ff_grads[1], ff_grads[2].T,
    )


def solution(mesh):
    in_specs = (
        P("dp", ("hid", "wid"), None),
        P("dp", ("hid", "wid")),
        P("dp", ("hid", "wid"), None),
        P(("dp", "hid", "wid")),
        P(("dp", "hid", "wid"), None),
        P(("dp", "hid", "wid"), None),
        P(("dp", "hid", "wid"), None),
        P(("dp", "hid", "wid"), None),
        P(("dp", "hid", "wid"), None),
        P(),
        P(("dp", "hid", "wid"), None),
        P(("dp", "hid", "wid")),
        P(("dp", "wid"), "hid"),
        P(("dp", "wid"), "hid"),
        P("hid", ("dp", "wid")),
    )
    out_specs = (
        P("dp", ("hid", "wid"), None),
        P("dp", ("hid", "wid"), None),
        P(("dp", "hid", "wid")),
        P(("dp", "hid", "wid"), None),
        P(("dp", "hid", "wid"), None),
        P(("dp", "hid", "wid"), None),
        P(("dp", "hid", "wid"), None),
        P(("dp", "hid", "wid"), None),
        P(),
        P(("dp", "hid", "wid"), None),
        P(("dp", "hid", "wid")),
        P(("dp", "wid"), "hid"),
        P(("dp", "wid"), "hid"),
        P("hid", ("dp", "wid")),
    )
    return jax.shard_map(
        per_device, mesh=mesh, in_specs=in_specs, out_specs=out_specs, check_vma=False
    )
```

time: 3010 us -> 1110 us (0.37)
  waiting for transfers between devices: 1640 us -> 468 us
  matrix products: 505 us -> 107 us
  starting transfers between devices: 352 us -> 10.6 us
  other arithmetic: 293 us -> 41.7 us
  Pallas kernels: 0 us -> 157 us
  blocking collectives: 118 us -> 207 us
    ppermute x37 -> x4, waiting for transfers between devices: 622 us -> 5.02 us  [the longest x2 3.41 us: to_row(): lax.ppermute(lax.dynamic_index_in_dim(x, 1 - me, 0, False), 'wid', [(0, 1...]
    reduce_scatter x10 -> x6, waiting for transfers between devices: 793 us -> 253 us  [the longest x1 79.3 us: per_device(): lax.psum_scatter(ff_grads, ('hid', 'wid'), scatter_dimension=0, tiled=True)]
    dot_general x148 -> x21, matrix products: 477 us -> 107 us  [mm(): lax.dot_general(left, right, (dims, ((), ())), preferred_element_type=F32)]
    ppermute x37 -> x4, starting transfers between devices: 351 us -> 0.33 us  [the longest x2 0.18 us: from_row(): lax.ppermute(lax.dynamic_index_in_dim(parts, 1 - me, 0, False), 'wid', [(...]
    another operation x1 -> x3, other arithmetic: 237 us -> 3.06 us  [from_row(): jnp.stack([jnp.where(me == 0, mine, got), jnp.where(me == 0, got, mine)],...]
    pallas_call x0 -> x4, Pallas kernels: none -> 157 us  [run(): pl.pallas_call(body, grid=(grid,), in_specs=in_specs, out_specs=out_specs...]
    all_gather x11 -> x6, waiting for transfers between devices: 216 us -> 68.9 us  [the longest x1 32.2 us: per_device(): grad_all = lax.all_gather(grad_b, 'dp', axis=0, tiled=True)]
    unnamed x25 -> x14, waiting for transfers between devices: 6.25 us -> 126 us
  transfers between devices with their start and end apart: 60 -> 19, of which waited for: 28 -> 13; matrix products, arithmetic and copies ran while one was open for 28% -> 18% of each run, Pallas kernels for 0% -> 8%
where the time goes in v1:
time: 1110 us; the launch traced here: 1100 us
  waiting for transfers between devices  468 us (42%)
  blocking collectives  207 us (19%)
  Pallas kernels  157 us (14%)
  matrix products  107 us (10%)
  local copies, waits for them, and re-layouts  95.1 us (9%)
  other arithmetic  41.7 us (4%)
  between operations  15.1 us (1%)
    pallas_call x4, Pallas kernels, run(): pl.pallas_call(body, grid=(grid,), in_specs=in_specs, out_specs=out_specs...  157 us
    unnamed x14, waiting for transfers between devices  126 us
    dot_general x21, matrix products, mm(): lax.dot_general(left, right, (dims, ((), ())), preferred_element_type=F32)  107 us
    reduce_scatter x1, waiting for transfers between devices, per_device(): lax.psum_scatter(ff_grads, ('hid', 'wid'), scatter_dimension=0, tiled=True)  79.3 us
    reduce_scatter x1, waiting for transfers between devices, per_device(): lax.psum_scatter(cat_grad, ('dp', 'wid'), scatter_dimension=0, tiled=True)  54.3 us
    reduce_scatter x1, waiting for transfers between devices, per_device(): lax.psum_scatter(mm(hidden, down_wt, NT).astype(BF16), 'dp', scatter_dime...  43.5 us
    all_to_all x1, blocking collectives, per_device(): lax.all_to_all(att.reshape(n_hid, held, span), 'hid', 0, 0, tiled=True)  42.5 us
    unnamed x1, blocking collectives  41 us
  transfers between devices with their start and end apart: 19, of which 13 were waited for; matrix products, arithmetic and copies ran while one was open for 18% of the time, Pallas kernels for 8%

profile of v1, /device:TPU:8, one launch (start us, length us, event | category | flops | bytes accessed | tf_op | source)
XLA Modules:
  0.0 1101.9 jit_solution(520204752563732860)
XLA Ops:
  15.1 34.1 %all_to_all.30 = bf16[4,48,1536]{2,1,0:T(8,128)(2,1)} all-to-all(bf16[4,48,1536]{2,1,0:T(8,128)(2,1)S(1)} %reshape.237), channel_id=1, replica_groups=mesh['dp'=4,'hid'=4,'wid'=2] {'hid'}, dimensions={0} | all-to-all | bytes 1179648 | tf_op jit(solution)/shard_map/all_to_all | solution.py:372
  52.1 16.4 %all_to_all.31 = bf16[4,3,192,256]{3,2,1,0:T(8,128)(2,1)} all-to-all(bf16[4,3,192,256]{3,2,1,0:T(8,128)(2,1)S(1)} %copy.137), channel_id=1, replica_groups=mesh['dp'=4,'hid'=4,'wid'=2] {'dp'}, dimensions={0} | all-to-all | bytes 2359296 | tf_op jit(solution)/shard_map/all_to_all | solution.py:382
  69.1 41.0 %all-reduce = bf16[21504]{0:T(1024)(128)(2,1)S(1)} all-reduce(bf16[21504]{0:T(1024)(128)(2,1)S(1)} %dynamic-update-slice), channel_id=1, replica_groups=mesh['dp'=4,'hid'=4,'wid'=2] {'dp','hid','wid'}, use_global_device_ids=true, to_apply=%add | all-reduce | flops 21504 | bytes 86016
  111.0 9.0 all-gather.3
  122.8 2.8 fusion
  136.2 2.9 fusion.18.raw_ref
  141.8 64.1 %shard_map.254 = (bf16[1024,384]{1,0:T(8,128)(2,1)}, bf16[1024,384]{1,0:T(8,128)(2,1)}, bf16[1024,384]{1,0:T(8,128)(2,1)}, bf16[1024,384]{1,0:T(8,128)(2,1)}, f3...) custom-call(bf16[1024,384]{1,0:T(8,128)(2,1)} %convolution_convert_f, ...), custom_call_target="tpu_custom_call" | custom-call | flops 6241124352 | bytes 14168064 | tf_op jit(solution)/shard_map/pallas_call | solution.py:232
  206.0 27.4 %shard_map.255 = (bf16[1024,384]{1,0:T(8,128)(2,1)}, bf16[8,3,128,1024]{3,2,1,0:T(8,128)(2,1)}, bf16[8,3,1024,128]{3,2,1,0:T(8,128)(2,1)}) custom-call(bf16[1024,384]{1,0:T(8,128)(2,1)} %get-tuple-element.35.qin_ref, bf16[1024,384]{1,0:T(8,128)(2,1)} %get-tuple-element.36.kout_ref, bf16[1024,384]{1,0:T(8,128)(2,1)} %get-tuple-element.37.ptop_ref, ...), custom_call_target="tpu_custom_call" | custom-call | flops 3221225472 | bytes 18882560 | tf_op jit(solution)/shard_map/pallas_call | solution.py:232
  233.3 42.5 %all_to_all.32 = bf16[4,256,384]{2,1,0:T(8,128)(2,1)S(1)} all-to-all(bf16[4,256,384]{2,1,0:T(8,128)(2,1)} %bitcast.242), channel_id=1, replica_groups=mesh['dp'=4,'hid'=4,'wid'=2] {'hid'}, dimensions={0} | all-to-all | bytes 1572864 | tf_op jit(solution)/shard_map/all_to_all | solution.py:397
  284.5 4.2 multiply_reduce_fusion.3
  291.6 5.7 all-gather.21.cloned.1.call-done
  297.3 4.5 fusion.43
  316.3 30.9 %all-gather.15.cloned.1.call-done = bf16[1024,1536]{1,0:T(8,128)(2,1)} async-done(((bf16[256,1536]{1,0:T(8,128)(2,1)}), bf16[1024,1536]{1,0:T(8,128)(2,1)}) %all-gather.15.cloned.1.call-update) | async-done | bytes 3145744 | tf_op jit(solution)/shard_map/all_gather | solution.py:405
  347.3 8.5 fusion.46
  355.8 5.0 fusion.47
  360.8 32.2 %all-gather.17.cloned.1.call-done = bf16[1024,1536]{1,0:T(8,128)(2,1)} async-done(((bf16[256,1536]{1,0:T(8,128)(2,1)}), bf16[1024,1536]{1,0:T(8,128)(2,1)}) %all-gather.17.cloned.1.call-update) | async-done | bytes 3145744 | tf_op jit(solution)/shard_map/all_gather | solution.py:406
  393.0 11.5 %fusion.6 = (bf16[1024,1024]{1,0:T(8,128)(2,1)S(1)}, bf16[1024,1024]{1,0:T(8,128)(2,1)S(1)}, bf16[1024,1024]{1,0:T(8,128)(2,1)}) fusion(f32[1024,1024]{1,0:T(8,128)} %fusion.46, f32[1024,1024]{1,0:T(8,128)} %fusion.47, bf16[1024,1536]{1,0:T(8,128)(2,1)} %all-gather.17.cloned.1.call-done, bf16[1536,1024]{1,0:T(8,128)(2,1)} %bitcast.220), kind=kOutput, calls=%fused_computation.15 | convolution fusion | flops 3236954112 | bytes 20971520 | tf_op jit(solution)/shard_map/dot_general | solution.py:321
  404.5 3.5 fusion.48
  408.0 5.0 add_convert_fusion.1
  413.1 7.6 convolution_convert_fusion.5
  420.8 36.4 %reduce-scatter.9.cloned.1.call-done = bf16[256,1536]{1,0:T(8,128)(2,1)} async-done(((bf16[1024,1536]{1,0:T(8,128)(2,1)}), bf16[256,1536]{1,0:T(8,128)(2,1)}) %reduce-scatter.9.cloned.1.call-update) | async-done | bytes 786448 | tf_op jit(solution)/shard_map/reduce_scatter | solution.py:417
  460.6 43.5 %reduce-scatter.7.cloned.1.call-done = bf16[256,1536]{1,0:T(8,128)(2,1)} async-done(((bf16[1024,1536]{1,0:T(8,128)(2,1)}), bf16[256,1536]{1,0:T(8,128)(2,1)}) %reduce-scatter.7.cloned.1.call-update) | async-done | bytes 786448 | tf_op jit(solution)/shard_map/reduce_scatter | solution.py:411
  504.2 3.5 fusion.13
  507.7 4.3 convolution_convert_fusion.6
  514.1 24.0 %all_to_all.33 = bf16[4,256,384]{2,1,0:T(8,128)(2,1)} all-to-all(bf16[4,256,384]{2,1,0:T(8,128)(2,1)S(1)} %bitcast.228), channel_id=1, replica_groups=mesh['dp'=4,'hid'=4,'wid'=2] {'hid'}, dimensions={0} | all-to-all | bytes 1572864 | tf_op jit(solution)/shard_map/all_to_all | solution.py:432
  538.1 35.5 %shard_map.256 = (f32[1024,384]{1,0:T(8,128)}, bf16[1024,384]{1,0:T(8,128)(2,1)}, f32[1024,384]{1,0:T(8,128)}, f32[1024,384]{1,0:T(8,128)}, bf16[1024,384]{1,0:T(8,128)(2,1)}) custom-call(bf16[1024,384]{1,0:T(8,128)(2,1)} %bitcast.241, bf16[1024,384]{1,0:T(8,128)(2,1)} %convolution_convert_fusion.7.v_ref, ...), custom_call_target="tpu_custom_call" | custom-call | flops 5637144576 | bytes 22806528 | tf_op jit(solution)/shard_map/pallas_call | solution.py:232
  573.7 30.1 %shard_map.257 = (bf16[1024,384]{1,0:T(8,128)(2,1)}, bf16[1024,384]{1,0:T(8,128)(2,1)}, bf16[1024,384]{1,0:T(8,128)(2,1)}, f32[8,3,128]{2,1,0:T(4,128)}) custom-call(bf16[1024,384]{1,0:T(8,128)(2,1)} %convolution_convert_fusion.9.q_ref, bf16[1024,384]{1,0:T(8,128)(2,1)} %convolution_convert_fusion.8.k_ref, f32[1024,384]{1,0:T(8,128)} %fusion.18.raw_ref, ...), custom_call_target="tpu_custom_call" | custom-call | flops 6039797760 | bytes 17326080 | tf_op jit(solution)/shard_map/pallas_call | solution.py:232
  606.8 5.1 fusion.49
  611.9 2.9 add_convert_fusion
  614.9 5.2 convolution_convert_fusion.1
  620.4 7.5 convolution_convert_fusion
  630.4 7.7 fusion.8
  638.1 4.7 copy.149
  642.9 6.2 stack.74
  649.0 7.7 convolution_convert_fusion.3
  656.7 6.2 stack.73
  662.9 7.7 convolution_convert_fusion.4
  670.6 6.1 stack.72
  676.8 11.0 maximum_bitcast_fusion
  687.7 9.3 copy.150
  705.1 40.0 %psum.7 = f32[12]{0:T(128)} all-reduce(f32[12]{0:T(128)} %dynamic_update_slice.7), channel_id=1, replica_groups=mesh['dp'=4,'hid'=4,'wid'=2] {'dp','hid','wid'}, use_global_device_ids=true, to_apply=%region_13.14 | all-reduce | flops 12 | bytes 96 | tf_op jit(solution)/shard_map/psum | solution.py:465
  747.3 39.6 %reduce-scatter.15.cloned.1.call-done = bf16[48,1536]{1,0:T(8,128)(2,1)} async-done(((bf16[1536,1536]{1,0:T(8,128)(2,1)}), bf16[48,1536]{1,0:T(8,128)(2,1)}) %reduce-scatter.15.cloned.1.call-update) | async-done | bytes 147472 | tf_op jit(solution)/shard_map/reduce_scatter | solution.py:434
  789.7 54.3 %reduce-scatter.13.cloned.1.call-done = bf16[1,4,48,1536]{3,2,1,0:T(8,128)(2,1)} async-done(((bf16[8,4,48,1536]{3,2,1,0:T(8,128)(2,1)}), bf16[1,4,48,1536]{3,2,1,0:T(8,128)(2,1)}) %reduce-scatter.13.cloned.1.call-update) | async-done | bytes 589840 | tf_op jit(solution)/shard_map/reduce_scatter | solution.py:448
  844.0 5.1 all-to-all-start.4
  854.9 15.0 %all-to-all-done.4 = bf16[4,48,1536]{2,1,0:T(8,128)(2,1)} async-done(((bf16[4,48,1536]{2,1,0:T(8,128)(2,1)}), bf16[4,48,1536]{2,1,0:T(8,128)(2,1)}, u32[]{:S(2)}, u32[]{:S(2)}) %all-to-all-start.4) | async-done | bytes 589856 | tf_op jit(solution)/shard_map/all_to_all | solution.py:449
  869.9 79.3 %reduce-scatter.17.cloned.1.call-done = bf16[1,4,3,192,256]{4,3,2,1,0:T(8,128)(2,1)} async-done(((bf16[8,4,3,192,256]{4,3,2,1,0:T(8,128)(2,1)}), bf16[1,4,3,192,256]{4,3,2,1,0:T(8,128)(2,1)}) %reduce-scatter.17.cloned.1.call-update) | async-done | bytes 1179664 | tf_op jit(solution)/shard_map/reduce_scatter | solution.py:422
  949.2 4.3 all-to-all-start.5
  956.2 124.5 %all-reduce.4.cloned.1.call-done = f32[32,672]{1,0:T(8,128)} async-done(((f32[32,672]{1,0:T(8,128)}), f32[32,672]{1,0:T(8,128)}) %all-reduce.4.cloned.1.call-update) | async-done | bytes 86032
  (217 shorter events, 100.9 us)
Async XLA Ops:
  7.2 5.1 copy-start.16
  7.2 5.4 copy-start.17
  7.2 5.7 copy-start.18
  7.2 115.6 %all-gather.11.cloned.1.call-start = ((), (), s32[]{:S(2)}) async-start(), calls=%async_computation.12 | async-start | bytes 3932160 | tf_op jit(solution)/shard_map/all_gather | solution.py:360
  8.4 4.7 copy-start.19
  8.4 1.8 collective-permute-start
  12.2 116.0 %all-gather.19.cloned.1.call-start = ((), (), s32[]{:S(2)}) async-start(), calls=%async_computation.22 | async-start | bytes 5308416 | tf_op jit(solution)/shard_map/all_gather | solution.py:373
  12.9 37.1 %copy-start.11 = (bf16[1024,192]{0,1:T(8,128)(2,1)S(1)}, bf16[1024,192]{0,1:T(8,128)(2,1)}, u32[]{:S(2)}) copy-start(bf16[1024,192]{0,1:T(8,128)(2,1)} %param.29) | copy-start | bytes 1179652
  13.2 37.1 %copy-start.12 = (bf16[192,1024]{1,0:T(8,128)(2,1)S(1)}, bf16[192,1024]{1,0:T(8,128)(2,1)}, u32[]{:S(2)}) copy-start(bf16[192,1024]{1,0:T(8,128)(2,1)} %param.28) | copy-start | bytes 1179652
  13.5 37.1 %copy-start.13 = (bf16[192,1024]{1,0:T(8,128)(2,1)S(1)}, bf16[192,1024]{1,0:T(8,128)(2,1)}, u32[]{:S(2)}) copy-start(bf16[192,1024]{1,0:T(8,128)(2,1)} %param.27) | copy-start | bytes 1179652
  49.2 235.2 %all-gather.13.cloned.1.call-start = ((), (), s32[]{:S(2)}) async-start(), calls=%async_computation.13 | async-start | bytes 4866048 | tf_op jit(solution)/shard_map/all_gather | solution.py:376
  50.0 247.3 %all-gather.21.cloned.1.call-start = ((), (), s32[]{:S(2)}) async-start(), calls=%async_computation.23 | async-start | bytes 10616832 | tf_op jit(solution)/shard_map/all_gather | solution.py:383
  51.9 16.7 %copy-start.27 = (bf16[48,12]{0,1:T(8,128)(2,1)S(1)}, bf16[48,12]{0,1:T(8,128)(2,1)}, u32[]{:S(2)}) copy-start(bf16[48,12]{0,1:T(8,128)(2,1)} %param.23) | copy-start | bytes 3460
  51.9 16.7 %copy-start.30 = (bf16[48]{0:T(256)(128)(2,1)S(1)}, bf16[48]{0:T(256)(128)(2,1)}, u32[]{:S(2)}) copy-start(bf16[48]{0:T(256)(128)(2,1)} %param.26) | copy-start | bytes 292
  51.9 16.7 %copy-start.31 = (bf16[48]{0:T(256)(128)(2,1)S(1)}, bf16[48]{0:T(256)(128)(2,1)}, u32[]{:S(2)}) copy-start(bf16[48]{0:T(256)(128)(2,1)} %param.18) | copy-start | bytes 292
  51.9 59.1 %copy-start.28 = (s32[2,128]{1,0:T(2,128)S(1)}, s32[2,128]{1,0:T(2,128)}, u32[]{:S(2)}) copy-start(s32[2,128]{1,0:T(2,128)} %param.16) | copy-start | bytes 3076
  51.9 69.7 %copy-start.33 = (bf16[12]{0:T(256)(128)(2,1)S(1)}, bf16[12]{0:T(256)(128)(2,1)}, u32[]{:S(2)}) copy-start(bf16[12]{0:T(256)(128)(2,1)} %param.24) | copy-start | bytes 76
  68.5 278.8 %all-gather.15.cloned.1.call-start = ((), (), s32[]{:S(2)}) async-start(), calls=%async_computation.14 | async-start | bytes 3932160 | tf_op jit(solution)/shard_map/all_gather | solution.py:405
  122.8 3.8 copy-start.20
  130.8 8.3 copy-start.5
  280.7 1.8 collective-permute-start.1
  288.7 13.1 %copy-start.26 = (f32[256]{0:T(256)}, f32[256]{0:T(256)S(1)}, u32[]{:S(2)}) copy-start(f32[256]{0:T(256)S(1)} %get-tuple-element.161) | copy-start | bytes 3076
  290.9 102.0 %all-gather.17.cloned.1.call-start = ((), (), s32[]{:S(2)}) async-start(), calls=%async_computation.16 | async-start | bytes 3932160 | tf_op jit(solution)/shard_map/all_gather | solution.py:406
  291.5 165.7 %reduce-scatter.9.cloned.1.call-start = ((), (), s32[]{:S(2)}) async-start(), calls=%async_computation.17 | async-start | bytes 3932160 | tf_op jit(solution)/shard_map/reduce_scatter | solution.py:417
  347.3 8.5 copy-start.7
  347.3 8.5 copy-start.32
  393.0 11.5 %copy-start.6 = (bf16[192,8,4,256]{3,1,2,0:T(8,128)(2,1)S(1)}, bf16[192,8,4,256]{3,1,2,0:T(8,128)(2,1)}, u32[]{:S(2)}) copy-start(bf16[192,8,4,256]{3,1,2,0:T(8,128)(2,1)} %copy.158) | copy-start | bytes 9437188
  413.1 91.1 %reduce-scatter.7.cloned.1.call-start = ((), (), s32[]{:S(2)}) async-start(), calls=%async_computation.15 | async-start | bytes 3932160 | tf_op jit(solution)/shard_map/reduce_scatter | solution.py:411
  420.8 278.8 %reduce-scatter.11.cloned.1.call-start = ((), (), s32[]{:S(2)}) async-start(), calls=%async_computation.18 | async-start | bytes 3932160 | tf_op jit(solution)/shard_map/reduce_scatter | solution.py:440
  507.7 4.3 copy-start.1
  512.1 1.8 collective-permute-start.2
  573.7 33.1 %slice-start = ((s8[4718592]{0:T(1024)(128)(4,1)}), s8[4194304]{0:T(1024)(128)(4,1)S(1)}, s32[]{:S(2)}) async-start(s8[4718592]{0:T(1024)(128)(4,1)} %bitcast.214), calls=%async_computation.25 | async-start | bytes 8388608
  573.7 33.1 %slice-start.1 = ((s8[4718592]{0:T(1024)(128)(4,1)}), s8[524288]{0:T(1024)(128)(4,1)S(1)}, s32[]{:S(2)}) async-start(s8[4718592]{0:T(1024)(128)(4,1)} %bitcast.214), calls=%async_computation.26 | async-start | bytes 1048576
  606.8 5.1 copy-start.14
  606.8 5.1 copy-start.15
  614.8 172.2 %reduce-scatter.15.cloned.1.call-start = ((), (), s32[]{:S(2)}) async-start(), calls=%async_computation.20 | async-start | bytes 4866048 | tf_op jit(solution)/shard_map/reduce_scatter | solution.py:434
  620.1 223.9 %reduce-scatter.13.cloned.1.call-start = ((), (), s32[]{:S(2)}) async-start(), calls=%async_computation.19 | async-start | bytes 5308416 | tf_op jit(solution)/shard_map/reduce_scatter | solution.py:448
  630.4 318.8 %reduce-scatter.17.cloned.1.call-start = ((), (), s32[]{:S(2)}) async-start(), calls=%async_computation.21 | async-start | bytes 10616832 | tf_op jit(solution)/shard_map/reduce_scatter | solution.py:422
  701.4 87.3 %collective-permute-start.3 = (bf16[128,1536]{1,0:T(8,128)(2,1)}, bf16[128,1536]{1,0:T(8,128)(2,1)S(1)}, u32[]{:S(2)}, u32[]{:S(2)}) collective-permute-start(bf16[128,1536]{1,0:T(8,128)(2,1)} %dynamic-slice_bitcast_fusion), channel_id=1, source_target_pairs={{0,1},{1,0},{2,3},{3,2},{4,5},{5,4},{6,7},{7,6},{8,9},{9,8},{10,11... | collective-permute-start | bytes 1179656 | tf_op jit(solution)/shard_map/ppermute | solution.py:341
  746.2 103.2 %copy-start.4 = (bf16[2,128,1536]{2,1,0:T(8,128)(2,1)S(1)}, bf16[2,128,1536]{2,1,0:T(8,128)(2,1)}, u32[]{:S(2)}) copy-start(bf16[2,128,1536]{2,1,0:T(8,128)(2,1)} %param.15) | copy-start | bytes 2359300
  746.2 103.2 %copy-start.21 = (f32[1536]{0:T(1024)S(1)}, f32[1536]{0:T(1024)}, u32[]{:S(2)}) copy-start(f32[1536]{0:T(1024)} %copy-done.20) | copy-start | bytes 18436
  746.2 103.2 %copy-start.25 = (f32[2,128]{1,0:T(2,128)S(1)}, f32[2,128]{1,0:T(2,128)}, u32[]{:S(2)}) copy-start(f32[2,128]{1,0:T(2,128)} %fusion.40) | copy-start | bytes 3076
  746.2 104.0 %copy-start.22 = (f32[1536,1]{0,1:T(1,128)S(1)}, f32[1536,1]{0,1:T(1,128)}, u32[]{:S(2)}) copy-start(f32[1536,1]{0,1:T(1,128)} %broadcast_in_dim.36) | copy-start | bytes 18436
  788.6 65.0 %copy-start.24 = (f32[2,128]{1,0:T(2,128)S(1)}, f32[2,128]{1,0:T(2,128)}, u32[]{:S(2)}) copy-start(f32[2,128]{1,0:T(2,128)} %copy-done.23) | copy-start | bytes 3076
  844.0 25.9 %all-to-all-start.4 = ((bf16[4,48,1536]{2,1,0:T(8,128)(2,1)}), bf16[4,48,1536]{2,1,0:T(8,128)(2,1)}, u32[]{:S(2)}, u32[]{:S(2)}) async-start(bf16[4,48,1536]{2,1,0:T(8,128)(2,1)} %bitcast.249), calls=%async_computation.8 | async-start | bytes 1179648 | tf_op jit(solution)/shard_map/all_to_all | solution.py:449
  849.2 231.5 %all-reduce.4.cloned.1.call-start = ((), (), s32[]{:S(2)}) async-start(), calls=%async_computation.24 | async-start | bytes 196608
  850.2 103.2 %copy-start.2 = (f32[256,1536]{1,0:T(8,128)S(1)}, f32[256,1536]{1,0:T(8,128)}, u32[]{:S(2)}) copy-start(f32[256,1536]{1,0:T(8,128)} %copy-done.1) | copy-start | bytes 4718596
  949.2 139.7 %all-to-all-start.5 = ((bf16[4,3,192,256]{3,2,1,0:T(8,128)(2,1)}), bf16[4,3,192,256]{3,2,1,0:T(8,128)(2,1)}, u32[]{:S(2)}, u32[]{:S(2)}) async-start(bf16[4,3,192,256]{3,2,1,0:T(8,128)(2,1)} %bitcast.233), calls=%async_computation.11 | async-start | bytes 2359296 | tf_op jit(solution)/shard_map/all_to_all | solution.py:423
  (9 other events, 21.4 us)
Sparse Core Ops, SparseCore 0:
  12.3 71.5 all-gather.10
  85.8 41.5 all-gather.18
  130.4 64.7 all-gather.12
  196.7 100.5 all-gather.20
  299.6 47.6 all-gather.14
  349.0 43.9 all-gather.16
  413.2 43.9 reduce-scatter.8
  460.2 43.9 reduce-scatter.6
  614.9 59.1 reduce-scatter.10
  679.4 107.5 reduce-scatter.14
  790.8 53.1 reduce-scatter.12
  846.2 102.9 reduce-scatter.16
  955.3 125.3 all-reduce.3

commit v2 on v1

v2 whole, which is shorter than its diff:
```python
import functools
import math

import jax
import jax.numpy as jnp
from jax import lax
from jax.experimental import pallas as pl
from jax.experimental.pallas import tpu as pltpu
from jax.sharding import PartitionSpec as P

EPS = 1e-06
NEG = -1e30
F32 = jnp.float32
BF16 = jnp.bfloat16
NN = ((1,), (0,))
NT = ((1,), (1,))
TN = ((0,), (0,))
VMEM_BYTES = 56 * 1024 * 1024
SOME = 2


def mm(left, right, dims=NN):
    return lax.dot_general(left, right, (dims, ((), ())), preferred_element_type=F32)


def halves(x):
    if x.dtype == BF16:
        return (x,)
    top = x.astype(BF16)
    return (top, (x - top.astype(F32)).astype(BF16))


def dot(left, right, dims):
    picked = [(a, b) for a in range(len(left)) for b in range(len(right)) if a + b < 2]
    if len(picked) == 1:
        return mm(left[0], right[0], dims)
    x = jnp.concatenate([left[a] for a, _ in picked], axis=dims[0][0])
    y = jnp.concatenate([right[b] for _, b in picked], axis=dims[1][0])
    return mm(x, y, dims)


def iotas(size):
    rows = lax.broadcasted_iota(jnp.int32, (size, size), 0)
    cols = lax.broadcasted_iota(jnp.int32, (size, size), 1)
    return rows, cols


def unit_dirs(raw):
    inv = lax.rsqrt(jnp.sum(raw * raw, axis=-1, keepdims=True) + EPS)
    return raw * inv, inv


def local_forward(heads, size, q_ref, k_ref, raw_ref, logit_ref, qin_ref, kout_ref, ptop_ref, plow_ref,
                  intra_ref, t_ref, e_ref, cm_ref, s_ref):
    width = q_ref.shape[1] // heads
    rows, cols = iotas(size)
    strict, lower, diag = rows > cols, rows >= cols, rows == cols
    apart = rows ^ cols
    some = range(q_ref.shape[0] // size)
    at = [(slice(n * size, (n + 1) * size), slice(h * width, (h + 1) * width)) for n in some for h in range(heads)]
    wide = [(slice(n * width, (n + 1) * width), slice(h * width, (h + 1) * width)) for n in some for h in range(heads)]
    every = range(len(at))
    betas = [2.0 * jax.nn.sigmoid(logit_ref[n, h : h + 1, :]) for n in some for h in range(heads)]
    q, k = [q_ref[a] for a in at], [k_ref[a] for a in at]
    ws = [halves(unit_dirs(raw_ref[a])[0]) for a in at]
    gram = [jnp.where(strict, dot(w, w, NT), 0.0) for w in ws]
    beta = [jnp.where(diag, b, 0.0) for b in betas]
    beta_col = [jnp.sum(b, axis=1, keepdims=True) for b in beta]
    t = [beta[u] - jnp.where(apart == 1, beta_col[u] * gram[u] * betas[u], 0.0) for u in every]
    shift = 1
    while (1 << shift) < size:
        near = (apart >> shift) == 1
        part = [halves(jnp.where(near, g, 0.0)) for g in gram]
        ts = [halves(x) for x in t]
        once = [dot(ts[u], part[u], NN) for u in every]
        t = [t[u] - dot(halves(once[u]), ts[u], NN) for u in every]
        shift += 1
    ts = [halves(x) for x in t]
    bs = [halves(jnp.where(lower, dot((q[u],), ws[u], NT), 0.0)) for u in every]
    ms = [halves(jnp.where(strict, dot(ws[u], (k[u],), NT), 0.0)) for u in every]
    e = [dot(ts[u], ms[u], NN) for u in every]
    s = [dot(ts[u], ws[u], NN) for u in every]
    cm = [dot(bs[u], ts[u], NN) for u in every]
    es = [halves(x) for x in e]
    for u in every:
        t_ref[at[u]], e_ref[at[u]], cm_ref[at[u]], s_ref[at[u]] = t[u], e[u], cm[u], s[u]
        intra_ref[at[u]] = dot((q[u],), (k[u],), NT) - dot(bs[u], es[u], NN)
        qin_ref[at[u]] = (q[u].astype(F32) - dot(halves(cm[u]), ws[u], NN)).astype(BF16)
        kout_ref[at[u]] = (k[u].astype(F32) - dot(es[u], ws[u], TN)).astype(BF16)
        step = jnp.where(diag, 1.0, 0.0) - dot(ws[u], halves(s[u]), TN)
        ptop_ref[wide[u]], plow_ref[wide[u]] = halves(step)


def cross_forward(heads, group, scale, qin_ref, kout_ref, ptop_ref, plow_ref, intra_ref, v_ref,
                  segc_ref, segr_ref, out_ref, prob_ref, keep_ref, frame, score):
    size = qin_ref.shape[0]
    width = qin_ref.shape[1] // heads
    total = v_ref.shape[0]
    wide = group * size
    c = pl.program_id(0)
    parts = [slice(g * wide, (g + 1) * wide) for g in range(total // wide)]
    at = [slice(h * width, (h + 1) * width) for h in range(heads)]
    every = range(heads)

    @pl.when(c == 0)
    def _():
        frame[...] = jnp.zeros_like(frame)
        score[...] = jnp.full_like(score, NEG)

    rows, cols = iotas(size)
    own = pl.multiple_of(c * size, size)
    seg = segc_ref[...]
    for g, part in enumerate(parts):

        @pl.when(g * group < c)
        def _():
            raw = [mm(qin_ref[:, at[h]], frame[h, part, :], NT) for h in every]
            place = lax.broadcasted_iota(jnp.int32, (size, wide), 1) + g * wide
            permit = (place < own) & (seg == segr_ref[:, part])
            for h in every:
                score[h, :, part] = jnp.where(permit, scale * raw[h], NEG)

    permit = (rows >= cols) & (seg == segr_ref[:, pl.ds(own, size)])
    for h in every:
        score[h, :, pl.ds(own, size)] = jnp.where(permit, scale * intra_ref[:, at[h]], NEG)
    top = [jnp.max(score[h], axis=-1, keepdims=True) for h in every]
    e = [jnp.exp(score[h] - top[h]) for h in every]
    inv = [1.0 / jnp.sum(x, axis=-1, keepdims=True) for x in e]
    for h in every:
        prob_ref[0, h] = (e[h] * inv[h]).astype(BF16)
    for h in every:
        out_ref[:, at[h]] = mm(prob_ref[0, h], v_ref[:, at[h]]).astype(BF16)
        keep_ref[0, h] = frame[h]
    for g, part in enumerate(parts):

        @pl.when(g * group < c)
        def _():
            moved = [dot((frame[h, part, :],), (ptop_ref[:, at[h]], plow_ref[:, at[h]]), NT) for h in every]
            for h in every:
                frame[h, part, :] = moved[h].astype(BF16)

    for h in every:
        frame[h, pl.ds(own, size), :] = kout_ref[:, at[h]]


def cross_backward(heads, group, scale, grad_ref, v_ref, prob_ref, keep_ref, qin_ref, ptop_ref,
                   plow_ref, dqin_ref, dintra_ref, dkout_ref, dstep_ref, dv_ref, carry, dvals, ds_ref):
    size = grad_ref.shape[0]
    width = grad_ref.shape[1] // heads
    total = v_ref.shape[0]
    wide = group * size
    c = pl.num_programs(0) - 1 - pl.program_id(0)
    parts = [slice(g * wide, (g + 1) * wide) for g in range(total // wide)]
    at = [slice(h * width, (h + 1) * width) for h in range(heads)]
    every = range(heads)

    @pl.when(pl.program_id(0) == 0)
    def _():
        carry[...] = jnp.zeros_like(carry)
        dvals[...] = jnp.zeros_like(dvals)

    own = pl.multiple_of(c * size, size)
    dp = [mm(grad_ref[:, at[h]], v_ref[:, at[h]], NT) for h in every]
    pf = [prob_ref[0, h].astype(F32) for h in every]
    delta = [jnp.sum(pf[h] * dp[h], axis=-1, keepdims=True) for h in every]
    for h in every:
        ds_ref[h] = (pf[h] * (dp[h] - delta[h])).astype(BF16)
    low = [carry[h].astype(BF16) for h in every]
    dqin = [mm(ds_ref[h], keep_ref[0, h]) for h in every]
    dstep = [mm(low[h], keep_ref[0, h], TN) for h in every]
    for h in every:
        dqin_ref[:, at[h]] = scale * dqin[h]
        dstep_ref[:, at[h]] = dstep[h]
        dintra_ref[:, at[h]] = ds_ref[h, :, pl.ds(own, size)]
        dkout_ref[:, at[h]] = carry[h, pl.ds(own, size), :]
    for g, part in enumerate(parts):

        @pl.when(g * group <= c)
        def _():
            more = [mm(prob_ref[0, h, :, part], grad_ref[:, at[h]], TN) for h in every]
            for h in every:
                dvals[h, part, :] += more[h]

        @pl.when(g * group < c)
        def _():
            fresh = [mm(ds_ref[h, :, part], qin_ref[:, at[h]], TN) for h in every]
            moved = [dot((carry[h, part, :].astype(BF16),), (ptop_ref[:, at[h]], plow_ref[:, at[h]]), NN)
                     for h in every]
            for h in every:
                carry[h, part, :] = scale * fresh[h] + moved[h]

    @pl.when(c == 0)
    def _():
        for h in every:
            dv_ref[:, at[h]] = dvals[h].astype(BF16)


def local_backward(heads, size, scale, q_ref, k_ref, raw_ref, logit_ref, t_ref, e_ref, cm_ref, s_ref,
                   dqin_ref, dintra_ref, dkout_ref, dstep_ref, dq_ref, dk_ref, draw_ref, dlogit_ref):
    width = q_ref.shape[1] // heads
    rows, cols = iotas(size)
    strict, lower, diag = rows > cols, rows >= cols, rows == cols
    some = range(q_ref.shape[0] // size)
    units = [(n, h) for n in some for h in range(heads)]
    at = [(slice(n * size, (n + 1) * size), slice(h * width, (h + 1) * width)) for n, h in units]
    wide = [(slice(n * width, (n + 1) * width), slice(h * width, (h + 1) * width)) for n, h in units]
    every = range(len(units))
    q, k = [(q_ref[a],) for a in at], [(k_ref[a],) for a in at]
    both = [unit_dirs(raw_ref[a]) for a in at]
    betas = [2.0 * jax.nn.sigmoid(logit_ref[n, h : h + 1, :]) for n, h in units]
    ws = [halves(w) for w, _ in both]
    ts, es, cms, ss = ([halves(ref[a]) for a in at] for ref in (t_ref, e_ref, cm_ref, s_ref))
    dintra = [(dintra_ref[a],) for a in at]
    dqs, dks = [halves(dqin_ref[a]) for a in at], [halves(dkout_ref[a]) for a in at]
    dps = [halves(dstep_ref[a]) for a in wide]
    b = [halves(jnp.where(lower, dot(q[u], ws[u], NT), 0.0)) for u in every]
    d_s = [halves(-dot(ws[u], dps[u], NN)) for u in every]
    d_e = [halves(-(dot(ws[u], dks[u], NT) + scale * dot(b[u], dintra[u], TN))) for u in every]
    d_cm = [halves(-dot(dqs[u], ws[u], NT)) for u in every]
    y_s = [dot(ts[u], d_s[u], TN) for u in every]
    y_e = [dot(ts[u], d_e[u], TN) for u in every]
    y_c = [dot(d_cm[u], ts[u], NT) for u in every]
    d_x = [-(dot(halves(y_s[u]), ss[u], NT) + dot(halves(y_e[u]), es[u], NT) + dot(cms[u], halves(y_c[u]), TN))
           for u in every]
    d_b = [halves(jnp.where(lower, y_c[u] - scale * dot(dintra[u], es[u], NT), 0.0)) for u in every]
    d_m = [halves(jnp.where(strict, y_e[u], 0.0)) for u in every]
    d_a = [halves(jnp.where(strict, d_x[u], 0.0)) for u in every]
    for u in every:
        a = at[u]
        dq_ref[a] = (dqin_ref[a] + scale * dot(dintra[u], k[u], NN) + dot(d_b[u], ws[u], NN)).astype(BF16)
        dk_ref[a] = (dkout_ref[a] + scale * dot(dintra[u], q[u], TN) + dot(d_m[u], ws[u], TN)).astype(BF16)
    d_w = [y_s[u] - dot(ss[u], dps[u], NT) - dot(es[u], dks[u], NN) - dot(cms[u], dqs[u], TN)
           + dot(d_b[u], q[u], TN) + dot(d_m[u], k[u], NN) + dot(d_a[u], ws[u], NN) + dot(d_a[u], ws[u], TN)
           for u in every]
    for u, (n, h) in enumerate(units):
        raw, inv = raw_ref[at[u]], both[u][1]
        draw = inv * d_w[u] - raw * (inv * inv * inv) * jnp.sum(raw * d_w[u], axis=-1, keepdims=True)
        draw_ref[at[u]] = draw.astype(BF16)
        at_diag = jnp.sum(jnp.where(diag, d_x[u], 0.0), axis=0, keepdims=True)
        dlogit_ref[n, h : h + 1, :] = -at_diag * (1.0 - 0.5 * betas[u]) / betas[u]


def run(body, grid, inputs, in_specs, outputs, out_specs, scratch, flops):
    return pl.pallas_call(
        body, grid=(grid,), in_specs=in_specs, out_specs=out_specs, out_shape=outputs,
        scratch_shapes=scratch,
        compiler_params=pltpu.CompilerParams(
            dimension_semantics=("arbitrary",), vmem_limit_bytes=VMEM_BYTES),
        cost_estimate=pl.CostEstimate(
            flops=flops, transcendentals=0,
            bytes_accessed=sum(x.size * x.dtype.itemsize for x in (*inputs, *outputs))),
    )(*inputs)


def shape(dims, dtype):
    return jax.ShapeDtypeStruct(dims, dtype)


def group_of(blocks):
    return 4 if blocks % 4 == 0 else 1


def attention_local(q, k, raw, logits, size):
    tokens, width = q.shape
    blocks, heads, _ = logits.shape
    head = width // heads
    some = SOME if blocks % SOME == 0 else 1
    block = pl.BlockSpec((some * size, width), lambda c: (c, 0))
    square = pl.BlockSpec((some * head, width), lambda c: (c, 0))
    logit_block = pl.BlockSpec((some, heads, size), lambda c: (c, 0, 0))
    f, b = shape((tokens, width), F32), shape((tokens, width), BF16)
    stepped = shape((blocks * head, width), BF16)
    return run(
        functools.partial(local_forward, heads, size), blocks // some, (q, k, raw, logits),
        [block, block, block, logit_block], (b, b, stepped, stepped, f, f, f, f, f),
        [block, block, square, square, block, block, block, block, block], [],
        blocks * heads * 62 * 2 * size * size * head)


def attention_cross(q, k, v, raw, logits, segments, local, size):
    qin, kout, ptop, plow, intra, t, e, cm, s = local
    tokens, width = q.shape
    blocks, heads, _ = logits.shape
    head = width // heads
    block = pl.BlockSpec((size, width), lambda c: (c, 0))
    square = pl.BlockSpec((head, width), lambda c: (c, 0))
    b = shape((tokens, width), BF16)
    group = group_of(blocks)
    whole = pl.BlockSpec((tokens, width), lambda c: (0, 0))
    wide_prob = pl.BlockSpec((1, heads, size, tokens), lambda c: (c, 0, 0, 0))
    wide_keep = pl.BlockSpec((1, heads, tokens, head), lambda c: (c, 0, 0, 0))
    out, prob, keep = run(
        functools.partial(cross_forward, heads, group, 1.0 / math.sqrt(head)), blocks,
        (qin, kout, ptop, plow, intra, v, segments.reshape(tokens, 1), segments.reshape(1, tokens)),
        [block, block, square, square, block, whole,
         pl.BlockSpec((size, 1), lambda c: (c, 0)), pl.BlockSpec((1, tokens), lambda c: (0, 0))],
        (b, shape((blocks, heads, size, tokens), BF16), shape((blocks, heads, tokens, head), BF16)),
        [block, wide_prob, wide_keep],
        [pltpu.VMEM((heads, tokens, head), BF16), pltpu.VMEM((heads, size, tokens), F32)],
        blocks * heads * 4 * 2 * size * tokens * head)
    return out, (q, k, v, raw, logits, qin, ptop, plow, t, e, cm, s, prob, keep)


def attention_backward_cross(saved, grad, size):
    q, k, v, raw, logits, qin, ptop, plow, t, e, cm, s, prob, keep = saved
    tokens, width = q.shape
    blocks, heads, _ = logits.shape
    head = width // heads
    scale = 1.0 / math.sqrt(head)
    back = lambda c: (blocks - 1 - c, 0)
    block = pl.BlockSpec((size, width), back)
    square = pl.BlockSpec((head, width), back)
    whole = pl.BlockSpec((tokens, width), lambda c: (0, 0))
    wide_prob = pl.BlockSpec((1, heads, size, tokens), lambda c: (blocks - 1 - c, 0, 0, 0))
    wide_keep = pl.BlockSpec((1, heads, tokens, head), lambda c: (blocks - 1 - c, 0, 0, 0))
    f, b = shape((tokens, width), F32), shape((tokens, width), BF16)
    dqin, dintra, dkout, dstep, dv = run(
        functools.partial(cross_backward, heads, group_of(blocks), scale), blocks,
        (grad, v, prob, keep, qin, ptop, plow),
        [block, whole, wide_prob, wide_keep, block, square, square],
        (f, b, f, shape((blocks * head, width), F32), b),
        [block, block, block, square, whole],
        [pltpu.VMEM((heads, tokens, head), F32), pltpu.VMEM((heads, tokens, head), F32),
         pltpu.VMEM((heads, size, tokens), BF16)],
        blocks * heads * 7 * 2 * size * tokens * head)
    return dv, dqin, dintra, dkout, dstep


def attention_backward_local(saved, crossed, size):
    q, k, v, raw, logits, qin, ptop, plow, t, e, cm, s, prob, keep = saved
    tokens, width = q.shape
    blocks, heads, _ = logits.shape
    head = width // heads
    scale = 1.0 / math.sqrt(head)
    some = SOME if blocks % SOME == 0 else 1
    b = shape((tokens, width), BF16)
    block = pl.BlockSpec((some * size, width), lambda c: (c, 0))
    square = pl.BlockSpec((some * head, width), lambda c: (c, 0))
    logit_block = pl.BlockSpec((some, heads, size), lambda c: (c, 0, 0))
    return run(
        functools.partial(local_backward, heads, size, scale), blocks // some,
        (q, k, raw, logits, t, e, cm, s, *crossed),
        [block, block, block, logit_block, block, block, block, block, block, block, block, square],
        (b, b, b, shape((blocks, heads, size), F32)), [block, block, block, logit_block], [],
        blocks * heads * 60 * 2 * size * size * head)


def ff_forward(me_ref, act_ref, grad_ref, own_ref, other_ref, mlp_ref, dact_ref, hid_ref, dgate_ref, dup_ref,
               gate_w, up_w, down_w, mlp, dact):
    tokens = act_ref.shape[0]
    cores, chips, rows = own_ref.shape[1] + other_ref.shape[1], own_ref.shape[2], own_ref.shape[4]
    tile = min(tokens, 256)

    for r in range(chips):
        for n in range(cores):
            held = own_ref.at[0, 0, r] if n == 0 else other_ref.at[0, n - 1, r]
            chip, core = me_ref[0] ^ r, me_ref[1] ^ n
            to = pl.ds(pl.multiple_of((chip * cores + core) * rows, rows), rows)
            gate_w[to, :] = held[0]
            up_w[to, :] = held[1]
            down_w[to, :] = held[2]

    @pl.when(pl.program_id(0) == 0)
    def _():
        mlp[...] = jnp.zeros_like(mlp)
        dact[...] = jnp.zeros_like(dact)

    @pl.loop(0, tokens // tile)
    def _(i):
        at = pl.ds(pl.multiple_of(i * tile, tile), tile)
        act, grad = act_ref[at, :], grad_ref[at, :]
        gate, up = mm(act, gate_w[...]), mm(act, up_w[...])
        sig = jax.nn.sigmoid(gate)
        silu = gate * sig
        hidden = (silu * up).astype(BF16)
        d_hidden = mm(grad, down_w[...])
        d_gate = (d_hidden * up * sig * (1.0 + gate * (1.0 - sig))).astype(BF16)
        d_up = (d_hidden * silu).astype(BF16)
        hid_ref[at, :] = hidden
        dgate_ref[at, :] = d_gate
        dup_ref[at, :] = d_up
        mlp[at, :] += mm(hidden, down_w[...], NT)
        dact[at, :] += mm(d_gate, gate_w[...], NT) + mm(d_up, up_w[...], NT)

    @pl.when(pl.program_id(0) == pl.num_programs(0) - 1)
    def _():
        mlp_ref[...] = mlp[...].astype(BF16)
        dact_ref[...] = dact[...].astype(BF16)


def ff_weights(me_ref, act_ref, grad_ref, hid_ref, dgate_ref, dup_ref, own_ref, other_ref):
    cores, chips, rows = own_ref.shape[1] + other_ref.shape[1], own_ref.shape[2], own_ref.shape[4]
    for d in range(chips):
        at = slice(d * cores * rows, (d + 1) * cores * rows)
        act, grad = act_ref[:, at], grad_ref[:, at]
        r = me_ref[0] ^ d
        for i, part in enumerate((mm(act, dgate_ref[...], TN), mm(act, dup_ref[...], TN),
                                  mm(grad, hid_ref[...], TN))):
            pieces = [part[w * rows : (w + 1) * rows, :].astype(BF16) for w in range(cores)]
            for n in range(cores):
                piece = pieces[0]
                for w in range(1, cores):
                    piece = jnp.where((me_ref[1] ^ n) == w, pieces[w], piece)
                if n == 0:
                    own_ref[0, 0, r, i] = piece
                else:
                    other_ref[0, n - 1, r, i] = piece


def place_self():
    return jnp.stack([lax.axis_index("dp"), lax.axis_index("wid")]).astype(jnp.int32)


SCALARS = pl.BlockSpec(memory_space=pltpu.SMEM)


def feed_forward(act, grad, own, other):
    tokens, width = act.shape
    groups, part = own.shape[0], own.shape[5]
    whole = pl.BlockSpec((tokens, width), lambda h: (0, 0))
    units = pl.BlockSpec((tokens, part), lambda h: (0, h))
    held = [pl.BlockSpec((1,) + x.shape[1:], lambda h: (h, 0, 0, 0, 0, 0)) for x in (own, other)]
    full, some = shape((tokens, width), BF16), shape((tokens, groups * part), BF16)
    flops = 6 * 2 * tokens * width * groups * part
    return run(ff_forward, groups, (place_self(), act, grad, own, other), [SCALARS, whole, whole, *held],
               (full, full, some, some, some), [whole, whole, units, units, units],
               [pltpu.VMEM((width, part), BF16)] * 3 + [pltpu.VMEM((tokens, width), F32)] * 2, flops)


def feed_forward_weights(act, grad, hidden, d_gate, d_up, own, other):
    tokens, width = act.shape
    groups, part = own.shape[0], own.shape[5]
    whole = pl.BlockSpec((tokens, width), lambda h: (0, 0))
    units = pl.BlockSpec((tokens, part), lambda h: (0, h))
    held = [pl.BlockSpec((1,) + x.shape[1:], lambda h: (h, 0, 0, 0, 0, 0)) for x in (own, other)]
    return run(ff_weights, groups, (place_self(), act, grad, hidden, d_gate, d_up),
               [SCALARS, whole, whole, units, units, units],
               (shape(own.shape, BF16), shape(other.shape, BF16)), held, [],
               3 * 2 * tokens * width * groups * part)


def row_grads(me_ref, left_ref, right_ref, side_ref, own_ref, other_ref):
    cores, shards, rows = own_ref.shape[0] + other_ref.shape[0], own_ref.shape[2], own_ref.shape[3]
    columns, side = right_ref.shape[1], side_ref.shape[1]
    for start in range(0, columns, 512):
        stop = min(start + 512, columns)
        part = mm(left_ref[...], right_ref[:, start:stop], TN)
        if stop == columns:
            beside = side_ref[...]
            if side < stop - start:
                beside = jnp.concatenate([jnp.zeros((part.shape[0], stop - start - side), F32), beside], axis=1)
            part = part + beside
        part = part.astype(BF16)
        for h in range(shards):
            pieces = [part[(h * cores + w) * rows : (h * cores + w + 1) * rows, :] for w in range(cores)]
            for n in range(cores):
                piece = pieces[0]
                for w in range(1, cores):
                    piece = jnp.where((me_ref[1] ^ n) == w, pieces[w], piece)
                if n == 0:
                    own_ref[0, 0, h, :, start:stop] = piece
                else:
                    other_ref[n - 1, 0, h, :, start:stop] = piece


def row_gradients(left, right, side, chips, shards, cores):
    tokens, width = left.shape
    columns = right.shape[1]
    rows = width // (chips * shards * cores)
    if rows % 16:
        full = mm(left, right, TN) + jnp.pad(side, ((0, 0), (columns - side.shape[1], 0)))
        full = full.astype(BF16).reshape(chips, shards, cores, rows, columns)
        full = jnp.take(full, lax.axis_index("wid") ^ jnp.arange(cores), axis=2).transpose(2, 0, 1, 3, 4)
        return full[:1], full[1:]
    outs = [shape((n, chips, shards, rows, columns), BF16) for n in (1, cores - 1)]
    specs = [pl.BlockSpec((x.shape[0], 1, shards, rows, columns), lambda d: (0, d, 0, 0, 0)) for x in outs]
    return run(row_grads, chips, (place_self(), left, right, side),
               [SCALARS, pl.BlockSpec((tokens, width // chips), lambda d: (0, d)),
                pl.BlockSpec((tokens, columns), lambda d: (0, 0)),
                pl.BlockSpec((width // chips, side.shape[1]), lambda d: (d, 0))],
               tuple(outs), specs, [], 2 * tokens * width * columns)


def lay_rows(turned, me_ref, own_ref, other_ref, out_ref):
    cores, shards, rows = own_ref.shape[0] + other_ref.shape[0], own_ref.shape[2], own_ref.shape[3]
    for k in range(shards):
        h = lax.rem(me_ref[2] - k + shards, shards) if turned else k
        for n in range(cores):
            to = pl.ds(pl.multiple_of((h * cores + (me_ref[1] ^ n)) * rows, rows), rows)
            out_ref[to, :] = own_ref[0, 0, k] if n == 0 else other_ref[n - 1, 0, k]


def gathered_rows(own, other, turned=True):
    _, chips, shards, rows, columns = own.shape
    cores = 1 + other.shape[0]
    if rows % 16:
        full = jnp.concatenate([own, other], axis=0)
        full = jnp.take(full, lax.axis_index("wid") ^ jnp.arange(cores), axis=0)
        if turned:
            full = jnp.take(full, (lax.axis_index("hid") - jnp.arange(shards)) % shards, axis=2)
        return full.transpose(1, 2, 0, 3, 4).reshape(-1, columns)
    me = jnp.concatenate([place_self(), lax.axis_index("hid")[None].astype(jnp.int32)])
    specs = [pl.BlockSpec((x.shape[0], 1, shards, rows, columns), lambda d: (0, d, 0, 0, 0)) for x in (own, other)]
    size = cores * shards * rows
    return run(functools.partial(lay_rows, turned), chips, (me, own, other), [SCALARS, *specs],
               (shape((chips * size, columns), BF16),), [pl.BlockSpec((size, columns), lambda d: (d, 0))], [], 0)[0]


def norm_in(tensor, gain_vec):
    return tensor * lax.rsqrt(jnp.mean(tensor * tensor, axis=-1, keepdims=True) + EPS) * gain_vec


def pick(x, index, axis=0):
    return lax.dynamic_index_in_dim(x, index, axis, keepdims=False)


def place(buffer, piece, index, axis=0):
    return lax.dynamic_update_index_in_dim(buffer, piece, index, axis)


def add(left, *others):
    total = left.astype(F32)
    for other in others:
        total = total + other.astype(F32)
    return total.astype(left.dtype)


def to_row(x):
    cores, rows = lax.axis_size("wid"), x.shape[0]
    me = lax.axis_index("wid")
    if cores == rows == 2:
        got = lax.ppermute(pick(x, 1 - me), "wid", [(0, 1), (1, 0)])
        mine = pick(x, me)
        return jnp.concatenate([jnp.where(me == 0, mine, got), jnp.where(me == 0, got, mine)], axis=0)
    every = pick(lax.all_gather(x, "wid", axis=0, tiled=False), me // (cores // rows), 1)
    return every.reshape((-1,) + x.shape[2:])


def from_row(x, rows):
    cores = lax.axis_size("wid")
    me = lax.axis_index("wid")
    parts = x.reshape((cores, x.shape[0] // cores) + x.shape[1:])
    if cores == rows == 2:
        got = lax.ppermute(pick(parts, 1 - me), "wid", [(0, 1), (1, 0)])
        mine = pick(parts, me)
        return jnp.stack([jnp.where(me == 0, mine, got), jnp.where(me == 0, got, mine)], axis=0)
    return lax.all_to_all(parts, "wid", 0, 0, tiled=True)[:: cores // rows]


def line_step(right, left, axis):
    count = lax.axis_size(axis)
    return (lax.ppermute(right, axis, [(i, i + 1) for i in range(count - 1)]),
            lax.ppermute(left, axis, [(i + 1, i) for i in range(count - 1)]))


def line_pieces(steps, axis):
    count, me = lax.axis_size(axis), lax.axis_index(axis)
    pieces = [(me, steps[0][0])]
    for k in range(1, count):
        pieces.append((lax.rem(me - k + count, count), jnp.where(me >= k, steps[k][0], steps[count - k][1])))
    return pieces


def sum_send(pieces, received, t, axis):
    count, me = lax.axis_size(axis), lax.axis_index(axis)
    mine, yours = (pick(pieces, jnp.minimum(me + count - t, count - 1)), pick(pieces, jnp.maximum(me - count + t, 0)))
    if received:
        mine, yours = add(mine, received[0]), add(yours, received[1])
    mine, yours = together(mine, yours)
    return (lax.ppermute(mine, axis, [(i, i + 1) for i in range(t)]),
            lax.ppermute(yours, axis, [(count - 1 - i, count - 2 - i) for i in range(t)]))


def choose(parts, index):
    return lax.select_n(index.astype(jnp.int32), *parts)


def exchange(blocks, axis):
    count, me = lax.axis_size(axis), lax.axis_index(axis)
    got = [choose(blocks, me)]
    for k in range(1, count):
        sent = choose(blocks, lax.rem(me + k, count))
        got.append(lax.ppermute(sent, axis, [(i, (i + k) % count) for i in range(count)]))
    return got


def by_source(got, axis):
    count, me = lax.axis_size(axis), lax.axis_index(axis)
    return [choose(got, lax.rem(me - j + count, count)) for j in range(count)]


def pairs(count, flip):
    return [(i, i ^ flip) for i in range(count)]


def gather_near(x, axis):
    if lax.axis_size(axis) != 4:
        return (x,)
    return x, lax.ppermute(x, axis, pairs(4, 1)), lax.ppermute(x, axis, pairs(4, 2))


def gather_far(near, axis):
    if len(near) == 1:
        return near
    x, one, two = near
    half = x.shape[0] // 2
    return x, one, two, lax.ppermute(one[:half], axis, pairs(4, 2)), lax.ppermute(two[half:], axis, pairs(4, 1))


def gather_end(far, axis):
    if len(far) == 1:
        return lax.all_gather(far[0], axis, axis=0, tiled=False)
    x, one, two, top, low = far
    me = lax.axis_index(axis)
    out = jnp.zeros((4,) + x.shape, x.dtype)
    out = place(place(place(out, x, me), one, me ^ 1), two, me ^ 2)
    return place(out, jnp.concatenate([top, low], axis=0), me ^ 3)


def square_gather(x, axis):
    return gather_end(gather_far(gather_near(x, axis), axis), axis)


def sum_far(x, axis):
    if lax.axis_size(axis) != 4:
        return (x,)
    half = x.shape[1] // 2
    far = pick(x, lax.axis_index(axis) ^ 3)
    return x, lax.ppermute(far[:half], axis, pairs(4, 2)), lax.ppermute(far[half:], axis, pairs(4, 1))


def sum_near(far, axis):
    if len(far) == 1:
        return (lax.psum_scatter(far[0], axis, scatter_dimension=0, tiled=False),)
    x, top, low = far
    me = lax.axis_index(axis)
    half = x.shape[1] // 2
    one, two = pick(x, me ^ 1), pick(x, me ^ 2)
    one = jnp.concatenate([add(one[:half], top), one[half:]], axis=0)
    two = jnp.concatenate([two[:half], add(two[half:], low)], axis=0)
    one, two = together(one, two)
    return pick(x, me), lax.ppermute(one, axis, pairs(4, 1)), lax.ppermute(two, axis, pairs(4, 2))


def from_cores(x):
    cores = lax.axis_size("wid")
    return jnp.stack([lax.ppermute(x, "wid", pairs(cores, n)) for n in range(1, cores)], axis=0)


def core_sum(own, other):
    cores = lax.axis_size("wid")
    return add(own, *[lax.ppermute(other[n - 1 : n], "wid", pairs(cores, n)) for n in range(1, cores)])


def together(*values):
    return lax.optimization_barrier(values)


def per_device(layer_in, segment_ids, out_grad, gain_attn, w_query, w_key, w_value, w_dir, w_beta,
               b_beta, w_out, gain_mlp, w_gate, w_up, w_down):
    n_dp, n_hid, n_wid = (lax.axis_size(axis) for axis in ("dp", "hid", "wid"))
    row_count, tok, width = layer_in.shape
    heads = b_beta.shape[0]
    own_heads = heads // n_hid
    span = width // n_hid
    shard = w_query.shape[0]
    held = n_wid * tok
    copies = n_wid // row_count
    my_hid, my_dp = lax.axis_index("hid"), lax.axis_index("dp")
    side = 128
    columns = 4 * span + side

    row_own = to_row(layer_in)
    row_own, w_query, w_key, w_value, w_dir, w_beta = together(row_own, w_query, w_key, w_value, w_dir, w_beta)
    line = [(row_own, row_own)]
    line.append(line_step(*line[-1], "hid"))

    down_t = w_down.T
    ff_rows, ff_cols = down_t.shape
    part = ff_cols // n_dp

    blank = jnp.zeros((shard, side - own_heads - 2), BF16)
    blocks = []
    for j in range(n_hid):
        at = slice(j * span, (j + 1) * span)
        blocks.append(jnp.concatenate(
            [w_query[:, at], w_key[:, at], w_value[:, at], w_dir[:, at],
             w_beta[:, j * own_heads : (j + 1) * own_heads], gain_attn[:, None], gain_mlp[:, None], blank], axis=1))
    cat = exchange(blocks, "hid")
    cut = [jnp.stack([x[:, j * part : (j + 1) * part] for x in (w_gate, w_up, down_t)]) for j in range(n_dp)]
    cat, line[1], cut, w_out = together(cat, line[1], cut, w_out)
    line.append(line_step(*line[-1], "hid"))
    cat = gather_near(jnp.stack(cat, axis=0), "dp")
    wout = exchange([w_out] * n_hid, "hid")
    ff = [choose(cut, my_dp)]
    for r in range(1, n_dp):
        ff.append(lax.ppermute(choose(cut, my_dp ^ r), "dp", pairs(n_dp, r)))
    cat, line[2] = together(cat, line[2])
    line.append(line_step(*line[-1], "hid"))
    cat = gather_end(gather_far(cat, "dp"), "dp")
    cat = gathered_rows(cat[None], from_cores(cat))
    gain_one = cat[:, 4 * span + own_heads].astype(F32)
    gain_two = cat[:, 4 * span + own_heads + 1].astype(F32)
    beta_own = cat[:, 4 * span : 4 * span + own_heads]
    bias_own = lax.dynamic_slice_in_dim(b_beta, my_hid * own_heads, own_heads, 0).astype(F32)

    pieces = line_pieces(line, "hid")
    pieces, ff, wout, out_grad = together(pieces, ff, wout, out_grad)
    ff = lax.all_gather(jnp.stack(ff, axis=0), "hid", axis=0, tiled=False)
    wout = gather_near(jnp.stack(wout, axis=0), "dp")
    grad_b = out_grad.reshape(row_count * tok, width)
    grad_near = gather_near(grad_b, "dp")

    scaled = jnp.zeros((n_hid, held, width), BF16)
    act_one = jnp.zeros((n_hid, held, width), BF16)
    for index, piece in pieces:
        unit = norm_in(piece.astype(F32), 1.0)
        scaled = place(scaled, unit.astype(BF16), index)
        act_one = place(act_one, (unit * gain_one).astype(BF16), index)
    act_one = act_one.reshape(n_hid * held, width)
    scaled = scaled.reshape(n_hid * held, width)
    if n_wid == 2:
        segs = jnp.concatenate(by_source(exchange([to_row(segment_ids)] * n_hid, "hid"), "hid"), axis=0)
    else:
        segs = lax.all_gather(segment_ids, ("hid", "wid"), axis=0, tiled=False)
        segs = pick(segs, lax.axis_index("wid") // copies, 1).reshape(-1)

    query = mm(act_one, cat[:, :span]).astype(BF16)
    key = mm(act_one, cat[:, span : 2 * span]).astype(BF16)
    value = mm(act_one, cat[:, 2 * span : 3 * span]).astype(BF16)
    raw = mm(act_one, cat[:, 3 * span : 4 * span])
    logits = mm(act_one, beta_own) + bias_own
    logits = logits.reshape(-1, tok, own_heads).transpose(0, 2, 1)
    local = attention_local(query, key, raw, logits, tok)
    local, wout, grad_near = together(local, wout, grad_near)
    wout = gather_far(wout, "dp")
    grad_far = gather_far(grad_near, "dp")
    att, saved = attention_cross(query, key, value, raw, logits, segs, local, tok)
    att, wout, grad_far = together(att, wout, grad_far)

    att = exchange([att[j * held : (j + 1) * held] for j in range(n_hid)], "hid")
    ff_own, ff_other = ff[:, None], jnp.moveaxis(from_cores(ff), 0, 1)
    wout = gather_end(wout, "dp")
    wout_full = gathered_rows(wout[None], from_cores(wout))
    grad_all = gather_end(grad_far, "dp").reshape(-1, width)
    att = from_row(jnp.concatenate(by_source(att, "hid"), axis=1), row_count)
    att = att.reshape(row_count * tok, width)

    layer_f = layer_in.astype(F32).reshape(row_count * tok, width)
    middle = layer_f + mm(att, wout_full)
    act_two = norm_in(middle, gain_two).astype(BF16)
    act_all = square_gather(act_two, "dp").reshape(-1, width)
    mlp, d_act, hidden, d_gate, d_up = feed_forward(act_all, grad_all, ff_own, ff_other)
    d_act = sum_near(sum_far(d_act.reshape(n_dp, -1, width), "dp"), "dp")
    hidden, d_gate, d_up, mine = together(hidden, d_gate, d_up, d_act[0])
    g_own, g_other = feed_forward_weights(act_all, grad_all, hidden, d_gate, d_up, ff_own, ff_other)
    near, g_own, g_other = together(d_act[1:], g_own, g_other)
    d_act = add(mine, *near)

    _, pull_two = jax.vjp(norm_in, middle, gain_two)
    d_mid_norm, _ = pull_two(d_act.astype(F32))
    d_middle = grad_b.astype(F32) + d_mid_norm
    d_branch = d_middle.astype(BF16)
    d_att = mm(d_branch, wout_full, NT).astype(BF16).reshape(row_count, tok, width)
    d_att = to_row(d_att)
    ff_grads = core_sum(jnp.moveaxis(g_own, 1, 0), jnp.moveaxis(g_other, 1, 0))[0]
    d_att, ff_grads, att, mlp = together(d_att, ff_grads, att, mlp)
    d_att = exchange([d_att[:, j * span : (j + 1) * span] for j in range(n_hid)], "hid")
    ff_grads = lax.psum_scatter(ff_grads, "hid", scatter_dimension=0, tiled=False)
    mlp = sum_far(mlp.reshape(n_dp, -1, width), "dp")
    no_side = jnp.zeros((width, side), F32)
    wout_rows = row_gradients(att, d_branch, no_side, n_dp, n_hid, n_wid)
    d_att, wout_rows = together(d_att, wout_rows)
    d_att = jnp.concatenate(by_source(d_att, "hid"), axis=0)
    wout_grad = sum_far(core_sum(*wout_rows)[0], "dp")

    crossed = attention_backward_cross(saved, d_att, tok)
    crossed, wout_grad, mlp = together(crossed, wout_grad, mlp)
    wout_grad = sum_near(wout_grad, "dp")
    mlp = sum_near(mlp, "dp")
    dv, *crossed = crossed
    dq, dk, draw, dlogit = attention_backward_local(saved, crossed, tok)
    dq, dk, draw, dlogit, mlp, wout_grad = together(dq, dk, draw, dlogit, mlp, wout_grad)
    layer_out = (middle + add(*mlp).astype(F32)).astype(BF16)
    d_logit = dlogit.transpose(0, 2, 1).reshape(-1, own_heads).astype(BF16)
    d_cat = jnp.concatenate(
        [dq, dk, dv, draw, jnp.pad(d_logit, ((0, 0), (0, side - own_heads)))], axis=1)
    lanes = lax.broadcasted_iota(jnp.int32, (1, side), 1)
    d_act_one = mm(d_cat, cat, NT)
    d_act_one, ff_grads = together(d_act_one.astype(BF16), ff_grads)
    wout_grad = add(*wout_grad)
    wout_got = exchange([wout_grad[j] for j in range(n_hid)], "hid")
    ff_got = [ff_grads[0]]
    for r in range(1, n_dp):
        ff_got.append(lax.ppermute(ff_grads[r], "dp", pairs(n_dp, r)))
    d_sum = d_act_one.reshape(n_hid, held, width)
    received = sum_send(d_sum, (), 1, "hid")

    ones = lambda rows, lane: jnp.broadcast_to(jnp.where(lanes == lane, 1.0, 0.0).astype(BF16), (rows, side))
    in_row = (d_act_one.astype(F32) * scaled.astype(F32)).astype(BF16)
    in_own = (d_act.astype(F32) * norm_in(middle, 1.0)).astype(BF16)
    bias_grad = jnp.sum(d_logit.astype(F32), axis=0)
    row_of = lax.broadcasted_iota(jnp.int32, (width, side), 0) % shard
    beside = mm(in_row, ones(in_row.shape[0], own_heads), TN)
    for n in range(own_heads):
        beside = beside + jnp.where((row_of == n) & (lanes == own_heads + 2), bias_grad[n], 0.0)
    if copies > 1:
        first = lax.axis_index("wid") % copies == 0
        d_cat, beside = jnp.where(first, d_cat, 0), jnp.where(first, beside, 0.0)
    beside = beside + mm(in_own, ones(in_own.shape[0], own_heads + 1), TN)
    cat_grad = row_gradients(act_one, d_cat, beside, n_dp, n_hid, n_wid)
    received, cat_grad = together(received, cat_grad)
    for t in range(2, n_hid):
        received = sum_send(d_sum, received, t, "hid")
        if t == 2:
            cat_grad = sum_far(core_sum(*cat_grad)[0], "dp")
            received, cat_grad = together(received, cat_grad)
    cat_grad = sum_near(cat_grad, "dp")
    d_sum = add(pick(d_sum, my_hid), *received)
    d_sum, wout_got, ff_got, cat_grad = together(d_sum, wout_got, ff_got, cat_grad)
    cat_grad = add(*cat_grad)
    cat_grad = by_source(exchange([cat_grad[j] for j in range(n_hid)], "hid"), "hid")
    d_sum = from_row(d_sum, row_count).reshape(row_count * tok, width).astype(F32)
    grad_wout = sum(x.astype(F32) for x in wout_got)
    ff_grads = jnp.concatenate([choose(ff_got, my_dp ^ j) for j in range(n_dp)], axis=2).astype(F32)
    weight_grads = [
        jnp.concatenate([x[:, i * span : (i + 1) * span] for x in cat_grad], axis=1).astype(F32)
        for i in range(4)]
    tails = [x[:, 4 * span :].astype(F32) for x in cat_grad]
    grad_beta = jnp.concatenate([x[:, :own_heads] for x in tails], axis=1)
    gain_grads = sum(x[:, own_heads : own_heads + 2] for x in tails)
    grad_bias = jnp.concatenate([x[:own_heads, own_heads + 2] for x in tails], axis=0)

    _, pull_one = jax.vjp(lambda t: norm_in(t, gain_one), layer_f)
    grad_in = (d_middle + pull_one(d_sum)[0]).astype(BF16)

    return (
        layer_out.reshape(layer_in.shape), grad_in.reshape(layer_in.shape), gain_grads[:, 0],
        *weight_grads, grad_beta, grad_bias,
        grad_wout, gain_grads[:, 1], ff_grads[0], ff_grads[1], ff_grads[2].T,
    )


def solution(mesh):
    in_specs = (
        P("dp", ("hid", "wid"), None),
        P("dp", ("hid", "wid")),
        P("dp", ("hid", "wid"), None),
        P(("dp", "hid", "wid")),
        P(("dp", "hid", "wid"), None),
        P(("dp", "hid", "wid"), None),
        P(("dp", "hid", "wid"), None),
        P(("dp", "hid", "wid"), None),
        P(("dp", "hid", "wid"), None),
        P(),
        P(("dp", "hid", "wid"), None),
        P(("dp", "hid", "wid")),
        P(("dp", "wid"), "hid"),
        P(("dp", "wid"), "hid"),
        P("hid", ("dp", "wid")),
    )
    out_specs = (
        P("dp", ("hid", "wid"), None),
        P("dp", ("hid", "wid"), None),
        P(("dp", "hid", "wid")),
        P(("dp", "hid", "wid"), None),
        P(("dp", "hid", "wid"), None),
        P(("dp", "hid", "wid"), None),
        P(("dp", "hid", "wid"), None),
        P(("dp", "hid", "wid"), None),
        P(),
        P(("dp", "hid", "wid"), None),
        P(("dp", "hid", "wid")),
        P(("dp", "wid"), "hid"),
        P(("dp", "wid"), "hid"),
        P("hid", ("dp", "wid")),
    )
    return jax.shard_map(
        per_device, mesh=mesh, in_specs=in_specs, out_specs=out_specs, check_vma=False
    )
```

time: 1110 us -> 627 us (0.56)
  waiting for transfers between devices: 468 us -> 167 us
  blocking collectives: 207 us -> 0 us
  starting transfers between devices: 10.6 us -> 104 us
  matrix products: 107 us -> 35.1 us
  other arithmetic: 41.7 us -> 75.4 us
  local copies, waits for them, and re-layouts: 95.1 us -> 72.3 us
    reduce_scatter x6 -> x1, waiting for transfers between devices: 253 us -> 0.02 us  [per_device(): lax.psum_scatter(ff_grads, 'hid', scatter_dimension=0, tiled=False)]
    ppermute x4 -> x82, waiting for transfers between devices: 5.02 us -> 167 us  [the longest x21 51.6 us: exchange(): lax.ppermute(sent, axis, [(i, (i + k) % count) for i in range(count)])]
    unnamed x14 -> x2, waiting for transfers between devices: 126 us -> 0.03 us
    all_to_all x4 -> x0, blocking collectives: 117 us -> none  [the longest x1 42.5 us: per_device(): lax.all_to_all(att.reshape(n_hid, held, span), 'hid', 0, 0, tiled=True)]
    ppermute x4 -> x82, starting transfers between devices: 0.33 us -> 104 us  [the longest x21 26 us: exchange(): lax.ppermute(sent, axis, [(i, (i + k) % count) for i in range(count)])]
    dot_general x21 -> x10, matrix products: 107 us -> 35.1 us  [mm(): lax.dot_general(left, right, (dims, ((), ())), preferred_element_type=F32)]
    all_gather x6 -> x1, waiting for transfers between devices: 68.9 us -> 0.01 us  [per_device(): ff = lax.all_gather(jnp.stack(ff, axis=0), 'hid', axis=0, tiled=False)]
    unnamed x1 -> x0, blocking collectives: 41 us -> none
  transfers between devices with their start and end apart: 19 -> 84, of which waited for: 13 -> 32; matrix products, arithmetic and copies ran while one was open for 18% -> 24% of each run, Pallas kernels for 8% -> 19%
where the time goes in v2:
time: 627 us; the launch traced here: 619 us
  waiting for transfers between devices  167 us (27%)
  Pallas kernels  149 us (24%)
  starting transfers between devices  104 us (17%)
  other arithmetic  75.4 us (12%)
  local copies, waits for them, and re-layouts  72.3 us (12%)
  matrix products  35.1 us (6%)
  between operations  16.1 us (3%)
    pallas_call x10, Pallas kernels, run(): pl.pallas_call(body, grid=(grid,), in_specs=in_specs, out_specs=out_specs...  149 us
    ppermute x21, waiting for transfers between devices, exchange(): lax.ppermute(sent, axis, [(i, (i + k) % count) for i in range(count)])  51.6 us
    dot_general x10, matrix products, mm(): lax.dot_general(left, right, (dims, ((), ())), preferred_element_type=F32)  35.1 us
    ppermute x21, starting transfers between devices, exchange(): lax.ppermute(sent, axis, [(i, (i + k) % count) for i in range(count)])  26 us
    ppermute x3, waiting for transfers between devices, sum_send(): lax.ppermute(yours, axis, [(count - 1 - i, count - 2 - i) for i in range(...  22.6 us
    unnamed x172, local copies, waits for them, and re-layouts  17.4 us
    ppermute x4, waiting for transfers between devices, gather_near(): lax.ppermute(x, axis, pairs(4, 2))  15.5 us
    select_n x18, other arithmetic, choose(): return lax.select_n(index.astype(jnp.int32), *parts)  13.5 us
  transfers between devices with their start and end apart: 84, of which 32 were waited for; matrix products, arithmetic and copies ran while one was open for 24% of the time, Pallas kernels for 19%

profile of v2, /device:TPU:8, one launch (start us, length us, event | category | flops | bytes accessed | tf_op | source)
XLA Modules:
  0.0 618.9 jit_solution(2796649320618711385)
XLA Ops:
  16.7 3.5 collective-permute-start.4
  37.0 11.4 %collective-permute-done.1 = bf16[48,1664]{1,0:T(8,128)(2,1)S(1)} collective-permute-done((bf16[48,1664]{1,0:T(8,128)(2,1)S(1)}, bf16[48,1664]{1,0:T(8,128)(2,1)S(1)}, u32[]{:S(2)}, u32[]{:S(2)}) %collective-permute-start.1) | collective-permute-done | bytes 159776 | tf_op jit(solution)/shard_map/ppermute | solution.py:583
  50.8 3.4 collective-permute-start.28
  61.3 4.8 collective-permute-start.9
  72.6 8.2 %collective-permute-done.8 = bf16[256,1536]{1,0:T(8,128)(2,1)} collective-permute-done((bf16[256,1536]{1,0:T(8,128)(2,1)}, bf16[256,1536]{1,0:T(8,128)(2,1)}, u32[]{:S(2)}, u32[]{:S(2)}) %collective-permute-start.8) | collective-permute-done | bytes 786464 | tf_op jit(solution)/shard_map/ppermute | solution.py:552
  80.8 3.3 collective-permute-done.9
  84.1 3.1 collective-permute-start.10
  87.2 2.7 collective-permute-start.11
  94.7 4.5 collective-permute-done.19
  102.5 6.6 %collective-permute-done.10 = bf16[256,1536]{1,0:T(8,128)(2,1)S(1)} collective-permute-done((bf16[256,1536]{1,0:T(8,128)(2,1)}, bf16[256,1536]{1,0:T(8,128)(2,1)S(1)}, u32[]{:S(2)}, u32[]{:S(2)}) %collective-permute-start.10) | collective-permute-done | bytes 786464 | tf_op jit(solution)/shard_map/ppermute | solution.py:553
  115.9 4.7 collective-permute-done.13
  133.8 5.4 shard_map.254
  143.9 3.2 copy-done.5
  152.4 2.9 fusion.45.raw_ref
  156.9 17.7 %shard_map.255 = (bf16[1024,384]{1,0:T(8,128)(2,1)}, bf16[1024,384]{1,0:T(8,128)(2,1)}, bf16[1024,384]{1,0:T(8,128)(2,1)}, bf16[1024,384]{1,0:T(8,128)(2,1)}, f3...) custom-call(bf16[1024,384]{1,0:T(8,128)(2,1)} %convolution_convert_f, ...), custom_call_target="tpu_custom_call" | custom-call | flops 6241124352 | bytes 14168064 | tf_op jit(solution)/shard_map/pallas_call | solution.py:244
  180.2 2.7 convolution_convert_fusion.2.v_ref
  187.1 17.3 %shard_map.256 = (bf16[1024,384]{1,0:T(8,128)(2,1)}, bf16[8,3,128,1024]{3,2,1,0:T(8,128)(2,1)}, bf16[8,3,1024,128]{3,2,1,0:T(8,128)(2,1)}) custom-call(bf16[1024,384]{1,0:T(8,128)(2,1)} %get-tuple-element.231.qin_ref, bf16[1024,384]{1,0:T(8,128)(2,1)} %get-tuple-element.232.kout_ref, bf16[1024,384]{1,0:T(8,128)(2,1)} %get-tuple-element.233.ptop_ref, ...), custom_call_target="tpu_custom_call" | custom-call | flops 3221225472 | bytes 18882560 | tf_op jit(solution)/shard_map/pallas_call | solution.py:244
  217.3 9.5 %collective-permute-done.34 = bf16[256,384]{1,0:T(8,128)(2,1)S(1)} collective-permute-done((bf16[256,384]{1,0:T(8,128)(2,1)}, bf16[256,384]{1,0:T(8,128)(2,1)S(1)}, u32[]{:S(2)}, u32[]{:S(2)}) %collective-permute-start.34) | collective-permute-done | bytes 196640 | tf_op jit(solution)/shard_map/ppermute | solution.py:583
  226.8 6.5 %collective-permute-done.35 = bf16[256,384]{1,0:T(8,128)(2,1)S(1)} collective-permute-done((bf16[256,384]{1,0:T(8,128)(2,1)}, bf16[256,384]{1,0:T(8,128)(2,1)S(1)}, u32[]{:S(2)}, u32[]{:S(2)}) %collective-permute-start.35) | collective-permute-done | bytes 196640 | tf_op jit(solution)/shard_map/ppermute | solution.py:583
  239.7 5.4 shard_map.257
  245.1 3.8 multiply_reduce_fusion.2
  256.0 14.2 %collective-permute-done.39 = bf16[256,1536]{1,0:T(8,128)(2,1)S(1)} collective-permute-done((bf16[256,1536]{1,0:T(8,128)(2,1)S(1)}, bf16[256,1536]{1,0:T(8,128)(2,1)S(1)}, u32[]{:S(2)}, u32[]{:S(2)}) %collective-permute-start.39) | collective-permute-done | bytes 786464 | tf_op jit(solution)/shard_map/ppermute | solution.py:599
  272.6 7.7 %collective-permute-done.41 = bf16[128,1536]{1,0:T(8,128)(2,1)S(1)} collective-permute-done((bf16[128,1536]{1,0:T(8,128)(2,1)S(1)}, bf16[128,1536]{1,0:T(8,128)(2,1)S(1)}, u32[]{:S(2)}, u32[]{:S(2)}) %collective-permute-start.41) | collective-permute-done | bytes 393248 | tf_op jit(solution)/shard_map/ppermute | solution.py:607
  282.6 32.7 %shard_map.258 = (bf16[1024,1536]{1,0:T(8,128)(2,1)}, bf16[1024,1536]{1,0:T(8,128)(2,1)}, bf16[1024,1024]{1,0:T(8,128)(2,1)}, bf16[1024,1024]{1,0:T(8,128)(2,1)}, bf16[1024,1024]{1,0:T(8,128)(2,1)}) custom-call(s32[2]{0:T(128)} %pad_add_fusion.3.me_ref, bf16[1024,1536]{1,0:T(8,128)(2,1)} %bitcast.417, bf16[1024,1536]{1,0:T(8,128)(2,1)} %bitcast.420, ...), custom_call_target="tpu_custom_call" | custom-call | flops 19327352832 | bytes 28311560 | tf_op jit(solution)/shard_map/pallas_call | solution.py:244
  320.0 5.8 collective-permute-done.44
  329.4 15.9 %shard_map.259 = (bf16[4,1,4,3,192,256]{5,4,3,2,1,0:T(8,128)(2,1)}, bf16[4,1,4,3,192,256]{5,4,3,2,1,0:T(8,128)(2,1)}) custom-call(s32[2]{0:T(128)} %pad_add_fusion.3.me_ref, bf16[1024,1536]{1,0:T(8,128)(2,1)} %bitcast.418, bf16[1024,1536]{1,0:T(8,128)(2,1)} %bitcast.421, bf16[1024,1024]{1,0:T(8,128)(2,1)} %get-tuple-element.269.hid_ref, ...), custom_call_target="tpu_custom_call" | custom-call | flops 9663676416 | bytes 22020104 | tf_op jit(solution)/shard_map/pallas_call | solution.py:244
  350.6 4.1 collective-permute-done.47
  355.7 4.1 fusion.2
  365.4 5.6 shard_map.260
  371.0 8.9 %collective-permute-done.50 = bf16[256,384]{1,0:T(8,128)(2,1)} collective-permute-done((bf16[256,384]{1,0:T(8,128)(2,1)S(1)}, bf16[256,384]{1,0:T(8,128)(2,1)}, u32[]{:S(2)}, u32[]{:S(2)}) %collective-permute-start.50) | collective-permute-done | bytes 196640 | tf_op jit(solution)/shard_map/ppermute | solution.py:583
  394.1 20.6 %shard_map.261 = (f32[1024,384]{1,0:T(8,128)}, bf16[1024,384]{1,0:T(8,128)(2,1)}, f32[1024,384]{1,0:T(8,128)}, f32[1024,384]{1,0:T(8,128)}, bf16[1024,384]{1,0:T(8,128)(2,1)}) custom-call(bf16[1024,384]{1,0:T(8,128)(2,1)} %pad_maximum_fusion.7.grad_ref, bf16[1024,384]{1,0:T(8,128)(2,1)} %convolution_convert_fusion.2.v_ref, ...), custom_call_target="tpu_custom_call" | custom-call | flops 5637144576 | bytes 22806528 | tf_op jit(solution)/shard_map/pallas_call | solution.py:244
  427.5 18.3 %shard_map.262 = (bf16[1024,384]{1,0:T(8,128)(2,1)}, bf16[1024,384]{1,0:T(8,128)(2,1)}, bf16[1024,384]{1,0:T(8,128)(2,1)}, f32[8,3,128]{2,1,0:T(4,128)}) custom-call(bf16[1024,384]{1,0:T(8,128)(2,1)} %convolution_convert_fusion.4.q_ref, bf16[1024,384]{1,0:T(8,128)(2,1)} %convolution_convert_fusion.3.k_ref, f32[1024,384]{1,0:T(8,128)} %fusion.45.raw_ref, ...), custom_call_target="tpu_custom_call" | custom-call | flops 6039797760 | bytes 17326080 | tf_op jit(solution)/shard_map/pallas_call | solution.py:244
  445.9 5.2 collective-permute-done.59
  457.9 10.0 %convolution_convert_fusion = bf16[1024,1536]{1,0:T(8,128)(2,1)} fusion(bf16[1024,1664]{1,0:T(8,128)(2,1)S(1)} %pad_dynamic-update-slice_fusion.right_ref, bf16[1536,1664]{1,0:T(8,128)(2,1)} %shard_map.254), kind=kOutput, calls=%fused_computation.7 | convolution fusion | flops 5236064256 | bytes 11665408 | tf_op jit(solution)/shard_map/dot_general | solution.py:23
  472.5 6.0 fusion.11
  479.9 10.0 %shard_map.263 = (bf16[1,4,4,48,1664]{4,3,2,1,0:T(8,128)(2,1)}, bf16[1,4,4,48,1664]{4,3,2,1,0:T(8,128)(2,1)}) custom-call(s32[2]{0:T(128)} %pad_add_fusion.3.me_ref, bf16[1024,1536]{1,0:T(8,128)(2,1)} %bitcast.392, bf16[1024,1664]{1,0:T(8,128)(2,1)} %copy-done.56, f32[1536,128]{1,0:T(8,128)} %convolution_add_fusion.1.side_ref), custom_call_target="tpu_custom_call" | custom-call | flops 5234491392 | bytes 12451848 | tf_op jit(solution)/shard_map/pallas_call | solution.py:244
  494.3 5.1 collective-permute-start.63
  506.3 2.7 collective-permute-start.70
  509.0 8.5 %collective-permute-done.63 = bf16[256,1536]{1,0:T(8,128)(2,1)S(1)} collective-permute-done((bf16[256,1536]{1,0:T(8,128)(2,1)S(1)}, bf16[256,1536]{1,0:T(8,128)(2,1)S(1)}, u32[]{:S(2)}, u32[]{:S(2)}) %collective-permute-start.63) | collective-permute-done | bytes 786464 | tf_op jit(solution)/shard_map/ppermute | solution.py:570
  517.6 10.5 %collective-permute-done.64 = bf16[256,1536]{1,0:T(8,128)(2,1)S(1)} collective-permute-done((bf16[256,1536]{1,0:T(8,128)(2,1)S(1)}, bf16[256,1536]{1,0:T(8,128)(2,1)S(1)}, u32[]{:S(2)}, u32[]{:S(2)}) %collective-permute-start.64) | collective-permute-done | bytes 786464 | tf_op jit(solution)/shard_map/ppermute | solution.py:571
  530.4 3.9 collective-permute-start.68
  538.4 12.1 %collective-permute-done.69 = bf16[256,1536]{1,0:T(8,128)(2,1)S(1)} collective-permute-done((bf16[256,1536]{1,0:T(8,128)(2,1)S(1)}, bf16[256,1536]{1,0:T(8,128)(2,1)S(1)}, u32[]{:S(2)}, u32[]{:S(2)}) %collective-permute-start.69) | collective-permute-done | bytes 786464 | tf_op jit(solution)/shard_map/ppermute | solution.py:571
  553.8 3.5 collective-permute-done.73
  557.3 7.5 %collective-permute-done.74 = bf16[3,192,256]{2,1,0:T(8,128)(2,1)S(1)} collective-permute-done((bf16[3,192,256]{2,1,0:T(8,128)(2,1)S(1)}, bf16[3,192,256]{2,1,0:T(8,128)(2,1)S(1)}, u32[]{:S(2)}, u32[]{:S(2)}) %collective-permute-start.74) | collective-permute-done | bytes 294944 | tf_op jit(solution)/shard_map/ppermute | solution.py:795
  565.9 4.6 collective-permute-start.80
  573.5 7.7 %collective-permute-done.80 = bf16[48,1664]{1,0:T(8,128)(2,1)S(1)} collective-permute-done((bf16[48,1664]{1,0:T(8,128)(2,1)S(1)}, bf16[48,1664]{1,0:T(8,128)(2,1)S(1)}, u32[]{:S(2)}, u32[]{:S(2)}) %collective-permute-start.80) | collective-permute-done | bytes 159776 | tf_op jit(solution)/shard_map/ppermute | solution.py:583
  581.1 3.3 collective-permute-done.81
  608.3 3.6 fusion.36
  (502 shorter events, 230.3 us)
Async XLA Ops:
  7.2 229.9 %all-gather.3.cloned.1.call-start = ((), (), s32[]{:S(2)}) async-start(), calls=%async_computation.2 | async-start | bytes 5898240 | tf_op jit(solution)/shard_map/all_gather | solution.py:709
  10.3 24.0 %collective-permute-start.25 = (s32[128]{0:T(128)}, s32[128]{0:T(128)S(1)}, u32[]{:S(2)}, u32[]{:S(2)}) collective-permute-start(s32[128]{0:T(128)} %fusion.103), channel_id=1, source_target_pairs={{0,1},{1,0},{2,3},{3,2},{4,5},{5,4},{6,7},{7,6},{8,9},{9,8},{10,11... | collective-permute-start | bytes 1544 | tf_op jit(solution)/shard_map/ppermute | solution.py:532
  16.7 38.3 %collective-permute-start.4 = (bf16[256,1536]{1,0:T(8,128)(2,1)S(1)}, bf16[256,1536]{1,0:T(8,128)(2,1)S(1)}, u32[]{:S(2)}, u32[]{:S(2)}) collective-permute-start(bf16[256,1536]{1,0:T(8,128)(2,1)S(1)} %pad_maximum_fusion.1), channel_id=1, source_target_pairs={{0,2},{2,4},{4,6},{1,3},{3,5},{5,7},{8,10},{10,12},{12,14},{9,11},... | collective-permute-start | bytes 2359304 | tf_op jit(solution)/shard_map/ppermute | solution.py:552
  20.2 34.8 %collective-permute-start.5 = (bf16[256,1536]{1,0:T(8,128)(2,1)S(1)}, bf16[256,1536]{1,0:T(8,128)(2,1)S(1)}, u32[]{:S(2)}, u32[]{:S(2)}) collective-permute-start(bf16[256,1536]{1,0:T(8,128)(2,1)S(1)} %pad_maximum_fusion.1), channel_id=1, source_target_pairs={{2,0},{4,2},{6,4},{3,1},{5,3},{7,5},{10,8},{12,10},{14,12},{11,9},... | collective-permute-start | bytes 2359304 | tf_op jit(solution)/shard_map/ppermute | solution.py:553
  34.3 20.6 %collective-permute-start.3 = (bf16[48,1664]{1,0:T(8,128)(2,1)S(1)}, bf16[48,1664]{1,0:T(8,128)(2,1)S(1)}, u32[]{:S(2)}, u32[]{:S(2)}) collective-permute-start(bf16[48,1664]{1,0:T(8,128)(2,1)S(1)} %get-tuple-element.481), channel_id=1, source_target_pairs={{0,6},{2,0},{4,2},{6,4},{1,7},{3,1},{5,3},{7,5},{8,14},{10,8},{12,... | collective-permute-start | bytes 479240 | tf_op jit(solution)/shard_map/ppermute | solution.py:583
  59.3 21.5 %collective-permute-start.8 = (bf16[256,1536]{1,0:T(8,128)(2,1)}, bf16[256,1536]{1,0:T(8,128)(2,1)}, u32[]{:S(2)}, u32[]{:S(2)}) collective-permute-start(bf16[256,1536]{1,0:T(8,128)(2,1)} %copy-done.42), channel_id=1, source_target_pairs={{0,2},{2,4},{4,6},{1,3},{3,5},{5,7},{8,10},{10,12},{12,14},{9,11},... | collective-permute-start | bytes 2359304 | tf_op jit(solution)/shard_map/ppermute | solution.py:552
  61.3 22.9 %collective-permute-start.9 = (bf16[256,1536]{1,0:T(8,128)(2,1)}, bf16[256,1536]{1,0:T(8,128)(2,1)}, u32[]{:S(2)}, u32[]{:S(2)}) collective-permute-start(bf16[256,1536]{1,0:T(8,128)(2,1)} %copy-done.40), channel_id=1, source_target_pairs={{2,0},{4,2},{6,4},{3,1},{5,3},{7,5},{10,8},{12,10},{14,12},{11,9},... | collective-permute-start | bytes 2359304 | tf_op jit(solution)/shard_map/ppermute | solution.py:553
  67.1 43.4 %collective-permute-start.15 = (bf16[48,1536]{1,0:T(8,128)(2,1)}, bf16[48,1536]{1,0:T(8,128)(2,1)S(1)}, u32[]{:S(2)}, u32[]{:S(2)}) collective-permute-start(bf16[48,1536]{1,0:T(8,128)(2,1)} %param.25), channel_id=1, source_target_pairs={{0,2},{2,4},{4,6},{6,0},{1,3},{3,5},{5,7},{7,1},{8,10},{10,12},{12... | collective-permute-start | bytes 442376 | tf_op jit(solution)/shard_map/ppermute | solution.py:583
  84.1 25.0 %collective-permute-start.10 = (bf16[256,1536]{1,0:T(8,128)(2,1)}, bf16[256,1536]{1,0:T(8,128)(2,1)S(1)}, u32[]{:S(2)}, u32[]{:S(2)}) collective-permute-start(bf16[256,1536]{1,0:T(8,128)(2,1)} %collective-permute-done.9), channel_id=1, source_target_pairs={{2,0},{4,2},{6,4},{3,1},{5,3},{7,5},{10,8},{12,10},{14,12},{11,9},... | collective-permute-start | bytes 2359304 | tf_op jit(solution)/shard_map/ppermute | solution.py:553
  87.2 26.3 %collective-permute-start.11 = (bf16[256,1536]{1,0:T(8,128)(2,1)}, bf16[256,1536]{1,0:T(8,128)(2,1)S(1)}, u32[]{:S(2)}, u32[]{:S(2)}) collective-permute-start(bf16[256,1536]{1,0:T(8,128)(2,1)} %collective-permute-done.8), channel_id=1, source_target_pairs={{0,2},{2,4},{4,6},{1,3},{3,5},{5,7},{8,10},{10,12},{12,14},{9,11},... | collective-permute-start | bytes 2359304 | tf_op jit(solution)/shard_map/ppermute | solution.py:552
  113.6 18.6 %collective-permute-start.20 = (bf16[4,4,48,1664]{3,2,1,0:T(8,128)(2,1)S(1)}, bf16[4,4,48,1664]{3,2,1,0:T(8,128)(2,1)}, u32[]{:S(2)}, u32[]{:S(2)}) collective-permute-start(bf16[4,4,48,1664]{3,2,1,0:T(8,128)(2,1)S(1)} %fusion.77), channel_id=1, source_target_pairs={{0,1},{1,0},{2,3},{3,2},{4,5},{5,4},{6,7},{7,6},{8,9},{9,8},{10,11... | collective-permute-start | bytes 7667720 | tf_op jit(solution)/shard_map/ppermute | solution.py:647
  122.6 52.1 %collective-permute-start.21 = (bf16[4,48,1536]{2,1,0:T(8,128)(2,1)}, bf16[4,48,1536]{2,1,0:T(8,128)(2,1)}, u32[]{:S(2)}, u32[]{:S(2)}) collective-permute-start(bf16[4,48,1536]{2,1,0:T(8,128)(2,1)} %pad_maximum_fusion.13), channel_id=1, source_target_pairs={{0,8},{8,0},{16,24},{24,16},{1,9},{9,1},{17,25},{25,17},{2,10},{10... | collective-permute-start | bytes 1769480 | tf_op jit(solution)/shard_map/ppermute | solution.py:599
  124.1 50.6 %collective-permute-start.22 = (bf16[4,48,1536]{2,1,0:T(8,128)(2,1)}, bf16[4,48,1536]{2,1,0:T(8,128)(2,1)}, u32[]{:S(2)}, u32[]{:S(2)}) collective-permute-start(bf16[4,48,1536]{2,1,0:T(8,128)(2,1)} %pad_maximum_fusion.13), channel_id=1, source_target_pairs={{0,16},{8,24},{16,0},{24,8},{1,17},{9,25},{17,1},{25,9},{2,18},{10... | collective-permute-start | bytes 1769480 | tf_op jit(solution)/shard_map/ppermute | solution.py:599
  124.6 50.1 %collective-permute-start.23 = (bf16[256,1536]{1,0:T(8,128)(2,1)}, bf16[256,1536]{1,0:T(8,128)(2,1)}, u32[]{:S(2)}, u32[]{:S(2)}) collective-permute-start(bf16[256,1536]{1,0:T(8,128)(2,1)} %bitcast.405), channel_id=1, source_target_pairs={{0,8},{8,0},{16,24},{24,16},{1,9},{9,1},{17,25},{25,17},{2,10},{10... | collective-permute-start | bytes 2359304 | tf_op jit(solution)/shard_map/ppermute | solution.py:599
  125.1 49.6 %collective-permute-start.24 = (bf16[256,1536]{1,0:T(8,128)(2,1)}, bf16[256,1536]{1,0:T(8,128)(2,1)}, u32[]{:S(2)}, u32[]{:S(2)}) collective-permute-start(bf16[256,1536]{1,0:T(8,128)(2,1)} %bitcast.406), channel_id=1, source_target_pairs={{0,16},{8,24},{16,0},{24,8},{1,17},{9,25},{17,1},{25,9},{2,18},{10... | collective-permute-start | bytes 2359304 | tf_op jit(solution)/shard_map/ppermute | solution.py:599
  129.1 338.8 %reduce-scatter.2.cloned.1.call-start = ((), (), s32[]{:S(2)}) async-start(), calls=%async_computation.1 | async-start | bytes 5898240 | tf_op jit(solution)/shard_map/reduce_scatter | solution.py:769
  176.5 27.9 %collective-permute-start.31 = (bf16[128,1536]{1,0:T(8,128)(2,1)}, bf16[128,1536]{1,0:T(8,128)(2,1)}, u32[]{:S(2)}, u32[]{:S(2)}) collective-permute-start(bf16[128,1536]{1,0:T(8,128)(2,1)} %slice.491), channel_id=1, source_target_pairs={{0,16},{8,24},{16,0},{24,8},{1,17},{9,25},{17,1},{25,9},{2,18},{10... | collective-permute-start | bytes 1179656 | tf_op jit(solution)/shard_map/ppermute | solution.py:607
  178.8 25.6 %collective-permute-start.32 = (bf16[128,1536]{1,0:T(8,128)(2,1)}, bf16[128,1536]{1,0:T(8,128)(2,1)}, u32[]{:S(2)}, u32[]{:S(2)}) collective-permute-start(bf16[128,1536]{1,0:T(8,128)(2,1)} %slice.492), channel_id=1, source_target_pairs={{0,8},{8,0},{16,24},{24,16},{1,9},{9,1},{17,25},{25,17},{2,10},{10... | collective-permute-start | bytes 1179656 | tf_op jit(solution)/shard_map/ppermute | solution.py:607
  183.9 20.5 %collective-permute-start.29 = (bf16[2,48,1536]{2,1,0:T(8,128)(2,1)S(1)}, bf16[2,48,1536]{2,1,0:T(8,128)(2,1)S(1)}, u32[]{:S(2)}, u32[]{:S(2)}) collective-permute-start(bf16[2,48,1536]{2,1,0:T(8,128)(2,1)S(1)} %slice.489), channel_id=1, source_target_pairs={{0,16},{8,24},{16,0},{24,8},{1,17},{9,25},{17,1},{25,9},{2,18},{10... | collective-permute-start | bytes 884744 | tf_op jit(solution)/shard_map/ppermute | solution.py:607
  206.4 20.3 %collective-permute-start.34 = (bf16[256,384]{1,0:T(8,128)(2,1)}, bf16[256,384]{1,0:T(8,128)(2,1)S(1)}, u32[]{:S(2)}, u32[]{:S(2)}) collective-permute-start(bf16[256,384]{1,0:T(8,128)(2,1)} %get-tuple-element.475), channel_id=1, source_target_pairs={{0,4},{2,6},{4,0},{6,2},{1,5},{3,7},{5,1},{7,3},{8,12},{10,14},{12... | collective-permute-start | bytes 589832 | tf_op jit(solution)/shard_map/ppermute | solution.py:583
  210.7 22.6 %collective-permute-start.35 = (bf16[256,384]{1,0:T(8,128)(2,1)}, bf16[256,384]{1,0:T(8,128)(2,1)S(1)}, u32[]{:S(2)}, u32[]{:S(2)}) collective-permute-start(bf16[256,384]{1,0:T(8,128)(2,1)} %select_select_fusion.20), channel_id=1, source_target_pairs={{0,6},{2,0},{4,2},{6,4},{1,7},{3,1},{5,3},{7,5},{8,14},{10,8},{12,... | collective-permute-start | bytes 589832 | tf_op jit(solution)/shard_map/ppermute | solution.py:583
  210.7 22.6 %collective-permute-start.33 = (bf16[256,384]{1,0:T(8,128)(2,1)}, bf16[256,384]{1,0:T(8,128)(2,1)}, u32[]{:S(2)}, u32[]{:S(2)}) collective-permute-start(bf16[256,384]{1,0:T(8,128)(2,1)} %get-tuple-element.474), channel_id=1, source_target_pairs={{0,2},{2,4},{4,6},{6,0},{1,3},{3,5},{5,7},{7,1},{8,10},{10,12},{12... | collective-permute-start | bytes 589832 | tf_op jit(solution)/shard_map/ppermute | solution.py:583
  216.5 23.2 %collective-permute-start.37 = (bf16[4,4,48,1536]{3,2,1,0:T(8,128)(2,1)S(1)}, bf16[4,4,48,1536]{3,2,1,0:T(8,128)(2,1)}, u32[]{:S(2)}, u32[]{:S(2)}) collective-permute-start(bf16[4,4,48,1536]{3,2,1,0:T(8,128)(2,1)S(1)} %fusion.80), channel_id=1, source_target_pairs={{0,1},{1,0},{2,3},{3,2},{4,5},{5,4},{6,7},{7,6},{8,9},{9,8},{10,11... | collective-permute-start | bytes 7077896 | tf_op jit(solution)/shard_map/ppermute | solution.py:647
  237.1 43.7 %collective-permute-start.42 = (bf16[4,4,3,192,256]{4,3,2,1,0:T(8,128)(2,1)}, bf16[4,4,3,192,256]{4,3,2,1,0:T(8,128)(2,1)}, u32[]{:S(2)}, u32[]{:S(2)}) collective-permute-start(bf16[4,4,3,192,256]{4,3,2,1,0:T(8,128)(2,1)} %bitcast.455), channel_id=1, source_target_pairs={{0,1},{1,0},{2,3},{3,2},{4,5},{5,4},{6,7},{7,6},{8,9},{9,8},{10,11... | collective-permute-start | bytes 14155784 | tf_op jit(solution)/shard_map/ppermute | solution.py:647
  249.4 21.5 %collective-permute-start.38 = (bf16[256,1536]{1,0:T(8,128)(2,1)S(1)}, bf16[256,1536]{1,0:T(8,128)(2,1)S(1)}, u32[]{:S(2)}, u32[]{:S(2)}) collective-permute-start(bf16[256,1536]{1,0:T(8,128)(2,1)S(1)} %get-tuple-element.399), channel_id=1, source_target_pairs={{0,8},{8,0},{16,24},{24,16},{1,9},{9,1},{17,25},{25,17},{2,10},{10... | collective-permute-start | bytes 2359304 | tf_op jit(solution)/shard_map/ppermute | solution.py:599
  251.0 19.3 %collective-permute-start.39 = (bf16[256,1536]{1,0:T(8,128)(2,1)S(1)}, bf16[256,1536]{1,0:T(8,128)(2,1)S(1)}, u32[]{:S(2)}, u32[]{:S(2)}) collective-permute-start(bf16[256,1536]{1,0:T(8,128)(2,1)S(1)} %get-tuple-element.399), channel_id=1, source_target_pairs={{0,16},{8,24},{16,0},{24,8},{1,17},{9,25},{17,1},{25,9},{2,18},{10... | collective-permute-start | bytes 2359304 | tf_op jit(solution)/shard_map/ppermute | solution.py:599
  385.4 29.3 %collective-permute-start.55 = (bf16[128,1536]{1,0:T(8,128)(2,1)}, bf16[128,1536]{1,0:T(8,128)(2,1)}, u32[]{:S(2)}, u32[]{:S(2)}) collective-permute-start(bf16[128,1536]{1,0:T(8,128)(2,1)} %get-tuple-element.413), channel_id=1, source_target_pairs={{0,16},{8,24},{16,0},{24,8},{1,17},{9,25},{17,1},{25,9},{2,18},{10... | collective-permute-start | bytes 1179656 | tf_op jit(solution)/shard_map/ppermute | solution.py:629
  385.8 28.9 %collective-permute-start.56 = (bf16[128,1536]{1,0:T(8,128)(2,1)}, bf16[128,1536]{1,0:T(8,128)(2,1)}, u32[]{:S(2)}, u32[]{:S(2)}) collective-permute-start(bf16[128,1536]{1,0:T(8,128)(2,1)} %get-tuple-element.412), channel_id=1, source_target_pairs={{0,8},{8,0},{16,24},{24,16},{1,9},{9,1},{17,25},{25,17},{2,10},{10... | collective-permute-start | bytes 1179656 | tf_op jit(solution)/shard_map/ppermute | solution.py:629
  392.1 22.6 %collective-permute-start.53 = (bf16[2,48,1536]{2,1,0:T(8,128)(2,1)S(1)}, bf16[2,48,1536]{2,1,0:T(8,128)(2,1)S(1)}, u32[]{:S(2)}, u32[]{:S(2)}) collective-permute-start(bf16[2,48,1536]{2,1,0:T(8,128)(2,1)S(1)} %get-tuple-element.434), channel_id=1, source_target_pairs={{0,16},{8,24},{16,0},{24,8},{1,17},{9,25},{17,1},{25,9},{2,18},{10... | collective-permute-start | bytes 884744 | tf_op jit(solution)/shard_map/ppermute | solution.py:629
  393.7 21.1 %collective-permute-start.54 = (bf16[2,48,1536]{2,1,0:T(8,128)(2,1)S(1)}, bf16[2,48,1536]{2,1,0:T(8,128)(2,1)S(1)}, u32[]{:S(2)}, u32[]{:S(2)}) collective-permute-start(bf16[2,48,1536]{2,1,0:T(8,128)(2,1)S(1)} %get-tuple-element.433), channel_id=1, source_target_pairs={{0,8},{8,0},{16,24},{24,16},{1,9},{9,1},{17,25},{25,17},{2,10},{10... | collective-permute-start | bytes 884744 | tf_op jit(solution)/shard_map/ppermute | solution.py:629
  419.3 33.1 %collective-permute-start.57 = (bf16[256,1536]{1,0:T(8,128)(2,1)}, bf16[256,1536]{1,0:T(8,128)(2,1)S(1)}, u32[]{:S(2)}, u32[]{:S(2)}) collective-permute-start(bf16[256,1536]{1,0:T(8,128)(2,1)} %pad_maximum_fusion.8), channel_id=1, source_target_pairs={{0,8},{8,0},{16,24},{24,16},{1,9},{9,1},{17,25},{25,17},{2,10},{10... | collective-permute-start | bytes 2359304 | tf_op jit(solution)/shard_map/ppermute | solution.py:642
  420.9 31.5 %collective-permute-start.58 = (bf16[256,1536]{1,0:T(8,128)(2,1)}, bf16[256,1536]{1,0:T(8,128)(2,1)}, u32[]{:S(2)}, u32[]{:S(2)}) collective-permute-start(bf16[256,1536]{1,0:T(8,128)(2,1)} %pad_maximum_fusion.9), channel_id=1, source_target_pairs={{0,16},{8,24},{16,0},{24,8},{1,17},{9,25},{17,1},{25,9},{2,18},{10... | collective-permute-start | bytes 2359304 | tf_op jit(solution)/shard_map/ppermute | solution.py:642
  422.6 28.4 %collective-permute-start.59 = (bf16[4,48,1536]{2,1,0:T(8,128)(2,1)}, bf16[4,48,1536]{2,1,0:T(8,128)(2,1)S(1)}, u32[]{:S(2)}, u32[]{:S(2)}) collective-permute-start(bf16[4,48,1536]{2,1,0:T(8,128)(2,1)} %pad_maximum_fusion.14), channel_id=1, source_target_pairs={{0,8},{8,0},{16,24},{24,16},{1,9},{9,1},{17,25},{25,17},{2,10},{10... | collective-permute-start | bytes 1769480 | tf_op jit(solution)/shard_map/ppermute | solution.py:642
  423.0 29.4 %collective-permute-start.60 = (bf16[4,48,1536]{2,1,0:T(8,128)(2,1)S(1)}, bf16[4,48,1536]{2,1,0:T(8,128)(2,1)}, u32[]{:S(2)}, u32[]{:S(2)}) collective-permute-start(bf16[4,48,1536]{2,1,0:T(8,128)(2,1)S(1)} %pad_maximum_fusion.15), channel_id=1, source_target_pairs={{0,16},{8,24},{16,0},{24,8},{1,17},{9,25},{17,1},{25,9},{2,18},{10... | collective-permute-start | bytes 1769480 | tf_op jit(solution)/shard_map/ppermute | solution.py:642
  469.6 20.3 %collective-permute-start.61 = (bf16[256,1536]{1,0:T(8,128)(2,1)S(1)}, bf16[256,1536]{1,0:T(8,128)(2,1)}, u32[]{:S(2)}, u32[]{:S(2)}) collective-permute-start(bf16[256,1536]{1,0:T(8,128)(2,1)S(1)} %get-tuple-element.325), channel_id=1, source_target_pairs={{0,2},{1,3},{8,10},{9,11},{16,18},{17,19},{24,26},{25,27}} | collective-permute-start | bytes 2359304 | tf_op jit(solution)/shard_map/ppermute | solution.py:570
  470.9 19.0 %collective-permute-start.62 = (bf16[256,1536]{1,0:T(8,128)(2,1)S(1)}, bf16[256,1536]{1,0:T(8,128)(2,1)}, u32[]{:S(2)}, u32[]{:S(2)}) collective-permute-start(bf16[256,1536]{1,0:T(8,128)(2,1)S(1)} %get-tuple-element.326), channel_id=1, source_target_pairs={{6,4},{7,5},{14,12},{15,13},{22,20},{23,21},{30,28},{31,29}} | collective-permute-start | bytes 2359304 | tf_op jit(solution)/shard_map/ppermute | solution.py:571
  494.3 23.2 %collective-permute-start.63 = (bf16[256,1536]{1,0:T(8,128)(2,1)S(1)}, bf16[256,1536]{1,0:T(8,128)(2,1)S(1)}, u32[]{:S(2)}, u32[]{:S(2)}) collective-permute-start(bf16[256,1536]{1,0:T(8,128)(2,1)S(1)} %get-tuple-element.331), channel_id=1, source_target_pairs={{0,2},{2,4},{1,3},{3,5},{8,10},{10,12},{9,11},{11,13},{16,18},{18,... | collective-permute-start | bytes 2359304 | tf_op jit(solution)/shard_map/ppermute | solution.py:570
  499.4 28.6 %collective-permute-start.64 = (bf16[256,1536]{1,0:T(8,128)(2,1)S(1)}, bf16[256,1536]{1,0:T(8,128)(2,1)S(1)}, u32[]{:S(2)}, u32[]{:S(2)}) collective-permute-start(bf16[256,1536]{1,0:T(8,128)(2,1)S(1)} %get-tuple-element.332), channel_id=1, source_target_pairs={{6,4},{4,2},{7,5},{5,3},{14,12},{12,10},{15,13},{13,11},{22,20},{2... | collective-permute-start | bytes 2359304 | tf_op jit(solution)/shard_map/ppermute | solution.py:571
  503.2 24.8 %collective-permute-start.66 = (bf16[2,48,1664]{2,1,0:T(8,128)(2,1)S(1)}, bf16[2,48,1664]{2,1,0:T(8,128)(2,1)S(1)}, u32[]{:S(2)}, u32[]{:S(2)}) collective-permute-start(bf16[2,48,1664]{2,1,0:T(8,128)(2,1)S(1)} %get-tuple-element.425), channel_id=1, source_target_pairs={{0,16},{8,24},{16,0},{24,8},{1,17},{9,25},{17,1},{25,9},{2,18},{10... | collective-permute-start | bytes 958472 | tf_op jit(solution)/shard_map/ppermute | solution.py:629
  504.7 23.3 %collective-permute-start.67 = (bf16[2,48,1664]{2,1,0:T(8,128)(2,1)S(1)}, bf16[2,48,1664]{2,1,0:T(8,128)(2,1)S(1)}, u32[]{:S(2)}, u32[]{:S(2)}) collective-permute-start(bf16[2,48,1664]{2,1,0:T(8,128)(2,1)S(1)} %get-tuple-element.424), channel_id=1, source_target_pairs={{0,8},{8,0},{16,24},{24,16},{1,9},{9,1},{17,25},{25,17},{2,10},{10... | collective-permute-start | bytes 958472 | tf_op jit(solution)/shard_map/ppermute | solution.py:629
  506.3 28.5 %collective-permute-start.70 = (bf16[48,1536]{1,0:T(8,128)(2,1)S(1)}, bf16[48,1536]{1,0:T(8,128)(2,1)S(1)}, u32[]{:S(2)}, u32[]{:S(2)}) collective-permute-start(bf16[48,1536]{1,0:T(8,128)(2,1)S(1)} %get-tuple-element.488), channel_id=1, source_target_pairs={{0,2},{2,4},{4,6},{6,0},{1,3},{3,5},{5,7},{7,1},{8,10},{10,12},{12... | collective-permute-start | bytes 442376 | tf_op jit(solution)/shard_map/ppermute | solution.py:583
  517.5 18.7 %collective-permute-start.71 = (bf16[48,1536]{1,0:T(8,128)(2,1)S(1)}, bf16[48,1536]{1,0:T(8,128)(2,1)S(1)}, u32[]{:S(2)}, u32[]{:S(2)}) collective-permute-start(bf16[48,1536]{1,0:T(8,128)(2,1)S(1)} %get-tuple-element.487), channel_id=1, source_target_pairs={{0,4},{2,6},{4,0},{6,2},{1,5},{3,7},{5,1},{7,3},{8,12},{10,14},{12... | collective-permute-start | bytes 442376 | tf_op jit(solution)/shard_map/ppermute | solution.py:583
  528.4 22.1 %collective-permute-start.69 = (bf16[256,1536]{1,0:T(8,128)(2,1)S(1)}, bf16[256,1536]{1,0:T(8,128)(2,1)S(1)}, u32[]{:S(2)}, u32[]{:S(2)}) collective-permute-start(bf16[256,1536]{1,0:T(8,128)(2,1)S(1)} %get-tuple-element.338), channel_id=1, source_target_pairs={{6,4},{4,2},{2,0},{7,5},{5,3},{3,1},{14,12},{12,10},{10,8},{15,13}... | collective-permute-start | bytes 2359304 | tf_op jit(solution)/shard_map/ppermute | solution.py:571
  530.4 21.6 %collective-permute-start.68 = (bf16[256,1536]{1,0:T(8,128)(2,1)S(1)}, bf16[256,1536]{1,0:T(8,128)(2,1)S(1)}, u32[]{:S(2)}, u32[]{:S(2)}) collective-permute-start(bf16[256,1536]{1,0:T(8,128)(2,1)S(1)} %get-tuple-element.337), channel_id=1, source_target_pairs={{0,2},{2,4},{4,6},{1,3},{3,5},{5,7},{8,10},{10,12},{12,14},{9,11},... | collective-permute-start | bytes 2359304 | tf_op jit(solution)/shard_map/ppermute | solution.py:570
  534.7 30.0 %collective-permute-start.76 = (bf16[4,48,1664]{2,1,0:T(8,128)(2,1)S(1)}, bf16[4,48,1664]{2,1,0:T(8,128)(2,1)S(1)}, u32[]{:S(2)}, u32[]{:S(2)}) collective-permute-start(bf16[4,48,1664]{2,1,0:T(8,128)(2,1)S(1)} %pad_maximum_fusion.11), channel_id=1, source_target_pairs={{0,8},{8,0},{16,24},{24,16},{1,9},{9,1},{17,25},{25,17},{2,10},{10... | collective-permute-start | bytes 1916936 | tf_op jit(solution)/shard_map/ppermute | solution.py:642
  536.3 28.5 %collective-permute-start.77 = (bf16[4,48,1664]{2,1,0:T(8,128)(2,1)S(1)}, bf16[4,48,1664]{2,1,0:T(8,128)(2,1)S(1)}, u32[]{:S(2)}, u32[]{:S(2)}) collective-permute-start(bf16[4,48,1664]{2,1,0:T(8,128)(2,1)S(1)} %pad_maximum_fusion.12), channel_id=1, source_target_pairs={{0,16},{8,24},{16,0},{24,8},{1,17},{9,25},{17,1},{25,9},{2,18},{10... | collective-permute-start | bytes 1916936 | tf_op jit(solution)/shard_map/ppermute | solution.py:642
  537.8 19.4 %collective-permute-start.73 = (bf16[3,192,256]{2,1,0:T(8,128)(2,1)S(1)}, bf16[3,192,256]{2,1,0:T(8,128)(2,1)S(1)}, u32[]{:S(2)}, u32[]{:S(2)}) collective-permute-start(bf16[3,192,256]{2,1,0:T(8,128)(2,1)S(1)} %get-tuple-element.445), channel_id=1, source_target_pairs={{0,8},{8,0},{16,24},{24,16},{1,9},{9,1},{17,25},{25,17},{2,10},{10... | collective-permute-start | bytes 884744 | tf_op jit(solution)/shard_map/ppermute | solution.py:795
  565.9 40.9 %collective-permute-start.78 = (bf16[128,1536]{1,0:T(8,128)(2,1)}, bf16[128,1536]{1,0:T(8,128)(2,1)S(1)}, u32[]{:S(2)}, u32[]{:S(2)}) collective-permute-start(bf16[128,1536]{1,0:T(8,128)(2,1)} %dynamic-slice_bitcast_fusion.18), channel_id=1, source_target_pairs={{0,1},{1,0},{2,3},{3,2},{4,5},{5,4},{6,7},{7,6},{8,9},{9,8},{10,11... | collective-permute-start | bytes 1179656 | tf_op jit(solution)/shard_map/ppermute | solution.py:544
  (120 other events, 1048.3 us)
Sparse Core Ops, SparseCore 0:
  129.3 98.1 all-gather.2
  380.4 86.1 reduce-scatter.1

commit v3 on v2

--- a/solution.py
+++ b/solution.py
@@ -439,71 +439,201 @@
                3 * 2 * tokens * width * groups * part)
 
 
-def row_grads(me_ref, left_ref, right_ref, side_ref, own_ref, other_ref):
+def split_rows(me_ref, part, at, own_ref, other_ref):
     cores, shards, rows = own_ref.shape[0] + other_ref.shape[0], own_ref.shape[2], own_ref.shape[3]
-    columns, side = right_ref.shape[1], side_ref.shape[1]
+    for h in range(shards):
+        pieces = [part[(h * cores + w) * rows : (h * cores + w + 1) * rows, :] for w in range(cores)]
+        for n in range(cores):
+            piece = pieces[0]
+            for w in range(1, cores):
+                piece = jnp.where((me_ref[1] ^ n) == w, pieces[w], piece)
+            if n == 0:
+                own_ref[0, 0, h, :, at] = piece
+            else:
+                other_ref[n - 1, 0, h, :, at] = piece
+
+
+def row_grads(me_ref, left_ref, right_ref, own_ref, other_ref):
+    columns = right_ref.shape[1]
     for start in range(0, columns, 512):
-        stop = min(start + 512, columns)
-        part = mm(left_ref[...], right_ref[:, start:stop], TN)
-        if stop == columns:
-            beside = side_ref[...]
-            if side < stop - start:
-                beside = jnp.concatenate([jnp.zeros((part.shape[0], stop - start - side), F32), beside], axis=1)
-            part = part + beside
-        part = part.astype(BF16)
-        for h in range(shards):
-            pieces = [part[(h * cores + w) * rows : (h * cores + w + 1) * rows, :] for w in range(cores)]
-            for n in range(cores):
-                piece = pieces[0]
-                for w in range(1, cores):
-                    piece = jnp.where((me_ref[1] ^ n) == w, pieces[w], piece)
-                if n == 0:
-                    own_ref[0, 0, h, :, start:stop] = piece
-                else:
-                    other_ref[n - 1, 0, h, :, start:stop] = piece
-
-
-def row_gradients(left, right, side, chips, shards, cores):
+        at = slice(start, min(start + 512, columns))
+        split_rows(me_ref, mm(left_ref[...], right_ref[:, at], TN).astype(BF16), at, own_ref, other_ref)
+
+
+def split_whole(full, chips, shards, cores, rows):
+    full = full.astype(BF16).reshape(chips, shards, cores, rows, full.shape[1])
+    full = jnp.take(full, lax.axis_index("wid") ^ jnp.arange(cores), axis=2).transpose(2, 0, 1, 3, 4)
+    return full[:1], full[1:]
+
+
+def row_gradients(left, right, chips, shards, cores):
     tokens, width = left.shape
     columns = right.shape[1]
     rows = width // (chips * shards * cores)
     if rows % 16:
-        full = mm(left, right, TN) + jnp.pad(side, ((0, 0), (columns - side.shape[1], 0)))
-        full = full.astype(BF16).reshape(chips, shards, cores, rows, columns)
-        full = jnp.take(full, lax.axis_index("wid") ^ jnp.arange(cores), axis=2).transpose(2, 0, 1, 3, 4)
-        return full[:1], full[1:]
+        return split_whole(mm(left, right, TN), chips, shards, cores, rows)
     outs = [shape((n, chips, shards, rows, columns), BF16) for n in (1, cores - 1)]
     specs = [pl.BlockSpec((x.shape[0], 1, shards, rows, columns), lambda d: (0, d, 0, 0, 0)) for x in outs]
-    return run(row_grads, chips, (place_self(), left, right, side),
+    return run(row_grads, chips, (place_self(), left, right),
                [SCALARS, pl.BlockSpec((tokens, width // chips), lambda d: (0, d)),
-                pl.BlockSpec((tokens, columns), lambda d: (0, 0)),
-                pl.BlockSpec((width // chips, side.shape[1]), lambda d: (d, 0))],
+                pl.BlockSpec((tokens, columns), lambda d: (0, 0))],
                tuple(outs), specs, [], 2 * tokens * width * columns)
 
 
-def lay_rows(turned, me_ref, own_ref, other_ref, out_ref):
+def input_grads(me_ref, bias_ref, left_ref, right_ref, w_ref, two_ref, din_ref, own_ref, other_ref):
+    columns, side = right_ref.shape[1], 128
+    heads, rows = bias_ref.shape[0], own_ref.shape[3]
+    din_ref[...] = mm(right_ref[...], w_ref[...], NT).astype(BF16)
+    spans = [(start, min(start + 512, columns - side)) for start in range(0, columns - side, 512)]
+    gain_sum = jnp.zeros((left_ref.shape[1], 1), F32)
+    for start, stop in spans + [(columns - side, columns)]:
+        part = mm(left_ref[...], right_ref[:, start:stop], TN)
+        weight = w_ref[:, start:stop].astype(F32)
+        lane = lax.broadcasted_iota(jnp.int32, part.shape, 1)
+        if stop == columns:
+            gain_sum = gain_sum + jnp.sum(jnp.where(lane < heads, part * weight, 0.0), axis=1, keepdims=True)
+            gain = jnp.sum(jnp.where(lane == heads, weight, 0.0), axis=1, keepdims=True)
+            row = lax.rem(lax.broadcasted_iota(jnp.int32, part.shape, 0), rows)
+            two = jnp.transpose(jnp.broadcast_to(two_ref[...], (side, part.shape[0])))
+            part = jnp.where(lane < heads, part, 0.0) + jnp.where(lane == heads, gain_sum / gain, 0.0)
+            for n in range(heads):
+                part = part + jnp.where((lane == heads + 2) & (row == n), bias_ref[n], 0.0)
+            part = jnp.where(me_ref[2] == 1, part, 0.0) + jnp.where(lane == heads + 1, two, 0.0)
+        else:
+            gain_sum = gain_sum + jnp.sum(part * weight, axis=1, keepdims=True)
+            part = jnp.where(me_ref[2] == 1, part, 0.0)
+        split_rows(me_ref, part.astype(BF16), slice(start, stop), own_ref, other_ref)
+
+
+def input_gradients(left, right, weights, two, bias, once, chips, shards, cores):
+    tokens, width = left.shape
+    columns, heads = right.shape[1], bias.shape[0]
+    rows = width // (chips * shards * cores)
+    if rows % 16:
+        full = mm(left, right, TN)
+        lane = lax.broadcasted_iota(jnp.int32, (width, columns), 1) - (columns - 128)
+        row = lax.broadcasted_iota(jnp.int32, (width, columns), 0) % rows
+        wide = weights.astype(F32)
+        gain = jnp.sum(jnp.where(lane < heads, full * wide, 0.0), axis=1, keepdims=True)
+        gain = gain / wide[:, columns - 128 + heads][:, None]
+        full = full + jnp.where(lane == heads, gain, 0.0)
+        for n in range(heads):
+            full = full + jnp.where((lane == heads + 2) & (row == n), bias[n], 0.0)
+        full = jnp.where(once, full, 0.0) + jnp.where(lane == heads + 1, two.T, 0.0)
+        return (mm(right, weights, NT).astype(BF16), *split_whole(full, chips, shards, cores, rows))
+    outs = [shape((n, chips, shards, rows, columns), BF16) for n in (1, cores - 1)]
+    specs = [pl.BlockSpec((x.shape[0], 1, shards, rows, columns), lambda d: (0, d, 0, 0, 0)) for x in outs]
+    features = pl.BlockSpec((tokens, width // chips), lambda d: (0, d))
+    me = jnp.concatenate([place_self(), once[None].astype(jnp.int32)])
+    return run(input_grads, chips, (me, bias, left, right, weights, two),
+               [SCALARS, SCALARS, features, pl.BlockSpec((tokens, columns), lambda d: (0, 0)),
+                pl.BlockSpec((width // chips, columns), lambda d: (d, 0)), pl.BlockSpec((1, width // chips), lambda d: (0, d))],
+               (shape((tokens, width), BF16), *outs), [features, *specs], [], 4 * tokens * width * columns)
+
+
+def lay_columns(me_ref, *refs):
+    *got, a_ref, b_ref, c_ref, d_ref, tail_ref = refs
+    count, span = len(got), a_ref.shape[1] // len(got)
+    for k, ref in enumerate(got):
+        source = lax.rem(me_ref[0] - k + count, count)
+        to = pl.ds(pl.multiple_of(source * span, 128), span)
+        for i, out in enumerate((a_ref, b_ref, c_ref, d_ref)):
+            out[:, to] = ref[:, i * span : (i + 1) * span].astype(F32)
+        tail_ref[source] = ref[:, 4 * span :].astype(F32)
+
+
+def laid_columns(got, side):
+    count, (rows, columns) = len(got), got[0].shape
+    span = (columns - side) // 4
+    if rows % 16 or span % 128:
+        got = by_source(got, "hid")
+        whole = [jnp.concatenate([x[:, i * span : (i + 1) * span] for x in got], axis=1).astype(F32) for i in range(4)]
+        return (*whole, jnp.stack([x[:, 4 * span :] for x in got]).astype(F32))
+    one = pl.BlockSpec((rows, columns), lambda i: (0, 0))
+    out = pl.BlockSpec((rows, count * span), lambda i: (0, 0))
+    return run(lay_columns, 1, (lax.axis_index("hid")[None].astype(jnp.int32), *got), [SCALARS] + [one] * count,
+               (shape((rows, count * span), F32),) * 4 + (shape((count, rows, side), F32),),
+               [out] * 4 + [pl.BlockSpec((count, rows, side), lambda i: (0, 0, 0))], [], 0)
+
+
+def lay_ff(me_ref, *refs):
+    *got, gate_ref, up_ref, down_ref = refs
+    part = got[0].shape[2]
+    for r, ref in enumerate(got):
+        to = pl.ds(pl.multiple_of((me_ref[0] ^ r) * part, 128), part)
+        gate_ref[:, to] = ref[0].astype(F32)
+        up_ref[:, to] = ref[1].astype(F32)
+        down_ref[to, :] = jnp.transpose(ref[2].astype(F32))
+
+
+def laid_ff(got):
+    count, (_, rows, part) = len(got), got[0].shape
+    outs = ((rows, count * part), (rows, count * part), (count * part, rows))
+    return run(lay_ff, 1, (lax.axis_index("dp")[None].astype(jnp.int32), *got),
+               [SCALARS] + [pl.BlockSpec((3, rows, part), lambda i: (0, 0, 0))] * count,
+               tuple(shape(x, F32) for x in outs), [pl.BlockSpec(x, lambda i: (0, 0)) for x in outs], [], 0)
+
+
+def lay_rows(me_ref, own_ref, other_ref, out_ref, *turned):
     cores, shards, rows = own_ref.shape[0] + other_ref.shape[0], own_ref.shape[2], own_ref.shape[3]
     for k in range(shards):
-        h = lax.rem(me_ref[2] - k + shards, shards) if turned else k
+        h = lax.rem(me_ref[2] - k + shards, shards)
         for n in range(cores):
             to = pl.ds(pl.multiple_of((h * cores + (me_ref[1] ^ n)) * rows, rows), rows)
             out_ref[to, :] = own_ref[0, 0, k] if n == 0 else other_ref[n - 1, 0, k]
-
-
-def gathered_rows(own, other, turned=True):
+    for ref in turned:
+        ref[...] = jnp.transpose(out_ref[:, -ref.shape[0] :].astype(F32))
+
+
+def gathered_rows(own, other, side):
     _, chips, shards, rows, columns = own.shape
     cores = 1 + other.shape[0]
     if rows % 16:
         full = jnp.concatenate([own, other], axis=0)
         full = jnp.take(full, lax.axis_index("wid") ^ jnp.arange(cores), axis=0)
-        if turned:
-            full = jnp.take(full, (lax.axis_index("hid") - jnp.arange(shards)) % shards, axis=2)
-        return full.transpose(1, 2, 0, 3, 4).reshape(-1, columns)
+        full = jnp.take(full, (lax.axis_index("hid") - jnp.arange(shards)) % shards, axis=2)
+        full = full.transpose(1, 2, 0, 3, 4).reshape(-1, columns)
+        return full, (full[:, columns - side :].astype(F32).T if side else None)
     me = jnp.concatenate([place_self(), lax.axis_index("hid")[None].astype(jnp.int32)])
     specs = [pl.BlockSpec((x.shape[0], 1, shards, rows, columns), lambda d: (0, d, 0, 0, 0)) for x in (own, other)]
     size = cores * shards * rows
-    return run(functools.partial(lay_rows, turned), chips, (me, own, other), [SCALARS, *specs],
-               (shape((chips * size, columns), BF16),), [pl.BlockSpec((size, columns), lambda d: (d, 0))], [], 0)[0]
+    outs, out_specs = [shape((chips * size, columns), BF16)], [pl.BlockSpec((size, columns), lambda d: (d, 0))]
+    if side:
+        outs.append(shape((side, chips * size), F32))
+        out_specs.append(pl.BlockSpec((side, size), lambda d: (0, d)))
+    out = run(lay_rows, chips, (me, own, other), [SCALARS, *specs], tuple(outs), out_specs, [], 0)
+    return out[0], (out[1] if side else None)
+
+
+def project(heads, tok, bias_ref, x_ref, w_ref, gain_ref, act_ref, q_ref, k_ref, v_ref, raw_ref, logit_ref):
+    x = x_ref[...].astype(F32)
+    unit = x * lax.rsqrt(jnp.mean(x * x, axis=-1, keepdims=True) + EPS)
+    act_ref[...] = (unit * gain_ref[...]).astype(BF16)
+    act, span = act_ref[...], q_ref.shape[1]
+    for i, out in enumerate((q_ref, k_ref, v_ref, raw_ref)):
+        out[...] = mm(act, w_ref[:, i * span : (i + 1) * span]).astype(out.dtype)
+    beside = mm(act, w_ref[:, 4 * span :])
+    for n in range(beside.shape[0] // tok):
+        rows = jnp.transpose(beside[n * tok : (n + 1) * tok, :])
+        for h in range(heads):
+            logit_ref[n, h : h + 1, :] = rows[h : h + 1, :] + bias_ref[h]
+
+
+def projected(x, weights, gain, bias, heads, tok):
+    tokens, width = x.shape
+    span = (weights.shape[1] - 128) // 4
+    blocks = tokens // tok
+    some = 2 if blocks % 2 == 0 else 1
+    wide, narrow = (pl.BlockSpec((some * tok, n), lambda c: (c, 0)) for n in (width, span))
+    whole = lambda c: (0, 0)
+    return run(
+        functools.partial(project, heads, tok), blocks // some, (bias, x, weights, gain),
+        [SCALARS, wide, pl.BlockSpec(weights.shape, whole), pl.BlockSpec((1, width), whole)],
+        (shape((tokens, width), BF16), shape((tokens, span), BF16),
+         shape((tokens, span), BF16), shape((tokens, span), BF16), shape((tokens, span), F32),
+         shape((blocks, heads, tok), F32)),
+        [wide, narrow, narrow, narrow, narrow, pl.BlockSpec((some, heads, tok), lambda c: (c, 0, 0))], [],
+        2 * tokens * width * weights.shape[1])
 
 
 def norm_in(tensor, gain_vec):
@@ -547,30 +677,6 @@
     return lax.all_to_all(parts, "wid", 0, 0, tiled=True)[:: cores // rows]
 
 
-def line_step(right, left, axis):
-    count = lax.axis_size(axis)
-    return (lax.ppermute(right, axis, [(i, i + 1) for i in range(count - 1)]),
-            lax.ppermute(left, axis, [(i + 1, i) for i in range(count - 1)]))
-
-
-def line_pieces(steps, axis):
-    count, me = lax.axis_size(axis), lax.axis_index(axis)
-    pieces = [(me, steps[0][0])]
-    for k in range(1, count):
-        pieces.append((lax.rem(me - k + count, count), jnp.where(me >= k, steps[k][0], steps[count - k][1])))
-    return pieces
-
-
-def sum_send(pieces, received, t, axis):
-    count, me = lax.axis_size(axis), lax.axis_index(axis)
-    mine, yours = (pick(pieces, jnp.minimum(me + count - t, count - 1)), pick(pieces, jnp.maximum(me - count + t, 0)))
-    if received:
-        mine, yours = add(mine, received[0]), add(yours, received[1])
-    mine, yours = together(mine, yours)
-    return (lax.ppermute(mine, axis, [(i, i + 1) for i in range(t)]),
-            lax.ppermute(yours, axis, [(count - 1 - i, count - 2 - i) for i in range(t)]))
-
-
 def choose(parts, index):
     return lax.select_n(index.astype(jnp.int32), *parts)
 
@@ -582,6 +688,13 @@
         sent = choose(blocks, lax.rem(me + k, count))
         got.append(lax.ppermute(sent, axis, [(i, (i + k) % count) for i in range(count)]))
     return got
+
+
+def exchange_rows(x, axis):
+    count, me = lax.axis_size(axis), lax.axis_index(axis)
+    sent = together(*[pick(x, lax.rem(me + k, count)) for k in range(1, count)])
+    return [pick(x, me)] + [lax.ppermute(sent[k - 1], axis, [(i, (i + k) % count) for i in range(count)])
+                            for k in range(1, count)]
 
 
 def by_source(got, axis):
@@ -671,78 +784,62 @@
     columns = 4 * span + side
 
     row_own = to_row(layer_in)
-    row_own, w_query, w_key, w_value, w_dir, w_beta = together(row_own, w_query, w_key, w_value, w_dir, w_beta)
-    line = [(row_own, row_own)]
-    line.append(line_step(*line[-1], "hid"))
+    row_own, w_query, w_key, w_value, w_dir, w_beta, w_out, w_gate, w_up, w_down, out_grad = together(
+        row_own, w_query, w_key, w_value, w_dir, w_beta, w_out, w_gate, w_up, w_down, out_grad)
+    row_in = lax.all_gather(row_own, "hid", axis=0, tiled=True)
 
     down_t = w_down.T
     ff_rows, ff_cols = down_t.shape
     part = ff_cols // n_dp
 
-    blank = jnp.zeros((shard, side - own_heads - 2), BF16)
+    spare = side // 2
+    ride = n_wid == row_count == 2 and own_heads + 2 <= spare and shard * spare >= held
+    seg_rows = to_row(segment_ids).astype(BF16) if ride else jnp.zeros((held,), BF16)
+    seg_rows = jnp.pad(seg_rows[: shard * spare], (0, max(0, shard * spare - held))).reshape(shard, spare)
+    blank = jnp.zeros((shard, spare - own_heads - 2), BF16)
     blocks = []
     for j in range(n_hid):
         at = slice(j * span, (j + 1) * span)
         blocks.append(jnp.concatenate(
-            [w_query[:, at], w_key[:, at], w_value[:, at], w_dir[:, at],
-             w_beta[:, j * own_heads : (j + 1) * own_heads], gain_attn[:, None], gain_mlp[:, None], blank], axis=1))
+            [w_query[:, at], w_key[:, at], w_value[:, at], w_dir[:, at], w_beta[:, j * own_heads : (j + 1) * own_heads],
+             gain_attn[:, None], gain_mlp[:, None], blank, seg_rows], axis=1))
     cat = exchange(blocks, "hid")
+    segs = [x[:, columns - spare :].reshape(-1)[:held].astype(jnp.int32) for x in cat]
+    cat = gather_near(jnp.stack(cat, axis=0), "dp")
+    grad_b = out_grad.reshape(row_count * tok, width)
+    wout = exchange([w_out] * n_hid, "hid")
     cut = [jnp.stack([x[:, j * part : (j + 1) * part] for x in (w_gate, w_up, down_t)]) for j in range(n_dp)]
-    cat, line[1], cut, w_out = together(cat, line[1], cut, w_out)
-    line.append(line_step(*line[-1], "hid"))
-    cat = gather_near(jnp.stack(cat, axis=0), "dp")
-    wout = exchange([w_out] * n_hid, "hid")
+    cat, cut = together(cat, cut)
+    cat = gather_end(gather_far(cat, "dp"), "dp")
     ff = [choose(cut, my_dp)]
     for r in range(1, n_dp):
         ff.append(lax.ppermute(choose(cut, my_dp ^ r), "dp", pairs(n_dp, r)))
-    cat, line[2] = together(cat, line[2])
-    line.append(line_step(*line[-1], "hid"))
-    cat = gather_end(gather_far(cat, "dp"), "dp")
-    cat = gathered_rows(cat[None], from_cores(cat))
-    gain_one = cat[:, 4 * span + own_heads].astype(F32)
-    gain_two = cat[:, 4 * span + own_heads + 1].astype(F32)
-    beta_own = cat[:, 4 * span : 4 * span + own_heads]
+    cat, gains = gathered_rows(cat[None], from_cores(cat), side)
     bias_own = lax.dynamic_slice_in_dim(b_beta, my_hid * own_heads, own_heads, 0).astype(F32)
 
-    pieces = line_pieces(line, "hid")
-    pieces, ff, wout, out_grad = together(pieces, ff, wout, out_grad)
+    row_in, cat, ff, wout, grad_b, segs = together(row_in, cat, ff, wout, grad_b, segs)
     ff = lax.all_gather(jnp.stack(ff, axis=0), "hid", axis=0, tiled=False)
-    wout = gather_near(jnp.stack(wout, axis=0), "dp")
-    grad_b = out_grad.reshape(row_count * tok, width)
-    grad_near = gather_near(grad_b, "dp")
-
-    scaled = jnp.zeros((n_hid, held, width), BF16)
-    act_one = jnp.zeros((n_hid, held, width), BF16)
-    for index, piece in pieces:
-        unit = norm_in(piece.astype(F32), 1.0)
-        scaled = place(scaled, unit.astype(BF16), index)
-        act_one = place(act_one, (unit * gain_one).astype(BF16), index)
-    act_one = act_one.reshape(n_hid * held, width)
-    scaled = scaled.reshape(n_hid * held, width)
-    if n_wid == 2:
-        segs = jnp.concatenate(by_source(exchange([to_row(segment_ids)] * n_hid, "hid"), "hid"), axis=0)
+    gain_one, gain_two = gains[own_heads], gains[own_heads + 1]
+    if ride:
+        segs = jnp.concatenate(by_source(segs, "hid"), axis=0)
     else:
         segs = lax.all_gather(segment_ids, ("hid", "wid"), axis=0, tiled=False)
         segs = pick(segs, lax.axis_index("wid") // copies, 1).reshape(-1)
-
-    query = mm(act_one, cat[:, :span]).astype(BF16)
-    key = mm(act_one, cat[:, span : 2 * span]).astype(BF16)
-    value = mm(act_one, cat[:, 2 * span : 3 * span]).astype(BF16)
-    raw = mm(act_one, cat[:, 3 * span : 4 * span])
-    logits = mm(act_one, beta_own) + bias_own
-    logits = logits.reshape(-1, tok, own_heads).transpose(0, 2, 1)
+    act_one, query, key, value, raw, logits = projected(row_in, cat, gain_one[None], bias_own, own_heads, tok)
+    raw, wout, grad_b = together(raw, wout, grad_b)
+    wout = gather_near(jnp.stack(wout, axis=0), "dp")
+    grad_all = gather_near(grad_b, "dp")
     local = attention_local(query, key, raw, logits, tok)
-    local, wout, grad_near = together(local, wout, grad_near)
+    local, wout, grad_all = together(local, wout, grad_all)
     wout = gather_far(wout, "dp")
-    grad_far = gather_far(grad_near, "dp")
+    grad_all = gather_far(grad_all, "dp")
     att, saved = attention_cross(query, key, value, raw, logits, segs, local, tok)
-    att, wout, grad_far = together(att, wout, grad_far)
-
     att = exchange([att[j * held : (j + 1) * held] for j in range(n_hid)], "hid")
+    wout = gather_end(wout, "dp")
+    wout_full, _ = gathered_rows(wout[None], from_cores(wout), 0)
+    grad_all = gather_end(grad_all, "dp").reshape(-1, width)
+    att, wout_full = together(att, wout_full)
     ff_own, ff_other = ff[:, None], jnp.moveaxis(from_cores(ff), 0, 1)
-    wout = gather_end(wout, "dp")
-    wout_full = gathered_rows(wout[None], from_cores(wout))
-    grad_all = gather_end(grad_far, "dp").reshape(-1, width)
     att = from_row(jnp.concatenate(by_source(att, "hid"), axis=1), row_count)
     att = att.reshape(row_count * tok, width)
 
@@ -763,14 +860,13 @@
     d_branch = d_middle.astype(BF16)
     d_att = mm(d_branch, wout_full, NT).astype(BF16).reshape(row_count, tok, width)
     d_att = to_row(d_att)
+    d_att, att = together(d_att, att)
+    d_att = exchange([d_att[:, j * span : (j + 1) * span] for j in range(n_hid)], "hid")
     ff_grads = core_sum(jnp.moveaxis(g_own, 1, 0), jnp.moveaxis(g_other, 1, 0))[0]
-    d_att, ff_grads, att, mlp = together(d_att, ff_grads, att, mlp)
-    d_att = exchange([d_att[:, j * span : (j + 1) * span] for j in range(n_hid)], "hid")
+    wout_rows = row_gradients(att, d_branch, n_dp, n_hid, n_wid)
+    d_att, wout_rows, ff_grads, mlp = together(d_att, wout_rows, ff_grads, mlp)
+    mlp = sum_far(mlp.reshape(n_dp, -1, width), "dp")
     ff_grads = lax.psum_scatter(ff_grads, "hid", scatter_dimension=0, tiled=False)
-    mlp = sum_far(mlp.reshape(n_dp, -1, width), "dp")
-    no_side = jnp.zeros((width, side), F32)
-    wout_rows = row_gradients(att, d_branch, no_side, n_dp, n_hid, n_wid)
-    d_att, wout_rows = together(d_att, wout_rows)
     d_att = jnp.concatenate(by_source(d_att, "hid"), axis=0)
     wout_grad = sum_far(core_sum(*wout_rows)[0], "dp")
 
@@ -780,56 +876,37 @@
     mlp = sum_near(mlp, "dp")
     dv, *crossed = crossed
     dq, dk, draw, dlogit = attention_backward_local(saved, crossed, tok)
-    dq, dk, draw, dlogit, mlp, wout_grad = together(dq, dk, draw, dlogit, mlp, wout_grad)
-    layer_out = (middle + add(*mlp).astype(F32)).astype(BF16)
     d_logit = dlogit.transpose(0, 2, 1).reshape(-1, own_heads).astype(BF16)
     d_cat = jnp.concatenate(
         [dq, dk, dv, draw, jnp.pad(d_logit, ((0, 0), (0, side - own_heads)))], axis=1)
-    lanes = lax.broadcasted_iota(jnp.int32, (1, side), 1)
-    d_act_one = mm(d_cat, cat, NT)
-    d_act_one, ff_grads = together(d_act_one.astype(BF16), ff_grads)
+    d_gain_two = jnp.sum(d_act.astype(F32) * norm_in(middle, 1.0), axis=0, keepdims=True)
+    bias_grad = jnp.sum(d_logit.astype(F32), axis=0)
+    once = lax.axis_index("wid") % copies == 0
+    d_act_one, *cat_grad = input_gradients(act_one, d_cat, cat, d_gain_two, bias_grad, once, n_dp, n_hid, n_wid)
+    d_act_one, cat_grad, wout_grad, mlp = together(d_act_one, cat_grad, wout_grad, mlp)
+    d_parts = d_act_one.reshape(n_hid, held, width)
+    first_half = exchange_rows(d_parts[:, : held // 2], "hid")
+    last_half = exchange_rows(d_parts[:, held // 2 :], "hid")
     wout_grad = add(*wout_grad)
     wout_got = exchange([wout_grad[j] for j in range(n_hid)], "hid")
+    layer_out = (middle + add(*mlp).astype(F32)).astype(BF16)
+    cat_grad = sum_far(core_sum(*cat_grad)[0], "dp")
     ff_got = [ff_grads[0]]
     for r in range(1, n_dp):
         ff_got.append(lax.ppermute(ff_grads[r], "dp", pairs(n_dp, r)))
-    d_sum = d_act_one.reshape(n_hid, held, width)
-    received = sum_send(d_sum, (), 1, "hid")
-
-    ones = lambda rows, lane: jnp.broadcast_to(jnp.where(lanes == lane, 1.0, 0.0).astype(BF16), (rows, side))
-    in_row = (d_act_one.astype(F32) * scaled.astype(F32)).astype(BF16)
-    in_own = (d_act.astype(F32) * norm_in(middle, 1.0)).astype(BF16)
-    bias_grad = jnp.sum(d_logit.astype(F32), axis=0)
-    row_of = lax.broadcasted_iota(jnp.int32, (width, side), 0) % shard
-    beside = mm(in_row, ones(in_row.shape[0], own_heads), TN)
-    for n in range(own_heads):
-        beside = beside + jnp.where((row_of == n) & (lanes == own_heads + 2), bias_grad[n], 0.0)
-    if copies > 1:
-        first = lax.axis_index("wid") % copies == 0
-        d_cat, beside = jnp.where(first, d_cat, 0), jnp.where(first, beside, 0.0)
-    beside = beside + mm(in_own, ones(in_own.shape[0], own_heads + 1), TN)
-    cat_grad = row_gradients(act_one, d_cat, beside, n_dp, n_hid, n_wid)
-    received, cat_grad = together(received, cat_grad)
-    for t in range(2, n_hid):
-        received = sum_send(d_sum, received, t, "hid")
-        if t == 2:
-            cat_grad = sum_far(core_sum(*cat_grad)[0], "dp")
-            received, cat_grad = together(received, cat_grad)
+    cat_grad, wout_got, ff_got, first_half = together(cat_grad, wout_got, ff_got, first_half)
     cat_grad = sum_near(cat_grad, "dp")
-    d_sum = add(pick(d_sum, my_hid), *received)
-    d_sum, wout_got, ff_got, cat_grad = together(d_sum, wout_got, ff_got, cat_grad)
+    cat_grad, last_half = together(cat_grad, last_half)
     cat_grad = add(*cat_grad)
-    cat_grad = by_source(exchange([cat_grad[j] for j in range(n_hid)], "hid"), "hid")
+    cat_got = exchange([cat_grad[j] for j in range(n_hid)], "hid")
+    d_sum = jnp.concatenate([add(*first_half), add(*last_half)], axis=0)
     d_sum = from_row(d_sum, row_count).reshape(row_count * tok, width).astype(F32)
+    grad_gate, grad_up, grad_down = laid_ff(ff_got)
+    *weight_grads, tails = laid_columns(cat_got, side)
     grad_wout = sum(x.astype(F32) for x in wout_got)
-    ff_grads = jnp.concatenate([choose(ff_got, my_dp ^ j) for j in range(n_dp)], axis=2).astype(F32)
-    weight_grads = [
-        jnp.concatenate([x[:, i * span : (i + 1) * span] for x in cat_grad], axis=1).astype(F32)
-        for i in range(4)]
-    tails = [x[:, 4 * span :].astype(F32) for x in cat_grad]
-    grad_beta = jnp.concatenate([x[:, :own_heads] for x in tails], axis=1)
-    gain_grads = sum(x[:, own_heads : own_heads + 2] for x in tails)
-    grad_bias = jnp.concatenate([x[:own_heads, own_heads + 2] for x in tails], axis=0)
+    grad_beta = tails[:, :, :own_heads].transpose(1, 0, 2).reshape(shard, heads)
+    gain_grads = jnp.sum(tails[:, :, own_heads : own_heads + 2], axis=0)
+    grad_bias = tails[:, :own_heads, own_heads + 2].reshape(heads)
 
     _, pull_one = jax.vjp(lambda t: norm_in(t, gain_one), layer_f)
     grad_in = (d_middle + pull_one(d_sum)[0]).astype(BF16)
@@ -837,7 +914,7 @@
     return (
         layer_out.reshape(layer_in.shape), grad_in.reshape(layer_in.shape), gain_grads[:, 0],
         *weight_grads, grad_beta, grad_bias,
-        grad_wout, gain_grads[:, 1], ff_grads[0], ff_grads[1], ff_grads[2].T,
+        grad_wout, gain_grads[:, 1], grad_gate, grad_up, grad_down,
     )
 
 

time: 627 us -> 572 us (0.912)
  matrix products: 35.1 us -> 5.56 us
  starting transfers between devices: 104 us -> 76.2 us
  Pallas kernels: 149 us -> 175 us
  local copies, waits for them, and re-layouts: 72.3 us -> 55 us
  other arithmetic: 75.4 us -> 64.2 us
  waiting for transfers between devices: 167 us -> 175 us
    dot_general x10 -> x2, matrix products: 35.1 us -> 5.56 us  [mm(): lax.dot_general(left, right, (dims, ((), ())), preferred_element_type=F32)]
    ppermute x21 -> x18, waiting for transfers between devices: 51.6 us -> 79.2 us  [exchange(): lax.ppermute(sent, axis, [(i, (i + k) % count) for i in range(count)])]
    ppermute x12 -> x6, starting transfers between devices: 33.4 us -> 6.61 us  [exchange_rows(): lax.ppermute(sent[k - 1], axis, [(i, (i + k) % count) for i in range(coun...]
    ppermute x12 -> x6, waiting for transfers between devices: 49.2 us -> 22.9 us  [exchange_rows(): lax.ppermute(sent[k - 1], axis, [(i, (i + k) % count) for i in range(coun...]
    pallas_call x10 -> x13, Pallas kernels: 149 us -> 175 us  [run(): pl.pallas_call(body, grid=(grid,), in_specs=in_specs, out_specs=out_specs...]
    ppermute x4, waiting for transfers between devices: 12.2 us -> 33.1 us  [gather_far(): lax.ppermute(two[half:], axis, pairs(4, 1))]
    ppermute x4, waiting for transfers between devices: 1.6 us -> 18.1 us  [gather_near(): lax.ppermute(x, axis, pairs(4, 1))]
    ppermute x4, waiting for transfers between devices: 15.5 us -> 2.78 us  [gather_near(): lax.ppermute(x, axis, pairs(4, 2))]
  transfers between devices with their start and end apart: 84 -> 76, of which waited for: 32 -> 36; matrix products, arithmetic and copies ran while one was open for 24% -> 17% of each run, Pallas kernels for 19% -> 25%
where the time goes in v3:
time: 572 us; the launch traced here: 566 us
  waiting for transfers between devices  175 us (31%)
  Pallas kernels  175 us (31%)
  starting transfers between devices  76.2 us (13%)
  other arithmetic  64.2 us (11%)
  local copies, waits for them, and re-layouts  55 us (10%)
  between operations  15.2 us (3%)
    pallas_call x13, Pallas kernels, run(): pl.pallas_call(body, grid=(grid,), in_specs=in_specs, out_specs=out_specs...  175 us
    ppermute x18, waiting for transfers between devices, exchange(): lax.ppermute(sent, axis, [(i, (i + k) % count) for i in range(count)])  79.2 us
    ppermute x4, waiting for transfers between devices, gather_far(): lax.ppermute(two[half:], axis, pairs(4, 1))  33.1 us
    ppermute x18, starting transfers between devices, exchange(): lax.ppermute(sent, axis, [(i, (i + k) % count) for i in range(count)])  25.7 us
    ppermute x6, waiting for transfers between devices, exchange_rows(): lax.ppermute(sent[k - 1], axis, [(i, (i + k) % count) for i in range(coun...  22.9 us
    ppermute x4, waiting for transfers between devices, gather_near(): lax.ppermute(x, axis, pairs(4, 1))  18.1 us
    convert_element_type x10, other arithmetic, add(): return total.astype(left.dtype)  15.4 us
    unnamed x141, local copies, waits for them, and re-layouts  14.4 us
  transfers between devices with their start and end apart: 76, of which 36 were waited for; matrix products, arithmetic and copies ran while one was open for 17% of the time, Pallas kernels for 25%

profile of v3, /device:TPU:8, one launch (start us, length us, event | category | flops | bytes accessed | tf_op | source)
XLA Modules:
  0.0 566.3 jit_solution(9066570443169595580)
XLA Ops:
  17.3 3.0 collective-permute-start.3
  20.4 2.5 collective-permute-start.2
  23.8 15.5 %collective-permute-done.3 = bf16[48,1664]{1,0:T(8,128)(2,1)S(1)} collective-permute-done((bf16[48,1664]{1,0:T(8,128)(2,1)}, bf16[48,1664]{1,0:T(8,128)(2,1)S(1)}, u32[]{:S(2)}, u32[]{:S(2)}) %collective-permute-start.3) | collective-permute-done | bytes 159776 | tf_op jit(solution)/shard_map/ppermute | solution.py:689
  39.3 12.0 %collective-permute-done.2 = bf16[48,1664]{1,0:T(8,128)(2,1)S(1)} collective-permute-done((bf16[48,1664]{1,0:T(8,128)(2,1)}, bf16[48,1664]{1,0:T(8,128)(2,1)S(1)}, u32[]{:S(2)}, u32[]{:S(2)}) %collective-permute-start.2) | collective-permute-done | bytes 159776 | tf_op jit(solution)/shard_map/ppermute | solution.py:689
  56.2 9.2 %collective-permute-done.5 = bf16[4,48,1664]{2,1,0:T(8,128)(2,1)S(1)} collective-permute-done((bf16[4,48,1664]{2,1,0:T(8,128)(2,1)S(1)}, bf16[4,48,1664]{2,1,0:T(8,128)(2,1)S(1)}, u32[]{:S(2)}, u32[]{:S(2)}) %collective-permute-start.5) | collective-permute-done | bytes 639008 | tf_op jit(solution)/shard_map/ppermute | solution.py:712
  76.0 2.7 collective-permute-start.13
  80.3 2.1 select_select_fusion
  87.5 3.9 collective-permute-start.15
  92.2 5.5 shard_map.254
  97.7 2.8 collective-permute-done.15
  100.6 2.2 pad_maximum_fusion
  105.4 12.4 %shard_map.255 = (bf16[1024,1536]{1,0:T(8,128)(2,1)}, bf16[1024,384]{1,0:T(8,128)(2,1)}, bf16[1024,384]{1,0:T(8,128)(2,1)}, bf16[1024,384]{1,0:T(8,128)(2,1)}, f...) custom-call(f32[3]{0:T(128)} %dynamic-slice_convert_fusion.bias_ref, bf16[1024,1536]{1,0:T(8,128)(2,1)} %all-gather.4.cloned.1.call-done.x_ref, ...), custom_call_target="tpu_custom_call" | custom-call | flops 5234491392 | bytes 15353868 | tf_op jit(solution)/shard_map/pallas_call | solution.py:244
  123.1 17.7 %shard_map.256 = (bf16[1024,384]{1,0:T(8,128)(2,1)}, bf16[1024,384]{1,0:T(8,128)(2,1)}, bf16[1024,384]{1,0:T(8,128)(2,1)}, bf16[1024,384]{1,0:T(8,128)(2,1)}, f3...) custom-call(bf16[1024,384]{1,0:T(8,128)(2,1)} %get-tuple-element.218, ...), custom_call_target="tpu_custom_call" | custom-call | flops 6241124352 | bytes 14168064 | tf_op jit(solution)/shard_map/pallas_call | solution.py:244
  140.9 9.0 %collective-permute-done.16 = bf16[4,48,1536]{2,1,0:T(8,128)(2,1)S(1)} collective-permute-done((bf16[4,48,1536]{2,1,0:T(8,128)(2,1)S(1)}, bf16[4,48,1536]{2,1,0:T(8,128)(2,1)S(1)}, u32[]{:S(2)}, u32[]{:S(2)}) %collective-permute-start.16) | collective-permute-done | bytes 589856 | tf_op jit(solution)/shard_map/ppermute | solution.py:712
  161.3 16.9 %shard_map.257 = (bf16[1024,384]{1,0:T(8,128)(2,1)}, bf16[8,3,128,1024]{3,2,1,0:T(8,128)(2,1)}, bf16[8,3,1024,128]{3,2,1,0:T(8,128)(2,1)}) custom-call(bf16[1024,384]{1,0:T(8,128)(2,1)} %get-tuple-element.242.qin_ref, bf16[1024,384]{1,0:T(8,128)(2,1)} %get-tuple-element.243.kout_ref, bf16[1024,384]{1,0:T(8,128)(2,1)} %get-tuple-element.244.ptop_ref, ...), custom_call_target="tpu_custom_call" | custom-call | flops 3221225472 | bytes 18882560 | tf_op jit(solution)/shard_map/pallas_call | solution.py:244
  179.8 2.2 collective-permute-start.22
  182.6 5.1 shard_map.258
  187.7 5.1 collective-permute-done.20
  192.8 11.4 %collective-permute-done.21 = bf16[256,384]{1,0:T(8,128)(2,1)S(1)} collective-permute-done((bf16[256,384]{1,0:T(8,128)(2,1)S(1)}, bf16[256,384]{1,0:T(8,128)(2,1)S(1)}, u32[]{:S(2)}, u32[]{:S(2)}) %collective-permute-start.21) | collective-permute-done | bytes 196640 | tf_op jit(solution)/shard_map/ppermute | solution.py:689
  204.3 2.8 collective-permute-done.22
  217.2 23.7 %collective-permute-done.32 = bf16[128,1536]{1,0:T(8,128)(2,1)S(1)} collective-permute-done((bf16[128,1536]{1,0:T(8,128)(2,1)S(1)}, bf16[128,1536]{1,0:T(8,128)(2,1)S(1)}, u32[]{:S(2)}, u32[]{:S(2)}) %collective-permute-start.32) | collective-permute-done | bytes 393248 | tf_op jit(solution)/shard_map/ppermute | solution.py:720
  244.5 7.7 %collective-permute-done.30 = bf16[128,1536]{1,0:T(8,128)(2,1)S(1)} collective-permute-done((bf16[128,1536]{1,0:T(8,128)(2,1)S(1)}, bf16[128,1536]{1,0:T(8,128)(2,1)S(1)}, u32[]{:S(2)}, u32[]{:S(2)}) %collective-permute-start.30) | collective-permute-done | bytes 393248 | tf_op jit(solution)/shard_map/ppermute | solution.py:720
  254.5 32.7 %shard_map.259 = (bf16[1024,1536]{1,0:T(8,128)(2,1)}, bf16[1024,1536]{1,0:T(8,128)(2,1)}, bf16[1024,1024]{1,0:T(8,128)(2,1)}, bf16[1024,1024]{1,0:T(8,128)(2,1)}, bf16[1024,1024]{1,0:T(8,128)(2,1)}) custom-call(s32[2]{0:T(128)} %pad_add_fusion.4.me_ref, bf16[1024,1536]{1,0:T(8,128)(2,1)} %bitcast.370, bf16[1024,1536]{1,0:T(8,128)(2,1)} %bitcast.372, ...), custom_call_target="tpu_custom_call" | custom-call | flops 19327352832 | bytes 28311560 | tf_op jit(solution)/shard_map/pallas_call | solution.py:244
  291.8 5.9 %collective-permute-done.35 = bf16[128,1536]{1,0:T(8,128)(2,1)S(1)} collective-permute-done((bf16[128,1536]{1,0:T(8,128)(2,1)S(1)}, bf16[128,1536]{1,0:T(8,128)(2,1)S(1)}, u32[]{:S(2)}, u32[]{:S(2)}) %collective-permute-start.35) | collective-permute-done | bytes 393248 | tf_op jit(solution)/shard_map/ppermute | solution.py:742
  301.3 15.6 %shard_map.260 = (bf16[4,1,4,3,192,256]{5,4,3,2,1,0:T(8,128)(2,1)}, bf16[4,1,4,3,192,256]{5,4,3,2,1,0:T(8,128)(2,1)}) custom-call(s32[2]{0:T(128)} %pad_add_fusion.4.me_ref, bf16[1024,1536]{1,0:T(8,128)(2,1)} %bitcast.371, bf16[1024,1536]{1,0:T(8,128)(2,1)} %bitcast.373, bf16[1024,1024]{1,0:T(8,128)(2,1)} %get-tuple-element.279.hid_ref, ...), custom_call_target="tpu_custom_call" | custom-call | flops 9663676416 | bytes 22020104 | tf_op jit(solution)/shard_map/pallas_call | solution.py:244
  319.7 4.1 convolution_convert_fusion
  330.2 5.5 shard_map.261
  335.7 6.5 %fusion.1 = bf16[4,4,3,192,256]{4,3,2,1,0:T(8,128)(2,1)} fusion(bf16[1,4,4,3,192,256]{5,4,3,2,1,0:T(8,128)(2,1)} %collective-permute-done.42, bf16[4,1,4,3,192,256]{5,4,3,2,1,0:T(8,128)(2,1)S(1)} %bitcast.364), kind=kLoop, calls=%fused_computation.3 | loop fusion | flops 9437184 | bytes 14155776 | tf_op jit(solution)/shard_map/squeeze | solution.py:865
  342.2 2.4 collective-permute-done.40
  354.1 2.4 add_convert_fusion.1
  358.7 20.7 %shard_map.262 = (f32[1024,384]{1,0:T(8,128)}, bf16[1024,384]{1,0:T(8,128)(2,1)}, f32[1024,384]{1,0:T(8,128)}, f32[1024,384]{1,0:T(8,128)}, bf16[1024,384]{1,0:T(8,128)(2,1)}) custom-call(bf16[1024,384]{1,0:T(8,128)(2,1)} %pad_maximum_fusion.7.grad_ref, bf16[1024,384]{1,0:T(8,128)(2,1)} %get-tuple-element.247.v_ref, ...), custom_call_target="tpu_custom_call" | custom-call | flops 5637144576 | bytes 22806528 | tf_op jit(solution)/shard_map/pallas_call | solution.py:244
  379.4 18.8 %shard_map.263 = (bf16[1024,384]{1,0:T(8,128)(2,1)}, bf16[1024,384]{1,0:T(8,128)(2,1)}, bf16[1024,384]{1,0:T(8,128)(2,1)}, f32[8,3,128]{2,1,0:T(4,128)}) custom-call(bf16[1024,384]{1,0:T(8,128)(2,1)} %get-tuple-element.218.q_ref, bf16[1024,384]{1,0:T(8,128)(2,1)} %get-tuple-element.219.k_ref, f32[1024,384]{1,0:T(8,128)} %get-tuple-element.226.raw_ref, ...), custom_call_target="tpu_custom_call" | custom-call | flops 6039797760 | bytes 17326080 | tf_op jit(solution)/shard_map/pallas_call | solution.py:244
  415.0 19.0 %shard_map.264 = (bf16[1024,1536]{1,0:T(8,128)(2,1)}, bf16[1,4,4,48,1664]{4,3,2,1,0:T(8,128)(2,1)}, bf16[1,4,4,48,1664]{4,3,2,1,0:T(8,128)(2,1)}) custom-call(s32[3]{0:T(128)} %pad_add_fusion.3.me_ref, f32[3]{0:T(128)} %get-tuple-element.570.bias_ref, bf16[1024,1536]{1,0:T(8,128)(2,1)} %get-tuple-element.312.left_ref, bf16[1024,1664]{1,0:T(8,128)(2,1)} %copy-done.43, ...), custom_call_target="tpu_custom_call" | custom-call | flops 10468982784 | bytes 19929112 | tf_op jit(solution)/shard_map/pallas_call | solution.py:244
  439.5 2.3 collective-permute-start.56
  446.9 2.5 collective-permute-start.62
  449.5 2.4 add_convert_fusion
  455.9 16.8 %collective-permute-done.57 = bf16[48,1536]{1,0:T(8,128)(2,1)} collective-permute-done((bf16[48,1536]{1,0:T(8,128)(2,1)S(1)}, bf16[48,1536]{1,0:T(8,128)(2,1)}, u32[]{:S(2)}, u32[]{:S(2)}) %collective-permute-start.57) | collective-permute-done | bytes 147488 | tf_op jit(solution)/shard_map/ppermute | solution.py:689
  473.5 2.1 slice_bitcast_fusion
  475.7 3.0 collective-permute-done.61
  479.6 7.3 %collective-permute-done.62 = bf16[128,1536]{1,0:T(8,128)(2,1)} collective-permute-done((bf16[128,1536]{1,0:T(8,128)(2,1)}, bf16[128,1536]{1,0:T(8,128)(2,1)}, u32[]{:S(2)}, u32[]{:S(2)}) %collective-permute-start.62) | collective-permute-done | bytes 393248 | tf_op jit(solution)/shard_map/ppermute | solution.py:696
  495.8 6.3 %collective-permute-done.59.refs_2_ = bf16[3,192,256]{2,1,0:T(8,128)(2,1)S(1)} collective-permute-done((bf16[3,192,256]{2,1,0:T(8,128)(2,1)S(1)}, bf16[3,192,256]{2,1,0:T(8,128)(2,1)S(1)}, u32[]{:S(2)}, u32[]{:S(2)}) %collective-permute-start.59) | collective-permute-done | bytes 294944 | tf_op jit(solution)/shard_map/ppermute | solution.py:896
  507.1 2.9 shard_map.266
  510.1 2.4 copy.126
  516.8 9.3 %collective-permute-done.67 = bf16[128,1536]{1,0:T(8,128)(2,1)} collective-permute-done((bf16[128,1536]{1,0:T(8,128)(2,1)}, bf16[128,1536]{1,0:T(8,128)(2,1)}, u32[]{:S(2)}, u32[]{:S(2)}) %collective-permute-start.67) | collective-permute-done | bytes 393248 | tf_op jit(solution)/shard_map/ppermute | solution.py:696
  532.0 2.4 collective-permute-start.72
  537.6 6.8 %collective-permute-done.71.refs_2_ = bf16[48,1664]{1,0:T(8,128)(2,1)S(1)} collective-permute-done((bf16[48,1664]{1,0:T(8,128)(2,1)S(1)}, bf16[48,1664]{1,0:T(8,128)(2,1)S(1)}, u32[]{:S(2)}, u32[]{:S(2)}) %collective-permute-start.71) | collective-permute-done | bytes 159776 | tf_op jit(solution)/shard_map/ppermute | solution.py:689
  546.3 2.3 shard_map.265
  555.9 3.8 fusion.8
  (421 shorter events, 169.7 us)
Async XLA Ops:
  7.2 93.4 %all-gather.4.cloned.1.call-start = ((), (), s32[]{:S(2)}) async-start(), calls=%async_computation.1 | async-start | bytes 3932160 | tf_op jit(solution)/shard_map/all_gather | solution.py:789
  15.5 192.0 %all-gather.6.cloned.1.call-start = ((), (), s32[]{:S(2)}) async-start(), calls=%async_computation.3 | async-start | bytes 5898240 | tf_op jit(solution)/shard_map/all_gather | solution.py:821
  17.3 22.0 %collective-permute-start.3 = (bf16[48,1664]{1,0:T(8,128)(2,1)}, bf16[48,1664]{1,0:T(8,128)(2,1)S(1)}, u32[]{:S(2)}, u32[]{:S(2)}) collective-permute-start(bf16[48,1664]{1,0:T(8,128)(2,1)} %get-tuple-element.520), channel_id=1, source_target_pairs={{0,4},{2,6},{4,0},{6,2},{1,5},{3,7},{5,1},{7,3},{8,12},{10,14},{12... | collective-permute-start | bytes 479240 | tf_op jit(solution)/shard_map/ppermute | solution.py:689
  20.4 31.0 %collective-permute-start.2 = (bf16[48,1664]{1,0:T(8,128)(2,1)}, bf16[48,1664]{1,0:T(8,128)(2,1)S(1)}, u32[]{:S(2)}, u32[]{:S(2)}) collective-permute-start(bf16[48,1664]{1,0:T(8,128)(2,1)} %get-tuple-element.518), channel_id=1, source_target_pairs={{0,2},{2,4},{4,6},{6,0},{1,3},{3,5},{5,7},{7,1},{8,10},{10,12},{12... | collective-permute-start | bytes 479240 | tf_op jit(solution)/shard_map/ppermute | solution.py:689
  82.4 18.1 %collective-permute-start.10 = (bf16[3,192,256]{2,1,0:T(8,128)(2,1)}, bf16[3,192,256]{2,1,0:T(8,128)(2,1)S(1)}, u32[]{:S(2)}, u32[]{:S(2)}) collective-permute-start(bf16[3,192,256]{2,1,0:T(8,128)(2,1)} %get-tuple-element.493), channel_id=1, source_target_pairs={{0,8},{8,0},{16,24},{24,16},{1,9},{9,1},{17,25},{25,17},{2,10},{10... | collective-permute-start | bytes 884744 | tf_op jit(solution)/shard_map/ppermute | solution.py:816
  84.0 16.5 %collective-permute-start.11 = (bf16[3,192,256]{2,1,0:T(8,128)(2,1)}, bf16[3,192,256]{2,1,0:T(8,128)(2,1)S(1)}, u32[]{:S(2)}, u32[]{:S(2)}) collective-permute-start(bf16[3,192,256]{2,1,0:T(8,128)(2,1)} %get-tuple-element.492), channel_id=1, source_target_pairs={{0,16},{8,24},{16,0},{24,8},{1,17},{9,25},{17,1},{25,9},{2,18},{10... | collective-permute-start | bytes 884744 | tf_op jit(solution)/shard_map/ppermute | solution.py:816
  85.6 14.9 %collective-permute-start.12 = (bf16[3,192,256]{2,1,0:T(8,128)(2,1)}, bf16[3,192,256]{2,1,0:T(8,128)(2,1)}, u32[]{:S(2)}, u32[]{:S(2)}) collective-permute-start(bf16[3,192,256]{2,1,0:T(8,128)(2,1)} %get-tuple-element.491), channel_id=1, source_target_pairs={{0,24},{8,16},{16,8},{24,0},{1,25},{9,17},{17,9},{25,1},{2,26},{10... | collective-permute-start | bytes 884744 | tf_op jit(solution)/shard_map/ppermute | solution.py:816
  102.8 370.7 %reduce-scatter.2.cloned.1.call-start = ((), (), s32[]{:S(2)}) async-start(), calls=%async_computation.2 | async-start | bytes 5898240 | tf_op jit(solution)/shard_map/reduce_scatter | solution.py:869
  117.8 33.3 %collective-permute-start.18 = (bf16[256,1536]{1,0:T(8,128)(2,1)S(1)}, bf16[256,1536]{1,0:T(8,128)(2,1)S(1)}, u32[]{:S(2)}, u32[]{:S(2)}) collective-permute-start(bf16[256,1536]{1,0:T(8,128)(2,1)S(1)} %bitcast.357), channel_id=1, source_target_pairs={{0,8},{8,0},{16,24},{24,16},{1,9},{9,1},{17,25},{25,17},{2,10},{10... | collective-permute-start | bytes 2359304 | tf_op jit(solution)/shard_map/ppermute | solution.py:712
  119.4 31.7 %collective-permute-start.19 = (bf16[256,1536]{1,0:T(8,128)(2,1)S(1)}, bf16[256,1536]{1,0:T(8,128)(2,1)S(1)}, u32[]{:S(2)}, u32[]{:S(2)}) collective-permute-start(bf16[256,1536]{1,0:T(8,128)(2,1)S(1)} %bitcast.358), channel_id=1, source_target_pairs={{0,16},{8,24},{16,0},{24,8},{1,17},{9,25},{17,1},{25,9},{2,18},{10... | collective-permute-start | bytes 2359304 | tf_op jit(solution)/shard_map/ppermute | solution.py:712
  122.1 27.7 %collective-permute-start.16 = (bf16[4,48,1536]{2,1,0:T(8,128)(2,1)S(1)}, bf16[4,48,1536]{2,1,0:T(8,128)(2,1)S(1)}, u32[]{:S(2)}, u32[]{:S(2)}) collective-permute-start(bf16[4,48,1536]{2,1,0:T(8,128)(2,1)S(1)} %pad_maximum_fusion.14), channel_id=1, source_target_pairs={{0,8},{8,0},{16,24},{24,16},{1,9},{9,1},{17,25},{25,17},{2,10},{10... | collective-permute-start | bytes 1769480 | tf_op jit(solution)/shard_map/ppermute | solution.py:712
  122.6 28.5 %collective-permute-start.17 = (bf16[4,48,1536]{2,1,0:T(8,128)(2,1)S(1)}, bf16[4,48,1536]{2,1,0:T(8,128)(2,1)S(1)}, u32[]{:S(2)}, u32[]{:S(2)}) collective-permute-start(bf16[4,48,1536]{2,1,0:T(8,128)(2,1)S(1)} %pad_maximum_fusion.14), channel_id=1, source_target_pairs={{0,16},{8,24},{16,0},{24,8},{1,17},{9,25},{17,1},{25,9},{2,18},{10... | collective-permute-start | bytes 1769480 | tf_op jit(solution)/shard_map/ppermute | solution.py:712
  160.2 22.4 %collective-permute-start.25 = (bf16[4,4,48,1536]{3,2,1,0:T(8,128)(2,1)}, bf16[4,4,48,1536]{3,2,1,0:T(8,128)(2,1)}, u32[]{:S(2)}, u32[]{:S(2)}) collective-permute-start(bf16[4,4,48,1536]{3,2,1,0:T(8,128)(2,1)} %fusion.19), channel_id=1, source_target_pairs={{0,1},{1,0},{2,3},{3,2},{4,5},{5,4},{6,7},{7,6},{8,9},{9,8},{10,11... | collective-permute-start | bytes 7077896 | tf_op jit(solution)/shard_map/ppermute | solution.py:760
  179.8 24.5 %collective-permute-start.21 = (bf16[256,384]{1,0:T(8,128)(2,1)S(1)}, bf16[256,384]{1,0:T(8,128)(2,1)S(1)}, u32[]{:S(2)}, u32[]{:S(2)}) collective-permute-start(bf16[256,384]{1,0:T(8,128)(2,1)S(1)} %get-tuple-element.512), channel_id=1, source_target_pairs={{0,4},{2,6},{4,0},{6,2},{1,5},{3,7},{5,1},{7,3},{8,12},{10,14},{12... | collective-permute-start | bytes 589832 | tf_op jit(solution)/shard_map/ppermute | solution.py:689
  179.8 27.3 %collective-permute-start.22 = (bf16[256,384]{1,0:T(8,128)(2,1)S(1)}, bf16[256,384]{1,0:T(8,128)(2,1)S(1)}, u32[]{:S(2)}, u32[]{:S(2)}) collective-permute-start(bf16[256,384]{1,0:T(8,128)(2,1)S(1)} %get-tuple-element.510), channel_id=1, source_target_pairs={{0,6},{2,0},{4,2},{6,4},{1,7},{3,1},{5,3},{7,5},{8,14},{10,8},{12,... | collective-permute-start | bytes 589832 | tf_op jit(solution)/shard_map/ppermute | solution.py:689
  207.5 45.3 %collective-permute-start.33 = (bf16[4,4,3,192,256]{4,3,2,1,0:T(8,128)(2,1)}, bf16[4,4,3,192,256]{4,3,2,1,0:T(8,128)(2,1)}, u32[]{:S(2)}, u32[]{:S(2)}) collective-permute-start(bf16[4,4,3,192,256]{4,3,2,1,0:T(8,128)(2,1)} %bitcast.403), channel_id=1, source_target_pairs={{0,1},{1,0},{2,3},{3,2},{4,5},{5,4},{6,7},{7,6},{8,9},{9,8},{10,11... | collective-permute-start | bytes 14155784 | tf_op jit(solution)/shard_map/ppermute | solution.py:760
  212.9 30.0 %collective-permute-start.27 = (bf16[256,1536]{1,0:T(8,128)(2,1)S(1)}, bf16[256,1536]{1,0:T(8,128)(2,1)S(1)}, u32[]{:S(2)}, u32[]{:S(2)}) collective-permute-start(bf16[256,1536]{1,0:T(8,128)(2,1)S(1)} %get-tuple-element.444), channel_id=1, source_target_pairs={{0,8},{8,0},{16,24},{24,16},{1,9},{9,1},{17,25},{25,17},{2,10},{10... | collective-permute-start | bytes 2359304 | tf_op jit(solution)/shard_map/ppermute | solution.py:712
  214.4 27.8 %collective-permute-start.28 = (bf16[256,1536]{1,0:T(8,128)(2,1)S(1)}, bf16[256,1536]{1,0:T(8,128)(2,1)S(1)}, u32[]{:S(2)}, u32[]{:S(2)}) collective-permute-start(bf16[256,1536]{1,0:T(8,128)(2,1)S(1)} %get-tuple-element.444), channel_id=1, source_target_pairs={{0,16},{8,24},{16,0},{24,8},{1,17},{9,25},{17,1},{25,9},{2,18},{10... | collective-permute-start | bytes 2359304 | tf_op jit(solution)/shard_map/ppermute | solution.py:712
  216.0 24.9 %collective-permute-start.32 = (bf16[128,1536]{1,0:T(8,128)(2,1)S(1)}, bf16[128,1536]{1,0:T(8,128)(2,1)S(1)}, u32[]{:S(2)}, u32[]{:S(2)}) collective-permute-start(bf16[128,1536]{1,0:T(8,128)(2,1)S(1)} %slice.412), channel_id=1, source_target_pairs={{0,8},{8,0},{16,24},{24,16},{1,9},{9,1},{17,25},{25,17},{2,10},{10... | collective-permute-start | bytes 1179656 | tf_op jit(solution)/shard_map/ppermute | solution.py:720
  216.6 25.5 %collective-permute-start.31 = (bf16[128,1536]{1,0:T(8,128)(2,1)S(1)}, bf16[128,1536]{1,0:T(8,128)(2,1)S(1)}, u32[]{:S(2)}, u32[]{:S(2)}) collective-permute-start(bf16[128,1536]{1,0:T(8,128)(2,1)S(1)} %slice.411), channel_id=1, source_target_pairs={{0,16},{8,24},{16,0},{24,8},{1,17},{9,25},{17,1},{25,9},{2,18},{10... | collective-permute-start | bytes 1179656 | tf_op jit(solution)/shard_map/ppermute | solution.py:720
  299.1 17.8 %collective-permute-start.36 = (bf16[256,1536]{1,0:T(8,128)(2,1)S(1)}, bf16[256,1536]{1,0:T(8,128)(2,1)S(1)}, u32[]{:S(2)}, u32[]{:S(2)}) collective-permute-start(bf16[256,1536]{1,0:T(8,128)(2,1)S(1)} %pad_maximum_fusion.4), channel_id=1, source_target_pairs={{0,8},{8,0},{16,24},{24,16},{1,9},{9,1},{17,25},{25,17},{2,10},{10... | collective-permute-start | bytes 2359304 | tf_op jit(solution)/shard_map/ppermute | solution.py:755
  299.8 17.1 %collective-permute-start.37 = (bf16[256,1536]{1,0:T(8,128)(2,1)S(1)}, bf16[256,1536]{1,0:T(8,128)(2,1)S(1)}, u32[]{:S(2)}, u32[]{:S(2)}) collective-permute-start(bf16[256,1536]{1,0:T(8,128)(2,1)S(1)} %pad_maximum_fusion.5), channel_id=1, source_target_pairs={{0,16},{8,24},{16,0},{24,8},{1,17},{9,25},{17,1},{25,9},{2,18},{10... | collective-permute-start | bytes 2359304 | tf_op jit(solution)/shard_map/ppermute | solution.py:755
  316.9 18.8 %collective-permute-start.42 = (bf16[1,4,4,3,192,256]{5,4,3,2,1,0:T(8,128)(2,1)}, bf16[1,4,4,3,192,256]{5,4,3,2,1,0:T(8,128)(2,1)}, u32[]{:S(2)}, u32[]{:S(2)}) collective-permute-start(bf16[1,4,4,3,192,256]{5,4,3,2,1,0:T(8,128)(2,1)} %bitcast.405), channel_id=1, source_target_pairs={{0,1},{1,0},{2,3},{3,2},{4,5},{5,4},{6,7},{7,6},{8,9},{9,8},{10,11... | collective-permute-start | bytes 14155784 | tf_op jit(solution)/shard_map/ppermute | solution.py:765
  326.7 15.5 %collective-permute-start.39 = (bf16[256,384]{1,0:T(8,128)(2,1)}, bf16[256,384]{1,0:T(8,128)(2,1)S(1)}, u32[]{:S(2)}, u32[]{:S(2)}) collective-permute-start(bf16[256,384]{1,0:T(8,128)(2,1)} %get-tuple-element.504), channel_id=1, source_target_pairs={{0,2},{2,4},{4,6},{6,0},{1,3},{3,5},{5,7},{7,1},{8,10},{10,12},{12... | collective-permute-start | bytes 589832 | tf_op jit(solution)/shard_map/ppermute | solution.py:689
  326.7 17.9 %collective-permute-start.40 = (bf16[256,384]{1,0:T(8,128)(2,1)}, bf16[256,384]{1,0:T(8,128)(2,1)}, u32[]{:S(2)}, u32[]{:S(2)}) collective-permute-start(bf16[256,384]{1,0:T(8,128)(2,1)} %get-tuple-element.503), channel_id=1, source_target_pairs={{0,4},{2,6},{4,0},{6,2},{1,5},{3,7},{5,1},{7,3},{8,12},{10,14},{12... | collective-permute-start | bytes 589832 | tf_op jit(solution)/shard_map/ppermute | solution.py:689
  328.3 17.5 %collective-permute-start.41 = (bf16[256,384]{1,0:T(8,128)(2,1)}, bf16[256,384]{1,0:T(8,128)(2,1)}, u32[]{:S(2)}, u32[]{:S(2)}) collective-permute-start(bf16[256,384]{1,0:T(8,128)(2,1)} %get-tuple-element.501), channel_id=1, source_target_pairs={{0,6},{2,0},{4,2},{6,4},{1,7},{3,1},{5,3},{7,5},{8,14},{10,8},{12,... | collective-permute-start | bytes 589832 | tf_op jit(solution)/shard_map/ppermute | solution.py:689
  349.8 29.6 %collective-permute-start.46 = (bf16[128,1536]{1,0:T(8,128)(2,1)}, bf16[128,1536]{1,0:T(8,128)(2,1)}, u32[]{:S(2)}, u32[]{:S(2)}) collective-permute-start(bf16[128,1536]{1,0:T(8,128)(2,1)} %get-tuple-element.452), channel_id=1, source_target_pairs={{0,16},{8,24},{16,0},{24,8},{1,17},{9,25},{17,1},{25,9},{2,18},{10... | collective-permute-start | bytes 1179656 | tf_op jit(solution)/shard_map/ppermute | solution.py:742
  350.6 28.8 %collective-permute-start.47 = (bf16[128,1536]{1,0:T(8,128)(2,1)}, bf16[128,1536]{1,0:T(8,128)(2,1)}, u32[]{:S(2)}, u32[]{:S(2)}) collective-permute-start(bf16[128,1536]{1,0:T(8,128)(2,1)} %get-tuple-element.451), channel_id=1, source_target_pairs={{0,8},{8,0},{16,24},{24,16},{1,9},{9,1},{17,25},{25,17},{2,10},{10... | collective-permute-start | bytes 1179656 | tf_op jit(solution)/shard_map/ppermute | solution.py:742
  356.6 22.8 %collective-permute-start.44 = (bf16[2,48,1536]{2,1,0:T(8,128)(2,1)S(1)}, bf16[2,48,1536]{2,1,0:T(8,128)(2,1)S(1)}, u32[]{:S(2)}, u32[]{:S(2)}) collective-permute-start(bf16[2,48,1536]{2,1,0:T(8,128)(2,1)S(1)} %get-tuple-element.470), channel_id=1, source_target_pairs={{0,16},{8,24},{16,0},{24,8},{1,17},{9,25},{17,1},{25,9},{2,18},{10... | collective-permute-start | bytes 884744 | tf_op jit(solution)/shard_map/ppermute | solution.py:742
  358.1 21.3 %collective-permute-start.45 = (bf16[2,48,1536]{2,1,0:T(8,128)(2,1)S(1)}, bf16[2,48,1536]{2,1,0:T(8,128)(2,1)S(1)}, u32[]{:S(2)}, u32[]{:S(2)}) collective-permute-start(bf16[2,48,1536]{2,1,0:T(8,128)(2,1)S(1)} %get-tuple-element.469), channel_id=1, source_target_pairs={{0,8},{8,0},{16,24},{24,16},{1,9},{9,1},{17,25},{25,17},{2,10},{10... | collective-permute-start | bytes 884744 | tf_op jit(solution)/shard_map/ppermute | solution.py:742
  404.3 32.6 %collective-permute-start.48 = (bf16[4,48,1536]{2,1,0:T(8,128)(2,1)}, bf16[4,48,1536]{2,1,0:T(8,128)(2,1)}, u32[]{:S(2)}, u32[]{:S(2)}) collective-permute-start(bf16[4,48,1536]{2,1,0:T(8,128)(2,1)} %pad_maximum_fusion.15), channel_id=1, source_target_pairs={{0,8},{8,0},{16,24},{24,16},{1,9},{9,1},{17,25},{25,17},{2,10},{10... | collective-permute-start | bytes 1769480 | tf_op jit(solution)/shard_map/ppermute | solution.py:755
  405.7 31.1 %collective-permute-start.49 = (bf16[4,48,1536]{2,1,0:T(8,128)(2,1)}, bf16[4,48,1536]{2,1,0:T(8,128)(2,1)}, u32[]{:S(2)}, u32[]{:S(2)}) collective-permute-start(bf16[4,48,1536]{2,1,0:T(8,128)(2,1)} %pad_maximum_fusion.16), channel_id=1, source_target_pairs={{0,16},{8,24},{16,0},{24,8},{1,17},{9,25},{17,1},{25,9},{2,18},{10... | collective-permute-start | bytes 1769480 | tf_op jit(solution)/shard_map/ppermute | solution.py:755
  410.0 26.9 %collective-permute-start.50 = (bf16[256,1536]{1,0:T(8,128)(2,1)}, bf16[256,1536]{1,0:T(8,128)(2,1)}, u32[]{:S(2)}, u32[]{:S(2)}) collective-permute-start(bf16[256,1536]{1,0:T(8,128)(2,1)} %pad_maximum_fusion.8), channel_id=1, source_target_pairs={{0,8},{8,0},{16,24},{24,16},{1,9},{9,1},{17,25},{25,17},{2,10},{10... | collective-permute-start | bytes 2359304 | tf_op jit(solution)/shard_map/ppermute | solution.py:755
  410.7 26.9 %collective-permute-start.51 = (bf16[256,1536]{1,0:T(8,128)(2,1)}, bf16[256,1536]{1,0:T(8,128)(2,1)}, u32[]{:S(2)}, u32[]{:S(2)}) collective-permute-start(bf16[256,1536]{1,0:T(8,128)(2,1)} %pad_maximum_fusion.9), channel_id=1, source_target_pairs={{0,16},{8,24},{16,0},{24,8},{1,17},{9,25},{17,1},{25,9},{2,18},{10... | collective-permute-start | bytes 2359304 | tf_op jit(solution)/shard_map/ppermute | solution.py:755
  442.5 30.2 %collective-permute-start.57 = (bf16[48,1536]{1,0:T(8,128)(2,1)S(1)}, bf16[48,1536]{1,0:T(8,128)(2,1)}, u32[]{:S(2)}, u32[]{:S(2)}) collective-permute-start(bf16[48,1536]{1,0:T(8,128)(2,1)S(1)} %get-tuple-element.521), channel_id=1, source_target_pairs={{0,6},{2,0},{4,2},{6,4},{1,7},{3,1},{5,3},{7,5},{8,14},{10,8},{12,... | collective-permute-start | bytes 442376 | tf_op jit(solution)/shard_map/ppermute | solution.py:689
  446.9 31.8 %collective-permute-start.61 = (bf16[128,1536]{1,0:T(8,128)(2,1)}, bf16[128,1536]{1,0:T(8,128)(2,1)}, u32[]{:S(2)}, u32[]{:S(2)}) collective-permute-start(bf16[128,1536]{1,0:T(8,128)(2,1)} %get-tuple-element.340), channel_id=1, source_target_pairs={{0,2},{2,4},{4,6},{6,0},{1,3},{3,5},{5,7},{7,1},{8,10},{10,12},{12... | collective-permute-start | bytes 1179656 | tf_op jit(solution)/shard_map/ppermute | solution.py:696
  446.9 39.9 %collective-permute-start.62 = (bf16[128,1536]{1,0:T(8,128)(2,1)}, bf16[128,1536]{1,0:T(8,128)(2,1)}, u32[]{:S(2)}, u32[]{:S(2)}) collective-permute-start(bf16[128,1536]{1,0:T(8,128)(2,1)} %get-tuple-element.341), channel_id=1, source_target_pairs={{0,4},{2,6},{4,0},{6,2},{1,5},{3,7},{5,1},{7,3},{8,12},{10,14},{12... | collective-permute-start | bytes 1179656 | tf_op jit(solution)/shard_map/ppermute | solution.py:696
  451.9 37.6 %collective-permute-start.63 = (bf16[128,1536]{1,0:T(8,128)(2,1)}, bf16[128,1536]{1,0:T(8,128)(2,1)}, u32[]{:S(2)}, u32[]{:S(2)}) collective-permute-start(bf16[128,1536]{1,0:T(8,128)(2,1)} %get-tuple-element.342), channel_id=1, source_target_pairs={{0,6},{2,0},{4,2},{6,4},{1,7},{3,1},{5,3},{7,5},{8,14},{10,8},{12,... | collective-permute-start | bytes 1179656 | tf_op jit(solution)/shard_map/ppermute | solution.py:696
  454.9 37.1 %collective-permute-start.53 = (bf16[2,48,1664]{2,1,0:T(8,128)(2,1)}, bf16[2,48,1664]{2,1,0:T(8,128)(2,1)}, u32[]{:S(2)}, u32[]{:S(2)}) collective-permute-start(bf16[2,48,1664]{2,1,0:T(8,128)(2,1)} %get-tuple-element.464), channel_id=1, source_target_pairs={{0,16},{8,24},{16,0},{24,8},{1,17},{9,25},{17,1},{25,9},{2,18},{10... | collective-permute-start | bytes 958472 | tf_op jit(solution)/shard_map/ppermute | solution.py:742
  472.7 19.3 %collective-permute-start.54 = (bf16[2,48,1664]{2,1,0:T(8,128)(2,1)}, bf16[2,48,1664]{2,1,0:T(8,128)(2,1)}, u32[]{:S(2)}, u32[]{:S(2)}) collective-permute-start(bf16[2,48,1664]{2,1,0:T(8,128)(2,1)} %get-tuple-element.463), channel_id=1, source_target_pairs={{0,8},{8,0},{16,24},{24,16},{1,9},{9,1},{17,25},{25,17},{2,10},{10... | collective-permute-start | bytes 958472 | tf_op jit(solution)/shard_map/ppermute | solution.py:742
  478.6 15.2 %collective-permute-start.58 = (bf16[3,192,256]{2,1,0:T(8,128)(2,1)S(1)}, bf16[3,192,256]{2,1,0:T(8,128)(2,1)S(1)}, u32[]{:S(2)}, u32[]{:S(2)}) collective-permute-start(bf16[3,192,256]{2,1,0:T(8,128)(2,1)S(1)} %get-tuple-element.485), channel_id=1, source_target_pairs={{0,8},{8,0},{16,24},{24,16},{1,9},{9,1},{17,25},{25,17},{2,10},{10... | collective-permute-start | bytes 884744 | tf_op jit(solution)/shard_map/ppermute | solution.py:896
  486.9 15.2 %collective-permute-start.59 = (bf16[3,192,256]{2,1,0:T(8,128)(2,1)S(1)}, bf16[3,192,256]{2,1,0:T(8,128)(2,1)S(1)}, u32[]{:S(2)}, u32[]{:S(2)}) collective-permute-start(bf16[3,192,256]{2,1,0:T(8,128)(2,1)S(1)} %get-tuple-element.484), channel_id=1, source_target_pairs={{0,16},{8,24},{16,0},{24,8},{1,17},{9,25},{17,1},{25,9},{2,18},{10... | collective-permute-start | bytes 884744 | tf_op jit(solution)/shard_map/ppermute | solution.py:896
  492.0 24.9 %collective-permute-start.66 = (bf16[128,1536]{1,0:T(8,128)(2,1)}, bf16[128,1536]{1,0:T(8,128)(2,1)}, u32[]{:S(2)}, u32[]{:S(2)}) collective-permute-start(bf16[128,1536]{1,0:T(8,128)(2,1)} %get-tuple-element.352), channel_id=1, source_target_pairs={{0,2},{2,4},{4,6},{6,0},{1,3},{3,5},{5,7},{7,1},{8,10},{10,12},{12... | collective-permute-start | bytes 1179656 | tf_op jit(solution)/shard_map/ppermute | solution.py:696
  492.0 34.2 %collective-permute-start.67 = (bf16[128,1536]{1,0:T(8,128)(2,1)}, bf16[128,1536]{1,0:T(8,128)(2,1)}, u32[]{:S(2)}, u32[]{:S(2)}) collective-permute-start(bf16[128,1536]{1,0:T(8,128)(2,1)} %get-tuple-element.353), channel_id=1, source_target_pairs={{0,4},{2,6},{4,0},{6,2},{1,5},{3,7},{5,1},{7,3},{8,12},{10,14},{12... | collective-permute-start | bytes 1179656 | tf_op jit(solution)/shard_map/ppermute | solution.py:696
  493.8 34.0 %collective-permute-start.68 = (bf16[128,1536]{1,0:T(8,128)(2,1)}, bf16[128,1536]{1,0:T(8,128)(2,1)}, u32[]{:S(2)}, u32[]{:S(2)}) collective-permute-start(bf16[128,1536]{1,0:T(8,128)(2,1)} %get-tuple-element.354), channel_id=1, source_target_pairs={{0,6},{2,0},{4,2},{6,4},{1,7},{3,1},{5,3},{7,5},{8,14},{10,8},{12,... | collective-permute-start | bytes 1179656 | tf_op jit(solution)/shard_map/ppermute | solution.py:696
  505.4 22.5 %collective-permute-start.64 = (bf16[4,48,1664]{2,1,0:T(8,128)(2,1)}, bf16[4,48,1664]{2,1,0:T(8,128)(2,1)}, u32[]{:S(2)}, u32[]{:S(2)}) collective-permute-start(bf16[4,48,1664]{2,1,0:T(8,128)(2,1)} %pad_maximum_fusion.12), channel_id=1, source_target_pairs={{0,8},{8,0},{16,24},{24,16},{1,9},{9,1},{17,25},{25,17},{2,10},{10... | collective-permute-start | bytes 1916936 | tf_op jit(solution)/shard_map/ppermute | solution.py:755
  506.0 21.9 %collective-permute-start.65 = (bf16[4,48,1664]{2,1,0:T(8,128)(2,1)}, bf16[4,48,1664]{2,1,0:T(8,128)(2,1)}, u32[]{:S(2)}, u32[]{:S(2)}) collective-permute-start(bf16[4,48,1664]{2,1,0:T(8,128)(2,1)} %pad_maximum_fusion.13), channel_id=1, source_target_pairs={{0,16},{8,24},{16,0},{24,8},{1,17},{9,25},{17,1},{25,9},{2,18},{10... | collective-permute-start | bytes 1916936 | tf_op jit(solution)/shard_map/ppermute | solution.py:755
  537.6 15.8 %collective-permute-start.69 = (bf16[128,1536]{1,0:T(8,128)(2,1)}, bf16[128,1536]{1,0:T(8,128)(2,1)}, u32[]{:S(2)}, u32[]{:S(2)}) collective-permute-start(bf16[128,1536]{1,0:T(8,128)(2,1)} %dynamic-slice_bitcast_fusion.16), channel_id=1, source_target_pairs={{0,1},{1,0},{2,3},{3,2},{4,5},{5,4},{6,7},{7,6},{8,9},{9,8},{10,11... | collective-permute-start | bytes 1179656 | tf_op jit(solution)/shard_map/ppermute | solution.py:674
  (96 other events, 756.9 us)
Sparse Core Ops, SparseCore 0:
  15.6 72.6 all-gather.3
  102.9 91.8 all-gather.5
  352.0 84.9 reduce-scatter.1

commit v4 on v3

--- a/solution.py
+++ b/solution.py
@@ -196,7 +196,7 @@
 
 
 def local_backward(heads, size, scale, q_ref, k_ref, raw_ref, logit_ref, t_ref, e_ref, cm_ref, s_ref,
-                   dqin_ref, dintra_ref, dkout_ref, dstep_ref, dq_ref, dk_ref, draw_ref, dlogit_ref):
+                   dqin_ref, dintra_ref, dkout_ref, dstep_ref, dv_ref, out_ref):
     width = q_ref.shape[1] // heads
     rows, cols = iotas(size)
     strict, lower, diag = rows > cols, rows >= cols, rows == cols
@@ -205,6 +205,8 @@
     at = [(slice(n * size, (n + 1) * size), slice(h * width, (h + 1) * width)) for n, h in units]
     wide = [(slice(n * width, (n + 1) * width), slice(h * width, (h + 1) * width)) for n, h in units]
     every = range(len(units))
+    span = heads * width
+    out = lambda u, part: (at[u][0], slice(part * span + units[u][1] * width, part * span + (units[u][1] + 1) * width))
     q, k = [(q_ref[a],) for a in at], [(k_ref[a],) for a in at]
     both = [unit_dirs(raw_ref[a]) for a in at]
     betas = [2.0 * jax.nn.sigmoid(logit_ref[n, h : h + 1, :]) for n, h in units]
@@ -227,17 +229,25 @@
     d_a = [halves(jnp.where(strict, d_x[u], 0.0)) for u in every]
     for u in every:
         a = at[u]
-        dq_ref[a] = (dqin_ref[a] + scale * dot(dintra[u], k[u], NN) + dot(d_b[u], ws[u], NN)).astype(BF16)
-        dk_ref[a] = (dkout_ref[a] + scale * dot(dintra[u], q[u], TN) + dot(d_m[u], ws[u], TN)).astype(BF16)
+        out_ref[out(u, 0)] = (dqin_ref[a] + scale * dot(dintra[u], k[u], NN) + dot(d_b[u], ws[u], NN)).astype(BF16)
+        out_ref[out(u, 1)] = (dkout_ref[a] + scale * dot(dintra[u], q[u], TN) + dot(d_m[u], ws[u], TN)).astype(BF16)
     d_w = [y_s[u] - dot(ss[u], dps[u], NT) - dot(es[u], dks[u], NN) - dot(cms[u], dqs[u], TN)
            + dot(d_b[u], q[u], TN) + dot(d_m[u], k[u], NN) + dot(d_a[u], ws[u], NN) + dot(d_a[u], ws[u], TN)
            for u in every]
-    for u, (n, h) in enumerate(units):
+    for u in every:
         raw, inv = raw_ref[at[u]], both[u][1]
         draw = inv * d_w[u] - raw * (inv * inv * inv) * jnp.sum(raw * d_w[u], axis=-1, keepdims=True)
-        draw_ref[at[u]] = draw.astype(BF16)
-        at_diag = jnp.sum(jnp.where(diag, d_x[u], 0.0), axis=0, keepdims=True)
-        dlogit_ref[n, h : h + 1, :] = -at_diag * (1.0 - 0.5 * betas[u]) / betas[u]
+        out_ref[out(u, 3)] = draw.astype(BF16)
+    out_ref[:, 2 * span : 3 * span] = dv_ref[...]
+    side = out_ref.shape[1] - 4 * span
+    for n in some:
+        lines = []
+        for h in range(heads):
+            u = n * heads + h
+            at_diag = jnp.sum(jnp.where(diag, d_x[u], 0.0), axis=0, keepdims=True)
+            lines.append(-at_diag * (1.0 - 0.5 * betas[u]) / betas[u])
+        lines.append(jnp.zeros((side - heads, size), F32))
+        out_ref[n * size : (n + 1) * size, 4 * span :] = jnp.transpose(jnp.concatenate(lines, axis=0)).astype(BF16)
 
 
 def run(body, grid, inputs, in_specs, outputs, out_specs, scratch, flops):
@@ -326,23 +336,22 @@
     return dv, dqin, dintra, dkout, dstep
 
 
-def attention_backward_local(saved, crossed, size):
+def attention_backward_local(saved, dv, crossed, size, side):
     q, k, v, raw, logits, qin, ptop, plow, t, e, cm, s, prob, keep = saved
     tokens, width = q.shape
     blocks, heads, _ = logits.shape
     head = width // heads
     scale = 1.0 / math.sqrt(head)
     some = SOME if blocks % SOME == 0 else 1
-    b = shape((tokens, width), BF16)
     block = pl.BlockSpec((some * size, width), lambda c: (c, 0))
     square = pl.BlockSpec((some * head, width), lambda c: (c, 0))
     logit_block = pl.BlockSpec((some, heads, size), lambda c: (c, 0, 0))
     return run(
         functools.partial(local_backward, heads, size, scale), blocks // some,
-        (q, k, raw, logits, t, e, cm, s, *crossed),
-        [block, block, block, logit_block, block, block, block, block, block, block, block, square],
-        (b, b, b, shape((blocks, heads, size), F32)), [block, block, block, logit_block], [],
-        blocks * heads * 60 * 2 * size * size * head)
+        (q, k, raw, logits, t, e, cm, s, *crossed, dv),
+        [block, block, block, logit_block, block, block, block, block, block, block, block, square, block],
+        (shape((tokens, 4 * width + side), BF16),), [pl.BlockSpec((some * size, 4 * width + side), lambda c: (c, 0))], [],
+        blocks * heads * 60 * 2 * size * size * head)[0]
 
 
 def ff_forward(me_ref, act_ref, grad_ref, own_ref, other_ref, mlp_ref, dact_ref, hid_ref, dgate_ref, dup_ref,
@@ -388,14 +397,20 @@
         dact_ref[...] = dact[...].astype(BF16)
 
 
-def ff_weights(me_ref, act_ref, grad_ref, hid_ref, dgate_ref, dup_ref, own_ref, other_ref):
+def ff_weights(me_ref, *refs):
+    *ins, own_ref, other_ref = refs
+    groups = [ins[5 * n : 5 * n + 5] for n in range(len(ins) // 5)]
     cores, chips, rows = own_ref.shape[1] + other_ref.shape[1], own_ref.shape[2], own_ref.shape[4]
     for d in range(chips):
         at = slice(d * cores * rows, (d + 1) * cores * rows)
-        act, grad = act_ref[:, at], grad_ref[:, at]
         r = me_ref[0] ^ d
-        for i, part in enumerate((mm(act, dgate_ref[...], TN), mm(act, dup_ref[...], TN),
-                                  mm(grad, hid_ref[...], TN))):
+        gate = up = down = 0.0
+        for act_ref, grad_ref, hid_ref, dgate_ref, dup_ref in groups:
+            act, grad = act_ref[:, at], grad_ref[:, at]
+            gate = gate + mm(act, dgate_ref[...], TN)
+            up = up + mm(act, dup_ref[...], TN)
+            down = down + mm(grad, hid_ref[...], TN)
+        for i, part in enumerate((gate, up, down)):
             pieces = [part[w * rows : (w + 1) * rows, :].astype(BF16) for w in range(cores)]
             for n in range(cores):
                 piece = pieces[0]
@@ -427,16 +442,18 @@
                [pltpu.VMEM((width, part), BF16)] * 3 + [pltpu.VMEM((tokens, width), F32)] * 2, flops)
 
 
-def feed_forward_weights(act, grad, hidden, d_gate, d_up, own, other):
-    tokens, width = act.shape
+def feed_forward_weights(acts, grads, saved, own, other):
+    width = acts[0].shape[1]
     groups, part = own.shape[0], own.shape[5]
-    whole = pl.BlockSpec((tokens, width), lambda h: (0, 0))
-    units = pl.BlockSpec((tokens, part), lambda h: (0, h))
+    values, specs = [], []
+    for act, grad, some in zip(acts, grads, saved):
+        values += [act, grad, *some]
+        specs += [pl.BlockSpec(act.shape, lambda h: (0, 0))] * 2
+        specs += [pl.BlockSpec((act.shape[0], part), lambda h: (0, h))] * 3
     held = [pl.BlockSpec((1,) + x.shape[1:], lambda h: (h, 0, 0, 0, 0, 0)) for x in (own, other)]
-    return run(ff_weights, groups, (place_self(), act, grad, hidden, d_gate, d_up),
-               [SCALARS, whole, whole, units, units, units],
+    return run(ff_weights, groups, (place_self(), *values), [SCALARS, *specs],
                (shape(own.shape, BF16), shape(other.shape, BF16)), held, [],
-               3 * 2 * tokens * width * groups * part)
+               3 * 2 * sum(x.shape[0] for x in acts) * width * groups * part)
 
 
 def split_rows(me_ref, part, at, own_ref, other_ref):
@@ -734,25 +751,22 @@
     return gather_end(gather_far(gather_near(x, axis), axis), axis)
 
 
-def sum_far(x, axis):
-    if lax.axis_size(axis) != 4:
-        return (x,)
-    half = x.shape[1] // 2
-    far = pick(x, lax.axis_index(axis) ^ 3)
-    return x, lax.ppermute(far[:half], axis, pairs(4, 2)), lax.ppermute(far[half:], axis, pairs(4, 1))
-
-
-def sum_near(far, axis):
-    if len(far) == 1:
-        return (lax.psum_scatter(far[0], axis, scatter_dimension=0, tiled=False),)
-    x, top, low = far
-    me = lax.axis_index(axis)
-    half = x.shape[1] // 2
-    one, two = pick(x, me ^ 1), pick(x, me ^ 2)
-    one = jnp.concatenate([add(one[:half], top), one[half:]], axis=0)
-    two = jnp.concatenate([two[:half], add(two[half:], low)], axis=0)
+def by_distance(far):
+    x, one, two, top, low = far
+    return x, jnp.concatenate([one, two], axis=0), jnp.concatenate([top, low], axis=0)
+
+
+def sum_far(far, axis):
+    half = far.shape[0] // 2
+    return lax.ppermute(far[:half], axis, pairs(4, 2)), lax.ppermute(far[half:], axis, pairs(4, 1))
+
+
+def sum_near(one, two, came, axis):
+    half = one.shape[0] // 2
+    one = jnp.concatenate([add(one[:half], came[0]), one[half:]], axis=0)
+    two = jnp.concatenate([two[:half], add(two[half:], came[1])], axis=0)
     one, two = together(one, two)
-    return pick(x, me), lax.ppermute(one, axis, pairs(4, 1)), lax.ppermute(two, axis, pairs(4, 2))
+    return lax.ppermute(one, axis, pairs(4, 1)), lax.ppermute(two, axis, pairs(4, 2))
 
 
 def from_cores(x):
@@ -805,19 +819,22 @@
              gain_attn[:, None], gain_mlp[:, None], blank, seg_rows], axis=1))
     cat = exchange(blocks, "hid")
     segs = [x[:, columns - spare :].reshape(-1)[:held].astype(jnp.int32) for x in cat]
+    grad_b = out_grad.reshape(row_count * tok, width)
+    cat, grads = together(cat, gather_near(grad_b, "dp"))
     cat = gather_near(jnp.stack(cat, axis=0), "dp")
-    grad_b = out_grad.reshape(row_count * tok, width)
     wout = exchange([w_out] * n_hid, "hid")
     cut = [jnp.stack([x[:, j * part : (j + 1) * part] for x in (w_gate, w_up, down_t)]) for j in range(n_dp)]
     cat, cut = together(cat, cut)
     cat = gather_end(gather_far(cat, "dp"), "dp")
+    grads = by_distance(gather_far(grads, "dp"))
     ff = [choose(cut, my_dp)]
     for r in range(1, n_dp):
         ff.append(lax.ppermute(choose(cut, my_dp ^ r), "dp", pairs(n_dp, r)))
     cat, gains = gathered_rows(cat[None], from_cores(cat), side)
     bias_own = lax.dynamic_slice_in_dim(b_beta, my_hid * own_heads, own_heads, 0).astype(F32)
 
-    row_in, cat, ff, wout, grad_b, segs = together(row_in, cat, ff, wout, grad_b, segs)
+    row_in, cat, ff, wout, grads, segs = together(row_in, cat, ff, wout, grads, segs)
+    wout = gather_near(jnp.stack(wout, axis=0), "dp")
     ff = lax.all_gather(jnp.stack(ff, axis=0), "hid", axis=0, tiled=False)
     gain_one, gain_two = gains[own_heads], gains[own_heads + 1]
     if ride:
@@ -826,33 +843,39 @@
         segs = lax.all_gather(segment_ids, ("hid", "wid"), axis=0, tiled=False)
         segs = pick(segs, lax.axis_index("wid") // copies, 1).reshape(-1)
     act_one, query, key, value, raw, logits = projected(row_in, cat, gain_one[None], bias_own, own_heads, tok)
-    raw, wout, grad_b = together(raw, wout, grad_b)
-    wout = gather_near(jnp.stack(wout, axis=0), "dp")
-    grad_all = gather_near(grad_b, "dp")
+    raw, wout = together(raw, wout)
+    wout = gather_far(wout, "dp")
     local = attention_local(query, key, raw, logits, tok)
-    local, wout, grad_all = together(local, wout, grad_all)
-    wout = gather_far(wout, "dp")
-    grad_all = gather_far(grad_all, "dp")
     att, saved = attention_cross(query, key, value, raw, logits, segs, local, tok)
+    att, wout = together(att, wout)
     att = exchange([att[j * held : (j + 1) * held] for j in range(n_hid)], "hid")
     wout = gather_end(wout, "dp")
     wout_full, _ = gathered_rows(wout[None], from_cores(wout), 0)
-    grad_all = gather_end(grad_all, "dp").reshape(-1, width)
     att, wout_full = together(att, wout_full)
-    ff_own, ff_other = ff[:, None], jnp.moveaxis(from_cores(ff), 0, 1)
     att = from_row(jnp.concatenate(by_source(att, "hid"), axis=1), row_count)
     att = att.reshape(row_count * tok, width)
 
     layer_f = layer_in.astype(F32).reshape(row_count * tok, width)
     middle = layer_f + mm(att, wout_full)
     act_two = norm_in(middle, gain_two).astype(BF16)
-    act_all = square_gather(act_two, "dp").reshape(-1, width)
-    mlp, d_act, hidden, d_gate, d_up = feed_forward(act_all, grad_all, ff_own, ff_other)
-    d_act = sum_near(sum_far(d_act.reshape(n_dp, -1, width), "dp"), "dp")
-    hidden, d_gate, d_up, mine = together(hidden, d_gate, d_up, d_act[0])
-    g_own, g_other = feed_forward_weights(act_all, grad_all, hidden, d_gate, d_up, ff_own, ff_other)
-    near, g_own, g_other = together(d_act[1:], g_own, g_other)
-    d_act = add(mine, *near)
+    act_two, ff = together(act_two, ff)
+    ff_own, ff_other = ff[:, None], jnp.moveaxis(from_cores(ff), 0, 1)
+    near = gather_near(act_two, "dp")
+    own = feed_forward(act_two, grads[0], ff_own, ff_other)
+    own, near = together(own, near)
+    far = gather_far(near, "dp")
+    acts = by_distance(far)
+    mid = feed_forward(acts[1], grads[1], ff_own, ff_other)
+    mid, end = together(mid, acts[2])
+    end = feed_forward(end, grads[2], ff_own, ff_other)
+    tokens = row_count * tok
+    came = sum_far(end[1], "dp")
+    near = sum_near(mid[1][:tokens], mid[1][tokens:], came, "dp")
+    own, mid, end, near_sent = together(own, mid, end, came)
+    g_own, g_other = feed_forward_weights(
+        (act_two, *acts[1:]), grads, [(x[2], x[3], x[4]) for x in (own, mid, end)], ff_own, ff_other)
+    near, g_own, g_other = together(near, g_own, g_other)
+    d_act = add(own[1], *near)
 
     _, pull_two = jax.vjp(norm_in, middle, gain_two)
     d_mid_norm, _ = pull_two(d_act.astype(F32))
@@ -864,50 +887,49 @@
     d_att = exchange([d_att[:, j * span : (j + 1) * span] for j in range(n_hid)], "hid")
     ff_grads = core_sum(jnp.moveaxis(g_own, 1, 0), jnp.moveaxis(g_other, 1, 0))[0]
     wout_rows = row_gradients(att, d_branch, n_dp, n_hid, n_wid)
-    d_att, wout_rows, ff_grads, mlp = together(d_att, wout_rows, ff_grads, mlp)
-    mlp = sum_far(mlp.reshape(n_dp, -1, width), "dp")
+    d_att, wout_rows, ff_grads = together(d_att, wout_rows, ff_grads)
     ff_grads = lax.psum_scatter(ff_grads, "hid", scatter_dimension=0, tiled=False)
     d_att = jnp.concatenate(by_source(d_att, "hid"), axis=0)
-    wout_grad = sum_far(core_sum(*wout_rows)[0], "dp")
+    my = lambda x, r: pick(x, my_dp ^ r)
+    wout_sum = core_sum(*wout_rows)[0]
+    wout_came = sum_far(my(wout_sum, 3), "dp")
 
     crossed = attention_backward_cross(saved, d_att, tok)
-    crossed, wout_grad, mlp = together(crossed, wout_grad, mlp)
-    wout_grad = sum_near(wout_grad, "dp")
-    mlp = sum_near(mlp, "dp")
+    crossed, wout_came, mlp_far = together(crossed, wout_came, end[0])
+    wout_grad = sum_near(my(wout_sum, 1), my(wout_sum, 2), wout_came, "dp")
+    mlp_came = sum_far(mlp_far, "dp")
     dv, *crossed = crossed
-    dq, dk, draw, dlogit = attention_backward_local(saved, crossed, tok)
-    d_logit = dlogit.transpose(0, 2, 1).reshape(-1, own_heads).astype(BF16)
-    d_cat = jnp.concatenate(
-        [dq, dk, dv, draw, jnp.pad(d_logit, ((0, 0), (0, side - own_heads)))], axis=1)
+    d_cat = attention_backward_local(saved, dv, crossed, tok, side)
     d_gain_two = jnp.sum(d_act.astype(F32) * norm_in(middle, 1.0), axis=0, keepdims=True)
-    bias_grad = jnp.sum(d_logit.astype(F32), axis=0)
+    bias_grad = jnp.sum(d_cat[:, 4 * span : 4 * span + own_heads].astype(F32), axis=0)
     once = lax.axis_index("wid") % copies == 0
     d_act_one, *cat_grad = input_gradients(act_one, d_cat, cat, d_gain_two, bias_grad, once, n_dp, n_hid, n_wid)
-    d_act_one, cat_grad, wout_grad, mlp = together(d_act_one, cat_grad, wout_grad, mlp)
+    d_act_one, cat_grad, wout_grad, mlp_came = together(d_act_one, cat_grad, wout_grad, mlp_came)
     d_parts = d_act_one.reshape(n_hid, held, width)
     first_half = exchange_rows(d_parts[:, : held // 2], "hid")
     last_half = exchange_rows(d_parts[:, held // 2 :], "hid")
-    wout_grad = add(*wout_grad)
-    wout_got = exchange([wout_grad[j] for j in range(n_hid)], "hid")
-    layer_out = (middle + add(*mlp).astype(F32)).astype(BF16)
-    cat_grad = sum_far(core_sum(*cat_grad)[0], "dp")
+    wout_grad = add(my(wout_sum, 0), *wout_grad)
+    grad_wout = lax.psum_scatter(wout_grad, "hid", scatter_dimension=0, tiled=False).astype(F32)
+    cat_sum = core_sum(*cat_grad)[0]
+    cat_came = sum_far(my(cat_sum, 3), "dp")
     ff_got = [ff_grads[0]]
     for r in range(1, n_dp):
         ff_got.append(lax.ppermute(ff_grads[r], "dp", pairs(n_dp, r)))
-    cat_grad, wout_got, ff_got, first_half = together(cat_grad, wout_got, ff_got, first_half)
-    cat_grad = sum_near(cat_grad, "dp")
+    cat_came, ff_got, first_half = together(cat_came, ff_got, first_half)
+    cat_grad = sum_near(my(cat_sum, 1), my(cat_sum, 2), cat_came, "dp")
     cat_grad, last_half = together(cat_grad, last_half)
-    cat_grad = add(*cat_grad)
+    cat_grad = add(my(cat_sum, 0), *cat_grad)
+    mlp = sum_near(mid[0][:tokens], mid[0][tokens:], mlp_came, "dp")
     cat_got = exchange([cat_grad[j] for j in range(n_hid)], "hid")
     d_sum = jnp.concatenate([add(*first_half), add(*last_half)], axis=0)
     d_sum = from_row(d_sum, row_count).reshape(row_count * tok, width).astype(F32)
     grad_gate, grad_up, grad_down = laid_ff(ff_got)
     *weight_grads, tails = laid_columns(cat_got, side)
-    grad_wout = sum(x.astype(F32) for x in wout_got)
     grad_beta = tails[:, :, :own_heads].transpose(1, 0, 2).reshape(shard, heads)
     gain_grads = jnp.sum(tails[:, :, own_heads : own_heads + 2], axis=0)
     grad_bias = tails[:, :own_heads, own_heads + 2].reshape(heads)
 
+    layer_out = (middle + add(own[0], *mlp).astype(F32)).astype(BF16)
     _, pull_one = jax.vjp(lambda t: norm_in(t, gain_one), layer_f)
     grad_in = (d_middle + pull_one(d_sum)[0]).astype(BF16)
 

time: 572 us -> 547 us (0.956)
  waiting for transfers between devices: 175 us -> 158 us
  local copies, waits for them, and re-layouts: 55 us -> 42.8 us
  Pallas kernels: 175 us -> 182 us
    ppermute x4, waiting for transfers between devices: 33.1 us -> 6.7 us  [gather_far(): lax.ppermute(two[half:], axis, pairs(4, 1))]
    ppermute x6, waiting for transfers between devices: 22.9 us -> 36.4 us  [exchange_rows(): lax.ppermute(sent[k - 1], axis, [(i, (i + k) % count) for i in range(coun...]
    ppermute x18 -> x15, waiting for transfers between devices: 79.2 us -> 67.9 us  [exchange(): lax.ppermute(sent, axis, [(i, (i + k) % count) for i in range(count)])]
    pallas_call x13 -> x15, Pallas kernels: 175 us -> 182 us  [run(): pl.pallas_call(body, grid=(grid,), in_specs=in_specs, out_specs=out_specs...]
    ppermute x4, waiting for transfers between devices: 1.11 us -> 7.72 us  [sum_far(): lax.ppermute(far[:half], axis, pairs(4, 2))]
    ppermute x4, waiting for transfers between devices: 18.1 us -> 12.3 us  [gather_near(): lax.ppermute(x, axis, pairs(4, 1))]
    unnamed x141 -> x125, local copies, waits for them, and re-layouts: 14.4 us -> 12 us
    ppermute x18 -> x15, starting transfers between devices: 25.7 us -> 24 us  [exchange(): lax.ppermute(sent, axis, [(i, (i + k) % count) for i in range(count)])]
  transfers between devices with their start and end apart: 76 -> 74, of which waited for: 36 -> 29; matrix products, arithmetic and copies ran while one was open for 17% -> 17% of each run, Pallas kernels for 25% -> 32%
where the time goes in v4:
time: 547 us; the launch traced here: 540 us
  Pallas kernels  182 us (33%)
  waiting for transfers between devices  158 us (29%)
  starting transfers between devices  73.1 us (13%)
  other arithmetic  63.2 us (12%)
  local copies, waits for them, and re-layouts  42.8 us (8%)
  between operations  15.3 us (3%)
  matrix products  5.57 us (1%)
    pallas_call x15, Pallas kernels, run(): pl.pallas_call(body, grid=(grid,), in_specs=in_specs, out_specs=out_specs...  182 us
    ppermute x15, waiting for transfers between devices, exchange(): lax.ppermute(sent, axis, [(i, (i + k) % count) for i in range(count)])  67.9 us
    ppermute x6, waiting for transfers between devices, exchange_rows(): lax.ppermute(sent[k - 1], axis, [(i, (i + k) % count) for i in range(coun...  36.4 us
    ppermute x15, starting transfers between devices, exchange(): lax.ppermute(sent, axis, [(i, (i + k) % count) for i in range(count)])  24 us
    convert_element_type x10, other arithmetic, add(): return total.astype(left.dtype)  15.7 us
    ppermute x4, waiting for transfers between devices, gather_near(): lax.ppermute(x, axis, pairs(4, 1))  12.3 us
    unnamed x125, local copies, waits for them, and re-layouts  12 us
  transfers between devices with their start and end apart: 74, of which 29 were waited for; matrix products, arithmetic and copies ran while one was open for 17% of the time, Pallas kernels for 32%

profile of v4, /device:TPU:8, one launch (start us, length us, event | category | flops | bytes accessed | tf_op | source)
XLA Modules:
  0.0 539.7 jit_solution(9739226366477656458)
XLA Ops:
  25.7 12.6 %collective-permute-done.2 = bf16[48,1664]{1,0:T(8,128)(2,1)S(1)} collective-permute-done((bf16[48,1664]{1,0:T(8,128)(2,1)}, bf16[48,1664]{1,0:T(8,128)(2,1)S(1)}, u32[]{:S(2)}, u32[]{:S(2)}) %collective-permute-start.2) | collective-permute-done | bytes 159776 | tf_op jit(solution)/shard_map/ppermute | solution.py:706
  38.2 10.2 %collective-permute-done.3 = bf16[48,1664]{1,0:T(8,128)(2,1)} collective-permute-done((bf16[48,1664]{1,0:T(8,128)(2,1)}, bf16[48,1664]{1,0:T(8,128)(2,1)}, u32[]{:S(2)}, u32[]{:S(2)}) %collective-permute-start.3) | collective-permute-done | bytes 159776 | tf_op jit(solution)/shard_map/ppermute | solution.py:706
  53.2 11.1 %collective-permute-done.7 = bf16[4,48,1664]{2,1,0:T(8,128)(2,1)S(1)} collective-permute-done((bf16[4,48,1664]{2,1,0:T(8,128)(2,1)S(1)}, bf16[4,48,1664]{2,1,0:T(8,128)(2,1)S(1)}, u32[]{:S(2)}, u32[]{:S(2)}) %collective-permute-start.7) | collective-permute-done | bytes 639008 | tf_op jit(solution)/shard_map/ppermute | solution.py:729
  66.8 4.5 collective-permute-done.10
  83.2 5.8 %collective-permute-done.18 = bf16[128,1536]{1,0:T(8,128)(2,1)S(1)} collective-permute-done((bf16[128,1536]{1,0:T(8,128)(2,1)S(1)}, bf16[128,1536]{1,0:T(8,128)(2,1)S(1)}, u32[]{:S(2)}, u32[]{:S(2)}) %collective-permute-start.18) | collective-permute-done | bytes 393248 | tf_op jit(solution)/shard_map/ppermute | solution.py:737
  94.3 2.2 collective-permute-start.16
  96.5 5.5 %shard_map.254 = (bf16[1536,1664]{1,0:T(8,128)(2,1)}, f32[128,1536]{1,0:T(8,128)}) custom-call(s32[3]{0:T(128)} %pad_add_fusion.1.me_ref, bf16[1,4,4,48,1664]{4,3,2,1,0:T(8,128)(2,1)} %bitcast.247, bf16[1,4,4,48,1664]{4,3,2,1,0:T(8,128)(2,1)} %bitcast.33.other_ref), custom_call_target="tpu_custom_call" | custom-call | bytes 11010060 | tf_op jit(solution)/shard_map/pallas_call | solution.py:254
  113.5 12.3 %shard_map.255 = (bf16[1024,1536]{1,0:T(8,128)(2,1)}, bf16[1024,384]{1,0:T(8,128)(2,1)}, bf16[1024,384]{1,0:T(8,128)(2,1)}, bf16[1024,384]{1,0:T(8,128)(2,1)}, f...) custom-call(f32[3]{0:T(128)} %dynamic-slice_convert_fusion.bias_ref, bf16[1024,1536]{1,0:T(8,128)(2,1)} %all-gather.4.cloned.1.call-done.x_ref, ...), custom_call_target="tpu_custom_call" | custom-call | flops 5234491392 | bytes 15353868 | tf_op jit(solution)/shard_map/pallas_call | solution.py:254
  128.4 17.8 %shard_map.256 = (bf16[1024,384]{1,0:T(8,128)(2,1)}, bf16[1024,384]{1,0:T(8,128)(2,1)}, bf16[1024,384]{1,0:T(8,128)(2,1)}, bf16[1024,384]{1,0:T(8,128)(2,1)}, f3...) custom-call(bf16[1024,384]{1,0:T(8,128)(2,1)} %get-tuple-element.241, ...), custom_call_target="tpu_custom_call" | custom-call | flops 6241124352 | bytes 14168064 | tf_op jit(solution)/shard_map/pallas_call | solution.py:254
  146.2 16.9 %shard_map.257 = (bf16[1024,384]{1,0:T(8,128)(2,1)}, bf16[8,3,128,1024]{3,2,1,0:T(8,128)(2,1)}, bf16[8,3,1024,128]{3,2,1,0:T(8,128)(2,1)}) custom-call(bf16[1024,384]{1,0:T(8,128)(2,1)} %get-tuple-element.250.qin_ref, bf16[1024,384]{1,0:T(8,128)(2,1)} %get-tuple-element.251.kout_ref, bf16[1024,384]{1,0:T(8,128)(2,1)} %get-tuple-element.252.ptop_ref, ...), custom_call_target="tpu_custom_call" | custom-call | flops 3221225472 | bytes 18882560 | tf_op jit(solution)/shard_map/pallas_call | solution.py:254
  165.4 3.9 collective-permute-start.25
  171.3 5.0 shard_map.258
  176.3 9.6 %collective-permute-done.24 = bf16[256,384]{1,0:T(8,128)(2,1)S(1)} collective-permute-done((bf16[256,384]{1,0:T(8,128)(2,1)S(1)}, bf16[256,384]{1,0:T(8,128)(2,1)S(1)}, u32[]{:S(2)}, u32[]{:S(2)}) %collective-permute-start.24) | collective-permute-done | bytes 196640 | tf_op jit(solution)/shard_map/ppermute | solution.py:706
  186.0 17.9 %collective-permute-done.25 = bf16[256,384]{1,0:T(8,128)(2,1)S(1)} collective-permute-done((bf16[256,384]{1,0:T(8,128)(2,1)S(1)}, bf16[256,384]{1,0:T(8,128)(2,1)S(1)}, u32[]{:S(2)}, u32[]{:S(2)}) %collective-permute-start.25) | collective-permute-done | bytes 196640 | tf_op jit(solution)/shard_map/ppermute | solution.py:706
  203.8 3.1 collective-permute-done.26
  211.4 3.4 all-gather.6.cloned.1.call-done
  218.6 4.5 collective-permute-done.29
  223.1 10.6 %shard_map.259 = (bf16[256,1536]{1,0:T(8,128)(2,1)}, bf16[256,1536]{1,0:T(8,128)(2,1)}, bf16[256,1024]{1,0:T(8,128)(2,1)}, bf16[256,1024]{1,0:T(8,128)(2,1)}, bf16[256,1024]{1,0:T(8,128)(2,1)}) custom-call(s32[2]{0:T(128)} %pad_add_fusion.3.me_ref, bf16[256,1536]{1,0:T(8,128)(2,1)} %copy-done.32, bf16[256,1536]{1,0:T(8,128)(2,1)} %bitcast.252, ...), custom_call_target="tpu_custom_call" | custom-call | flops 4831838208 | bytes 14155784 | tf_op jit(solution)/shard_map/pallas_call | solution.py:254
  239.7 18.0 %shard_map.260 = (bf16[512,1536]{1,0:T(8,128)(2,1)}, bf16[512,1536]{1,0:T(8,128)(2,1)}, bf16[512,1024]{1,0:T(8,128)(2,1)}, bf16[512,1024]{1,0:T(8,128)(2,1)}, bf16[512,1024]{1,0:T(8,128)(2,1)}) custom-call(s32[2]{0:T(128)} %pad_add_fusion.3.me_ref, bf16[512,1536]{1,0:T(8,128)(2,1)} %copy-done.37, bf16[512,1536]{1,0:T(8,128)(2,1)} %pad_maximum_fusion.grad_ref.refs_6_, ...), custom_call_target="tpu_custom_call" | custom-call | flops 9663676416 | bytes 18874376 | tf_op jit(solution)/shard_map/pallas_call | solution.py:254
  258.6 10.5 %shard_map.261 = (bf16[256,1536]{1,0:T(8,128)(2,1)}, bf16[256,1536]{1,0:T(8,128)(2,1)}, bf16[256,1024]{1,0:T(8,128)(2,1)}, bf16[256,1024]{1,0:T(8,128)(2,1)}, bf16[256,1024]{1,0:T(8,128)(2,1)}) custom-call(s32[2]{0:T(128)} %pad_add_fusion.3.me_ref, bf16[256,1536]{1,0:T(8,128)(2,1)} %copy-done.42, bf16[256,1536]{1,0:T(8,128)(2,1)} %pad_maximum_fusion.3.grad_ref.refs_11_, ...), custom_call_target="tpu_custom_call" | custom-call | flops 4831838208 | bytes 14155784 | tf_op jit(solution)/shard_map/pallas_call | solution.py:254
  272.7 7.7 %collective-permute-done.34 = bf16[128,1536]{1,0:T(8,128)(2,1)S(1)} collective-permute-done((bf16[128,1536]{1,0:T(8,128)(2,1)S(1)}, bf16[128,1536]{1,0:T(8,128)(2,1)S(1)}, u32[]{:S(2)}, u32[]{:S(2)}) %collective-permute-start.34) | collective-permute-done | bytes 393248 | tf_op jit(solution)/shard_map/ppermute | solution.py:761
  283.9 16.0 %shard_map.262 = (bf16[4,1,4,3,192,256]{5,4,3,2,1,0:T(8,128)(2,1)}, bf16[4,1,4,3,192,256]{5,4,3,2,1,0:T(8,128)(2,1)}) custom-call(s32[2]{0:T(128)} %pad_add_fusion.3.me_ref, bf16[256,1536]{1,0:T(8,128)(2,1)} %copy-done.32, bf16[256,1536]{1,0:T(8,128)(2,1)} %bitcast.253, bf16[256,1024]{1,0:T(8,128)(2,1)} %get-tuple-element.321.refs_2_, ...), custom_call_target="tpu_custom_call" | custom-call | flops 9663676416 | bytes 22020104 | tf_op jit(solution)/shard_map/pallas_call | solution.py:254
  301.9 4.1 convolution_convert_fusion
  309.4 2.3 collective-permute-start.39
  311.7 4.5 collective-permute-start.40
  316.9 5.3 shard_map.263
  322.2 6.5 %fusion.1 = bf16[4,4,3,192,256]{4,3,2,1,0:T(8,128)(2,1)} fusion(bf16[1,4,4,3,192,256]{5,4,3,2,1,0:T(8,128)(2,1)} %collective-permute-done.42, bf16[4,1,4,3,192,256]{5,4,3,2,1,0:T(8,128)(2,1)S(1)} %bitcast.251), kind=kLoop, calls=%fused_computation.3 | loop fusion | flops 9437184 | bytes 14155776 | tf_op jit(solution)/shard_map/squeeze | solution.py:888
  329.2 4.0 collective-permute-done.41
  338.2 2.4 add_convert_fusion.1
  342.8 20.8 %shard_map.264 = (f32[1024,384]{1,0:T(8,128)}, bf16[1024,384]{1,0:T(8,128)(2,1)}, f32[1024,384]{1,0:T(8,128)}, f32[1024,384]{1,0:T(8,128)}, bf16[1024,384]{1,0:T(8,128)(2,1)}) custom-call(bf16[1024,384]{1,0:T(8,128)(2,1)} %pad_maximum_fusion.9.grad_ref, bf16[1024,384]{1,0:T(8,128)(2,1)} %get-tuple-element.255.v_ref, ...), custom_call_target="tpu_custom_call" | custom-call | flops 5637144576 | bytes 22806528 | tf_op jit(solution)/shard_map/pallas_call | solution.py:254
  370.4 18.8 %shard_map.265.right_ref = bf16[1024,1664]{1,0:T(8,128)(2,1)} custom-call(bf16[1024,384]{1,0:T(8,128)(2,1)} %get-tuple-element.241.q_ref, bf16[1024,384]{1,0:T(8,128)(2,1)} %get-tuple-element.242.k_ref, f32[1024,384]{1,0:T(8,128)} %get-tuple-element.248.raw_ref, f32[8,3,128]{2,1,0:T(4,128)} %get-tuple-element.249.logit_ref, ...), custom_call_target="tpu_custom_call" | custom-call | flops 6039797760 | bytes 19148800 | tf_op jit(solution)/shard_map/pallas_call | solution.py:254
  390.9 19.0 %shard_map.266 = (bf16[1024,1536]{1,0:T(8,128)(2,1)}, bf16[1,4,4,48,1664]{4,3,2,1,0:T(8,128)(2,1)}, bf16[1,4,4,48,1664]{4,3,2,1,0:T(8,128)(2,1)}) custom-call(s32[3]{0:T(128)} %pad_add_fusion.4.me_ref, f32[3]{0:T(128)} %convert_reduce_fusion.bias_ref, bf16[1024,1536]{1,0:T(8,128)(2,1)} %get-tuple-element.359.left_ref, ...), custom_call_target="tpu_custom_call" | custom-call | flops 10468982784 | bytes 19929112 | tf_op jit(solution)/shard_map/pallas_call | solution.py:254
  411.1 3.2 fusion.34
  415.5 2.3 collective-permute-start.60
  417.8 2.3 fusion.13
  420.1 2.7 dynamic-slice_bitcast_fusion.1
  422.8 2.2 add_convert_fusion.7
  425.0 2.4 add_convert_fusion
  435.0 24.8 %collective-permute-done.59 = bf16[128,1536]{1,0:T(8,128)(2,1)} collective-permute-done((bf16[128,1536]{1,0:T(8,128)(2,1)}, bf16[128,1536]{1,0:T(8,128)(2,1)}, u32[]{:S(2)}, u32[]{:S(2)}) %collective-permute-start.59) | collective-permute-done | bytes 393248 | tf_op jit(solution)/shard_map/ppermute | solution.py:713
  464.6 3.0 collective-permute-start.64
  469.6 5.3 collective-permute-done.56.refs_2_
  482.0 3.0 shard_map.268
  485.0 2.4 copy.102
  489.9 8.8 %collective-permute-done.64 = bf16[128,1536]{1,0:T(8,128)(2,1)} collective-permute-done((bf16[128,1536]{1,0:T(8,128)(2,1)}, bf16[128,1536]{1,0:T(8,128)(2,1)}, u32[]{:S(2)}, u32[]{:S(2)}) %collective-permute-start.64) | collective-permute-done | bytes 393248 | tf_op jit(solution)/shard_map/ppermute | solution.py:713
  498.9 2.8 collective-permute-done.65
  511.2 7.1 %collective-permute-done.68.refs_2_ = bf16[48,1664]{1,0:T(8,128)(2,1)S(1)} collective-permute-done((bf16[48,1664]{1,0:T(8,128)(2,1)S(1)}, bf16[48,1664]{1,0:T(8,128)(2,1)S(1)}, u32[]{:S(2)}, u32[]{:S(2)}) %collective-permute-start.68) | collective-permute-done | bytes 159776 | tf_op jit(solution)/shard_map/ppermute | solution.py:706
  519.1 2.3 shard_map.267
  529.1 3.8 fusion.8
  (384 shorter events, 149.2 us)
Async XLA Ops:
  7.2 100.0 %all-gather.4.cloned.1.call-start = ((), (), s32[]{:S(2)}) async-start(), calls=%async_computation.2 | async-start | bytes 3932160 | tf_op jit(solution)/shard_map/all_gather | solution.py:803
  14.0 34.6 %collective-permute-start.5 = (bf16[256,1536]{1,0:T(8,128)(2,1)S(1)}, bf16[256,1536]{1,0:T(8,128)(2,1)S(1)}, u32[]{:S(2)}, u32[]{:S(2)}) collective-permute-start(bf16[256,1536]{1,0:T(8,128)(2,1)S(1)} %bitcast.254), channel_id=1, source_target_pairs={{0,8},{8,0},{16,24},{24,16},{1,9},{9,1},{17,25},{25,17},{2,10},{10... | collective-permute-start | bytes 2359304 | tf_op jit(solution)/shard_map/ppermute | solution.py:729
  15.4 33.1 %collective-permute-start.6 = (bf16[256,1536]{1,0:T(8,128)(2,1)S(1)}, bf16[256,1536]{1,0:T(8,128)(2,1)S(1)}, u32[]{:S(2)}, u32[]{:S(2)}) collective-permute-start(bf16[256,1536]{1,0:T(8,128)(2,1)S(1)} %bitcast.255), channel_id=1, source_target_pairs={{0,16},{8,24},{16,0},{24,8},{1,17},{9,25},{17,1},{25,9},{2,18},{10... | collective-permute-start | bytes 2359304 | tf_op jit(solution)/shard_map/ppermute | solution.py:729
  19.7 18.6 %collective-permute-start.2 = (bf16[48,1664]{1,0:T(8,128)(2,1)}, bf16[48,1664]{1,0:T(8,128)(2,1)S(1)}, u32[]{:S(2)}, u32[]{:S(2)}) collective-permute-start(bf16[48,1664]{1,0:T(8,128)(2,1)} %get-tuple-element.550), channel_id=1, source_target_pairs={{0,2},{2,4},{4,6},{6,0},{1,3},{3,5},{5,7},{7,1},{8,10},{10,12},{12... | collective-permute-start | bytes 479240 | tf_op jit(solution)/shard_map/ppermute | solution.py:706
  21.2 27.2 %collective-permute-start.3 = (bf16[48,1664]{1,0:T(8,128)(2,1)}, bf16[48,1664]{1,0:T(8,128)(2,1)}, u32[]{:S(2)}, u32[]{:S(2)}) collective-permute-start(bf16[48,1664]{1,0:T(8,128)(2,1)} %get-tuple-element.549), channel_id=1, source_target_pairs={{0,4},{2,6},{4,0},{6,2},{1,5},{3,7},{5,1},{7,3},{8,12},{10,14},{12... | collective-permute-start | bytes 479240 | tf_op jit(solution)/shard_map/ppermute | solution.py:706
  22.5 26.1 %collective-permute-start.4 = (bf16[48,1664]{1,0:T(8,128)(2,1)}, bf16[48,1664]{1,0:T(8,128)(2,1)}, u32[]{:S(2)}, u32[]{:S(2)}) collective-permute-start(bf16[48,1664]{1,0:T(8,128)(2,1)} %get-tuple-element.548), channel_id=1, source_target_pairs={{0,6},{2,0},{4,2},{6,4},{1,7},{3,1},{5,3},{7,5},{8,14},{10,8},{12,... | collective-permute-start | bytes 479240 | tf_op jit(solution)/shard_map/ppermute | solution.py:706
  24.3 190.5 %all-gather.6.cloned.1.call-start = ((), (), s32[]{:S(2)}) async-start(), calls=%async_computation.5 | async-start | bytes 5898240 | tf_op jit(solution)/shard_map/all_gather | solution.py:838
  73.2 21.0 %collective-permute-start.11 = (bf16[4,4,48,1664]{3,2,1,0:T(8,128)(2,1)S(1)}, bf16[4,4,48,1664]{3,2,1,0:T(8,128)(2,1)}, u32[]{:S(2)}, u32[]{:S(2)}) collective-permute-start(bf16[4,4,48,1664]{3,2,1,0:T(8,128)(2,1)S(1)} %fusion.14), channel_id=1, source_target_pairs={{0,1},{1,0},{2,3},{3,2},{4,5},{5,4},{6,7},{7,6},{8,9},{9,8},{10,11... | collective-permute-start | bytes 7667720 | tf_op jit(solution)/shard_map/ppermute | solution.py:774
  74.9 27.0 %collective-permute-start.15 = (bf16[48,1536]{1,0:T(8,128)(2,1)}, bf16[48,1536]{1,0:T(8,128)(2,1)}, u32[]{:S(2)}, u32[]{:S(2)}) collective-permute-start(bf16[48,1536]{1,0:T(8,128)(2,1)} %param.25), channel_id=1, source_target_pairs={{0,2},{2,4},{4,6},{6,0},{1,3},{3,5},{5,7},{7,1},{8,10},{10,12},{12... | collective-permute-start | bytes 442376 | tf_op jit(solution)/shard_map/ppermute | solution.py:706
  81.9 25.2 %collective-permute-start.12 = (bf16[3,192,256]{2,1,0:T(8,128)(2,1)S(1)}, bf16[3,192,256]{2,1,0:T(8,128)(2,1)S(1)}, u32[]{:S(2)}, u32[]{:S(2)}) collective-permute-start(bf16[3,192,256]{2,1,0:T(8,128)(2,1)S(1)} %get-tuple-element.519), channel_id=1, source_target_pairs={{0,8},{8,0},{16,24},{24,16},{1,9},{9,1},{17,25},{25,17},{2,10},{10... | collective-permute-start | bytes 884744 | tf_op jit(solution)/shard_map/ppermute | solution.py:832
  89.0 18.1 %collective-permute-start.13 = (bf16[3,192,256]{2,1,0:T(8,128)(2,1)S(1)}, bf16[3,192,256]{2,1,0:T(8,128)(2,1)S(1)}, u32[]{:S(2)}, u32[]{:S(2)}) collective-permute-start(bf16[3,192,256]{2,1,0:T(8,128)(2,1)S(1)} %get-tuple-element.518), channel_id=1, source_target_pairs={{0,16},{8,24},{16,0},{24,8},{1,17},{9,25},{17,1},{25,9},{2,18},{10... | collective-permute-start | bytes 884744 | tf_op jit(solution)/shard_map/ppermute | solution.py:832
  108.2 17.6 %collective-permute-start.20 = (bf16[4,48,1536]{2,1,0:T(8,128)(2,1)S(1)}, bf16[4,48,1536]{2,1,0:T(8,128)(2,1)S(1)}, u32[]{:S(2)}, u32[]{:S(2)}) collective-permute-start(bf16[4,48,1536]{2,1,0:T(8,128)(2,1)S(1)} %pad_maximum_fusion.16), channel_id=1, source_target_pairs={{0,8},{8,0},{16,24},{24,16},{1,9},{9,1},{17,25},{25,17},{2,10},{10... | collective-permute-start | bytes 1769480 | tf_op jit(solution)/shard_map/ppermute | solution.py:729
  112.0 320.0 %reduce-scatter.3.cloned.1.call-start = ((), (), s32[]{:S(2)}) async-start(), calls=%async_computation.3 | async-start | bytes 5898240 | tf_op jit(solution)/shard_map/reduce_scatter | solution.py:891
  125.8 37.2 %collective-permute-start.22 = (bf16[2,48,1536]{2,1,0:T(8,128)(2,1)S(1)}, bf16[2,48,1536]{2,1,0:T(8,128)(2,1)S(1)}, u32[]{:S(2)}, u32[]{:S(2)}) collective-permute-start(bf16[2,48,1536]{2,1,0:T(8,128)(2,1)S(1)} %slice.379), channel_id=1, source_target_pairs={{0,16},{8,24},{16,0},{24,8},{1,17},{9,25},{17,1},{25,9},{2,18},{10... | collective-permute-start | bytes 884744 | tf_op jit(solution)/shard_map/ppermute | solution.py:737
  127.7 35.4 %collective-permute-start.23 = (bf16[2,48,1536]{2,1,0:T(8,128)(2,1)S(1)}, bf16[2,48,1536]{2,1,0:T(8,128)(2,1)S(1)}, u32[]{:S(2)}, u32[]{:S(2)}) collective-permute-start(bf16[2,48,1536]{2,1,0:T(8,128)(2,1)S(1)} %slice.380), channel_id=1, source_target_pairs={{0,8},{8,0},{16,24},{24,16},{1,9},{9,1},{17,25},{25,17},{2,10},{10... | collective-permute-start | bytes 884744 | tf_op jit(solution)/shard_map/ppermute | solution.py:737
  164.7 21.3 %collective-permute-start.24 = (bf16[256,384]{1,0:T(8,128)(2,1)S(1)}, bf16[256,384]{1,0:T(8,128)(2,1)S(1)}, u32[]{:S(2)}, u32[]{:S(2)}) collective-permute-start(bf16[256,384]{1,0:T(8,128)(2,1)S(1)} %get-tuple-element.543), channel_id=1, source_target_pairs={{0,2},{2,4},{4,6},{6,0},{1,3},{3,5},{5,7},{7,1},{8,10},{10,12},{12... | collective-permute-start | bytes 589832 | tf_op jit(solution)/shard_map/ppermute | solution.py:706
  165.4 38.4 %collective-permute-start.25 = (bf16[256,384]{1,0:T(8,128)(2,1)S(1)}, bf16[256,384]{1,0:T(8,128)(2,1)S(1)}, u32[]{:S(2)}, u32[]{:S(2)}) collective-permute-start(bf16[256,384]{1,0:T(8,128)(2,1)S(1)} %get-tuple-element.542), channel_id=1, source_target_pairs={{0,4},{2,6},{4,0},{6,2},{1,5},{3,7},{5,1},{7,3},{8,12},{10,14},{12... | collective-permute-start | bytes 589832 | tf_op jit(solution)/shard_map/ppermute | solution.py:706
  169.3 37.6 %collective-permute-start.26 = (bf16[256,384]{1,0:T(8,128)(2,1)S(1)}, bf16[256,384]{1,0:T(8,128)(2,1)S(1)}, u32[]{:S(2)}, u32[]{:S(2)}) collective-permute-start(bf16[256,384]{1,0:T(8,128)(2,1)S(1)} %get-tuple-element.540), channel_id=1, source_target_pairs={{0,6},{2,0},{4,2},{6,4},{1,7},{3,1},{5,3},{7,5},{8,14},{10,8},{12,... | collective-permute-start | bytes 589832 | tf_op jit(solution)/shard_map/ppermute | solution.py:706
  214.9 19.9 %collective-permute-start.30 = (bf16[256,1536]{1,0:T(8,128)(2,1)S(1)}, bf16[256,1536]{1,0:T(8,128)(2,1)S(1)}, u32[]{:S(2)}, u32[]{:S(2)}) collective-permute-start(bf16[256,1536]{1,0:T(8,128)(2,1)S(1)} %multiply_convert_fusion.act_ref.refs_0_), channel_id=1, source_target_pairs={{0,8},{8,0},{16,24},{24,16},{1,9},{9,1},{17,25},{25,17},{2,10},{10... | collective-permute-start | bytes 2359304 | tf_op jit(solution)/shard_map/ppermute | solution.py:729
  216.6 19.6 %collective-permute-start.31 = (bf16[256,1536]{1,0:T(8,128)(2,1)S(1)}, bf16[256,1536]{1,0:T(8,128)(2,1)S(1)}, u32[]{:S(2)}, u32[]{:S(2)}) collective-permute-start(bf16[256,1536]{1,0:T(8,128)(2,1)S(1)} %multiply_convert_fusion.act_ref.refs_0_), channel_id=1, source_target_pairs={{0,16},{8,24},{16,0},{24,8},{1,17},{9,25},{17,1},{25,9},{2,18},{10... | collective-permute-start | bytes 2359304 | tf_op jit(solution)/shard_map/ppermute | solution.py:729
  236.3 21.4 %collective-permute-start.32 = (bf16[128,1536]{1,0:T(8,128)(2,1)S(1)}, bf16[128,1536]{1,0:T(8,128)(2,1)S(1)}, u32[]{:S(2)}, u32[]{:S(2)}) collective-permute-start(bf16[128,1536]{1,0:T(8,128)(2,1)S(1)} %slice.386), channel_id=1, source_target_pairs={{0,16},{8,24},{16,0},{24,8},{1,17},{9,25},{17,1},{25,9},{2,18},{10... | collective-permute-start | bytes 1179656 | tf_op jit(solution)/shard_map/ppermute | solution.py:737
  237.8 19.9 %collective-permute-start.33 = (bf16[128,1536]{1,0:T(8,128)(2,1)S(1)}, bf16[128,1536]{1,0:T(8,128)(2,1)S(1)}, u32[]{:S(2)}, u32[]{:S(2)}) collective-permute-start(bf16[128,1536]{1,0:T(8,128)(2,1)S(1)} %slice.387), channel_id=1, source_target_pairs={{0,8},{8,0},{16,24},{24,16},{1,9},{9,1},{17,25},{25,17},{2,10},{10... | collective-permute-start | bytes 1179656 | tf_op jit(solution)/shard_map/ppermute | solution.py:737
  281.0 18.9 %collective-permute-start.36 = (bf16[256,1536]{1,0:T(8,128)(2,1)S(1)}, bf16[256,1536]{1,0:T(8,128)(2,1)S(1)}, u32[]{:S(2)}, u32[]{:S(2)}) collective-permute-start(bf16[256,1536]{1,0:T(8,128)(2,1)S(1)} %pad_maximum_fusion.6), channel_id=1, source_target_pairs={{0,8},{8,0},{16,24},{24,16},{1,9},{9,1},{17,25},{25,17},{2,10},{10... | collective-permute-start | bytes 2359304 | tf_op jit(solution)/shard_map/ppermute | solution.py:769
  282.5 17.4 %collective-permute-start.37 = (bf16[256,1536]{1,0:T(8,128)(2,1)S(1)}, bf16[256,1536]{1,0:T(8,128)(2,1)S(1)}, u32[]{:S(2)}, u32[]{:S(2)}) collective-permute-start(bf16[256,1536]{1,0:T(8,128)(2,1)S(1)} %pad_maximum_fusion.7), channel_id=1, source_target_pairs={{0,16},{8,24},{16,0},{24,8},{1,17},{9,25},{17,1},{25,9},{2,18},{10... | collective-permute-start | bytes 2359304 | tf_op jit(solution)/shard_map/ppermute | solution.py:769
  299.9 22.3 %collective-permute-start.42 = (bf16[1,4,4,3,192,256]{5,4,3,2,1,0:T(8,128)(2,1)}, bf16[1,4,4,3,192,256]{5,4,3,2,1,0:T(8,128)(2,1)}, u32[]{:S(2)}, u32[]{:S(2)}) collective-permute-start(bf16[1,4,4,3,192,256]{5,4,3,2,1,0:T(8,128)(2,1)} %bitcast.285), channel_id=1, source_target_pairs={{0,1},{1,0},{2,3},{3,2},{4,5},{5,4},{6,7},{7,6},{8,9},{9,8},{10,11... | collective-permute-start | bytes 14155784 | tf_op jit(solution)/shard_map/ppermute | solution.py:779
  309.4 19.3 %collective-permute-start.39 = (bf16[256,384]{1,0:T(8,128)(2,1)}, bf16[256,384]{1,0:T(8,128)(2,1)S(1)}, u32[]{:S(2)}, u32[]{:S(2)}) collective-permute-start(bf16[256,384]{1,0:T(8,128)(2,1)} %get-tuple-element.532), channel_id=1, source_target_pairs={{0,2},{2,4},{4,6},{6,0},{1,3},{3,5},{5,7},{7,1},{8,10},{10,12},{12... | collective-permute-start | bytes 589832 | tf_op jit(solution)/shard_map/ppermute | solution.py:706
  311.7 17.5 %collective-permute-start.40 = (bf16[256,384]{1,0:T(8,128)(2,1)}, bf16[256,384]{1,0:T(8,128)(2,1)}, u32[]{:S(2)}, u32[]{:S(2)}) collective-permute-start(bf16[256,384]{1,0:T(8,128)(2,1)} %get-tuple-element.531), channel_id=1, source_target_pairs={{0,4},{2,6},{4,0},{6,2},{1,5},{3,7},{5,1},{7,3},{8,12},{10,14},{12... | collective-permute-start | bytes 589832 | tf_op jit(solution)/shard_map/ppermute | solution.py:706
  316.9 16.3 %collective-permute-start.41 = (bf16[256,384]{1,0:T(8,128)(2,1)}, bf16[256,384]{1,0:T(8,128)(2,1)}, u32[]{:S(2)}, u32[]{:S(2)}) collective-permute-start(bf16[256,384]{1,0:T(8,128)(2,1)} %get-tuple-element.529), channel_id=1, source_target_pairs={{0,6},{2,0},{4,2},{6,4},{1,7},{3,1},{5,3},{7,5},{8,14},{10,8},{12,... | collective-permute-start | bytes 589832 | tf_op jit(solution)/shard_map/ppermute | solution.py:706
  333.2 147.2 %reduce-scatter.5.cloned.1.call-start = ((), (), s32[]{:S(2)}) async-start(), calls=%async_computation.4 | async-start | bytes 737280 | tf_op jit(solution)/shard_map/reduce_scatter | solution.py:912
  340.7 22.9 %collective-permute-start.44 = (bf16[2,48,1536]{2,1,0:T(8,128)(2,1)S(1)}, bf16[2,48,1536]{2,1,0:T(8,128)(2,1)S(1)}, u32[]{:S(2)}, u32[]{:S(2)}) collective-permute-start(bf16[2,48,1536]{2,1,0:T(8,128)(2,1)S(1)} %get-tuple-element.484), channel_id=1, source_target_pairs={{0,16},{8,24},{16,0},{24,8},{1,17},{9,25},{17,1},{25,9},{2,18},{10... | collective-permute-start | bytes 884744 | tf_op jit(solution)/shard_map/ppermute | solution.py:761
  341.8 21.9 %collective-permute-start.45 = (bf16[2,48,1536]{2,1,0:T(8,128)(2,1)S(1)}, bf16[2,48,1536]{2,1,0:T(8,128)(2,1)S(1)}, u32[]{:S(2)}, u32[]{:S(2)}) collective-permute-start(bf16[2,48,1536]{2,1,0:T(8,128)(2,1)S(1)} %get-tuple-element.486), channel_id=1, source_target_pairs={{0,8},{8,0},{16,24},{24,16},{1,9},{9,1},{17,25},{25,17},{2,10},{10... | collective-permute-start | bytes 884744 | tf_op jit(solution)/shard_map/ppermute | solution.py:761
  365.6 44.4 %collective-permute-start.46 = (bf16[4,48,1536]{2,1,0:T(8,128)(2,1)}, bf16[4,48,1536]{2,1,0:T(8,128)(2,1)}, u32[]{:S(2)}, u32[]{:S(2)}) collective-permute-start(bf16[4,48,1536]{2,1,0:T(8,128)(2,1)} %pad_maximum_fusion.17), channel_id=1, source_target_pairs={{0,8},{8,0},{16,24},{24,16},{1,9},{9,1},{17,25},{25,17},{2,10},{10... | collective-permute-start | bytes 1769480 | tf_op jit(solution)/shard_map/ppermute | solution.py:769
  366.6 43.4 %collective-permute-start.47 = (bf16[4,48,1536]{2,1,0:T(8,128)(2,1)}, bf16[4,48,1536]{2,1,0:T(8,128)(2,1)}, u32[]{:S(2)}, u32[]{:S(2)}) collective-permute-start(bf16[4,48,1536]{2,1,0:T(8,128)(2,1)} %pad_maximum_fusion.18), channel_id=1, source_target_pairs={{0,16},{8,24},{16,0},{24,8},{1,17},{9,25},{17,1},{25,9},{2,18},{10... | collective-permute-start | bytes 1769480 | tf_op jit(solution)/shard_map/ppermute | solution.py:769
  368.4 41.5 %collective-permute-start.48 = (bf16[128,1536]{1,0:T(8,128)(2,1)}, bf16[128,1536]{1,0:T(8,128)(2,1)S(1)}, u32[]{:S(2)}, u32[]{:S(2)}) collective-permute-start(bf16[128,1536]{1,0:T(8,128)(2,1)} %get-tuple-element.524), channel_id=1, source_target_pairs={{0,16},{8,24},{16,0},{24,8},{1,17},{9,25},{17,1},{25,9},{2,18},{10... | collective-permute-start | bytes 1179656 | tf_op jit(solution)/shard_map/ppermute | solution.py:761
  369.4 40.5 %collective-permute-start.49 = (bf16[128,1536]{1,0:T(8,128)(2,1)S(1)}, bf16[128,1536]{1,0:T(8,128)(2,1)S(1)}, u32[]{:S(2)}, u32[]{:S(2)}) collective-permute-start(bf16[128,1536]{1,0:T(8,128)(2,1)S(1)} %get-tuple-element.523), channel_id=1, source_target_pairs={{0,8},{8,0},{16,24},{24,16},{1,9},{9,1},{17,25},{25,17},{2,10},{10... | collective-permute-start | bytes 1179656 | tf_op jit(solution)/shard_map/ppermute | solution.py:761
  415.5 18.7 %collective-permute-start.58 = (bf16[128,1536]{1,0:T(8,128)(2,1)}, bf16[128,1536]{1,0:T(8,128)(2,1)}, u32[]{:S(2)}, u32[]{:S(2)}) collective-permute-start(bf16[128,1536]{1,0:T(8,128)(2,1)} %get-tuple-element.376), channel_id=1, source_target_pairs={{0,2},{2,4},{4,6},{6,0},{1,3},{3,5},{5,7},{7,1},{8,10},{10,12},{12... | collective-permute-start | bytes 1179656 | tf_op jit(solution)/shard_map/ppermute | solution.py:713
  415.5 44.3 %collective-permute-start.59 = (bf16[128,1536]{1,0:T(8,128)(2,1)}, bf16[128,1536]{1,0:T(8,128)(2,1)}, u32[]{:S(2)}, u32[]{:S(2)}) collective-permute-start(bf16[128,1536]{1,0:T(8,128)(2,1)} %get-tuple-element.377), channel_id=1, source_target_pairs={{0,4},{2,6},{4,0},{6,2},{1,5},{3,7},{5,1},{7,3},{8,12},{10,14},{12... | collective-permute-start | bytes 1179656 | tf_op jit(solution)/shard_map/ppermute | solution.py:713
  415.5 45.2 %collective-permute-start.60 = (bf16[128,1536]{1,0:T(8,128)(2,1)}, bf16[128,1536]{1,0:T(8,128)(2,1)}, u32[]{:S(2)}, u32[]{:S(2)}) collective-permute-start(bf16[128,1536]{1,0:T(8,128)(2,1)} %get-tuple-element.378), channel_id=1, source_target_pairs={{0,6},{2,0},{4,2},{6,4},{1,7},{3,1},{5,3},{7,5},{8,14},{10,8},{12,... | collective-permute-start | bytes 1179656 | tf_op jit(solution)/shard_map/ppermute | solution.py:713
  430.0 34.6 %collective-permute-start.53 = (bf16[2,48,1664]{2,1,0:T(8,128)(2,1)}, bf16[2,48,1664]{2,1,0:T(8,128)(2,1)}, u32[]{:S(2)}, u32[]{:S(2)}) collective-permute-start(bf16[2,48,1664]{2,1,0:T(8,128)(2,1)} %get-tuple-element.478), channel_id=1, source_target_pairs={{0,16},{8,24},{16,0},{24,8},{1,17},{9,25},{17,1},{25,9},{2,18},{10... | collective-permute-start | bytes 958472 | tf_op jit(solution)/shard_map/ppermute | solution.py:761
  430.9 33.7 %collective-permute-start.54 = (bf16[2,48,1664]{2,1,0:T(8,128)(2,1)}, bf16[2,48,1664]{2,1,0:T(8,128)(2,1)}, u32[]{:S(2)}, u32[]{:S(2)}) collective-permute-start(bf16[2,48,1664]{2,1,0:T(8,128)(2,1)} %get-tuple-element.480), channel_id=1, source_target_pairs={{0,8},{8,0},{16,24},{24,16},{1,9},{9,1},{17,25},{25,17},{2,10},{10... | collective-permute-start | bytes 958472 | tf_op jit(solution)/shard_map/ppermute | solution.py:761
  434.2 33.4 %collective-permute-start.55 = (bf16[3,192,256]{2,1,0:T(8,128)(2,1)S(1)}, bf16[3,192,256]{2,1,0:T(8,128)(2,1)S(1)}, u32[]{:S(2)}, u32[]{:S(2)}) collective-permute-start(bf16[3,192,256]{2,1,0:T(8,128)(2,1)S(1)} %get-tuple-element.511), channel_id=1, source_target_pairs={{0,8},{8,0},{16,24},{24,16},{1,9},{9,1},{17,25},{25,17},{2,10},{10... | collective-permute-start | bytes 884744 | tf_op jit(solution)/shard_map/ppermute | solution.py:917
  464.6 24.3 %collective-permute-start.63 = (bf16[128,1536]{1,0:T(8,128)(2,1)}, bf16[128,1536]{1,0:T(8,128)(2,1)}, u32[]{:S(2)}, u32[]{:S(2)}) collective-permute-start(bf16[128,1536]{1,0:T(8,128)(2,1)} %get-tuple-element.387), channel_id=1, source_target_pairs={{0,2},{2,4},{4,6},{6,0},{1,3},{3,5},{5,7},{7,1},{8,10},{10,12},{12... | collective-permute-start | bytes 1179656 | tf_op jit(solution)/shard_map/ppermute | solution.py:713
  464.6 34.2 %collective-permute-start.64 = (bf16[128,1536]{1,0:T(8,128)(2,1)}, bf16[128,1536]{1,0:T(8,128)(2,1)}, u32[]{:S(2)}, u32[]{:S(2)}) collective-permute-start(bf16[128,1536]{1,0:T(8,128)(2,1)} %get-tuple-element.388), channel_id=1, source_target_pairs={{0,4},{2,6},{4,0},{6,2},{1,5},{3,7},{5,1},{7,3},{8,12},{10,14},{12... | collective-permute-start | bytes 1179656 | tf_op jit(solution)/shard_map/ppermute | solution.py:713
  467.6 34.1 %collective-permute-start.65 = (bf16[128,1536]{1,0:T(8,128)(2,1)}, bf16[128,1536]{1,0:T(8,128)(2,1)}, u32[]{:S(2)}, u32[]{:S(2)}) collective-permute-start(bf16[128,1536]{1,0:T(8,128)(2,1)} %get-tuple-element.389), channel_id=1, source_target_pairs={{0,6},{2,0},{4,2},{6,4},{1,7},{3,1},{5,3},{7,5},{8,14},{10,8},{12,... | collective-permute-start | bytes 1179656 | tf_op jit(solution)/shard_map/ppermute | solution.py:713
  478.4 23.3 %collective-permute-start.61 = (bf16[4,48,1664]{2,1,0:T(8,128)(2,1)}, bf16[4,48,1664]{2,1,0:T(8,128)(2,1)}, u32[]{:S(2)}, u32[]{:S(2)}) collective-permute-start(bf16[4,48,1664]{2,1,0:T(8,128)(2,1)} %pad_maximum_fusion.14), channel_id=1, source_target_pairs={{0,8},{8,0},{16,24},{24,16},{1,9},{9,1},{17,25},{25,17},{2,10},{10... | collective-permute-start | bytes 1916936 | tf_op jit(solution)/shard_map/ppermute | solution.py:769
  479.4 22.3 %collective-permute-start.62 = (bf16[4,48,1664]{2,1,0:T(8,128)(2,1)}, bf16[4,48,1664]{2,1,0:T(8,128)(2,1)}, u32[]{:S(2)}, u32[]{:S(2)}) collective-permute-start(bf16[4,48,1664]{2,1,0:T(8,128)(2,1)} %pad_maximum_fusion.15), channel_id=1, source_target_pairs={{0,16},{8,24},{16,0},{24,8},{1,17},{9,25},{17,1},{25,9},{2,18},{10... | collective-permute-start | bytes 1916936 | tf_op jit(solution)/shard_map/ppermute | solution.py:769
  488.9 39.0 %collective-permute-start.50 = (bf16[256,1536]{1,0:T(8,128)(2,1)}, bf16[256,1536]{1,0:T(8,128)(2,1)}, u32[]{:S(2)}, u32[]{:S(2)}) collective-permute-start(bf16[256,1536]{1,0:T(8,128)(2,1)} %pad_maximum_fusion.10), channel_id=1, source_target_pairs={{0,8},{8,0},{16,24},{24,16},{1,9},{9,1},{17,25},{25,17},{2,10},{10... | collective-permute-start | bytes 2359304 | tf_op jit(solution)/shard_map/ppermute | solution.py:769
  498.8 29.2 %collective-permute-start.51 = (bf16[256,1536]{1,0:T(8,128)(2,1)}, bf16[256,1536]{1,0:T(8,128)(2,1)}, u32[]{:S(2)}, u32[]{:S(2)}) collective-permute-start(bf16[256,1536]{1,0:T(8,128)(2,1)} %pad_maximum_fusion.11), channel_id=1, source_target_pairs={{0,16},{8,24},{16,0},{24,8},{1,17},{9,25},{17,1},{25,9},{2,18},{10... | collective-permute-start | bytes 2359304 | tf_op jit(solution)/shard_map/ppermute | solution.py:769
  (87 other events, 758.3 us)
Sparse Core Ops, SparseCore 0:
  24.4 64.4 all-gather.3
  112.2 102.5 all-gather.5
  333.4 82.7 reduce-scatter.2
  420.2 39.8 reduce-scatter.4

commit v5 on v4

--- a/solution.py
+++ b/solution.py
@@ -924,14 +924,14 @@
     d_sum = jnp.concatenate([add(*first_half), add(*last_half)], axis=0)
     d_sum = from_row(d_sum, row_count).reshape(row_count * tok, width).astype(F32)
     grad_gate, grad_up, grad_down = laid_ff(ff_got)
+    layer_out = (middle + add(own[0], *mlp).astype(F32)).astype(BF16)
+    _, pull_one = jax.vjp(lambda t: norm_in(t, gain_one), layer_f)
+    grad_in = (d_middle + pull_one(d_sum)[0]).astype(BF16)
+    cat_got, grad_in, layer_out = together(cat_got, grad_in, layer_out)
     *weight_grads, tails = laid_columns(cat_got, side)
     grad_beta = tails[:, :, :own_heads].transpose(1, 0, 2).reshape(shard, heads)
     gain_grads = jnp.sum(tails[:, :, own_heads : own_heads + 2], axis=0)
     grad_bias = tails[:, :own_heads, own_heads + 2].reshape(heads)
-
-    layer_out = (middle + add(own[0], *mlp).astype(F32)).astype(BF16)
-    _, pull_one = jax.vjp(lambda t: norm_in(t, gain_one), layer_f)
-    grad_in = (d_middle + pull_one(d_sum)[0]).astype(BF16)
 
     return (
         layer_out.reshape(layer_in.shape), grad_in.reshape(layer_in.shape), gain_grads[:, 0],

time: 547 us -> 542 us (level)
    ppermute x15, waiting for transfers between devices: 67.9 us -> 60.7 us  [exchange(): lax.ppermute(sent, axis, [(i, (i + k) % count) for i in range(count)])]
    ppermute x4, waiting for transfers between devices: 0.01 us -> 6.54 us  [sum_near(): lax.ppermute(two, axis, pairs(4, 2))]
    unnamed x125 -> x129, local copies, waits for them, and re-layouts: 12 us -> 9.95 us
  transfers between devices with their start and end apart: 74 -> 74, of which waited for: 29 -> 31; matrix products, arithmetic and copies ran while one was open for 17% -> 17% of each run, Pallas kernels for 32% -> 32%
where the time goes in v5:
time: 542 us; the launch traced here: 536 us
  Pallas kernels  182 us (34%)
  waiting for transfers between devices  159 us (29%)
  starting transfers between devices  73.3 us (14%)
  other arithmetic  60.9 us (11%)
  local copies, waits for them, and re-layouts  40 us (7%)
  between operations  15.3 us (3%)
  matrix products  5.57 us (1%)
    pallas_call x15, Pallas kernels, run(): pl.pallas_call(body, grid=(grid,), in_specs=in_specs, out_specs=out_specs...  182 us
    ppermute x15, waiting for transfers between devices, exchange(): lax.ppermute(sent, axis, [(i, (i + k) % count) for i in range(count)])  60.7 us
    ppermute x6, waiting for transfers between devices, exchange_rows(): lax.ppermute(sent[k - 1], axis, [(i, (i + k) % count) for i in range(coun...  36.2 us
    ppermute x15, starting transfers between devices, exchange(): lax.ppermute(sent, axis, [(i, (i + k) % count) for i in range(count)])  24.1 us
    convert_element_type x10, other arithmetic, add(): return total.astype(left.dtype)  16 us
    ppermute x4, waiting for transfers between devices, gather_near(): lax.ppermute(x, axis, pairs(4, 1))  12.3 us
  transfers between devices with their start and end apart: 74, of which 31 were waited for; matrix products, arithmetic and copies ran while one was open for 17% of the time, Pallas kernels for 32%

profile of v5, /device:TPU:8, one launch (start us, length us, event | category | flops | bytes accessed | tf_op | source)
XLA Modules:
  0.0 535.5 jit_solution(9224619709457622165)
XLA Ops:
  25.7 12.6 %collective-permute-done.2 = bf16[48,1664]{1,0:T(8,128)(2,1)S(1)} collective-permute-done((bf16[48,1664]{1,0:T(8,128)(2,1)}, bf16[48,1664]{1,0:T(8,128)(2,1)S(1)}, u32[]{:S(2)}, u32[]{:S(2)}) %collective-permute-start.2) | collective-permute-done | bytes 159776 | tf_op jit(solution)/shard_map/ppermute | solution.py:706
  38.2 10.2 %collective-permute-done.3 = bf16[48,1664]{1,0:T(8,128)(2,1)} collective-permute-done((bf16[48,1664]{1,0:T(8,128)(2,1)}, bf16[48,1664]{1,0:T(8,128)(2,1)}, u32[]{:S(2)}, u32[]{:S(2)}) %collective-permute-start.3) | collective-permute-done | bytes 159776 | tf_op jit(solution)/shard_map/ppermute | solution.py:706
  53.3 11.1 %collective-permute-done.7 = bf16[4,48,1664]{2,1,0:T(8,128)(2,1)S(1)} collective-permute-done((bf16[4,48,1664]{2,1,0:T(8,128)(2,1)S(1)}, bf16[4,48,1664]{2,1,0:T(8,128)(2,1)S(1)}, u32[]{:S(2)}, u32[]{:S(2)}) %collective-permute-start.7) | collective-permute-done | bytes 639008 | tf_op jit(solution)/shard_map/ppermute | solution.py:729
  67.0 4.5 collective-permute-done.10
  83.5 5.7 %collective-permute-done.18 = bf16[128,1536]{1,0:T(8,128)(2,1)S(1)} collective-permute-done((bf16[128,1536]{1,0:T(8,128)(2,1)S(1)}, bf16[128,1536]{1,0:T(8,128)(2,1)S(1)}, u32[]{:S(2)}, u32[]{:S(2)}) %collective-permute-start.18) | collective-permute-done | bytes 393248 | tf_op jit(solution)/shard_map/ppermute | solution.py:737
  94.4 2.2 collective-permute-start.16
  96.7 5.5 %shard_map.254 = (bf16[1536,1664]{1,0:T(8,128)(2,1)}, f32[128,1536]{1,0:T(8,128)}) custom-call(s32[3]{0:T(128)} %pad_add_fusion.3.me_ref, bf16[1,4,4,48,1664]{4,3,2,1,0:T(8,128)(2,1)} %bitcast.247, bf16[1,4,4,48,1664]{4,3,2,1,0:T(8,128)(2,1)} %bitcast.32.other_ref), custom_call_target="tpu_custom_call" | custom-call | bytes 11010060 | tf_op jit(solution)/shard_map/pallas_call | solution.py:254
  113.7 12.3 %shard_map.255 = (bf16[1024,1536]{1,0:T(8,128)(2,1)}, bf16[1024,384]{1,0:T(8,128)(2,1)}, bf16[1024,384]{1,0:T(8,128)(2,1)}, bf16[1024,384]{1,0:T(8,128)(2,1)}, f...) custom-call(f32[3]{0:T(128)} %dynamic-slice_convert_fusion.bias_ref, bf16[1024,1536]{1,0:T(8,128)(2,1)} %all-gather.4.cloned.1.call-done.x_ref, ...), custom_call_target="tpu_custom_call" | custom-call | flops 5234491392 | bytes 15353868 | tf_op jit(solution)/shard_map/pallas_call | solution.py:254
  128.6 17.7 %shard_map.256 = (bf16[1024,384]{1,0:T(8,128)(2,1)}, bf16[1024,384]{1,0:T(8,128)(2,1)}, bf16[1024,384]{1,0:T(8,128)(2,1)}, bf16[1024,384]{1,0:T(8,128)(2,1)}, f3...) custom-call(bf16[1024,384]{1,0:T(8,128)(2,1)} %get-tuple-element.247, ...), custom_call_target="tpu_custom_call" | custom-call | flops 6241124352 | bytes 14168064 | tf_op jit(solution)/shard_map/pallas_call | solution.py:254
  146.3 16.9 %shard_map.257 = (bf16[1024,384]{1,0:T(8,128)(2,1)}, bf16[8,3,128,1024]{3,2,1,0:T(8,128)(2,1)}, bf16[8,3,1024,128]{3,2,1,0:T(8,128)(2,1)}) custom-call(bf16[1024,384]{1,0:T(8,128)(2,1)} %get-tuple-element.260.qin_ref, bf16[1024,384]{1,0:T(8,128)(2,1)} %get-tuple-element.261.kout_ref, bf16[1024,384]{1,0:T(8,128)(2,1)} %get-tuple-element.262.ptop_ref, ...), custom_call_target="tpu_custom_call" | custom-call | flops 3221225472 | bytes 18882560 | tf_op jit(solution)/shard_map/pallas_call | solution.py:254
  165.6 3.9 collective-permute-start.25
  171.4 5.0 shard_map.258
  176.5 9.7 %collective-permute-done.24 = bf16[256,384]{1,0:T(8,128)(2,1)S(1)} collective-permute-done((bf16[256,384]{1,0:T(8,128)(2,1)S(1)}, bf16[256,384]{1,0:T(8,128)(2,1)S(1)}, u32[]{:S(2)}, u32[]{:S(2)}) %collective-permute-start.24) | collective-permute-done | bytes 196640 | tf_op jit(solution)/shard_map/ppermute | solution.py:706
  186.2 17.8 %collective-permute-done.25 = bf16[256,384]{1,0:T(8,128)(2,1)S(1)} collective-permute-done((bf16[256,384]{1,0:T(8,128)(2,1)S(1)}, bf16[256,384]{1,0:T(8,128)(2,1)S(1)}, u32[]{:S(2)}, u32[]{:S(2)}) %collective-permute-start.25) | collective-permute-done | bytes 196640 | tf_op jit(solution)/shard_map/ppermute | solution.py:706
  204.0 3.1 collective-permute-done.26
  211.5 3.4 all-gather.6.cloned.1.call-done
  218.8 4.5 collective-permute-done.29
  223.2 10.6 %shard_map.259 = (bf16[256,1536]{1,0:T(8,128)(2,1)}, bf16[256,1536]{1,0:T(8,128)(2,1)}, bf16[256,1024]{1,0:T(8,128)(2,1)}, bf16[256,1024]{1,0:T(8,128)(2,1)}, bf16[256,1024]{1,0:T(8,128)(2,1)}) custom-call(s32[2]{0:T(128)} %pad_add_fusion.4.me_ref, bf16[256,1536]{1,0:T(8,128)(2,1)} %copy-done.34, bf16[256,1536]{1,0:T(8,128)(2,1)} %bitcast.252, ...), custom_call_target="tpu_custom_call" | custom-call | flops 4831838208 | bytes 14155784 | tf_op jit(solution)/shard_map/pallas_call | solution.py:254
  239.8 18.0 %shard_map.260 = (bf16[512,1536]{1,0:T(8,128)(2,1)}, bf16[512,1536]{1,0:T(8,128)(2,1)}, bf16[512,1024]{1,0:T(8,128)(2,1)}, bf16[512,1024]{1,0:T(8,128)(2,1)}, bf16[512,1024]{1,0:T(8,128)(2,1)}) custom-call(s32[2]{0:T(128)} %pad_add_fusion.4.me_ref, bf16[512,1536]{1,0:T(8,128)(2,1)} %copy-done.39, bf16[512,1536]{1,0:T(8,128)(2,1)} %pad_maximum_fusion.grad_ref.refs_6_, ...), custom_call_target="tpu_custom_call" | custom-call | flops 9663676416 | bytes 18874376 | tf_op jit(solution)/shard_map/pallas_call | solution.py:254
  258.8 10.5 %shard_map.261 = (bf16[256,1536]{1,0:T(8,128)(2,1)}, bf16[256,1536]{1,0:T(8,128)(2,1)}, bf16[256,1024]{1,0:T(8,128)(2,1)}, bf16[256,1024]{1,0:T(8,128)(2,1)}, bf16[256,1024]{1,0:T(8,128)(2,1)}) custom-call(s32[2]{0:T(128)} %pad_add_fusion.4.me_ref, bf16[256,1536]{1,0:T(8,128)(2,1)} %copy-done.44, bf16[256,1536]{1,0:T(8,128)(2,1)} %pad_maximum_fusion.3.grad_ref.refs_11_, ...), custom_call_target="tpu_custom_call" | custom-call | flops 4831838208 | bytes 14155784 | tf_op jit(solution)/shard_map/pallas_call | solution.py:254
  272.8 7.7 %collective-permute-done.34 = bf16[128,1536]{1,0:T(8,128)(2,1)S(1)} collective-permute-done((bf16[128,1536]{1,0:T(8,128)(2,1)S(1)}, bf16[128,1536]{1,0:T(8,128)(2,1)S(1)}, u32[]{:S(2)}, u32[]{:S(2)}) %collective-permute-start.34) | collective-permute-done | bytes 393248 | tf_op jit(solution)/shard_map/ppermute | solution.py:761
  284.1 16.0 %shard_map.262 = (bf16[4,1,4,3,192,256]{5,4,3,2,1,0:T(8,128)(2,1)}, bf16[4,1,4,3,192,256]{5,4,3,2,1,0:T(8,128)(2,1)}) custom-call(s32[2]{0:T(128)} %pad_add_fusion.4.me_ref, bf16[256,1536]{1,0:T(8,128)(2,1)} %copy-done.34, bf16[256,1536]{1,0:T(8,128)(2,1)} %bitcast.253, bf16[256,1024]{1,0:T(8,128)(2,1)} %get-tuple-element.325.refs_2_, ...), custom_call_target="tpu_custom_call" | custom-call | flops 9663676416 | bytes 22020104 | tf_op jit(solution)/shard_map/pallas_call | solution.py:254
  302.0 4.1 convolution_convert_fusion
  309.5 2.3 collective-permute-start.39
  311.8 4.5 collective-permute-start.40
  317.1 5.2 shard_map.263
  322.4 6.5 %fusion.1 = bf16[4,4,3,192,256]{4,3,2,1,0:T(8,128)(2,1)} fusion(bf16[1,4,4,3,192,256]{5,4,3,2,1,0:T(8,128)(2,1)} %collective-permute-done.42, bf16[4,1,4,3,192,256]{5,4,3,2,1,0:T(8,128)(2,1)S(1)} %bitcast.251), kind=kLoop, calls=%fused_computation.3 | loop fusion | flops 9437184 | bytes 14155776 | tf_op jit(solution)/shard_map/squeeze | solution.py:888
  329.3 4.0 collective-permute-done.41
  338.4 2.4 add_convert_fusion.1
  342.9 20.9 %shard_map.264 = (f32[1024,384]{1,0:T(8,128)}, bf16[1024,384]{1,0:T(8,128)(2,1)}, f32[1024,384]{1,0:T(8,128)}, f32[1024,384]{1,0:T(8,128)}, bf16[1024,384]{1,0:T(8,128)(2,1)}) custom-call(bf16[1024,384]{1,0:T(8,128)(2,1)} %pad_maximum_fusion.9.grad_ref, bf16[1024,384]{1,0:T(8,128)(2,1)} %get-tuple-element.265.v_ref, ...), custom_call_target="tpu_custom_call" | custom-call | flops 5637144576 | bytes 22806528 | tf_op jit(solution)/shard_map/pallas_call | solution.py:254
  370.6 18.8 %shard_map.265.right_ref = bf16[1024,1664]{1,0:T(8,128)(2,1)} custom-call(bf16[1024,384]{1,0:T(8,128)(2,1)} %get-tuple-element.247.q_ref, bf16[1024,384]{1,0:T(8,128)(2,1)} %get-tuple-element.248.k_ref, f32[1024,384]{1,0:T(8,128)} %get-tuple-element.254.raw_ref, f32[8,3,128]{2,1,0:T(4,128)} %get-tuple-element.255.logit_ref, ...), custom_call_target="tpu_custom_call" | custom-call | flops 6039797760 | bytes 19148800 | tf_op jit(solution)/shard_map/pallas_call | solution.py:254
  391.0 19.1 %shard_map.266 = (bf16[1024,1536]{1,0:T(8,128)(2,1)}, bf16[1,4,4,48,1664]{4,3,2,1,0:T(8,128)(2,1)}, bf16[1,4,4,48,1664]{4,3,2,1,0:T(8,128)(2,1)}) custom-call(s32[3]{0:T(128)} %pad_add_fusion.1.me_ref, f32[3]{0:T(128)} %convert_reduce_fusion.bias_ref, bf16[1024,1536]{1,0:T(8,128)(2,1)} %get-tuple-element.363.left_ref, ...), custom_call_target="tpu_custom_call" | custom-call | flops 10468982784 | bytes 19929112 | tf_op jit(solution)/shard_map/pallas_call | solution.py:254
  411.3 3.2 fusion.34
  415.7 2.3 collective-permute-start.58
  417.9 2.3 fusion.13
  420.3 2.7 dynamic-slice_bitcast_fusion.1
  423.0 2.2 add_convert_fusion.5
  425.1 2.4 add_convert_fusion
  435.2 24.8 %collective-permute-done.57 = bf16[128,1536]{1,0:T(8,128)(2,1)} collective-permute-done((bf16[128,1536]{1,0:T(8,128)(2,1)}, bf16[128,1536]{1,0:T(8,128)(2,1)}, u32[]{:S(2)}, u32[]{:S(2)}) %collective-permute-start.57) | collective-permute-done | bytes 393248 | tf_op jit(solution)/shard_map/ppermute | solution.py:713
  464.8 3.0 collective-permute-start.62
  469.8 5.3 collective-permute-done.54.refs_2_
  482.2 2.9 shard_map.268
  485.2 2.5 copy.102
  490.4 8.6 %collective-permute-done.62 = bf16[128,1536]{1,0:T(8,128)(2,1)} collective-permute-done((bf16[128,1536]{1,0:T(8,128)(2,1)}, bf16[128,1536]{1,0:T(8,128)(2,1)}, u32[]{:S(2)}, u32[]{:S(2)}) %collective-permute-start.62) | collective-permute-done | bytes 393248 | tf_op jit(solution)/shard_map/ppermute | solution.py:713
  499.1 2.8 collective-permute-done.63
  511.1 6.5 %collective-permute-done.69 = bf16[256,1536]{1,0:T(8,128)(2,1)S(1)} collective-permute-done((bf16[256,1536]{1,0:T(8,128)(2,1)S(1)}, bf16[256,1536]{1,0:T(8,128)(2,1)S(1)}, u32[]{:S(2)}, u32[]{:S(2)}) %collective-permute-start.69) | collective-permute-done | bytes 786464 | tf_op jit(solution)/shard_map/ppermute | solution.py:769
  517.6 2.2 add_convert_fusion.2
  521.7 2.3 shard_map.267
  (388 shorter events, 147.4 us)
Async XLA Ops:
  7.2 100.2 %all-gather.4.cloned.1.call-start = ((), (), s32[]{:S(2)}) async-start(), calls=%async_computation.2 | async-start | bytes 3932160 | tf_op jit(solution)/shard_map/all_gather | solution.py:803
  14.0 34.6 %collective-permute-start.5 = (bf16[256,1536]{1,0:T(8,128)(2,1)S(1)}, bf16[256,1536]{1,0:T(8,128)(2,1)S(1)}, u32[]{:S(2)}, u32[]{:S(2)}) collective-permute-start(bf16[256,1536]{1,0:T(8,128)(2,1)S(1)} %bitcast.254), channel_id=1, source_target_pairs={{0,8},{8,0},{16,24},{24,16},{1,9},{9,1},{17,25},{25,17},{2,10},{10... | collective-permute-start | bytes 2359304 | tf_op jit(solution)/shard_map/ppermute | solution.py:729
  15.4 33.1 %collective-permute-start.6 = (bf16[256,1536]{1,0:T(8,128)(2,1)S(1)}, bf16[256,1536]{1,0:T(8,128)(2,1)S(1)}, u32[]{:S(2)}, u32[]{:S(2)}) collective-permute-start(bf16[256,1536]{1,0:T(8,128)(2,1)S(1)} %bitcast.255), channel_id=1, source_target_pairs={{0,16},{8,24},{16,0},{24,8},{1,17},{9,25},{17,1},{25,9},{2,18},{10... | collective-permute-start | bytes 2359304 | tf_op jit(solution)/shard_map/ppermute | solution.py:729
  19.7 18.6 %collective-permute-start.2 = (bf16[48,1664]{1,0:T(8,128)(2,1)}, bf16[48,1664]{1,0:T(8,128)(2,1)S(1)}, u32[]{:S(2)}, u32[]{:S(2)}) collective-permute-start(bf16[48,1664]{1,0:T(8,128)(2,1)} %get-tuple-element.562), channel_id=1, source_target_pairs={{0,2},{2,4},{4,6},{6,0},{1,3},{3,5},{5,7},{7,1},{8,10},{10,12},{12... | collective-permute-start | bytes 479240 | tf_op jit(solution)/shard_map/ppermute | solution.py:706
  21.2 27.2 %collective-permute-start.3 = (bf16[48,1664]{1,0:T(8,128)(2,1)}, bf16[48,1664]{1,0:T(8,128)(2,1)}, u32[]{:S(2)}, u32[]{:S(2)}) collective-permute-start(bf16[48,1664]{1,0:T(8,128)(2,1)} %get-tuple-element.561), channel_id=1, source_target_pairs={{0,4},{2,6},{4,0},{6,2},{1,5},{3,7},{5,1},{7,3},{8,12},{10,14},{12... | collective-permute-start | bytes 479240 | tf_op jit(solution)/shard_map/ppermute | solution.py:706
  22.5 26.1 %collective-permute-start.4 = (bf16[48,1664]{1,0:T(8,128)(2,1)}, bf16[48,1664]{1,0:T(8,128)(2,1)}, u32[]{:S(2)}, u32[]{:S(2)}) collective-permute-start(bf16[48,1664]{1,0:T(8,128)(2,1)} %get-tuple-element.560), channel_id=1, source_target_pairs={{0,6},{2,0},{4,2},{6,4},{1,7},{3,1},{5,3},{7,5},{8,14},{10,8},{12,... | collective-permute-start | bytes 479240 | tf_op jit(solution)/shard_map/ppermute | solution.py:706
  24.3 190.7 %all-gather.6.cloned.1.call-start = ((), (), s32[]{:S(2)}) async-start(), calls=%async_computation.5 | async-start | bytes 5898240 | tf_op jit(solution)/shard_map/all_gather | solution.py:838
  73.3 21.1 %collective-permute-start.11 = (bf16[4,4,48,1664]{3,2,1,0:T(8,128)(2,1)S(1)}, bf16[4,4,48,1664]{3,2,1,0:T(8,128)(2,1)}, u32[]{:S(2)}, u32[]{:S(2)}) collective-permute-start(bf16[4,4,48,1664]{3,2,1,0:T(8,128)(2,1)S(1)} %fusion.14), channel_id=1, source_target_pairs={{0,1},{1,0},{2,3},{3,2},{4,5},{5,4},{6,7},{7,6},{8,9},{9,8},{10,11... | collective-permute-start | bytes 7667720 | tf_op jit(solution)/shard_map/ppermute | solution.py:774
  75.0 27.1 %collective-permute-start.15 = (bf16[48,1536]{1,0:T(8,128)(2,1)}, bf16[48,1536]{1,0:T(8,128)(2,1)}, u32[]{:S(2)}, u32[]{:S(2)}) collective-permute-start(bf16[48,1536]{1,0:T(8,128)(2,1)} %param.25), channel_id=1, source_target_pairs={{0,2},{2,4},{4,6},{6,0},{1,3},{3,5},{5,7},{7,1},{8,10},{10,12},{12... | collective-permute-start | bytes 442376 | tf_op jit(solution)/shard_map/ppermute | solution.py:706
  82.1 25.3 %collective-permute-start.12 = (bf16[3,192,256]{2,1,0:T(8,128)(2,1)S(1)}, bf16[3,192,256]{2,1,0:T(8,128)(2,1)S(1)}, u32[]{:S(2)}, u32[]{:S(2)}) collective-permute-start(bf16[3,192,256]{2,1,0:T(8,128)(2,1)S(1)} %get-tuple-element.531), channel_id=1, source_target_pairs={{0,8},{8,0},{16,24},{24,16},{1,9},{9,1},{17,25},{25,17},{2,10},{10... | collective-permute-start | bytes 884744 | tf_op jit(solution)/shard_map/ppermute | solution.py:832
  89.2 18.1 %collective-permute-start.13 = (bf16[3,192,256]{2,1,0:T(8,128)(2,1)S(1)}, bf16[3,192,256]{2,1,0:T(8,128)(2,1)S(1)}, u32[]{:S(2)}, u32[]{:S(2)}) collective-permute-start(bf16[3,192,256]{2,1,0:T(8,128)(2,1)S(1)} %get-tuple-element.530), channel_id=1, source_target_pairs={{0,16},{8,24},{16,0},{24,8},{1,17},{9,25},{17,1},{25,9},{2,18},{10... | collective-permute-start | bytes 884744 | tf_op jit(solution)/shard_map/ppermute | solution.py:832
  108.4 17.6 %collective-permute-start.20 = (bf16[4,48,1536]{2,1,0:T(8,128)(2,1)S(1)}, bf16[4,48,1536]{2,1,0:T(8,128)(2,1)S(1)}, u32[]{:S(2)}, u32[]{:S(2)}) collective-permute-start(bf16[4,48,1536]{2,1,0:T(8,128)(2,1)S(1)} %pad_maximum_fusion.16), channel_id=1, source_target_pairs={{0,8},{8,0},{16,24},{24,16},{1,9},{9,1},{17,25},{25,17},{2,10},{10... | collective-permute-start | bytes 1769480 | tf_op jit(solution)/shard_map/ppermute | solution.py:729
  112.2 320.0 %reduce-scatter.3.cloned.1.call-start = ((), (), s32[]{:S(2)}) async-start(), calls=%async_computation.3 | async-start | bytes 5898240 | tf_op jit(solution)/shard_map/reduce_scatter | solution.py:891
  126.0 37.2 %collective-permute-start.22 = (bf16[2,48,1536]{2,1,0:T(8,128)(2,1)S(1)}, bf16[2,48,1536]{2,1,0:T(8,128)(2,1)S(1)}, u32[]{:S(2)}, u32[]{:S(2)}) collective-permute-start(bf16[2,48,1536]{2,1,0:T(8,128)(2,1)S(1)} %slice.379), channel_id=1, source_target_pairs={{0,16},{8,24},{16,0},{24,8},{1,17},{9,25},{17,1},{25,9},{2,18},{10... | collective-permute-start | bytes 884744 | tf_op jit(solution)/shard_map/ppermute | solution.py:737
  127.8 35.4 %collective-permute-start.23 = (bf16[2,48,1536]{2,1,0:T(8,128)(2,1)S(1)}, bf16[2,48,1536]{2,1,0:T(8,128)(2,1)S(1)}, u32[]{:S(2)}, u32[]{:S(2)}) collective-permute-start(bf16[2,48,1536]{2,1,0:T(8,128)(2,1)S(1)} %slice.380), channel_id=1, source_target_pairs={{0,8},{8,0},{16,24},{24,16},{1,9},{9,1},{17,25},{25,17},{2,10},{10... | collective-permute-start | bytes 884744 | tf_op jit(solution)/shard_map/ppermute | solution.py:737
  164.8 21.3 %collective-permute-start.24 = (bf16[256,384]{1,0:T(8,128)(2,1)S(1)}, bf16[256,384]{1,0:T(8,128)(2,1)S(1)}, u32[]{:S(2)}, u32[]{:S(2)}) collective-permute-start(bf16[256,384]{1,0:T(8,128)(2,1)S(1)} %get-tuple-element.555), channel_id=1, source_target_pairs={{0,2},{2,4},{4,6},{6,0},{1,3},{3,5},{5,7},{7,1},{8,10},{10,12},{12... | collective-permute-start | bytes 589832 | tf_op jit(solution)/shard_map/ppermute | solution.py:706
  165.6 38.4 %collective-permute-start.25 = (bf16[256,384]{1,0:T(8,128)(2,1)S(1)}, bf16[256,384]{1,0:T(8,128)(2,1)S(1)}, u32[]{:S(2)}, u32[]{:S(2)}) collective-permute-start(bf16[256,384]{1,0:T(8,128)(2,1)S(1)} %get-tuple-element.554), channel_id=1, source_target_pairs={{0,4},{2,6},{4,0},{6,2},{1,5},{3,7},{5,1},{7,3},{8,12},{10,14},{12... | collective-permute-start | bytes 589832 | tf_op jit(solution)/shard_map/ppermute | solution.py:706
  169.5 37.6 %collective-permute-start.26 = (bf16[256,384]{1,0:T(8,128)(2,1)S(1)}, bf16[256,384]{1,0:T(8,128)(2,1)S(1)}, u32[]{:S(2)}, u32[]{:S(2)}) collective-permute-start(bf16[256,384]{1,0:T(8,128)(2,1)S(1)} %get-tuple-element.552), channel_id=1, source_target_pairs={{0,6},{2,0},{4,2},{6,4},{1,7},{3,1},{5,3},{7,5},{8,14},{10,8},{12,... | collective-permute-start | bytes 589832 | tf_op jit(solution)/shard_map/ppermute | solution.py:706
  215.0 19.9 %collective-permute-start.30 = (bf16[256,1536]{1,0:T(8,128)(2,1)S(1)}, bf16[256,1536]{1,0:T(8,128)(2,1)S(1)}, u32[]{:S(2)}, u32[]{:S(2)}) collective-permute-start(bf16[256,1536]{1,0:T(8,128)(2,1)S(1)} %multiply_convert_fusion.act_ref.refs_0_), channel_id=1, source_target_pairs={{0,8},{8,0},{16,24},{24,16},{1,9},{9,1},{17,25},{25,17},{2,10},{10... | collective-permute-start | bytes 2359304 | tf_op jit(solution)/shard_map/ppermute | solution.py:729
  216.7 19.6 %collective-permute-start.31 = (bf16[256,1536]{1,0:T(8,128)(2,1)S(1)}, bf16[256,1536]{1,0:T(8,128)(2,1)S(1)}, u32[]{:S(2)}, u32[]{:S(2)}) collective-permute-start(bf16[256,1536]{1,0:T(8,128)(2,1)S(1)} %multiply_convert_fusion.act_ref.refs_0_), channel_id=1, source_target_pairs={{0,16},{8,24},{16,0},{24,8},{1,17},{9,25},{17,1},{25,9},{2,18},{10... | collective-permute-start | bytes 2359304 | tf_op jit(solution)/shard_map/ppermute | solution.py:729
  236.4 21.4 %collective-permute-start.32 = (bf16[128,1536]{1,0:T(8,128)(2,1)S(1)}, bf16[128,1536]{1,0:T(8,128)(2,1)S(1)}, u32[]{:S(2)}, u32[]{:S(2)}) collective-permute-start(bf16[128,1536]{1,0:T(8,128)(2,1)S(1)} %slice.386), channel_id=1, source_target_pairs={{0,16},{8,24},{16,0},{24,8},{1,17},{9,25},{17,1},{25,9},{2,18},{10... | collective-permute-start | bytes 1179656 | tf_op jit(solution)/shard_map/ppermute | solution.py:737
  238.0 19.9 %collective-permute-start.33 = (bf16[128,1536]{1,0:T(8,128)(2,1)S(1)}, bf16[128,1536]{1,0:T(8,128)(2,1)S(1)}, u32[]{:S(2)}, u32[]{:S(2)}) collective-permute-start(bf16[128,1536]{1,0:T(8,128)(2,1)S(1)} %slice.387), channel_id=1, source_target_pairs={{0,8},{8,0},{16,24},{24,16},{1,9},{9,1},{17,25},{25,17},{2,10},{10... | collective-permute-start | bytes 1179656 | tf_op jit(solution)/shard_map/ppermute | solution.py:737
  281.1 18.9 %collective-permute-start.36 = (bf16[256,1536]{1,0:T(8,128)(2,1)S(1)}, bf16[256,1536]{1,0:T(8,128)(2,1)S(1)}, u32[]{:S(2)}, u32[]{:S(2)}) collective-permute-start(bf16[256,1536]{1,0:T(8,128)(2,1)S(1)} %pad_maximum_fusion.6), channel_id=1, source_target_pairs={{0,8},{8,0},{16,24},{24,16},{1,9},{9,1},{17,25},{25,17},{2,10},{10... | collective-permute-start | bytes 2359304 | tf_op jit(solution)/shard_map/ppermute | solution.py:769
  282.6 17.4 %collective-permute-start.37 = (bf16[256,1536]{1,0:T(8,128)(2,1)S(1)}, bf16[256,1536]{1,0:T(8,128)(2,1)S(1)}, u32[]{:S(2)}, u32[]{:S(2)}) collective-permute-start(bf16[256,1536]{1,0:T(8,128)(2,1)S(1)} %pad_maximum_fusion.7), channel_id=1, source_target_pairs={{0,16},{8,24},{16,0},{24,8},{1,17},{9,25},{17,1},{25,9},{2,18},{10... | collective-permute-start | bytes 2359304 | tf_op jit(solution)/shard_map/ppermute | solution.py:769
  300.1 22.3 %collective-permute-start.42 = (bf16[1,4,4,3,192,256]{5,4,3,2,1,0:T(8,128)(2,1)}, bf16[1,4,4,3,192,256]{5,4,3,2,1,0:T(8,128)(2,1)}, u32[]{:S(2)}, u32[]{:S(2)}) collective-permute-start(bf16[1,4,4,3,192,256]{5,4,3,2,1,0:T(8,128)(2,1)} %bitcast.285), channel_id=1, source_target_pairs={{0,1},{1,0},{2,3},{3,2},{4,5},{5,4},{6,7},{7,6},{8,9},{9,8},{10,11... | collective-permute-start | bytes 14155784 | tf_op jit(solution)/shard_map/ppermute | solution.py:779
  309.5 19.3 %collective-permute-start.39 = (bf16[256,384]{1,0:T(8,128)(2,1)}, bf16[256,384]{1,0:T(8,128)(2,1)S(1)}, u32[]{:S(2)}, u32[]{:S(2)}) collective-permute-start(bf16[256,384]{1,0:T(8,128)(2,1)} %get-tuple-element.544), channel_id=1, source_target_pairs={{0,2},{2,4},{4,6},{6,0},{1,3},{3,5},{5,7},{7,1},{8,10},{10,12},{12... | collective-permute-start | bytes 589832 | tf_op jit(solution)/shard_map/ppermute | solution.py:706
  311.8 17.5 %collective-permute-start.40 = (bf16[256,384]{1,0:T(8,128)(2,1)}, bf16[256,384]{1,0:T(8,128)(2,1)}, u32[]{:S(2)}, u32[]{:S(2)}) collective-permute-start(bf16[256,384]{1,0:T(8,128)(2,1)} %get-tuple-element.543), channel_id=1, source_target_pairs={{0,4},{2,6},{4,0},{6,2},{1,5},{3,7},{5,1},{7,3},{8,12},{10,14},{12... | collective-permute-start | bytes 589832 | tf_op jit(solution)/shard_map/ppermute | solution.py:706
  317.1 16.3 %collective-permute-start.41 = (bf16[256,384]{1,0:T(8,128)(2,1)}, bf16[256,384]{1,0:T(8,128)(2,1)}, u32[]{:S(2)}, u32[]{:S(2)}) collective-permute-start(bf16[256,384]{1,0:T(8,128)(2,1)} %get-tuple-element.541), channel_id=1, source_target_pairs={{0,6},{2,0},{4,2},{6,4},{1,7},{3,1},{5,3},{7,5},{8,14},{10,8},{12,... | collective-permute-start | bytes 589832 | tf_op jit(solution)/shard_map/ppermute | solution.py:706
  333.4 147.2 %reduce-scatter.5.cloned.1.call-start = ((), (), s32[]{:S(2)}) async-start(), calls=%async_computation.4 | async-start | bytes 737280 | tf_op jit(solution)/shard_map/reduce_scatter | solution.py:912
  340.9 22.9 %collective-permute-start.44 = (bf16[2,48,1536]{2,1,0:T(8,128)(2,1)S(1)}, bf16[2,48,1536]{2,1,0:T(8,128)(2,1)S(1)}, u32[]{:S(2)}, u32[]{:S(2)}) collective-permute-start(bf16[2,48,1536]{2,1,0:T(8,128)(2,1)S(1)} %get-tuple-element.496), channel_id=1, source_target_pairs={{0,16},{8,24},{16,0},{24,8},{1,17},{9,25},{17,1},{25,9},{2,18},{10... | collective-permute-start | bytes 884744 | tf_op jit(solution)/shard_map/ppermute | solution.py:761
  341.9 21.9 %collective-permute-start.45 = (bf16[2,48,1536]{2,1,0:T(8,128)(2,1)S(1)}, bf16[2,48,1536]{2,1,0:T(8,128)(2,1)S(1)}, u32[]{:S(2)}, u32[]{:S(2)}) collective-permute-start(bf16[2,48,1536]{2,1,0:T(8,128)(2,1)S(1)} %get-tuple-element.498), channel_id=1, source_target_pairs={{0,8},{8,0},{16,24},{24,16},{1,9},{9,1},{17,25},{25,17},{2,10},{10... | collective-permute-start | bytes 884744 | tf_op jit(solution)/shard_map/ppermute | solution.py:761
  365.7 44.4 %collective-permute-start.46 = (bf16[4,48,1536]{2,1,0:T(8,128)(2,1)}, bf16[4,48,1536]{2,1,0:T(8,128)(2,1)}, u32[]{:S(2)}, u32[]{:S(2)}) collective-permute-start(bf16[4,48,1536]{2,1,0:T(8,128)(2,1)} %pad_maximum_fusion.17), channel_id=1, source_target_pairs={{0,8},{8,0},{16,24},{24,16},{1,9},{9,1},{17,25},{25,17},{2,10},{10... | collective-permute-start | bytes 1769480 | tf_op jit(solution)/shard_map/ppermute | solution.py:769
  366.7 43.5 %collective-permute-start.47 = (bf16[4,48,1536]{2,1,0:T(8,128)(2,1)}, bf16[4,48,1536]{2,1,0:T(8,128)(2,1)}, u32[]{:S(2)}, u32[]{:S(2)}) collective-permute-start(bf16[4,48,1536]{2,1,0:T(8,128)(2,1)} %pad_maximum_fusion.18), channel_id=1, source_target_pairs={{0,16},{8,24},{16,0},{24,8},{1,17},{9,25},{17,1},{25,9},{2,18},{10... | collective-permute-start | bytes 1769480 | tf_op jit(solution)/shard_map/ppermute | solution.py:769
  368.6 41.5 %collective-permute-start.48 = (bf16[128,1536]{1,0:T(8,128)(2,1)}, bf16[128,1536]{1,0:T(8,128)(2,1)S(1)}, u32[]{:S(2)}, u32[]{:S(2)}) collective-permute-start(bf16[128,1536]{1,0:T(8,128)(2,1)} %get-tuple-element.536), channel_id=1, source_target_pairs={{0,16},{8,24},{16,0},{24,8},{1,17},{9,25},{17,1},{25,9},{2,18},{10... | collective-permute-start | bytes 1179656 | tf_op jit(solution)/shard_map/ppermute | solution.py:761
  369.5 40.6 %collective-permute-start.49 = (bf16[128,1536]{1,0:T(8,128)(2,1)S(1)}, bf16[128,1536]{1,0:T(8,128)(2,1)S(1)}, u32[]{:S(2)}, u32[]{:S(2)}) collective-permute-start(bf16[128,1536]{1,0:T(8,128)(2,1)S(1)} %get-tuple-element.535), channel_id=1, source_target_pairs={{0,8},{8,0},{16,24},{24,16},{1,9},{9,1},{17,25},{25,17},{2,10},{10... | collective-permute-start | bytes 1179656 | tf_op jit(solution)/shard_map/ppermute | solution.py:761
  415.7 18.6 %collective-permute-start.56 = (bf16[128,1536]{1,0:T(8,128)(2,1)}, bf16[128,1536]{1,0:T(8,128)(2,1)}, u32[]{:S(2)}, u32[]{:S(2)}) collective-permute-start(bf16[128,1536]{1,0:T(8,128)(2,1)} %get-tuple-element.376), channel_id=1, source_target_pairs={{0,2},{2,4},{4,6},{6,0},{1,3},{3,5},{5,7},{7,1},{8,10},{10,12},{12... | collective-permute-start | bytes 1179656 | tf_op jit(solution)/shard_map/ppermute | solution.py:713
  415.7 44.3 %collective-permute-start.57 = (bf16[128,1536]{1,0:T(8,128)(2,1)}, bf16[128,1536]{1,0:T(8,128)(2,1)}, u32[]{:S(2)}, u32[]{:S(2)}) collective-permute-start(bf16[128,1536]{1,0:T(8,128)(2,1)} %get-tuple-element.377), channel_id=1, source_target_pairs={{0,4},{2,6},{4,0},{6,2},{1,5},{3,7},{5,1},{7,3},{8,12},{10,14},{12... | collective-permute-start | bytes 1179656 | tf_op jit(solution)/shard_map/ppermute | solution.py:713
  415.7 45.2 %collective-permute-start.58 = (bf16[128,1536]{1,0:T(8,128)(2,1)}, bf16[128,1536]{1,0:T(8,128)(2,1)}, u32[]{:S(2)}, u32[]{:S(2)}) collective-permute-start(bf16[128,1536]{1,0:T(8,128)(2,1)} %get-tuple-element.378), channel_id=1, source_target_pairs={{0,6},{2,0},{4,2},{6,4},{1,7},{3,1},{5,3},{7,5},{8,14},{10,8},{12,... | collective-permute-start | bytes 1179656 | tf_op jit(solution)/shard_map/ppermute | solution.py:713
  430.1 34.6 %collective-permute-start.51 = (bf16[2,48,1664]{2,1,0:T(8,128)(2,1)}, bf16[2,48,1664]{2,1,0:T(8,128)(2,1)}, u32[]{:S(2)}, u32[]{:S(2)}) collective-permute-start(bf16[2,48,1664]{2,1,0:T(8,128)(2,1)} %get-tuple-element.490), channel_id=1, source_target_pairs={{0,16},{8,24},{16,0},{24,8},{1,17},{9,25},{17,1},{25,9},{2,18},{10... | collective-permute-start | bytes 958472 | tf_op jit(solution)/shard_map/ppermute | solution.py:761
  431.1 33.7 %collective-permute-start.52 = (bf16[2,48,1664]{2,1,0:T(8,128)(2,1)}, bf16[2,48,1664]{2,1,0:T(8,128)(2,1)}, u32[]{:S(2)}, u32[]{:S(2)}) collective-permute-start(bf16[2,48,1664]{2,1,0:T(8,128)(2,1)} %get-tuple-element.491), channel_id=1, source_target_pairs={{0,8},{8,0},{16,24},{24,16},{1,9},{9,1},{17,25},{25,17},{2,10},{10... | collective-permute-start | bytes 958472 | tf_op jit(solution)/shard_map/ppermute | solution.py:761
  434.3 33.5 %collective-permute-start.53 = (bf16[3,192,256]{2,1,0:T(8,128)(2,1)S(1)}, bf16[3,192,256]{2,1,0:T(8,128)(2,1)S(1)}, u32[]{:S(2)}, u32[]{:S(2)}) collective-permute-start(bf16[3,192,256]{2,1,0:T(8,128)(2,1)S(1)} %get-tuple-element.523), channel_id=1, source_target_pairs={{0,8},{8,0},{16,24},{24,16},{1,9},{9,1},{17,25},{25,17},{2,10},{10... | collective-permute-start | bytes 884744 | tf_op jit(solution)/shard_map/ppermute | solution.py:917
  464.8 24.5 %collective-permute-start.61 = (bf16[128,1536]{1,0:T(8,128)(2,1)}, bf16[128,1536]{1,0:T(8,128)(2,1)}, u32[]{:S(2)}, u32[]{:S(2)}) collective-permute-start(bf16[128,1536]{1,0:T(8,128)(2,1)} %get-tuple-element.383), channel_id=1, source_target_pairs={{0,2},{2,4},{4,6},{6,0},{1,3},{3,5},{5,7},{7,1},{8,10},{10,12},{12... | collective-permute-start | bytes 1179656 | tf_op jit(solution)/shard_map/ppermute | solution.py:713
  464.8 34.2 %collective-permute-start.62 = (bf16[128,1536]{1,0:T(8,128)(2,1)}, bf16[128,1536]{1,0:T(8,128)(2,1)}, u32[]{:S(2)}, u32[]{:S(2)}) collective-permute-start(bf16[128,1536]{1,0:T(8,128)(2,1)} %get-tuple-element.384), channel_id=1, source_target_pairs={{0,4},{2,6},{4,0},{6,2},{1,5},{3,7},{5,1},{7,3},{8,12},{10,14},{12... | collective-permute-start | bytes 1179656 | tf_op jit(solution)/shard_map/ppermute | solution.py:713
  467.8 34.1 %collective-permute-start.63 = (bf16[128,1536]{1,0:T(8,128)(2,1)}, bf16[128,1536]{1,0:T(8,128)(2,1)}, u32[]{:S(2)}, u32[]{:S(2)}) collective-permute-start(bf16[128,1536]{1,0:T(8,128)(2,1)} %get-tuple-element.385), channel_id=1, source_target_pairs={{0,6},{2,0},{4,2},{6,4},{1,7},{3,1},{5,3},{7,5},{8,14},{10,8},{12,... | collective-permute-start | bytes 1179656 | tf_op jit(solution)/shard_map/ppermute | solution.py:713
  478.6 23.3 %collective-permute-start.59 = (bf16[4,48,1664]{2,1,0:T(8,128)(2,1)}, bf16[4,48,1664]{2,1,0:T(8,128)(2,1)}, u32[]{:S(2)}, u32[]{:S(2)}) collective-permute-start(bf16[4,48,1664]{2,1,0:T(8,128)(2,1)} %pad_maximum_fusion.14), channel_id=1, source_target_pairs={{0,8},{8,0},{16,24},{24,16},{1,9},{9,1},{17,25},{25,17},{2,10},{10... | collective-permute-start | bytes 1916936 | tf_op jit(solution)/shard_map/ppermute | solution.py:769
  479.6 22.3 %collective-permute-start.60 = (bf16[4,48,1664]{2,1,0:T(8,128)(2,1)}, bf16[4,48,1664]{2,1,0:T(8,128)(2,1)}, u32[]{:S(2)}, u32[]{:S(2)}) collective-permute-start(bf16[4,48,1664]{2,1,0:T(8,128)(2,1)} %pad_maximum_fusion.15), channel_id=1, source_target_pairs={{0,16},{8,24},{16,0},{24,8},{1,17},{9,25},{17,1},{25,9},{2,18},{10... | collective-permute-start | bytes 1916936 | tf_op jit(solution)/shard_map/ppermute | solution.py:769
  489.3 21.7 %collective-permute-start.68 = (bf16[256,1536]{1,0:T(8,128)(2,1)S(1)}, bf16[256,1536]{1,0:T(8,128)(2,1)S(1)}, u32[]{:S(2)}, u32[]{:S(2)}) collective-permute-start(bf16[256,1536]{1,0:T(8,128)(2,1)S(1)} %copy-done.33), channel_id=1, source_target_pairs={{0,8},{8,0},{16,24},{24,16},{1,9},{9,1},{17,25},{25,17},{2,10},{10... | collective-permute-start | bytes 2359304 | tf_op jit(solution)/shard_map/ppermute | solution.py:769
  498.9 18.6 %collective-permute-start.69 = (bf16[256,1536]{1,0:T(8,128)(2,1)S(1)}, bf16[256,1536]{1,0:T(8,128)(2,1)S(1)}, u32[]{:S(2)}, u32[]{:S(2)}) collective-permute-start(bf16[256,1536]{1,0:T(8,128)(2,1)S(1)} %copy-done.32), channel_id=1, source_target_pairs={{0,16},{8,24},{16,0},{24,8},{1,17},{9,25},{17,1},{25,9},{2,18},{10... | collective-permute-start | bytes 2359304 | tf_op jit(solution)/shard_map/ppermute | solution.py:769
  (89 other events, 812.4 us)
Sparse Core Ops, SparseCore 0:
  24.4 64.4 all-gather.3
  112.4 102.5 all-gather.5
  333.5 82.7 reduce-scatter.2
  420.4 39.8 reduce-scatter.4

commit v6 on v5

--- a/solution.py
+++ b/solution.py
@@ -358,7 +358,7 @@
                gate_w, up_w, down_w, mlp, dact):
     tokens = act_ref.shape[0]
     cores, chips, rows = own_ref.shape[1] + other_ref.shape[1], own_ref.shape[2], own_ref.shape[4]
-    tile = min(tokens, 256)
+    tile = min(tokens, 512)
 
     for r in range(chips):
         for n in range(cores):

time: 542 us -> 541 us (level)
  transfers between devices with their start and end apart: 74 -> 74, of which waited for: 31 -> 31; matrix products, arithmetic and copies ran while one was open for 17% -> 17% of each run, Pallas kernels for 32% -> 31%
where the time goes in v6:
time: 541 us; the launch traced here: 535 us
  Pallas kernels  181 us (33%)
  waiting for transfers between devices  159 us (29%)
  starting transfers between devices  73.3 us (14%)
  other arithmetic  60.9 us (11%)
  local copies, waits for them, and re-layouts  40 us (7%)
  between operations  15.3 us (3%)
  matrix products  5.57 us (1%)
    pallas_call x15, Pallas kernels, run(): pl.pallas_call(body, grid=(grid,), in_specs=in_specs, out_specs=out_specs...  181 us
    ppermute x15, waiting for transfers between devices, exchange(): lax.ppermute(sent, axis, [(i, (i + k) % count) for i in range(count)])  60.7 us
    ppermute x6, waiting for transfers between devices, exchange_rows(): lax.ppermute(sent[k - 1], axis, [(i, (i + k) % count) for i in range(coun...  36.2 us
    ppermute x15, starting transfers between devices, exchange(): lax.ppermute(sent, axis, [(i, (i + k) % count) for i in range(count)])  24.1 us
    convert_element_type x10, other arithmetic, add(): return total.astype(left.dtype)  16 us
    ppermute x4, waiting for transfers between devices, gather_near(): lax.ppermute(x, axis, pairs(4, 1))  12.3 us
  transfers between devices with their start and end apart: 74, of which 31 were waited for; matrix products, arithmetic and copies ran while one was open for 17% of the time, Pallas kernels for 31%

profile of v6, /device:TPU:8, one launch (start us, length us, event | category | flops | bytes accessed | tf_op | source)
XLA Modules:
  0.0 534.5 jit_solution(8835395164705440895)
XLA Ops:
  25.7 12.6 %collective-permute-done.2 = bf16[48,1664]{1,0:T(8,128)(2,1)S(1)} collective-permute-done((bf16[48,1664]{1,0:T(8,128)(2,1)}, bf16[48,1664]{1,0:T(8,128)(2,1)S(1)}, u32[]{:S(2)}, u32[]{:S(2)}) %collective-permute-start.2) | collective-permute-done | bytes 159776 | tf_op jit(solution)/shard_map/ppermute | solution.py:706
  38.2 10.2 %collective-permute-done.3 = bf16[48,1664]{1,0:T(8,128)(2,1)} collective-permute-done((bf16[48,1664]{1,0:T(8,128)(2,1)}, bf16[48,1664]{1,0:T(8,128)(2,1)}, u32[]{:S(2)}, u32[]{:S(2)}) %collective-permute-start.3) | collective-permute-done | bytes 159776 | tf_op jit(solution)/shard_map/ppermute | solution.py:706
  53.3 11.1 %collective-permute-done.7 = bf16[4,48,1664]{2,1,0:T(8,128)(2,1)S(1)} collective-permute-done((bf16[4,48,1664]{2,1,0:T(8,128)(2,1)S(1)}, bf16[4,48,1664]{2,1,0:T(8,128)(2,1)S(1)}, u32[]{:S(2)}, u32[]{:S(2)}) %collective-permute-start.7) | collective-permute-done | bytes 639008 | tf_op jit(solution)/shard_map/ppermute | solution.py:729
  67.0 4.5 collective-permute-done.10
  83.5 5.7 %collective-permute-done.18 = bf16[128,1536]{1,0:T(8,128)(2,1)S(1)} collective-permute-done((bf16[128,1536]{1,0:T(8,128)(2,1)S(1)}, bf16[128,1536]{1,0:T(8,128)(2,1)S(1)}, u32[]{:S(2)}, u32[]{:S(2)}) %collective-permute-start.18) | collective-permute-done | bytes 393248 | tf_op jit(solution)/shard_map/ppermute | solution.py:737
  94.4 2.2 collective-permute-start.16
  96.7 5.5 %shard_map.254 = (bf16[1536,1664]{1,0:T(8,128)(2,1)}, f32[128,1536]{1,0:T(8,128)}) custom-call(s32[3]{0:T(128)} %pad_add_fusion.3.me_ref, bf16[1,4,4,48,1664]{4,3,2,1,0:T(8,128)(2,1)} %bitcast.247, bf16[1,4,4,48,1664]{4,3,2,1,0:T(8,128)(2,1)} %bitcast.32.other_ref), custom_call_target="tpu_custom_call" | custom-call | bytes 11010060 | tf_op jit(solution)/shard_map/pallas_call | solution.py:254
  113.7 12.3 %shard_map.255 = (bf16[1024,1536]{1,0:T(8,128)(2,1)}, bf16[1024,384]{1,0:T(8,128)(2,1)}, bf16[1024,384]{1,0:T(8,128)(2,1)}, bf16[1024,384]{1,0:T(8,128)(2,1)}, f...) custom-call(f32[3]{0:T(128)} %dynamic-slice_convert_fusion.bias_ref, bf16[1024,1536]{1,0:T(8,128)(2,1)} %all-gather.4.cloned.1.call-done.x_ref, ...), custom_call_target="tpu_custom_call" | custom-call | flops 5234491392 | bytes 15353868 | tf_op jit(solution)/shard_map/pallas_call | solution.py:254
  128.6 17.7 %shard_map.256 = (bf16[1024,384]{1,0:T(8,128)(2,1)}, bf16[1024,384]{1,0:T(8,128)(2,1)}, bf16[1024,384]{1,0:T(8,128)(2,1)}, bf16[1024,384]{1,0:T(8,128)(2,1)}, f3...) custom-call(bf16[1024,384]{1,0:T(8,128)(2,1)} %get-tuple-element.247, ...), custom_call_target="tpu_custom_call" | custom-call | flops 6241124352 | bytes 14168064 | tf_op jit(solution)/shard_map/pallas_call | solution.py:254
  146.3 16.9 %shard_map.257 = (bf16[1024,384]{1,0:T(8,128)(2,1)}, bf16[8,3,128,1024]{3,2,1,0:T(8,128)(2,1)}, bf16[8,3,1024,128]{3,2,1,0:T(8,128)(2,1)}) custom-call(bf16[1024,384]{1,0:T(8,128)(2,1)} %get-tuple-element.260.qin_ref, bf16[1024,384]{1,0:T(8,128)(2,1)} %get-tuple-element.261.kout_ref, bf16[1024,384]{1,0:T(8,128)(2,1)} %get-tuple-element.262.ptop_ref, ...), custom_call_target="tpu_custom_call" | custom-call | flops 3221225472 | bytes 18882560 | tf_op jit(solution)/shard_map/pallas_call | solution.py:254
  165.6 3.9 collective-permute-start.25
  171.4 5.0 shard_map.258
  176.5 9.7 %collective-permute-done.24 = bf16[256,384]{1,0:T(8,128)(2,1)S(1)} collective-permute-done((bf16[256,384]{1,0:T(8,128)(2,1)S(1)}, bf16[256,384]{1,0:T(8,128)(2,1)S(1)}, u32[]{:S(2)}, u32[]{:S(2)}) %collective-permute-start.24) | collective-permute-done | bytes 196640 | tf_op jit(solution)/shard_map/ppermute | solution.py:706
  186.2 17.8 %collective-permute-done.25 = bf16[256,384]{1,0:T(8,128)(2,1)S(1)} collective-permute-done((bf16[256,384]{1,0:T(8,128)(2,1)S(1)}, bf16[256,384]{1,0:T(8,128)(2,1)S(1)}, u32[]{:S(2)}, u32[]{:S(2)}) %collective-permute-start.25) | collective-permute-done | bytes 196640 | tf_op jit(solution)/shard_map/ppermute | solution.py:706
  204.0 3.1 collective-permute-done.26
  211.5 3.4 all-gather.6.cloned.1.call-done
  218.8 4.5 collective-permute-done.29
  223.2 10.6 %shard_map.259 = (bf16[256,1536]{1,0:T(8,128)(2,1)}, bf16[256,1536]{1,0:T(8,128)(2,1)}, bf16[256,1024]{1,0:T(8,128)(2,1)}, bf16[256,1024]{1,0:T(8,128)(2,1)}, bf16[256,1024]{1,0:T(8,128)(2,1)}) custom-call(s32[2]{0:T(128)} %pad_add_fusion.4.me_ref, bf16[256,1536]{1,0:T(8,128)(2,1)} %copy-done.34, bf16[256,1536]{1,0:T(8,128)(2,1)} %bitcast.252, ...), custom_call_target="tpu_custom_call" | custom-call | flops 4831838208 | bytes 14155784 | tf_op jit(solution)/shard_map/pallas_call | solution.py:254
  239.8 17.0 %shard_map.260 = (bf16[512,1536]{1,0:T(8,128)(2,1)}, bf16[512,1536]{1,0:T(8,128)(2,1)}, bf16[512,1024]{1,0:T(8,128)(2,1)}, bf16[512,1024]{1,0:T(8,128)(2,1)}, bf16[512,1024]{1,0:T(8,128)(2,1)}) custom-call(s32[2]{0:T(128)} %pad_add_fusion.4.me_ref, bf16[512,1536]{1,0:T(8,128)(2,1)} %copy-done.39, bf16[512,1536]{1,0:T(8,128)(2,1)} %pad_maximum_fusion.grad_ref.refs_6_, ...), custom_call_target="tpu_custom_call" | custom-call | flops 9663676416 | bytes 18874376 | tf_op jit(solution)/shard_map/pallas_call | solution.py:254
  257.8 10.5 %shard_map.261 = (bf16[256,1536]{1,0:T(8,128)(2,1)}, bf16[256,1536]{1,0:T(8,128)(2,1)}, bf16[256,1024]{1,0:T(8,128)(2,1)}, bf16[256,1024]{1,0:T(8,128)(2,1)}, bf16[256,1024]{1,0:T(8,128)(2,1)}) custom-call(s32[2]{0:T(128)} %pad_add_fusion.4.me_ref, bf16[256,1536]{1,0:T(8,128)(2,1)} %copy-done.44, bf16[256,1536]{1,0:T(8,128)(2,1)} %pad_maximum_fusion.3.grad_ref.refs_11_, ...), custom_call_target="tpu_custom_call" | custom-call | flops 4831838208 | bytes 14155784 | tf_op jit(solution)/shard_map/pallas_call | solution.py:254
  271.8 7.7 %collective-permute-done.34 = bf16[128,1536]{1,0:T(8,128)(2,1)S(1)} collective-permute-done((bf16[128,1536]{1,0:T(8,128)(2,1)S(1)}, bf16[128,1536]{1,0:T(8,128)(2,1)S(1)}, u32[]{:S(2)}, u32[]{:S(2)}) %collective-permute-start.34) | collective-permute-done | bytes 393248 | tf_op jit(solution)/shard_map/ppermute | solution.py:761
  283.1 16.0 %shard_map.262 = (bf16[4,1,4,3,192,256]{5,4,3,2,1,0:T(8,128)(2,1)}, bf16[4,1,4,3,192,256]{5,4,3,2,1,0:T(8,128)(2,1)}) custom-call(s32[2]{0:T(128)} %pad_add_fusion.4.me_ref, bf16[256,1536]{1,0:T(8,128)(2,1)} %copy-done.34, bf16[256,1536]{1,0:T(8,128)(2,1)} %bitcast.253, bf16[256,1024]{1,0:T(8,128)(2,1)} %get-tuple-element.325.refs_2_, ...), custom_call_target="tpu_custom_call" | custom-call | flops 9663676416 | bytes 22020104 | tf_op jit(solution)/shard_map/pallas_call | solution.py:254
  301.1 4.1 convolution_convert_fusion
  308.6 2.3 collective-permute-start.39
  310.9 4.5 collective-permute-start.40
  316.1 5.3 shard_map.263
  321.4 6.5 %fusion.1 = bf16[4,4,3,192,256]{4,3,2,1,0:T(8,128)(2,1)} fusion(bf16[1,4,4,3,192,256]{5,4,3,2,1,0:T(8,128)(2,1)} %collective-permute-done.42, bf16[4,1,4,3,192,256]{5,4,3,2,1,0:T(8,128)(2,1)S(1)} %bitcast.251), kind=kLoop, calls=%fused_computation.3 | loop fusion | flops 9437184 | bytes 14155776 | tf_op jit(solution)/shard_map/squeeze | solution.py:888
  328.4 4.0 collective-permute-done.41
  337.4 2.4 add_convert_fusion.1
  341.9 20.9 %shard_map.264 = (f32[1024,384]{1,0:T(8,128)}, bf16[1024,384]{1,0:T(8,128)(2,1)}, f32[1024,384]{1,0:T(8,128)}, f32[1024,384]{1,0:T(8,128)}, bf16[1024,384]{1,0:T(8,128)(2,1)}) custom-call(bf16[1024,384]{1,0:T(8,128)(2,1)} %pad_maximum_fusion.9.grad_ref, bf16[1024,384]{1,0:T(8,128)(2,1)} %get-tuple-element.265.v_ref, ...), custom_call_target="tpu_custom_call" | custom-call | flops 5637144576 | bytes 22806528 | tf_op jit(solution)/shard_map/pallas_call | solution.py:254
  369.6 18.8 %shard_map.265.right_ref = bf16[1024,1664]{1,0:T(8,128)(2,1)} custom-call(bf16[1024,384]{1,0:T(8,128)(2,1)} %get-tuple-element.247.q_ref, bf16[1024,384]{1,0:T(8,128)(2,1)} %get-tuple-element.248.k_ref, f32[1024,384]{1,0:T(8,128)} %get-tuple-element.254.raw_ref, f32[8,3,128]{2,1,0:T(4,128)} %get-tuple-element.255.logit_ref, ...), custom_call_target="tpu_custom_call" | custom-call | flops 6039797760 | bytes 19148800 | tf_op jit(solution)/shard_map/pallas_call | solution.py:254
  390.0 19.1 %shard_map.266 = (bf16[1024,1536]{1,0:T(8,128)(2,1)}, bf16[1,4,4,48,1664]{4,3,2,1,0:T(8,128)(2,1)}, bf16[1,4,4,48,1664]{4,3,2,1,0:T(8,128)(2,1)}) custom-call(s32[3]{0:T(128)} %pad_add_fusion.1.me_ref, f32[3]{0:T(128)} %convert_reduce_fusion.bias_ref, bf16[1024,1536]{1,0:T(8,128)(2,1)} %get-tuple-element.363.left_ref, ...), custom_call_target="tpu_custom_call" | custom-call | flops 10468982784 | bytes 19929112 | tf_op jit(solution)/shard_map/pallas_call | solution.py:254
  410.3 3.2 fusion.34
  414.7 2.3 collective-permute-start.58
  417.0 2.3 fusion.13
  419.3 2.7 dynamic-slice_bitcast_fusion.1
  422.0 2.2 add_convert_fusion.5
  424.2 2.4 add_convert_fusion
  434.2 24.8 %collective-permute-done.57 = bf16[128,1536]{1,0:T(8,128)(2,1)} collective-permute-done((bf16[128,1536]{1,0:T(8,128)(2,1)}, bf16[128,1536]{1,0:T(8,128)(2,1)}, u32[]{:S(2)}, u32[]{:S(2)}) %collective-permute-start.57) | collective-permute-done | bytes 393248 | tf_op jit(solution)/shard_map/ppermute | solution.py:713
  463.8 3.0 collective-permute-start.62
  468.8 5.3 collective-permute-done.54.refs_2_
  481.3 2.9 shard_map.268
  484.2 2.5 copy.102
  489.4 8.6 %collective-permute-done.62 = bf16[128,1536]{1,0:T(8,128)(2,1)} collective-permute-done((bf16[128,1536]{1,0:T(8,128)(2,1)}, bf16[128,1536]{1,0:T(8,128)(2,1)}, u32[]{:S(2)}, u32[]{:S(2)}) %collective-permute-start.62) | collective-permute-done | bytes 393248 | tf_op jit(solution)/shard_map/ppermute | solution.py:713
  498.2 2.8 collective-permute-done.63
  510.1 6.6 %collective-permute-done.69 = bf16[256,1536]{1,0:T(8,128)(2,1)S(1)} collective-permute-done((bf16[256,1536]{1,0:T(8,128)(2,1)S(1)}, bf16[256,1536]{1,0:T(8,128)(2,1)S(1)}, u32[]{:S(2)}, u32[]{:S(2)}) %collective-permute-start.69) | collective-permute-done | bytes 786464 | tf_op jit(solution)/shard_map/ppermute | solution.py:769
  516.7 2.2 add_convert_fusion.2
  520.7 2.3 shard_map.267
  (388 shorter events, 147.4 us)
Async XLA Ops:
  7.2 100.2 %all-gather.4.cloned.1.call-start = ((), (), s32[]{:S(2)}) async-start(), calls=%async_computation.2 | async-start | bytes 3932160 | tf_op jit(solution)/shard_map/all_gather | solution.py:803
  14.0 34.6 %collective-permute-start.5 = (bf16[256,1536]{1,0:T(8,128)(2,1)S(1)}, bf16[256,1536]{1,0:T(8,128)(2,1)S(1)}, u32[]{:S(2)}, u32[]{:S(2)}) collective-permute-start(bf16[256,1536]{1,0:T(8,128)(2,1)S(1)} %bitcast.254), channel_id=1, source_target_pairs={{0,8},{8,0},{16,24},{24,16},{1,9},{9,1},{17,25},{25,17},{2,10},{10... | collective-permute-start | bytes 2359304 | tf_op jit(solution)/shard_map/ppermute | solution.py:729
  15.4 33.1 %collective-permute-start.6 = (bf16[256,1536]{1,0:T(8,128)(2,1)S(1)}, bf16[256,1536]{1,0:T(8,128)(2,1)S(1)}, u32[]{:S(2)}, u32[]{:S(2)}) collective-permute-start(bf16[256,1536]{1,0:T(8,128)(2,1)S(1)} %bitcast.255), channel_id=1, source_target_pairs={{0,16},{8,24},{16,0},{24,8},{1,17},{9,25},{17,1},{25,9},{2,18},{10... | collective-permute-start | bytes 2359304 | tf_op jit(solution)/shard_map/ppermute | solution.py:729
  19.7 18.6 %collective-permute-start.2 = (bf16[48,1664]{1,0:T(8,128)(2,1)}, bf16[48,1664]{1,0:T(8,128)(2,1)S(1)}, u32[]{:S(2)}, u32[]{:S(2)}) collective-permute-start(bf16[48,1664]{1,0:T(8,128)(2,1)} %get-tuple-element.562), channel_id=1, source_target_pairs={{0,2},{2,4},{4,6},{6,0},{1,3},{3,5},{5,7},{7,1},{8,10},{10,12},{12... | collective-permute-start | bytes 479240 | tf_op jit(solution)/shard_map/ppermute | solution.py:706
  21.2 27.2 %collective-permute-start.3 = (bf16[48,1664]{1,0:T(8,128)(2,1)}, bf16[48,1664]{1,0:T(8,128)(2,1)}, u32[]{:S(2)}, u32[]{:S(2)}) collective-permute-start(bf16[48,1664]{1,0:T(8,128)(2,1)} %get-tuple-element.561), channel_id=1, source_target_pairs={{0,4},{2,6},{4,0},{6,2},{1,5},{3,7},{5,1},{7,3},{8,12},{10,14},{12... | collective-permute-start | bytes 479240 | tf_op jit(solution)/shard_map/ppermute | solution.py:706
  22.5 26.1 %collective-permute-start.4 = (bf16[48,1664]{1,0:T(8,128)(2,1)}, bf16[48,1664]{1,0:T(8,128)(2,1)}, u32[]{:S(2)}, u32[]{:S(2)}) collective-permute-start(bf16[48,1664]{1,0:T(8,128)(2,1)} %get-tuple-element.560), channel_id=1, source_target_pairs={{0,6},{2,0},{4,2},{6,4},{1,7},{3,1},{5,3},{7,5},{8,14},{10,8},{12,... | collective-permute-start | bytes 479240 | tf_op jit(solution)/shard_map/ppermute | solution.py:706
  24.3 190.7 %all-gather.6.cloned.1.call-start = ((), (), s32[]{:S(2)}) async-start(), calls=%async_computation.5 | async-start | bytes 5898240 | tf_op jit(solution)/shard_map/all_gather | solution.py:838
  73.3 21.1 %collective-permute-start.11 = (bf16[4,4,48,1664]{3,2,1,0:T(8,128)(2,1)S(1)}, bf16[4,4,48,1664]{3,2,1,0:T(8,128)(2,1)}, u32[]{:S(2)}, u32[]{:S(2)}) collective-permute-start(bf16[4,4,48,1664]{3,2,1,0:T(8,128)(2,1)S(1)} %fusion.14), channel_id=1, source_target_pairs={{0,1},{1,0},{2,3},{3,2},{4,5},{5,4},{6,7},{7,6},{8,9},{9,8},{10,11... | collective-permute-start | bytes 7667720 | tf_op jit(solution)/shard_map/ppermute | solution.py:774
  75.0 27.1 %collective-permute-start.15 = (bf16[48,1536]{1,0:T(8,128)(2,1)}, bf16[48,1536]{1,0:T(8,128)(2,1)}, u32[]{:S(2)}, u32[]{:S(2)}) collective-permute-start(bf16[48,1536]{1,0:T(8,128)(2,1)} %param.25), channel_id=1, source_target_pairs={{0,2},{2,4},{4,6},{6,0},{1,3},{3,5},{5,7},{7,1},{8,10},{10,12},{12... | collective-permute-start | bytes 442376 | tf_op jit(solution)/shard_map/ppermute | solution.py:706
  82.1 25.3 %collective-permute-start.12 = (bf16[3,192,256]{2,1,0:T(8,128)(2,1)S(1)}, bf16[3,192,256]{2,1,0:T(8,128)(2,1)S(1)}, u32[]{:S(2)}, u32[]{:S(2)}) collective-permute-start(bf16[3,192,256]{2,1,0:T(8,128)(2,1)S(1)} %get-tuple-element.531), channel_id=1, source_target_pairs={{0,8},{8,0},{16,24},{24,16},{1,9},{9,1},{17,25},{25,17},{2,10},{10... | collective-permute-start | bytes 884744 | tf_op jit(solution)/shard_map/ppermute | solution.py:832
  89.2 18.1 %collective-permute-start.13 = (bf16[3,192,256]{2,1,0:T(8,128)(2,1)S(1)}, bf16[3,192,256]{2,1,0:T(8,128)(2,1)S(1)}, u32[]{:S(2)}, u32[]{:S(2)}) collective-permute-start(bf16[3,192,256]{2,1,0:T(8,128)(2,1)S(1)} %get-tuple-element.530), channel_id=1, source_target_pairs={{0,16},{8,24},{16,0},{24,8},{1,17},{9,25},{17,1},{25,9},{2,18},{10... | collective-permute-start | bytes 884744 | tf_op jit(solution)/shard_map/ppermute | solution.py:832
  108.4 17.6 %collective-permute-start.20 = (bf16[4,48,1536]{2,1,0:T(8,128)(2,1)S(1)}, bf16[4,48,1536]{2,1,0:T(8,128)(2,1)S(1)}, u32[]{:S(2)}, u32[]{:S(2)}) collective-permute-start(bf16[4,48,1536]{2,1,0:T(8,128)(2,1)S(1)} %pad_maximum_fusion.16), channel_id=1, source_target_pairs={{0,8},{8,0},{16,24},{24,16},{1,9},{9,1},{17,25},{25,17},{2,10},{10... | collective-permute-start | bytes 1769480 | tf_op jit(solution)/shard_map/ppermute | solution.py:729
  112.2 319.0 %reduce-scatter.3.cloned.1.call-start = ((), (), s32[]{:S(2)}) async-start(), calls=%async_computation.3 | async-start | bytes 5898240 | tf_op jit(solution)/shard_map/reduce_scatter | solution.py:891
  126.0 37.2 %collective-permute-start.22 = (bf16[2,48,1536]{2,1,0:T(8,128)(2,1)S(1)}, bf16[2,48,1536]{2,1,0:T(8,128)(2,1)S(1)}, u32[]{:S(2)}, u32[]{:S(2)}) collective-permute-start(bf16[2,48,1536]{2,1,0:T(8,128)(2,1)S(1)} %slice.379), channel_id=1, source_target_pairs={{0,16},{8,24},{16,0},{24,8},{1,17},{9,25},{17,1},{25,9},{2,18},{10... | collective-permute-start | bytes 884744 | tf_op jit(solution)/shard_map/ppermute | solution.py:737
  127.8 35.4 %collective-permute-start.23 = (bf16[2,48,1536]{2,1,0:T(8,128)(2,1)S(1)}, bf16[2,48,1536]{2,1,0:T(8,128)(2,1)S(1)}, u32[]{:S(2)}, u32[]{:S(2)}) collective-permute-start(bf16[2,48,1536]{2,1,0:T(8,128)(2,1)S(1)} %slice.380), channel_id=1, source_target_pairs={{0,8},{8,0},{16,24},{24,16},{1,9},{9,1},{17,25},{25,17},{2,10},{10... | collective-permute-start | bytes 884744 | tf_op jit(solution)/shard_map/ppermute | solution.py:737
  164.8 21.3 %collective-permute-start.24 = (bf16[256,384]{1,0:T(8,128)(2,1)S(1)}, bf16[256,384]{1,0:T(8,128)(2,1)S(1)}, u32[]{:S(2)}, u32[]{:S(2)}) collective-permute-start(bf16[256,384]{1,0:T(8,128)(2,1)S(1)} %get-tuple-element.555), channel_id=1, source_target_pairs={{0,2},{2,4},{4,6},{6,0},{1,3},{3,5},{5,7},{7,1},{8,10},{10,12},{12... | collective-permute-start | bytes 589832 | tf_op jit(solution)/shard_map/ppermute | solution.py:706
  165.6 38.4 %collective-permute-start.25 = (bf16[256,384]{1,0:T(8,128)(2,1)S(1)}, bf16[256,384]{1,0:T(8,128)(2,1)S(1)}, u32[]{:S(2)}, u32[]{:S(2)}) collective-permute-start(bf16[256,384]{1,0:T(8,128)(2,1)S(1)} %get-tuple-element.554), channel_id=1, source_target_pairs={{0,4},{2,6},{4,0},{6,2},{1,5},{3,7},{5,1},{7,3},{8,12},{10,14},{12... | collective-permute-start | bytes 589832 | tf_op jit(solution)/shard_map/ppermute | solution.py:706
  169.5 37.6 %collective-permute-start.26 = (bf16[256,384]{1,0:T(8,128)(2,1)S(1)}, bf16[256,384]{1,0:T(8,128)(2,1)S(1)}, u32[]{:S(2)}, u32[]{:S(2)}) collective-permute-start(bf16[256,384]{1,0:T(8,128)(2,1)S(1)} %get-tuple-element.552), channel_id=1, source_target_pairs={{0,6},{2,0},{4,2},{6,4},{1,7},{3,1},{5,3},{7,5},{8,14},{10,8},{12,... | collective-permute-start | bytes 589832 | tf_op jit(solution)/shard_map/ppermute | solution.py:706
  215.0 19.9 %collective-permute-start.30 = (bf16[256,1536]{1,0:T(8,128)(2,1)S(1)}, bf16[256,1536]{1,0:T(8,128)(2,1)S(1)}, u32[]{:S(2)}, u32[]{:S(2)}) collective-permute-start(bf16[256,1536]{1,0:T(8,128)(2,1)S(1)} %multiply_convert_fusion.act_ref.refs_0_), channel_id=1, source_target_pairs={{0,8},{8,0},{16,24},{24,16},{1,9},{9,1},{17,25},{25,17},{2,10},{10... | collective-permute-start | bytes 2359304 | tf_op jit(solution)/shard_map/ppermute | solution.py:729
  216.7 19.6 %collective-permute-start.31 = (bf16[256,1536]{1,0:T(8,128)(2,1)S(1)}, bf16[256,1536]{1,0:T(8,128)(2,1)S(1)}, u32[]{:S(2)}, u32[]{:S(2)}) collective-permute-start(bf16[256,1536]{1,0:T(8,128)(2,1)S(1)} %multiply_convert_fusion.act_ref.refs_0_), channel_id=1, source_target_pairs={{0,16},{8,24},{16,0},{24,8},{1,17},{9,25},{17,1},{25,9},{2,18},{10... | collective-permute-start | bytes 2359304 | tf_op jit(solution)/shard_map/ppermute | solution.py:729
  236.4 20.4 %collective-permute-start.32 = (bf16[128,1536]{1,0:T(8,128)(2,1)S(1)}, bf16[128,1536]{1,0:T(8,128)(2,1)S(1)}, u32[]{:S(2)}, u32[]{:S(2)}) collective-permute-start(bf16[128,1536]{1,0:T(8,128)(2,1)S(1)} %slice.386), channel_id=1, source_target_pairs={{0,16},{8,24},{16,0},{24,8},{1,17},{9,25},{17,1},{25,9},{2,18},{10... | collective-permute-start | bytes 1179656 | tf_op jit(solution)/shard_map/ppermute | solution.py:737
  238.0 18.9 %collective-permute-start.33 = (bf16[128,1536]{1,0:T(8,128)(2,1)S(1)}, bf16[128,1536]{1,0:T(8,128)(2,1)S(1)}, u32[]{:S(2)}, u32[]{:S(2)}) collective-permute-start(bf16[128,1536]{1,0:T(8,128)(2,1)S(1)} %slice.387), channel_id=1, source_target_pairs={{0,8},{8,0},{16,24},{24,16},{1,9},{9,1},{17,25},{25,17},{2,10},{10... | collective-permute-start | bytes 1179656 | tf_op jit(solution)/shard_map/ppermute | solution.py:737
  280.2 18.9 %collective-permute-start.36 = (bf16[256,1536]{1,0:T(8,128)(2,1)S(1)}, bf16[256,1536]{1,0:T(8,128)(2,1)S(1)}, u32[]{:S(2)}, u32[]{:S(2)}) collective-permute-start(bf16[256,1536]{1,0:T(8,128)(2,1)S(1)} %pad_maximum_fusion.6), channel_id=1, source_target_pairs={{0,8},{8,0},{16,24},{24,16},{1,9},{9,1},{17,25},{25,17},{2,10},{10... | collective-permute-start | bytes 2359304 | tf_op jit(solution)/shard_map/ppermute | solution.py:769
  281.7 17.4 %collective-permute-start.37 = (bf16[256,1536]{1,0:T(8,128)(2,1)S(1)}, bf16[256,1536]{1,0:T(8,128)(2,1)S(1)}, u32[]{:S(2)}, u32[]{:S(2)}) collective-permute-start(bf16[256,1536]{1,0:T(8,128)(2,1)S(1)} %pad_maximum_fusion.7), channel_id=1, source_target_pairs={{0,16},{8,24},{16,0},{24,8},{1,17},{9,25},{17,1},{25,9},{2,18},{10... | collective-permute-start | bytes 2359304 | tf_op jit(solution)/shard_map/ppermute | solution.py:769
  299.1 22.3 %collective-permute-start.42 = (bf16[1,4,4,3,192,256]{5,4,3,2,1,0:T(8,128)(2,1)}, bf16[1,4,4,3,192,256]{5,4,3,2,1,0:T(8,128)(2,1)}, u32[]{:S(2)}, u32[]{:S(2)}) collective-permute-start(bf16[1,4,4,3,192,256]{5,4,3,2,1,0:T(8,128)(2,1)} %bitcast.285), channel_id=1, source_target_pairs={{0,1},{1,0},{2,3},{3,2},{4,5},{5,4},{6,7},{7,6},{8,9},{9,8},{10,11... | collective-permute-start | bytes 14155784 | tf_op jit(solution)/shard_map/ppermute | solution.py:779
  308.6 19.3 %collective-permute-start.39 = (bf16[256,384]{1,0:T(8,128)(2,1)}, bf16[256,384]{1,0:T(8,128)(2,1)S(1)}, u32[]{:S(2)}, u32[]{:S(2)}) collective-permute-start(bf16[256,384]{1,0:T(8,128)(2,1)} %get-tuple-element.544), channel_id=1, source_target_pairs={{0,2},{2,4},{4,6},{6,0},{1,3},{3,5},{5,7},{7,1},{8,10},{10,12},{12... | collective-permute-start | bytes 589832 | tf_op jit(solution)/shard_map/ppermute | solution.py:706
  310.9 17.5 %collective-permute-start.40 = (bf16[256,384]{1,0:T(8,128)(2,1)}, bf16[256,384]{1,0:T(8,128)(2,1)}, u32[]{:S(2)}, u32[]{:S(2)}) collective-permute-start(bf16[256,384]{1,0:T(8,128)(2,1)} %get-tuple-element.543), channel_id=1, source_target_pairs={{0,4},{2,6},{4,0},{6,2},{1,5},{3,7},{5,1},{7,3},{8,12},{10,14},{12... | collective-permute-start | bytes 589832 | tf_op jit(solution)/shard_map/ppermute | solution.py:706
  316.1 16.3 %collective-permute-start.41 = (bf16[256,384]{1,0:T(8,128)(2,1)}, bf16[256,384]{1,0:T(8,128)(2,1)}, u32[]{:S(2)}, u32[]{:S(2)}) collective-permute-start(bf16[256,384]{1,0:T(8,128)(2,1)} %get-tuple-element.541), channel_id=1, source_target_pairs={{0,6},{2,0},{4,2},{6,4},{1,7},{3,1},{5,3},{7,5},{8,14},{10,8},{12,... | collective-permute-start | bytes 589832 | tf_op jit(solution)/shard_map/ppermute | solution.py:706
  332.4 147.2 %reduce-scatter.5.cloned.1.call-start = ((), (), s32[]{:S(2)}) async-start(), calls=%async_computation.4 | async-start | bytes 737280 | tf_op jit(solution)/shard_map/reduce_scatter | solution.py:912
  339.9 22.9 %collective-permute-start.44 = (bf16[2,48,1536]{2,1,0:T(8,128)(2,1)S(1)}, bf16[2,48,1536]{2,1,0:T(8,128)(2,1)S(1)}, u32[]{:S(2)}, u32[]{:S(2)}) collective-permute-start(bf16[2,48,1536]{2,1,0:T(8,128)(2,1)S(1)} %get-tuple-element.496), channel_id=1, source_target_pairs={{0,16},{8,24},{16,0},{24,8},{1,17},{9,25},{17,1},{25,9},{2,18},{10... | collective-permute-start | bytes 884744 | tf_op jit(solution)/shard_map/ppermute | solution.py:761
  340.9 21.9 %collective-permute-start.45 = (bf16[2,48,1536]{2,1,0:T(8,128)(2,1)S(1)}, bf16[2,48,1536]{2,1,0:T(8,128)(2,1)S(1)}, u32[]{:S(2)}, u32[]{:S(2)}) collective-permute-start(bf16[2,48,1536]{2,1,0:T(8,128)(2,1)S(1)} %get-tuple-element.498), channel_id=1, source_target_pairs={{0,8},{8,0},{16,24},{24,16},{1,9},{9,1},{17,25},{25,17},{2,10},{10... | collective-permute-start | bytes 884744 | tf_op jit(solution)/shard_map/ppermute | solution.py:761
  364.7 44.4 %collective-permute-start.46 = (bf16[4,48,1536]{2,1,0:T(8,128)(2,1)}, bf16[4,48,1536]{2,1,0:T(8,128)(2,1)}, u32[]{:S(2)}, u32[]{:S(2)}) collective-permute-start(bf16[4,48,1536]{2,1,0:T(8,128)(2,1)} %pad_maximum_fusion.17), channel_id=1, source_target_pairs={{0,8},{8,0},{16,24},{24,16},{1,9},{9,1},{17,25},{25,17},{2,10},{10... | collective-permute-start | bytes 1769480 | tf_op jit(solution)/shard_map/ppermute | solution.py:769
  365.7 43.5 %collective-permute-start.47 = (bf16[4,48,1536]{2,1,0:T(8,128)(2,1)}, bf16[4,48,1536]{2,1,0:T(8,128)(2,1)}, u32[]{:S(2)}, u32[]{:S(2)}) collective-permute-start(bf16[4,48,1536]{2,1,0:T(8,128)(2,1)} %pad_maximum_fusion.18), channel_id=1, source_target_pairs={{0,16},{8,24},{16,0},{24,8},{1,17},{9,25},{17,1},{25,9},{2,18},{10... | collective-permute-start | bytes 1769480 | tf_op jit(solution)/shard_map/ppermute | solution.py:769
  367.6 41.5 %collective-permute-start.48 = (bf16[128,1536]{1,0:T(8,128)(2,1)}, bf16[128,1536]{1,0:T(8,128)(2,1)S(1)}, u32[]{:S(2)}, u32[]{:S(2)}) collective-permute-start(bf16[128,1536]{1,0:T(8,128)(2,1)} %get-tuple-element.536), channel_id=1, source_target_pairs={{0,16},{8,24},{16,0},{24,8},{1,17},{9,25},{17,1},{25,9},{2,18},{10... | collective-permute-start | bytes 1179656 | tf_op jit(solution)/shard_map/ppermute | solution.py:761
  368.6 40.6 %collective-permute-start.49 = (bf16[128,1536]{1,0:T(8,128)(2,1)S(1)}, bf16[128,1536]{1,0:T(8,128)(2,1)S(1)}, u32[]{:S(2)}, u32[]{:S(2)}) collective-permute-start(bf16[128,1536]{1,0:T(8,128)(2,1)S(1)} %get-tuple-element.535), channel_id=1, source_target_pairs={{0,8},{8,0},{16,24},{24,16},{1,9},{9,1},{17,25},{25,17},{2,10},{10... | collective-permute-start | bytes 1179656 | tf_op jit(solution)/shard_map/ppermute | solution.py:761
  414.7 18.7 %collective-permute-start.56 = (bf16[128,1536]{1,0:T(8,128)(2,1)}, bf16[128,1536]{1,0:T(8,128)(2,1)}, u32[]{:S(2)}, u32[]{:S(2)}) collective-permute-start(bf16[128,1536]{1,0:T(8,128)(2,1)} %get-tuple-element.376), channel_id=1, source_target_pairs={{0,2},{2,4},{4,6},{6,0},{1,3},{3,5},{5,7},{7,1},{8,10},{10,12},{12... | collective-permute-start | bytes 1179656 | tf_op jit(solution)/shard_map/ppermute | solution.py:713
  414.7 44.3 %collective-permute-start.57 = (bf16[128,1536]{1,0:T(8,128)(2,1)}, bf16[128,1536]{1,0:T(8,128)(2,1)}, u32[]{:S(2)}, u32[]{:S(2)}) collective-permute-start(bf16[128,1536]{1,0:T(8,128)(2,1)} %get-tuple-element.377), channel_id=1, source_target_pairs={{0,4},{2,6},{4,0},{6,2},{1,5},{3,7},{5,1},{7,3},{8,12},{10,14},{12... | collective-permute-start | bytes 1179656 | tf_op jit(solution)/shard_map/ppermute | solution.py:713
  414.7 45.2 %collective-permute-start.58 = (bf16[128,1536]{1,0:T(8,128)(2,1)}, bf16[128,1536]{1,0:T(8,128)(2,1)}, u32[]{:S(2)}, u32[]{:S(2)}) collective-permute-start(bf16[128,1536]{1,0:T(8,128)(2,1)} %get-tuple-element.378), channel_id=1, source_target_pairs={{0,6},{2,0},{4,2},{6,4},{1,7},{3,1},{5,3},{7,5},{8,14},{10,8},{12,... | collective-permute-start | bytes 1179656 | tf_op jit(solution)/shard_map/ppermute | solution.py:713
  429.2 34.7 %collective-permute-start.51 = (bf16[2,48,1664]{2,1,0:T(8,128)(2,1)}, bf16[2,48,1664]{2,1,0:T(8,128)(2,1)}, u32[]{:S(2)}, u32[]{:S(2)}) collective-permute-start(bf16[2,48,1664]{2,1,0:T(8,128)(2,1)} %get-tuple-element.490), channel_id=1, source_target_pairs={{0,16},{8,24},{16,0},{24,8},{1,17},{9,25},{17,1},{25,9},{2,18},{10... | collective-permute-start | bytes 958472 | tf_op jit(solution)/shard_map/ppermute | solution.py:761
  430.1 33.7 %collective-permute-start.52 = (bf16[2,48,1664]{2,1,0:T(8,128)(2,1)}, bf16[2,48,1664]{2,1,0:T(8,128)(2,1)}, u32[]{:S(2)}, u32[]{:S(2)}) collective-permute-start(bf16[2,48,1664]{2,1,0:T(8,128)(2,1)} %get-tuple-element.491), channel_id=1, source_target_pairs={{0,8},{8,0},{16,24},{24,16},{1,9},{9,1},{17,25},{25,17},{2,10},{10... | collective-permute-start | bytes 958472 | tf_op jit(solution)/shard_map/ppermute | solution.py:761
  433.4 33.5 %collective-permute-start.53 = (bf16[3,192,256]{2,1,0:T(8,128)(2,1)S(1)}, bf16[3,192,256]{2,1,0:T(8,128)(2,1)S(1)}, u32[]{:S(2)}, u32[]{:S(2)}) collective-permute-start(bf16[3,192,256]{2,1,0:T(8,128)(2,1)S(1)} %get-tuple-element.523), channel_id=1, source_target_pairs={{0,8},{8,0},{16,24},{24,16},{1,9},{9,1},{17,25},{25,17},{2,10},{10... | collective-permute-start | bytes 884744 | tf_op jit(solution)/shard_map/ppermute | solution.py:917
  463.8 24.5 %collective-permute-start.61 = (bf16[128,1536]{1,0:T(8,128)(2,1)}, bf16[128,1536]{1,0:T(8,128)(2,1)}, u32[]{:S(2)}, u32[]{:S(2)}) collective-permute-start(bf16[128,1536]{1,0:T(8,128)(2,1)} %get-tuple-element.383), channel_id=1, source_target_pairs={{0,2},{2,4},{4,6},{6,0},{1,3},{3,5},{5,7},{7,1},{8,10},{10,12},{12... | collective-permute-start | bytes 1179656 | tf_op jit(solution)/shard_map/ppermute | solution.py:713
  463.8 34.2 %collective-permute-start.62 = (bf16[128,1536]{1,0:T(8,128)(2,1)}, bf16[128,1536]{1,0:T(8,128)(2,1)}, u32[]{:S(2)}, u32[]{:S(2)}) collective-permute-start(bf16[128,1536]{1,0:T(8,128)(2,1)} %get-tuple-element.384), channel_id=1, source_target_pairs={{0,4},{2,6},{4,0},{6,2},{1,5},{3,7},{5,1},{7,3},{8,12},{10,14},{12... | collective-permute-start | bytes 1179656 | tf_op jit(solution)/shard_map/ppermute | solution.py:713
  466.8 34.1 %collective-permute-start.63 = (bf16[128,1536]{1,0:T(8,128)(2,1)}, bf16[128,1536]{1,0:T(8,128)(2,1)}, u32[]{:S(2)}, u32[]{:S(2)}) collective-permute-start(bf16[128,1536]{1,0:T(8,128)(2,1)} %get-tuple-element.385), channel_id=1, source_target_pairs={{0,6},{2,0},{4,2},{6,4},{1,7},{3,1},{5,3},{7,5},{8,14},{10,8},{12,... | collective-permute-start | bytes 1179656 | tf_op jit(solution)/shard_map/ppermute | solution.py:713
  477.7 23.3 %collective-permute-start.59 = (bf16[4,48,1664]{2,1,0:T(8,128)(2,1)}, bf16[4,48,1664]{2,1,0:T(8,128)(2,1)}, u32[]{:S(2)}, u32[]{:S(2)}) collective-permute-start(bf16[4,48,1664]{2,1,0:T(8,128)(2,1)} %pad_maximum_fusion.14), channel_id=1, source_target_pairs={{0,8},{8,0},{16,24},{24,16},{1,9},{9,1},{17,25},{25,17},{2,10},{10... | collective-permute-start | bytes 1916936 | tf_op jit(solution)/shard_map/ppermute | solution.py:769
  478.7 22.3 %collective-permute-start.60 = (bf16[4,48,1664]{2,1,0:T(8,128)(2,1)}, bf16[4,48,1664]{2,1,0:T(8,128)(2,1)}, u32[]{:S(2)}, u32[]{:S(2)}) collective-permute-start(bf16[4,48,1664]{2,1,0:T(8,128)(2,1)} %pad_maximum_fusion.15), channel_id=1, source_target_pairs={{0,16},{8,24},{16,0},{24,8},{1,17},{9,25},{17,1},{25,9},{2,18},{10... | collective-permute-start | bytes 1916936 | tf_op jit(solution)/shard_map/ppermute | solution.py:769
  488.4 21.7 %collective-permute-start.68 = (bf16[256,1536]{1,0:T(8,128)(2,1)S(1)}, bf16[256,1536]{1,0:T(8,128)(2,1)S(1)}, u32[]{:S(2)}, u32[]{:S(2)}) collective-permute-start(bf16[256,1536]{1,0:T(8,128)(2,1)S(1)} %copy-done.33), channel_id=1, source_target_pairs={{0,8},{8,0},{16,24},{24,16},{1,9},{9,1},{17,25},{25,17},{2,10},{10... | collective-permute-start | bytes 2359304 | tf_op jit(solution)/shard_map/ppermute | solution.py:769
  498.0 18.6 %collective-permute-start.69 = (bf16[256,1536]{1,0:T(8,128)(2,1)S(1)}, bf16[256,1536]{1,0:T(8,128)(2,1)S(1)}, u32[]{:S(2)}, u32[]{:S(2)}) collective-permute-start(bf16[256,1536]{1,0:T(8,128)(2,1)S(1)} %copy-done.32), channel_id=1, source_target_pairs={{0,16},{8,24},{16,0},{24,8},{1,17},{9,25},{17,1},{25,9},{2,18},{10... | collective-permute-start | bytes 2359304 | tf_op jit(solution)/shard_map/ppermute | solution.py:769
  (89 other events, 811.6 us)
Sparse Core Ops, SparseCore 0:
  24.4 64.4 all-gather.3
  112.4 102.5 all-gather.5
  332.5 82.7 reduce-scatter.2
  419.4 39.8 reduce-scatter.4
